TPU v7x, 128 devices: a whole 4x4x4 slice. The times are simulated.
128 devices in a mesh: leaf: 32 (over z, y, core), tm: 4 (over x).
Axes of the slice: x: 4, y: 4, z: 4, core: 2. Of those that a mesh axis runs over, the one named last changes fastest.
Arguments:
- coords: float32 [4, 524288], P(None, ('leaf', 'tm')), may hold values from -6 to 6
- direction: float32 [8, 524288], P(None, ('leaf', 'tm')), may hold values from -16 to 16
- iterate: float32 [8, 524288], P(None, ('leaf', 'tm')), may hold values from -6 to 6
- residual: float32 [8, 524288], P(None, ('leaf', 'tm')), may hold values from -24 to 24
- order: int32 [524288], P(('leaf', 'tm')), may hold values from 0 to 4095, as said below
- bases: float32 [1024, 64, 512], P(('leaf', 'tm')), may hold values from -0.25 to 0.25
- transfer: float32 [128, 64, 512], P(('leaf', 'tm')), may hold values from -0.25 to 0.25
- near_list: int32 [1024, 8], P(('leaf', 'tm')), may hold values from 0 to 71, as said below
- near_count: int32 [1024], P(('leaf', 'tm')), may hold values from 1 to 8, as said below
- far_list: int32 [1024, 8], P(('leaf', 'tm')), may hold values from 0 to 71, as said below
- device_skel: int32 [128, 64], P(('leaf', 'tm')), may hold values from 0 to 511, as said below
- inv_scale: float32 [4], replicated, may hold values from 0.5 to 2
- noise: float32 [8], replicated, may hold values from 0.5 to 2
Outputs:
- new_iterate: float32 [8, 524288], P(None, ('leaf', 'tm'))
- new_residual: float32 [8, 524288], P(None, ('leaf', 'tm'))
Inputs may be any that keep to these rules, and one draw needn't show every extreme that they name: `order`: within each device's block the entries are a permutation of 0 to 4095. `near_list`: window indices name only devices inside the mesh; slot 0 is the leaf itself; the entries of one leaf's near and far lists are all distinct. `near_count`: slot 0 is always live; on every device some leaf has all 8 slots live. `far_list`: window indices name only devices inside the mesh, never the leaf itself nor a leaf of its near list. `device_skel`: the 64 slots of one device are distinct.
All inputs are finite; a program needn't handle non-finite values.
Results may differ from a plain program's by a relative error of at most 0.0003.
Values sent between devices are 32-bit elements; how exact they have to be, the bound alone decides.
No kernel may reach another device: no remote copies, remote signals or barrier semaphores. Data moves between devices by JAX's collectives and lax.ppermute only.
A program may use at most 64 MiB of HBM per device.

v0:
```python
import jax
import jax.numpy as jnp
from jax import lax
from jax.sharding import PartitionSpec as P

EXACT = lax.Precision.HIGHEST
ROOT_THREE = 1.7320508075688772


def extended(shard, sides, width):
    for axis, dim in sides:
        devices, length = (lax.axis_size(axis), shard.shape[dim])
        up = [(i, (i + 1) % devices) for i in range(devices - 1)]
        down = [(j, i) for i, j in up]
        last = lax.slice_in_dim(shard, length - width, length, axis=dim)
        initial = lax.slice_in_dim(shard, 0, width, axis=dim)
        before = lax.ppermute(last, axis, up)
        after = lax.ppermute(initial, axis, down)
        shard = jnp.concatenate([before, shard, after], axis=dim)
    return shard


def matern(targets, sources, inv_scale):
    scaled = (targets[..., :, :, None] - sources[..., :, None, :]) * inv_scale[:, None, None]
    distance = jnp.sqrt(jnp.sum(scaled * scaled, axis=-3))
    return (1.0 + ROOT_THREE * distance) * jnp.exp(-ROOT_THREE * distance)


def neighbourhood(block):
    cube = block[None, None]
    cube = extended(cube, (("leaf", 0), ("tm", 1)), 1)
    return cube.reshape((9,) + block.shape)


def shards(
    coords,
    direction,
    iterate,
    residual,
    order,
    bases,
    transfer,
    near_list,
    near_count,
    far_list,
    device_skel,
    inv_scale,
    noise,
):
    leaf_dev, rank, leaf_pts = bases.shape
    rhs_count = direction.shape[0]
    near_slots = near_list.shape[1]
    leaf_x = coords[:, order]
    leaf_p = direction[:, order]
    own_x = leaf_x.reshape(4, leaf_dev, leaf_pts)
    own_p = leaf_p.reshape(rhs_count, leaf_dev, leaf_pts)
    skel_coef = jnp.einsum("rlp,lsp->lrs", own_p, bases, precision=EXACT)
    window = neighbourhood(jnp.concatenate([leaf_x, leaf_p], axis=0))
    coef_cube = extended(skel_coef.reshape(1, 1, 1, -1), (("leaf", 0), ("tm", 1)), 1)
    win_coef = coef_cube.reshape(9, leaf_dev, rhs_count, rank)
    win_x = window[:, :4].reshape(9, 4, leaf_dev, leaf_pts)
    win_p = window[:, 4 : 4 + rhs_count].reshape(9, rhs_count, leaf_dev, leaf_pts)
    near_block = near_list // leaf_dev
    near_within = near_list % leaf_dev
    source_x = win_x[near_block, :, near_within]
    source_p = win_p[near_block, :, near_within]
    targets = own_x.transpose(1, 0, 2)
    live = (jnp.arange(near_slots, dtype=jnp.int32)[None, :] < near_count[:, None]).astype(
        jnp.float32
    )

    def near_leaf(item):
        target_x, tile_x, tile_p, weights = item
        kernel = matern(target_x, tile_x, inv_scale)
        return jnp.einsum("smn,srn,s->rm", kernel, tile_p, weights, precision=EXACT)

    near_field = lax.map(near_leaf, (targets, source_x, source_p, live))
    far_block = far_list // leaf_dev
    far_within = far_list % leaf_dev
    far_x = win_x[far_block, :, far_within, :rank]
    far_coef = win_coef[far_block, far_within]
    own_skel = targets[:, :, :rank]
    far_kernel = matern(own_skel[:, None], far_x, inv_scale)
    leaf_far = jnp.einsum("lfmn,lfrn->lrm", far_kernel, far_coef, precision=EXACT)
    slot_x = own_x[:, :, :rank].reshape(4, leaf_dev * rank)
    slot_coef = skel_coef.transpose(1, 0, 2).reshape(rhs_count, leaf_dev * rank)
    device_x = slot_x[:, device_skel[0]]
    device_w = jnp.einsum("rl,sl->rs", slot_coef, transfer[0], precision=EXACT)
    packed = jnp.concatenate([device_x, device_w], axis=0)[None]
    place_a = lax.axis_index("leaf")
    place_b = lax.axis_index("tm")
    tm_size = lax.axis_size("tm")
    piece = lax.all_gather(packed, ("leaf", "tm"), axis=0, tiled=True)
    source_ids = jnp.arange(piece.shape[0], dtype=jnp.int32)
    distant = (
        (jnp.abs(source_ids // tm_size - place_a) > 1)
        | (jnp.abs(source_ids % tm_size - place_b) > 1)
    ).astype(jnp.float32)
    kernel = matern(device_x, piece[:, :4], inv_scale)
    device_far = jnp.einsum("cmn,crn,c->rm", kernel, piece[:, 4:], distant, precision=EXACT)
    pushed = jnp.einsum("rs,sl->rl", device_far, transfer[0], precision=EXACT)
    pushed = pushed.reshape(rhs_count, leaf_dev, rank).transpose(1, 0, 2)
    leaf_out = near_field + jnp.einsum("lrs,lsp->lrp", leaf_far + pushed, bases, precision=EXACT)
    flat_out = leaf_out.transpose(1, 0, 2).reshape(rhs_count, leaf_dev * leaf_pts)
    kernel_part = jnp.zeros_like(direction).at[:, order].set(flat_out)
    image = kernel_part + noise[:, None] * direction
    along, squares = lax.psum(
        (jnp.sum(residual * image, axis=1), jnp.sum(image * image, axis=1)), ("leaf", "tm")
    )
    alpha = along / (squares + 1e-06)
    return (iterate + alpha[:, None] * direction, residual - alpha[:, None] * image)


def solution(mesh):
    return jax.shard_map(
        shards,
        mesh=mesh,
        in_specs=(
            P(None, ("leaf", "tm")),
            P(None, ("leaf", "tm")),
            P(None, ("leaf", "tm")),
            P(None, ("leaf", "tm")),
            P(("leaf", "tm")),
            P(("leaf", "tm"), None, None),
            P(("leaf", "tm"), None, None),
            P(("leaf", "tm"), None),
            P(("leaf", "tm")),
            P(("leaf", "tm"), None),
            P(("leaf", "tm"), None),
            P(),
            P(),
        ),
        out_specs=(P(None, ("leaf", "tm")), P(None, ("leaf", "tm"))),
        check_vma=False,
    )
```

profile of v0, /device:TPU:1, one launch (start us, length us, event | category | flops | bytes accessed | tf_op | source)
XLA Modules:
  0.0 465.9 jit_solution(11412745094327184548)
XLA Ops:
  2.1 2.9 copy.129
  4.9 12.4 %gather_fusion.1 = f32[4096,8]{1,0:T(8,128)S(1)} fusion(f32[8,4096]{0,1:T(8,128)} %copy.129, s32[4096]{0:T(1024)S(1)} %get-tuple-element.76), kind=kCustom, calls=%fused_computation.1 | custom fusion | bytes 278528 | tf_op jit(solution)/shard_map/gather | solution.py:54
  17.3 3.4 fusion.70
  20.8 3.3 collective-permute-start.5
  24.1 3.2 collective-permute-start.4
  27.4 2.0 copy.128
  29.3 12.4 %gather_fusion = f32[4096,4]{1,0:T(8,128)S(1)} fusion(f32[4,4096]{0,1:T(8,128)} %copy.128, s32[4096]{0:T(1024)S(1)} %get-tuple-element.76), kind=kCustom, calls=%fused_computation | custom fusion | bytes 147456 | tf_op jit(solution)/shard_map/gather | solution.py:53
  42.9 2.2 copy.131
  46.8 1.9 collective-permute-start.1
  48.8 3.6 collective-permute-start
  55.1 1.5 gather_fusion.6
  58.7 65.8 %all-gather.1 = f32[128,12,64]{2,1,0:T(8,128)S(1)} all-gather(f32[1,12,64]{2,1,0:T(8,128)S(1)} %maximum_bitcast_fusion), channel_id=2, replica_groups=mesh['leaf'=32,'tm'=4] {'leaf','tm'}, dimensions={0}, use_global_device_ids=true | all-gather | bytes 396288 | tf_op jit(solution)/shard_map/all_gather | solution.py:93
  127.3 2.2 multiply_reduce_fusion.1
  129.5 2.2 exponential_multiply_fusion
  131.7 5.6 %copy.144 = f32[128,64,64]{2,1,0:T(8,128)} copy(f32[128,64,64]{0,2,1:T(8,128)} %exponential_multiply_fusion) | data formatting | bytes 4194304 | tf_op jit(solution)/shard_map/mul | solution.py:26
  137.3 6.5 %fusion.39 = f32[8,64,1]{1,0,2:T(8,128)} fusion(f32[128,64,64]{2,1,0:T(8,128)} %copy.144, f32[128,12,64]{2,1,0:T(8,128)} %copy-done.2, f32[128]{0:T(128)S(1)} %or_convert_fusion), kind=kOutput, calls=%fused_computation.53 | convolution fusion | flops 50397184 | bytes 4721152 | tf_op jit(solution)/shard_map/cmn,crn,c->rm/dot_general | solution.py:100
  146.3 1.6 constant_dynamic-update-slice_fusion.2
  148.8 1.6 constant_dynamic-update-slice_fusion
  151.7 4.8 %collective-permute-start.2 = (f32[3,1,12,4096]{3,1,2,0:T(1,128)}, f32[3,1,12,4096]{3,1,2,0:T(1,128)}, u32[]{:S(2)}, u32[]{:S(2)}) collective-permute-start(f32[3,1,12,4096]{3,1,2,0:T(1,128)} %constant_dynamic-update-slice_fusion), channel_id=1, source_target_pairs={{0,1},{1,2},{2,3},{4,5},{5,6},{6,7},{8,9},{9,10},{10,11},{12,13},{... | collective-permute-start | bytes 1769480 | tf_op jit(solution)/shard_map/ppermute | solution.py:17
  159.1 4.0 collective-permute-start.6
  166.1 1.7 collective-permute-done.7
  170.2 1.5 gather_fusion.4
  176.8 1.8 gather_fusion.2
  179.6 180.9 %while.10 = (s32[]{:T(128)}, f32[8,8,512]{2,1,0:T(8,128)}, f32[8,8,8,512]{3,2,1,0:T(8,128)}, f32[8,8]{1,0:T(8,128)S(1)}, f32[8,4,512]{2,1,0:T(4,128)}, /*index=5...) while((s32[]{:T(128)}, f32[8,8,512]{2,1,0:T(8,128)}, f32[8,8,8,512]{3,2,1,0:T(8,128)}, ...), condition=%wide.region_2.3_spmd, body=%wide.region_0.2_spmd.sunk | while | flops 241205248 | bytes 17147096 | solution.py:77
  180.7 8.0 %multiply_reduce_fusion.6 = f32[8,512,512]{2,1,0:T(8,128)} fusion(f32[4]{0:T(128)S(1)} %get-tuple-element.145, f32[8,4,512]{2,1,0:T(4,128)S(1)} %dynamic-slice_bitcast_fusion.4, f32[4,512]{1,0:T(4,128)S(1)} %dynamic-slice_bitcast_fusion.5), kind=kLoop, calls=%fused_computation.8.clone.1 | loop fusion | flops 31457280 | bytes 8462352 | tf_op jit(solution)/shard_map/while/body/eval_jaxpr/reduce_sum | solution.py:25
  188.7 13.8 %fusion.85 = f32[8,8,512]{2,1,0:T(8,128)} fusion(f32[8,8,512]{2,1,0:T(8,128)} %get-tuple-element.132, s32[]{:T(128)S(6)} %copy.156, f32[8,512,512]{2,1,0:T(8,128)} %multiply_reduce_fusion.6, f32[8,8,8,512]{3,2,1,0:T(8,128)} %get-tuple-element.141, f32[8]{0:T(128)S(1)} %fusion.84), kind=kOutput, calls=%fused_computation.20.clone.1 | convolution fusion | flops 209747968 | bytes 8537120 | tf_op jit(solution)/shard_map/while/body/eval_jaxpr/smn,srn,s->rm/dot_general | solution.py:75
  203.2 8.0 %multiply_reduce_fusion.6 = f32[8,512,512]{2,1,0:T(8,128)} fusion(f32[4]{0:T(128)S(1)} %get-tuple-element.145, f32[8,4,512]{2,1,0:T(4,128)S(1)} %dynamic-slice_bitcast_fusion.4, f32[4,512]{1,0:T(4,128)S(1)} %dynamic-slice_bitcast_fusion.5), kind=kLoop, calls=%fused_computation.8.clone.1 | loop fusion | flops 31457280 | bytes 8462352 | tf_op jit(solution)/shard_map/while/body/eval_jaxpr/reduce_sum | solution.py:25
  211.3 13.8 %fusion.85 = f32[8,8,512]{2,1,0:T(8,128)} fusion(f32[8,8,512]{2,1,0:T(8,128)} %get-tuple-element.132, s32[]{:T(128)S(6)} %copy.156, f32[8,512,512]{2,1,0:T(8,128)} %multiply_reduce_fusion.6, f32[8,8,8,512]{3,2,1,0:T(8,128)} %get-tuple-element.141, f32[8]{0:T(128)S(1)} %fusion.84), kind=kOutput, calls=%fused_computation.20.clone.1 | convolution fusion | flops 209747968 | bytes 8537120 | tf_op jit(solution)/shard_map/while/body/eval_jaxpr/smn,srn,s->rm/dot_general | solution.py:75
  225.8 8.0 %multiply_reduce_fusion.6 = f32[8,512,512]{2,1,0:T(8,128)} fusion(f32[4]{0:T(128)S(1)} %get-tuple-element.145, f32[8,4,512]{2,1,0:T(4,128)S(1)} %dynamic-slice_bitcast_fusion.4, f32[4,512]{1,0:T(4,128)S(1)} %dynamic-slice_bitcast_fusion.5), kind=kLoop, calls=%fused_computation.8.clone.1 | loop fusion | flops 31457280 | bytes 8462352 | tf_op jit(solution)/shard_map/while/body/eval_jaxpr/reduce_sum | solution.py:25
  233.8 13.8 %fusion.85 = f32[8,8,512]{2,1,0:T(8,128)} fusion(f32[8,8,512]{2,1,0:T(8,128)} %get-tuple-element.132, s32[]{:T(128)S(6)} %copy.156, f32[8,512,512]{2,1,0:T(8,128)} %multiply_reduce_fusion.6, f32[8,8,8,512]{3,2,1,0:T(8,128)} %get-tuple-element.141, f32[8]{0:T(128)S(1)} %fusion.84), kind=kOutput, calls=%fused_computation.20.clone.1 | convolution fusion | flops 209747968 | bytes 8537120 | tf_op jit(solution)/shard_map/while/body/eval_jaxpr/smn,srn,s->rm/dot_general | solution.py:75
  248.3 8.0 %multiply_reduce_fusion.6 = f32[8,512,512]{2,1,0:T(8,128)} fusion(f32[4]{0:T(128)S(1)} %get-tuple-element.145, f32[8,4,512]{2,1,0:T(4,128)S(1)} %dynamic-slice_bitcast_fusion.4, f32[4,512]{1,0:T(4,128)S(1)} %dynamic-slice_bitcast_fusion.5), kind=kLoop, calls=%fused_computation.8.clone.1 | loop fusion | flops 31457280 | bytes 8462352 | tf_op jit(solution)/shard_map/while/body/eval_jaxpr/reduce_sum | solution.py:25
  256.3 13.8 %fusion.85 = f32[8,8,512]{2,1,0:T(8,128)} fusion(f32[8,8,512]{2,1,0:T(8,128)} %get-tuple-element.132, s32[]{:T(128)S(6)} %copy.156, f32[8,512,512]{2,1,0:T(8,128)} %multiply_reduce_fusion.6, f32[8,8,8,512]{3,2,1,0:T(8,128)} %get-tuple-element.141, f32[8]{0:T(128)S(1)} %fusion.84), kind=kOutput, calls=%fused_computation.20.clone.1 | convolution fusion | flops 209747968 | bytes 8537120 | tf_op jit(solution)/shard_map/while/body/eval_jaxpr/smn,srn,s->rm/dot_general | solution.py:75
  270.9 8.0 %multiply_reduce_fusion.6 = f32[8,512,512]{2,1,0:T(8,128)} fusion(f32[4]{0:T(128)S(1)} %get-tuple-element.145, f32[8,4,512]{2,1,0:T(4,128)S(1)} %dynamic-slice_bitcast_fusion.4, f32[4,512]{1,0:T(4,128)S(1)} %dynamic-slice_bitcast_fusion.5), kind=kLoop, calls=%fused_computation.8.clone.1 | loop fusion | flops 31457280 | bytes 8462352 | tf_op jit(solution)/shard_map/while/body/eval_jaxpr/reduce_sum | solution.py:25
  278.9 13.8 %fusion.85 = f32[8,8,512]{2,1,0:T(8,128)} fusion(f32[8,8,512]{2,1,0:T(8,128)} %get-tuple-element.132, s32[]{:T(128)S(6)} %copy.156, f32[8,512,512]{2,1,0:T(8,128)} %multiply_reduce_fusion.6, f32[8,8,8,512]{3,2,1,0:T(8,128)} %get-tuple-element.141, f32[8]{0:T(128)S(1)} %fusion.84), kind=kOutput, calls=%fused_computation.20.clone.1 | convolution fusion | flops 209747968 | bytes 8537120 | tf_op jit(solution)/shard_map/while/body/eval_jaxpr/smn,srn,s->rm/dot_general | solution.py:75
  293.4 8.0 %multiply_reduce_fusion.6 = f32[8,512,512]{2,1,0:T(8,128)} fusion(f32[4]{0:T(128)S(1)} %get-tuple-element.145, f32[8,4,512]{2,1,0:T(4,128)S(1)} %dynamic-slice_bitcast_fusion.4, f32[4,512]{1,0:T(4,128)S(1)} %dynamic-slice_bitcast_fusion.5), kind=kLoop, calls=%fused_computation.8.clone.1 | loop fusion | flops 31457280 | bytes 8462352 | tf_op jit(solution)/shard_map/while/body/eval_jaxpr/reduce_sum | solution.py:25
  301.4 13.8 %fusion.85 = f32[8,8,512]{2,1,0:T(8,128)} fusion(f32[8,8,512]{2,1,0:T(8,128)} %get-tuple-element.132, s32[]{:T(128)S(6)} %copy.156, f32[8,512,512]{2,1,0:T(8,128)} %multiply_reduce_fusion.6, f32[8,8,8,512]{3,2,1,0:T(8,128)} %get-tuple-element.141, f32[8]{0:T(128)S(1)} %fusion.84), kind=kOutput, calls=%fused_computation.20.clone.1 | convolution fusion | flops 209747968 | bytes 8537120 | tf_op jit(solution)/shard_map/while/body/eval_jaxpr/smn,srn,s->rm/dot_general | solution.py:75
  315.9 8.0 %multiply_reduce_fusion.6 = f32[8,512,512]{2,1,0:T(8,128)} fusion(f32[4]{0:T(128)S(1)} %get-tuple-element.145, f32[8,4,512]{2,1,0:T(4,128)S(1)} %dynamic-slice_bitcast_fusion.4, f32[4,512]{1,0:T(4,128)S(1)} %dynamic-slice_bitcast_fusion.5), kind=kLoop, calls=%fused_computation.8.clone.1 | loop fusion | flops 31457280 | bytes 8462352 | tf_op jit(solution)/shard_map/while/body/eval_jaxpr/reduce_sum | solution.py:25
  324.0 13.8 %fusion.85 = f32[8,8,512]{2,1,0:T(8,128)} fusion(f32[8,8,512]{2,1,0:T(8,128)} %get-tuple-element.132, s32[]{:T(128)S(6)} %copy.156, f32[8,512,512]{2,1,0:T(8,128)} %multiply_reduce_fusion.6, f32[8,8,8,512]{3,2,1,0:T(8,128)} %get-tuple-element.141, f32[8]{0:T(128)S(1)} %fusion.84), kind=kOutput, calls=%fused_computation.20.clone.1 | convolution fusion | flops 209747968 | bytes 8537120 | tf_op jit(solution)/shard_map/while/body/eval_jaxpr/smn,srn,s->rm/dot_general | solution.py:75
  338.5 8.0 %multiply_reduce_fusion.6 = f32[8,512,512]{2,1,0:T(8,128)} fusion(f32[4]{0:T(128)S(1)} %get-tuple-element.145, f32[8,4,512]{2,1,0:T(4,128)S(1)} %dynamic-slice_bitcast_fusion.4, f32[4,512]{1,0:T(4,128)S(1)} %dynamic-slice_bitcast_fusion.5), kind=kLoop, calls=%fused_computation.8.clone.1 | loop fusion | flops 31457280 | bytes 8462352 | tf_op jit(solution)/shard_map/while/body/eval_jaxpr/reduce_sum | solution.py:25
  346.5 13.8 %fusion.85 = f32[8,8,512]{2,1,0:T(8,128)} fusion(f32[8,8,512]{2,1,0:T(8,128)} %get-tuple-element.132, s32[]{:T(128)S(6)} %copy.156, f32[8,512,512]{2,1,0:T(8,128)} %multiply_reduce_fusion.6, f32[8,8,8,512]{3,2,1,0:T(8,128)} %get-tuple-element.141, f32[8]{0:T(128)S(1)} %fusion.84), kind=kOutput, calls=%fused_computation.20.clone.1 | convolution fusion | flops 209747968 | bytes 8537120 | tf_op jit(solution)/shard_map/while/body/eval_jaxpr/smn,srn,s->rm/dot_general | solution.py:75
  360.5 10.5 %copy.139 = f32[9,4,8,512]{1,2,0,3:T(8,128)} copy(f32[9,4,8,512]{3,2,1,0:T(8,128)S(1)} %reshape.81) | data formatting | bytes 1179648 | tf_op jit(solution)/shard_map/reshape | solution.py:61
  370.9 4.8 %gather_fusion.5 = f32[64,4,64]{1,0,2:T(8,128)S(1)} fusion(f32[9,4,8,512]{1,2,0,3:T(8,128)} %copy.139, s32[64]{0:T(128)S(1)} %reshape.116), kind=kCustom, calls=%fused_computation.5 | custom fusion | bytes 131840 | tf_op jit(solution)/shard_map/gather | solution.py:80
  377.0 2.8 multiply_reduce_fusion.2
  379.8 2.6 fusion.30
  383.8 2.0 copy.146
  385.7 11.4 %scatter_custom_fusion = f32[8,4096]{0,1:T(8,128)S(1)} fusion(s32[4096]{0:T(1024)} %get-tuple-element.77, f32[4096,8]{1,0:T(8,128)} %copy.146, f32[]{:T(128)} %constant.108.clone.1), kind=kCustom, calls=%fused_computation.50 | custom fusion | bytes 131584 | tf_op jit(solution)/shard_map/scatter | solution.py:105
  398.0 66.1 %all-reduce = (f32[8]{0:T(128)S(1)}, f32[8]{0:T(128)S(1)}) all-reduce(f32[8]{0:T(128)S(1)} %get-tuple-element.58, f32[8]{0:T(128)S(1)} %get-tuple-element.57), channel_id=1, replica_groups=mesh['leaf'=32,'tm'=4] {'leaf','tm'}, use_global_device_ids=true, to_apply=%region_7.8 | all-reduce | flops 16 | bytes 128 | tf_op jit(solution)/shard_map/psum | solution.py:107
  464.0 1.7 multiply_subtract_fusion
  (116 shorter events, 39.6 us)
Async XLA Ops:
  0.6 16.7 %copy-start = (f32[8,64,512]{2,1,0:T(8,128)S(1)}, f32[8,64,512]{2,1,0:T(8,128)}, u32[]{:S(2)}) copy-start(f32[8,64,512]{2,1,0:T(8,128)} %param.20) | copy-start | bytes 3145732
  4.9 22.4 %copy-start.11 = (f32[4,4096]{1,0:T(4,128)S(1)}, f32[4,4096]{1,0:T(4,128)}, u32[]{:S(2)}) copy-start(f32[4,4096]{1,0:T(4,128)} %param.15) | copy-start | bytes 196612
  17.3 10.0 %copy-start.1 = (f32[4096,8]{1,0:T(8,128)}, f32[4096,8]{1,0:T(8,128)S(1)}, u32[]{:S(2)}) copy-start(f32[4096,8]{1,0:T(8,128)S(1)} %gather_fusion.1) | copy-start | bytes 393220
  20.7 22.2 %copy-start.7 = (f32[8,8,64]{2,1,0:T(8,128)}, f32[8,8,64]{2,1,0:T(8,128)S(1)}, u32[]{:S(2)}) copy-start(f32[8,8,64]{2,1,0:T(8,128)S(1)} %fusion.70) | copy-start | bytes 49156
  20.8 135.7 %collective-permute-start.5 = (f32[1,1,1,4096]{3,2,1,0:T(1,128)S(1)}, f32[1,1,1,4096]{3,2,1,0:T(1,128)}, u32[]{:S(2)}, u32[]{:S(2)}) collective-permute-start(f32[1,1,1,4096]{3,2,1,0:T(1,128)S(1)} %reshape.83), channel_id=1, source_target_pairs={{4,0},{8,4},{12,8},{16,12},{20,16},{24,20},{28,24},{32,28},{36,32}... | collective-permute-start | bytes 49160 | tf_op jit(solution)/shard_map/ppermute | solution.py:18
  24.1 120.3 %collective-permute-start.4 = (f32[1,1,1,4096]{3,2,1,0:T(1,128)S(1)}, f32[1,1,1,4096]{3,2,1,0:T(1,128)}, u32[]{:S(2)}, u32[]{:S(2)}) collective-permute-start(f32[1,1,1,4096]{3,2,1,0:T(1,128)S(1)} %reshape.83), channel_id=1, source_target_pairs={{0,4},{4,8},{8,12},{12,16},{16,20},{20,24},{24,28},{28,32},{32,36}... | collective-permute-start | bytes 49160 | tf_op jit(solution)/shard_map/ppermute | solution.py:17
  46.8 102.0 %collective-permute-start.1 = (f32[1,1,12,4096]{3,1,2,0:T(1,128)}, f32[1,1,12,4096]{3,1,2,0:T(1,128)}, u32[]{:S(2)}, u32[]{:S(2)}) collective-permute-start(f32[1,1,12,4096]{3,1,2,0:T(1,128)} %broadcast_in_dim.30), channel_id=1, source_target_pairs={{4,0},{8,4},{12,8},{16,12},{20,16},{24,20},{28,24},{32,28},{36,32}... | collective-permute-start | bytes 589832 | tf_op jit(solution)/shard_map/ppermute | solution.py:18
  48.8 97.6 %collective-permute-start = (f32[1,1,12,4096]{3,1,2,0:T(1,128)}, f32[1,1,12,4096]{3,1,2,0:T(1,128)}, u32[]{:S(2)}, u32[]{:S(2)}) collective-permute-start(f32[1,1,12,4096]{3,1,2,0:T(1,128)} %broadcast_in_dim.30), channel_id=1, source_target_pairs={{0,4},{4,8},{8,12},{12,16},{16,20},{20,24},{24,28},{28,32},{32,36}... | collective-permute-start | bytes 589832 | tf_op jit(solution)/shard_map/ppermute | solution.py:17
  56.7 67.8 %copy-start.13 = (f32[64,4]{0,1:T(4,128)}, f32[64,4]{0,1:T(4,128)S(1)}, u32[]{:S(2)}) copy-start(f32[64,4]{0,1:T(4,128)S(1)} %copy.141) | copy-start | bytes 3076
  124.5 1.0 copy-start.2
  137.3 6.5 %copy-start.16 = (s32[8,8]{1,0:T(8,128)S(1)}, s32[8,8]{1,0:T(8,128)}, u32[]{:S(2)}) copy-start(s32[8,8]{1,0:T(8,128)} %param.24) | copy-start | bytes 772
  137.3 25.9 %copy-start.18 = (s32[8]{0:T(128)S(1)}, s32[8]{0:T(128)}, u32[]{:S(2)}) copy-start(s32[8]{0:T(128)} %param.23) | copy-start | bytes 100
  143.8 20.9 %copy-start.5 = (f32[1,64,512]{2,1,0:T(8,128)S(1)}, f32[1,64,512]{2,1,0:T(8,128)}, u32[]{:S(2)}) copy-start(f32[1,64,512]{2,1,0:T(8,128)} %param.21) | copy-start | bytes 393220
  148.8 15.8 %copy-start.14 = (s32[8,8]{1,0:T(8,128)S(1)}, s32[8,8]{1,0:T(8,128)}, u32[]{:S(2)}) copy-start(s32[8,8]{1,0:T(8,128)} %fusion.50) | copy-start | bytes 772
  150.4 22.6 %collective-permute-start.3 = (f32[3,1,12,4096]{3,1,2,0:T(1,128)}, f32[3,1,12,4096]{3,1,2,0:T(1,128)}, u32[]{:S(2)}, u32[]{:S(2)}) collective-permute-start(f32[3,1,12,4096]{3,1,2,0:T(1,128)} %constant_dynamic-update-slice_fusion), channel_id=1, source_target_pairs={{1,0},{2,1},{3,2},{5,4},{6,5},{7,6},{9,8},{10,9},{11,10},{13,12},{... | collective-permute-start | bytes 1769480 | tf_op jit(solution)/shard_map/ppermute | solution.py:18
  151.7 22.8 %collective-permute-start.2 = (f32[3,1,12,4096]{3,1,2,0:T(1,128)}, f32[3,1,12,4096]{3,1,2,0:T(1,128)}, u32[]{:S(2)}, u32[]{:S(2)}) collective-permute-start(f32[3,1,12,4096]{3,1,2,0:T(1,128)} %constant_dynamic-update-slice_fusion), channel_id=1, source_target_pairs={{0,1},{1,2},{2,3},{4,5},{5,6},{6,7},{8,9},{9,10},{10,11},{12,13},{... | collective-permute-start | bytes 1769480 | tf_op jit(solution)/shard_map/ppermute | solution.py:17
  157.9 10.0 %collective-permute-start.7 = (f32[3,1,1,4096]{3,2,1,0:T(1,128)}, f32[3,1,1,4096]{3,2,1,0:T(1,128)S(1)}, u32[]{:S(2)}, u32[]{:S(2)}) collective-permute-start(f32[3,1,1,4096]{3,2,1,0:T(1,128)} %constant_dynamic-update-slice_fusion.3), channel_id=1, source_target_pairs={{1,0},{2,1},{3,2},{5,4},{6,5},{7,6},{9,8},{10,9},{11,10},{13,12},{... | collective-permute-start | bytes 147464 | tf_op jit(solution)/shard_map/ppermute | solution.py:18
  159.1 9.6 %collective-permute-start.6 = (f32[3,1,1,4096]{3,2,1,0:T(1,128)}, f32[3,1,1,4096]{3,2,1,0:T(1,128)S(1)}, u32[]{:S(2)}, u32[]{:S(2)}) collective-permute-start(f32[3,1,1,4096]{3,2,1,0:T(1,128)} %constant_dynamic-update-slice_fusion.3), channel_id=1, source_target_pairs={{0,1},{1,2},{2,3},{4,5},{5,6},{6,7},{8,9},{9,10},{10,11},{12,13},{... | collective-permute-start | bytes 147464 | tf_op jit(solution)/shard_map/ppermute | solution.py:17
  163.8 10.7 %copy-start.9 = (f32[4,8,512]{2,0,1:T(4,128)}, f32[4,8,512]{2,0,1:T(4,128)S(1)}, u32[]{:S(2)}) copy-start(f32[4,8,512]{2,0,1:T(4,128)S(1)} %copy.136) | copy-start | bytes 196612
  176.4 3.2 copy-start.12
  375.8 4.0 copy-start.8
  379.7 2.7 copy-start.4
  379.8 2.7 copy-start.15
  379.8 3.4 copy-start.10
  385.7 12.0 %copy-start.3 = (f32[8,4096]{1,0:T(8,128)S(1)}, f32[8,4096]{1,0:T(8,128)}, u32[]{:S(2)}) copy-start(f32[8,4096]{1,0:T(8,128)} %param.16) | copy-start | bytes 393220
  385.7 12.0 %copy-start.6 = (f32[8,4096]{1,0:T(8,128)S(1)}, f32[8,4096]{1,0:T(8,128)}, u32[]{:S(2)}) copy-start(f32[8,4096]{1,0:T(8,128)} %param.18) | copy-start | bytes 393220
  385.7 12.0 %copy-start.17 = (f32[8]{0:T(128)S(1)}, f32[8]{0:T(128)}, u32[]{:S(2)}) copy-start(f32[8]{0:T(128)} %param.27) | copy-start | bytes 100
where the time goes:
time: 472 us; the launch traced here: 466 us
  blocking collectives  132 us (28%)
  matrix products  125 us (26%)
  local copies, waits for them, and re-layouts  101 us (21%)
  other arithmetic  79.6 us (17%)
  starting transfers between devices  23.4 us (5%)
    dot_general x8, matrix products, near_leaf(): return jnp.einsum('smn,srn,s->rm', kernel, tile_p, weights, precision=EXACT)  111 us
    reduce_sum x10, other arithmetic, matern(): distance = jnp.sqrt(jnp.sum(scaled * scaled, axis=-3))  69 us
    psum x1, blocking collectives, shards(): lax.psum((jnp.sum(residual * image, axis=1), jnp.sum(image * image, axis=...  66.1 us
    all_gather x1, blocking collectives, shards(): piece = lax.all_gather(packed, ('leaf', 'tm'), axis=0, tiled=True)  65.8 us
    ppermute x4, starting transfers between devices, extended(): before = lax.ppermute(last, axis, up)  15.6 us
    gather x2, local copies, waits for them, and re-layouts, shards(): leaf_p = direction[:, order]  14.5 us
    gather x2, local copies, waits for them, and re-layouts, shards(): leaf_x = coords[:, order]  13.6 us
    scatter x2, local copies, waits for them, and re-layouts, shards(): kernel_part = jnp.zeros_like(direction).at[:, order].set(flat_out)  12 us
  transfers between devices with their start and end apart: 8, of which 2 were waited for; matrix products, arithmetic and copies ran while one was open for 13% of the time, Pallas kernels for 0%

commit v1 on v0

v1 whole, which is shorter than its diff:
```python
import functools
import math

import jax
import jax.numpy as jnp
from jax import lax
from jax.experimental import pallas as pl
from jax.experimental.pallas import tpu as pltpu
from jax.sharding import PartitionSpec as P

F32 = jnp.float32
BF16 = jnp.bfloat16
EXACT = lax.Precision.HIGHEST
LN2 = math.log(2.0)
LOG2E = 1.0 / LN2
UNIT = math.sqrt(3.0) * LOG2E
VMEM = pl.BlockSpec(memory_space=pltpu.VMEM)
SMEM = pl.BlockSpec(memory_space=pltpu.SMEM)
LIMIT = 50 * 2**20


def params(**kw):
    return pltpu.CompilerParams(vmem_limit_bytes=LIMIT, **kw)


def contract(a, b, dims, precision=None):
    return lax.dot_general(
        a, b, ((dims[0], dims[1]), ((), ())), precision=precision, preferred_element_type=F32
    )


def rounded(x):
    return x.astype(BF16).astype(F32)


def row_ids(shape):
    return lax.broadcasted_iota(jnp.int32, shape, 0)


def lane_ids(shape):
    return lax.broadcasted_iota(jnp.int32, shape, 1)


def features(xx, want_source, want_target):
    row = row_ids(xx.shape)
    high = rounded(xx)
    low = rounded(xx - high)
    held = high + low
    square = held * held
    square = square + pltpu.roll(square, 1, 0)
    norm = square + pltpu.roll(square, 2, 0)
    n0 = rounded(norm)
    rest = norm - n0
    n1 = rounded(rest)
    n2 = rest - n1
    zero = jnp.zeros_like(xx)
    out = []
    if want_source:
        parts = jnp.where(row < 4, high, low)
        tail = jnp.where(row == 0, n0, jnp.where(row == 1, n1, jnp.where(row == 2, n2, jnp.where(row < 6, 1.0, 0.0))))
        out.append(jnp.concatenate([parts, parts, tail, zero], axis=0).astype(BF16))
    if want_target:
        tail = jnp.where(row < 3, 1.0, jnp.where(row == 3, n0, jnp.where(row == 4, n1, jnp.where(row == 5, n2, 0.0))))
        out.append(jnp.concatenate([-2.0 * high, -2.0 * low, tail, zero], axis=0).astype(BF16))
    return out


def halves(w):
    high = rounded(w)
    return jnp.concatenate([high, w - high], axis=0).astype(BF16)


def kernel_of(z):
    z = jnp.maximum(z, 1e-30)
    v = z * lax.rsqrt(z)
    return (v + LOG2E) * jnp.exp2(-v)


def split(k):
    high = k.astype(BF16)
    return high, (k - high.astype(F32)).astype(BF16)


def gather_lanes(chunks, ids):
    lane = ids & 127
    chunk = ids >> 7
    picked = [None] * len(chunks)
    for s in range(len(chunks[0])):
        here = chunk == s
        for i, source in enumerate(chunks):
            got = jnp.take_along_axis(source[s](), lane, axis=1, mode="promise_in_bounds")
            picked[i] = got if s == 0 else jnp.where(here, got, picked[i])
    return picked


def upward_body(order_ref, x_ref, p_ref, bases_ref, transfer_ref, skel_ref, halo_ref, node_ref, inv_ref, xx, first, slot, tally):
    leaf_dev, rank, leaf_pts = bases_ref.shape
    points = x_ref.shape[1]
    chunks = points // 128
    per_leaf = leaf_pts // 128
    xx[0:4, :] = x_ref[...]
    xx[4:8, :] = x_ref[...]
    tally[...] = jnp.zeros_like(tally)

    def loads(ref):
        return [lambda s=s: ref[:, s * 128 : (s + 1) * 128] for s in range(chunks)]

    def two_leaves(g, _):
        kept = []
        for h in range(2):
            leaf = 2 * g + h
            for j in range(per_leaf):
                c = leaf * per_leaf + j
                ids = order_ref[pl.ds(c, 1), :]
                got_x, got_p = gather_lanes([loads(xx), loads(p_ref)], jnp.broadcast_to(ids, (8, 128)))
                kept.append(got_x)
                halo_ref[pl.ds(pl.multiple_of(32 + leaf * 8, 8), 8), j * 128 : (j + 1) * 128] = got_p
                low = jnp.where(row_ids((128, 128)) == (ids & 127), 1.0, 0.0).astype(BF16)
                row = row_ids((chunks, 128)) == (ids >> 7)
                lane = lane_ids((chunks, 128))
                digit1 = jnp.where(row, (2 * c + (lane >> 6)).astype(F32), 0.0)
                digit0 = jnp.where(row, (lane & 63).astype(F32), 0.0)
                digits = jnp.concatenate([digit1, digit0], axis=0).astype(BF16)
                tally[...] += contract(digits, low, ((1,), (1,)))
            first[leaf] = kept[h * per_leaf]
        for j in range(per_leaf):
            both = jnp.where(row_ids((8, 128)) < 4, kept[j], kept[per_leaf + j])
            halo_ref[pl.ds(pl.multiple_of(g * 8, 8), 8), j * 128 : (j + 1) * 128] = both
        return 0

    lax.fori_loop(0, leaf_dev // 2, two_leaves, 0)
    inv_ref[...] = (64.0 * tally[0:chunks, :] + tally[chunks : 2 * chunks, :] + 0.5).astype(jnp.int32)
    for leaf in range(leaf_dev):
        coef = contract(halo_ref[32 + leaf * 8 : 40 + leaf * 8, :], bases_ref[leaf], ((1,), (1,)), EXACT)
        halo_ref[96:104, leaf * rank : (leaf + 1) * rank] = coef
        slot[:, leaf * rank : (leaf + 1) * rank] = first[leaf][:, :rank]
    weights = contract(halo_ref[96:104, :], transfer_ref[...], ((1,), (1,)), EXACT)
    slots = [lambda s=s: slot[:, s * 128 : (s + 1) * 128] for s in range(leaf_dev * rank // 128)]
    (node_x,) = gather_lanes([slots], jnp.broadcast_to(skel_ref[...], (8, 128)))
    tile = jnp.concatenate([weights, node_x[:, :rank]], axis=1)
    node_ref[...] = jnp.broadcast_to(tile[None], node_ref.shape)


def near_body(near_ref, count_ref, far_ref, scale_ref, up_ref, mid_ref, down_ref, out_ref, far_out_ref, src, tgt, wgt, coef, k_high, k_low):
    leaf_dev = out_ref.shape[0]
    rank = far_out_ref.shape[2]
    leaf_pts = out_ref.shape[2]
    slots = near_ref.shape[1]
    row = row_ids((8, leaf_pts))
    scale = jnp.where((row & 3) == 0, scale_ref[0], jnp.where((row & 3) == 1, scale_ref[1], jnp.where((row & 3) == 2, scale_ref[2], scale_ref[3]))) * UNIT

    def prepare(ref, k, base, middle):
        def one(g, _):
            both = ref[k, pl.ds(pl.multiple_of(g * 8, 8), 8), :] * scale
            turned = pltpu.roll(both, 4, 0)
            for h in range(2):
                leaf = 2 * g + h
                xx = jnp.where(row < 4, both, turned) if h == 0 else jnp.where(row < 4, turned, both)
                made = features(xx, True, middle)
                src[base + leaf] = made[0]
                if middle:
                    tgt[leaf] = made[1]
                wgt[base + leaf] = halves(ref[k, pl.ds(pl.multiple_of(32 + leaf * 8, 8), 8), :] * LN2)
            return 0

        lax.fori_loop(0, leaf_dev // 2, one, 0)
        for leaf in range(leaf_dev):
            coef[base + leaf] = halves(ref[k, 96:104, leaf * rank : (leaf + 1) * rank] * LN2)

    for k in range(3):
        prepare(up_ref, k, k * leaf_dev, False)
        prepare(mid_ref, k, (3 + k) * leaf_dev, k == 1)
        prepare(down_ref, k, (6 + k) * leaf_dev, False)

    def leaf_step(leaf, _):
        target = tgt[leaf]
        total = jnp.zeros((16, leaf_pts), F32)
        for j in range(slots):
            w = near_ref[leaf, j]
            live = jnp.where(j < count_ref[leaf], 1.0, 0.0).astype(BF16)
            for q in range(0, leaf_pts, 128):
                z = contract(src[w, :, q : q + 128], target, ((0,), (0,)))
                high, low = split(kernel_of(z))
                k_high[j, q : q + 128, :] = high
                k_low[j, q : q + 128, :] = low
            weight = wgt[w] * live
            total = total + jnp.dot(weight, k_high[j], preferred_element_type=F32)
            total = total + jnp.dot(weight, k_low[j], preferred_element_type=F32)
        out_ref[leaf] = total[:8] + total[8:]
        far = jnp.zeros((16, rank), F32)
        for j in range(far_ref.shape[1]):
            w = far_ref[leaf, j]
            z = contract(src[w, :, 0:rank], tgt[leaf, :, 0:rank], ((0,), (0,)))
            high, low = split(kernel_of(z))
            far = far + jnp.dot(coef[w], high, preferred_element_type=F32)
            far = far + jnp.dot(coef[w], low, preferred_element_type=F32)
        far_out_ref[leaf] = far[:8] + far[8:]
        return 0

    lax.fori_loop(0, leaf_dev, leaf_step, 0)


def downward_body(place_ref, scale_ref, noise_ref, node_ref, own_ref, transfer_ref, bases_ref, near_ref, far_ref, inv_ref, p_ref, res_ref, image_ref, sums_ref, src, wgt, flat):
    devices = node_ref.shape[0]
    leaf_dev, rank, leaf_pts = bases_ref.shape
    tm_size = place_ref[2]
    row = row_ids((8, 128))
    lane = lane_ids((8, 128))
    scale = jnp.where((row & 3) == 0, scale_ref[0], jnp.where((row & 3) == 1, scale_ref[1], jnp.where((row & 3) == 2, scale_ref[2], scale_ref[3]))) * UNIT

    def distant(e):
        far_a = jnp.abs(e // tm_size - place_ref[0]) > 1
        far_b = jnp.abs(e % tm_size - place_ref[1]) > 1
        return jnp.where(far_a | far_b, LN2, 0.0)

    def unpack(g, _):
        one, two = node_ref[2 * g], node_ref[2 * g + 1]
        xx = jnp.where(lane < 64, pltpu.roll(one, 64, 1), two) * scale
        w = jnp.where(lane < 64, one * distant(2 * g), pltpu.roll(two, 64, 1) * distant(2 * g + 1))
        at = pl.ds(pl.multiple_of(g * 128, 128), 128)
        src[:, at] = features(xx, True, False)[0]
        wgt[:, at] = halves(w)
        return 0

    lax.fori_loop(0, devices // 2, unpack, 0)
    own = own_ref[...]
    own_xx = pltpu.roll(own, 64, 1) * scale
    target = features(own_xx, False, True)[0][:, :rank]
    total = jnp.zeros((16, rank), F32)
    step = 512
    for q in range(0, devices * rank, step):
        z = contract(target, src[:, q : q + step], ((0,), (0,)))
        high, low = split(kernel_of(z))
        weight = wgt[:, q : q + step]
        total = total + contract(weight, high, ((1,), (1,)))
        total = total + contract(weight, low, ((1,), (1,)))
    device_far = total[:8] + total[8:]
    pushed = jnp.dot(device_far, transfer_ref[...], precision=EXACT, preferred_element_type=F32)
    for leaf in range(leaf_dev):
        incoming = far_ref[leaf] + pushed[:, leaf * rank : (leaf + 1) * rank]
        out = near_ref[leaf] + jnp.dot(incoming, bases_ref[leaf], precision=EXACT, preferred_element_type=F32)
        flat[:, leaf * leaf_pts : (leaf + 1) * leaf_pts] = out
    chunks = flat.shape[1] // 128
    source = [lambda s=s: flat[:, s * 128 : (s + 1) * 128] for s in range(chunks)]
    noise = jnp.zeros((8, 128), F32)
    for r in range(8):
        noise = jnp.where(row == r, noise_ref[r], noise)

    def place(c, sums):
        at = pl.ds(pl.multiple_of(c * 128, 128), 128)
        ids = jnp.broadcast_to(inv_ref[pl.ds(c, 1), :], (8, 128))
        (part,) = gather_lanes([source], ids)
        image = part + noise * p_ref[:, at]
        image_ref[:, at] = image
        return sums[0] + res_ref[:, at] * image, sums[1] + image * image

    zero = jnp.zeros((8, 128), F32)
    along, squares = lax.fori_loop(0, chunks, place, (zero, zero))
    along = jnp.sum(along, axis=1, keepdims=True)
    squares = jnp.sum(squares, axis=1, keepdims=True)
    both = jnp.where(lane == row, along, 0.0) + jnp.where(lane == row + 8, squares, 0.0)
    sums_ref[...] = jnp.broadcast_to(jnp.sum(both, axis=0, keepdims=True), sums_ref.shape)


def update_body(sums_ref, it_ref, p_ref, res_ref, image_ref, new_it_ref, new_res_ref):
    total = jnp.sum(sums_ref[...], axis=0, keepdims=True)
    row = row_ids((8, 128))
    lane = lane_ids((8, 128))
    along = jnp.sum(jnp.where(lane == row, total, 0.0), axis=1, keepdims=True)
    squares = jnp.sum(jnp.where(lane == row + 8, total, 0.0), axis=1, keepdims=True)
    alpha = along / (squares + 1e-06)
    new_it_ref[...] = it_ref[...] + alpha * p_ref[...]
    new_res_ref[...] = res_ref[...] - alpha * image_ref[...]


def shifted(x, axis, by):
    n = lax.axis_size(axis)
    return lax.ppermute(x, axis, [(i, i + by) for i in range(n) if 0 <= i + by < n])


def shards(coords, direction, iterate, residual, order, bases, transfer, near_list, near_count, far_list, device_skel, inv_scale, noise):
    leaf_dev, rank, leaf_pts = bases.shape
    rhs, points = direction.shape
    axes = ("leaf", "tm")
    devices = lax.axis_size("leaf") * lax.axis_size("tm")
    chunks = points // 128
    shape = jax.ShapeDtypeStruct
    skel = jnp.pad(device_skel, ((0, 0), (0, 128 - rank)))
    halo, node, inverse = pl.pallas_call(
        upward_body,
        in_specs=[VMEM] * 6,
        out_specs=[VMEM] * 3,
        out_shape=[shape((104, leaf_pts), F32), shape((devices, 8, 128), F32), shape((chunks, 128), jnp.int32)],
        scratch_shapes=[
            pltpu.VMEM((8, points), F32),
            pltpu.VMEM((leaf_dev, 8, 128), F32),
            pltpu.VMEM((8, leaf_dev * rank), F32),
            pltpu.VMEM((2 * chunks, 128), F32),
        ],
        compiler_params=params(),
        name="upward",
    )(order.reshape(chunks, 128), coords, direction, bases, transfer[0], skel)
    before = shifted(halo, "tm", 1)
    after = shifted(halo, "tm", -1)
    nodes = lax.all_to_all(node, axes, 0, 0)
    mid = jnp.stack([before, halo, after])
    up = shifted(mid, "leaf", 1)
    down = shifted(mid, "leaf", -1)
    near, far = pl.pallas_call(
        near_body,
        in_specs=[SMEM] * 4 + [VMEM] * 3,
        out_specs=[VMEM] * 2,
        out_shape=[shape((leaf_dev, rhs, leaf_pts), F32), shape((leaf_dev, rhs, rank), F32)],
        scratch_shapes=[
            pltpu.VMEM((9 * leaf_dev, 32, leaf_pts), BF16),
            pltpu.VMEM((leaf_dev, 32, leaf_pts), BF16),
            pltpu.VMEM((9 * leaf_dev, 16, leaf_pts), BF16),
            pltpu.VMEM((9 * leaf_dev, 16, rank), BF16),
            pltpu.VMEM((near_list.shape[1], leaf_pts, leaf_pts), BF16),
            pltpu.VMEM((near_list.shape[1], leaf_pts, leaf_pts), BF16),
        ],
        compiler_params=params(),
        name="near",
    )(near_list, near_count, far_list, inv_scale, up, mid, down)
    place = jnp.stack([lax.axis_index("leaf"), lax.axis_index("tm"), lax.axis_size("tm")]).astype(jnp.int32)
    image, sums = pl.pallas_call(
        downward_body,
        in_specs=[SMEM] * 3 + [VMEM] * 9,
        out_specs=[VMEM] * 2,
        out_shape=[shape((rhs, points), F32), shape((devices, 128), F32)],
        scratch_shapes=[
            pltpu.VMEM((32, devices * rank), BF16),
            pltpu.VMEM((16, devices * rank), BF16),
            pltpu.VMEM((rhs, points), F32),
        ],
        compiler_params=params(),
        name="downward",
    )(place, inv_scale, noise, nodes, node[0], transfer[0], bases, near, far, inverse, direction, residual)
    all_sums = lax.all_to_all(sums, axes, 0, 0, tiled=True)
    return pl.pallas_call(
        update_body,
        in_specs=[VMEM] * 5,
        out_specs=[VMEM] * 2,
        out_shape=[shape((rhs, points), F32)] * 2,
        compiler_params=params(),
        name="update",
    )(all_sums, iterate, direction, residual, image)


def solution(mesh):
    whole = P(None, ("leaf", "tm"))
    first = P(("leaf", "tm"))
    return jax.shard_map(
        shards,
        mesh=mesh,
        in_specs=(whole,) * 4 + (first,) * 7 + (P(), P()),
        out_specs=(whole, whole),
        check_vma=False,
    )
```

time: 472 us -> 116 us (0.25); the launches traced: 466 us -> 116 us
  matrix products: 125 us -> 0 us
  blocking collectives: 132 us -> 19.9 us
  local copies, waits for them, and re-layouts: 101 us -> 6.67 us
  other arithmetic: 79.6 us -> 0.12 us
  Pallas kernels: 0 us -> 59.4 us
    dot_general x14 -> x0, matrix products: 125 us -> none  [the longest x8 111 us: near_leaf(): return jnp.einsum('smn,srn,s->rm', kernel, tile_p, weights, precision=EXACT)]
    reduce_sum x11 -> x0, other arithmetic: 69.3 us -> none  [the longest x10 69 us: matern(): distance = jnp.sqrt(jnp.sum(scaled * scaled, axis=-3))]
    psum x1 -> x0, blocking collectives: 66.1 us -> none  [shards(): lax.psum((jnp.sum(residual * image, axis=1), jnp.sum(image * image, axis=...]
    all_gather x1 -> x0, blocking collectives: 65.8 us -> none  [shards(): piece = lax.all_gather(packed, ('leaf', 'tm'), axis=0, tiled=True)]
    pallas_call x0 -> x4, Pallas kernels: none -> 59.4 us  [the longest x1 39.6 us: shards(): pl.pallas_call(near_body, in_specs=[SMEM] * 4 + [VMEM] * 3, out_specs=[VM...]
    gather x11 -> x0, local copies, waits for them, and re-layouts: 40 us -> none  [the longest x2 14.5 us: shards(): leaf_p = direction[:, order]]
    all_to_all x0 -> x1, blocking collectives: none -> 19.9 us  [shards(): all_sums = lax.all_to_all(sums, axes, 0, 0, tiled=True)]
    reshape x7 -> x0, local copies, waits for them, and re-layouts: 13.8 us -> none  [the longest x2 10.9 us: shards(): win_x = window[:, :4].reshape(9, 4, leaf_dev, leaf_pts)]
  transfers between devices with their start and end apart: 8 -> 5, of which waited for: 2 -> 2; matrix products, arithmetic and copies ran while one was open for 13% -> 1% of each run, Pallas kernels for 0% -> 34%
where the time goes in v1:
time: 116 us
  Pallas kernels  59.4 us (51%)
  starting transfers between devices  22.4 us (19%)
  blocking collectives  19.9 us (17%)
  local copies, waits for them, and re-layouts  6.67 us (6%)
  waiting for transfers between devices  6.4 us (6%)
    pallas_call x1, Pallas kernels, shards(): pl.pallas_call(near_body, in_specs=[SMEM] * 4 + [VMEM] * 3, out_specs=[VM...  39.6 us
    all_to_all x1, blocking collectives, shards(): all_sums = lax.all_to_all(sums, axes, 0, 0, tiled=True)  19.9 us
    pallas_call x1, Pallas kernels, shards(): pl.pallas_call(downward_body, in_specs=[SMEM] * 3 + [VMEM] * 9, out_specs...  14.2 us
    ppermute x4, starting transfers between devices, shifted(): lax.ppermute(x, axis, [(i, i + by) for i in range(n) if 0 <= i + by < n])  12.1 us
    all_to_all x1, starting transfers between devices, shards(): nodes = lax.all_to_all(node, axes, 0, 0)  10.2 us
    ppermute x4, waiting for transfers between devices, shifted(): lax.ppermute(x, axis, [(i, i + by) for i in range(n) if 0 <= i + by < n])  6.4 us
    unnamed x30, local copies, waits for them, and re-layouts  5.26 us
    pallas_call x1, Pallas kernels, shards(): pl.pallas_call(upward_body, in_specs=[VMEM] * 6, out_specs=[VMEM] * 3, ou...  4.85 us
  transfers between devices with their start and end apart: 5, of which 2 were waited for; matrix products, arithmetic and copies ran while one was open for 1% of the time, Pallas kernels for 34%

profile of v1, /device:TPU:1, one launch (start us, length us, event | category | flops | bytes accessed | tf_op | source)
XLA Modules:
  0.0 115.7 jit_solution(11247810435893632602)
XLA Ops:
  0.6 0.7 pad.4.skel_ref
  1.3 0.0 copy-start
  1.3 1.2 %copy-done = f32[8,64,512]{2,1,0:T(8,128)S(1)} copy-done((f32[8,64,512]{2,1,0:T(8,128)S(1)}, f32[8,64,512]{2,1,0:T(8,128)}, u32[]{:S(2)}) %copy-start) | copy-done | bytes 1048600
  2.5 0.0 copy-start.2
  2.5 0.9 copy-done.2
  3.4 0.0 copy-start.4
  3.4 0.9 copy-done.4
  4.3 0.0 copy-start.8
  4.3 0.8 copy-done.8
  5.2 0.0 copy-start.9
  5.2 0.7 copy-done.9
  5.9 4.8 %upward.1 = (f32[104,512]{1,0:T(8,128)S(1)}, f32[128,8,128]{2,1,0:T(8,128)}, s32[32,128]{1,0:T(8,128)S(1)}) custom-call(s32[32,128]{1,0:T(8,128)S(1)} %bitcast.18, f32[4,4096]{1,0:T(4,128)S(1)} %copy-done.8, f32[8,4096]{1,0:T(8,128)S(1)} %copy-done.2, f32[8,64,512]{2,1,0:T(8,128)S(1)} %copy-done, f32[64,512]{1,0:T(8,128)S(1)} %bitcast.13, ...), custom_call_target="tpu_custom_call" | custom-call | tf_op jit(solution)/shard_map/upward/pallas_call | solution.py:289
  10.7 3.9 %collective-permute-start = (f32[104,512]{1,0:T(8,128)S(1)}, f32[104,512]{1,0:T(8,128)S(1)}, u32[]{:S(2)}, u32[]{:S(2)}) collective-permute-start(f32[104,512]{1,0:T(8,128)S(1)} %get-tuple-element.10), channel_id=1, source_target_pairs={{0,1},{1,2},{2,3},{4,5},{5,6},{6,7},{8,9},{9,10},{10,11},{12,13},{... | collective-permute-start | bytes 638984 | tf_op jit(solution)/shard_map/ppermute | solution.py:278
  14.7 1.3 %collective-permute-start.1 = (f32[104,512]{1,0:T(8,128)S(1)}, f32[104,512]{1,0:T(8,128)S(1)}, u32[]{:S(2)}, u32[]{:S(2)}) collective-permute-start(f32[104,512]{1,0:T(8,128)S(1)} %get-tuple-element.10), channel_id=1, source_target_pairs={{1,0},{2,1},{3,2},{5,4},{6,5},{7,6},{9,8},{10,9},{11,10},{13,12},{... | collective-permute-start | bytes 638984 | tf_op jit(solution)/shard_map/ppermute | solution.py:278
  16.0 2.6 %collective-permute-done = f32[104,512]{1,0:T(8,128)S(1)} collective-permute-done((f32[104,512]{1,0:T(8,128)S(1)}, f32[104,512]{1,0:T(8,128)S(1)}, u32[]{:S(2)}, u32[]{:S(2)}) %collective-permute-start) | collective-permute-done | bytes 213024 | tf_op jit(solution)/shard_map/ppermute | solution.py:278
  18.6 3.8 %collective-permute-done.1 = f32[104,512]{1,0:T(8,128)S(1)} collective-permute-done((f32[104,512]{1,0:T(8,128)S(1)}, f32[104,512]{1,0:T(8,128)S(1)}, u32[]{:S(2)}, u32[]{:S(2)}) %collective-permute-start.1) | collective-permute-done | bytes 213024 | tf_op jit(solution)/shard_map/ppermute | solution.py:278
  22.4 5.0 %collective-permute-start.2 = (f32[3,104,512]{2,1,0:T(8,128)S(1)}, f32[3,104,512]{2,1,0:T(8,128)S(1)}, u32[]{:S(2)}, u32[]{:S(2)}) collective-permute-start(f32[3,104,512]{2,1,0:T(8,128)S(1)} %pad_maximum_fusion.mid_ref), channel_id=1, source_target_pairs={{0,4},{4,8},{8,12},{12,16},{16,20},{20,24},{24,28},{28,32},{32,36}... | collective-permute-start | bytes 1916936 | tf_op jit(solution)/shard_map/ppermute | solution.py:278
  27.4 1.9 %collective-permute-start.3 = (f32[3,104,512]{2,1,0:T(8,128)S(1)}, f32[3,104,512]{2,1,0:T(8,128)}, u32[]{:S(2)}, u32[]{:S(2)}) collective-permute-start(f32[3,104,512]{2,1,0:T(8,128)S(1)} %pad_maximum_fusion.mid_ref), channel_id=1, source_target_pairs={{4,0},{8,4},{12,8},{16,12},{20,16},{24,20},{28,24},{32,28},{36,32}... | collective-permute-start | bytes 1916936 | tf_op jit(solution)/shard_map/ppermute | solution.py:278
  29.3 0.0 copy-start.10
  29.3 0.0 copy-start.11
  29.3 0.0 copy-start.12
  29.4 0.0 copy-start.13
  29.4 10.2 %all-to-all-start = ((f32[128,8,128]{2,1,0:T(8,128)}), f32[128,8,128]{2,1,0:T(8,128)S(1)}, u32[]{:S(2)}, u32[]{:S(2)}) async-start(f32[128,8,128]{2,1,0:T(8,128)} %get-tuple-element.9), calls=%async_computation | async-start | bytes 1048576 | tf_op jit(solution)/shard_map/all_to_all | solution.py:305
  39.6 0.0 copy-start.1
  39.6 0.1 pad_add_fusion.place_ref
  39.7 0.7 slice_bitcast_fusion.own_ref
  40.5 0.0 copy-start.3
  40.5 0.0 copy-start.5
  40.5 0.0 copy-start.6
  40.5 0.0 collective-permute-done.2.up_ref
  40.5 0.0 collective-permute-done.3.down_ref
  40.5 0.0 copy-done.10
  40.5 0.0 copy-done.11
  40.5 0.0 copy-done.12
  40.5 0.0 copy-done.13
  40.5 39.6 %near.1 = (f32[8,8,512]{2,1,0:T(8,128)S(1)}, f32[8,8,64]{2,1,0:T(8,128)S(1)}) custom-call(s32[8,8]{1,0:T(8,128)S(1)} %copy-done.10, s32[8]{0:T(128)S(1)} %copy-done.13, s32[8,8]{1,0:T(8,128)S(1)} %copy-done.11, f32[4]{0:T(128)S(1)} %copy-done.12, f32[3,104,512]{2,1,0:T(8,128)S(1)} %collective-permute-done.2.up_ref, ...), custom_call_target="tpu_custom_call" | custom-call | tf_op jit(solution)/shard_map/near/pallas_call | solution.py:309
  80.1 0.0 all-to-all-done.node_ref
  80.1 0.0 copy-start.14
  80.1 0.0 copy-done.1
  80.1 0.0 copy-done.3
  80.1 0.0 copy-done.5
  80.1 0.0 copy-done.6
  80.1 0.6 copy-done.14
  80.8 14.2 %downward.1 = (f32[8,4096]{1,0:T(8,128)S(1)}, f32[128,128]{1,0:T(8,128)S(1)}) custom-call(s32[3]{0:T(128)S(1)} %pad_add_fusion.place_ref, f32[4]{0:T(128)S(1)} %copy-done.12, f32[8]{0:T(128)S(1)} %copy-done.14, f32[128,8,128]{2,1,0:T(8,128)S(1)} %all-to-all-done.node_ref, f32[8,128]{1,0:T(8,128)S(1)} %slice_bitcast_fusion.own_ref, f32[64,512]{1,0:T(8,128)S(1)} %bitcast.14, ...), custom_call_target="tpu_custom_call" | custom-call | tf_op jit(solution)/shard_map/downward/pallas_call | solution.py:326
  94.9 0.0 copy-start.7
  94.9 19.9 %all_to_all.16 = f32[128,1,128]{2,1,0:T(1,128)S(1)} all-to-all(f32[128,1,128]{2,1,0:T(1,128)S(1)} %bitcast.17), channel_id=1, replica_groups=mesh['leaf'=32,'tm'=4] {'leaf','tm'}, dimensions={0} | all-to-all | bytes 131072 | tf_op jit(solution)/shard_map/all_to_all | solution.py:339
  114.8 0.0 copy-done.7
  114.8 0.8 update.1
  (1 shorter events, 0.0 us)
Async XLA Ops:
  1.3 1.2 %copy-start = (f32[8,64,512]{2,1,0:T(8,128)S(1)}, f32[8,64,512]{2,1,0:T(8,128)}, u32[]{:S(2)}) copy-start(f32[8,64,512]{2,1,0:T(8,128)} %bases_ref.3) | copy-start | bytes 3145732
  2.5 0.9 copy-start.2
  3.4 0.9 copy-start.4
  4.3 0.8 copy-start.8
  5.2 0.7 copy-start.9
  10.7 7.8 %collective-permute-start = (f32[104,512]{1,0:T(8,128)S(1)}, f32[104,512]{1,0:T(8,128)S(1)}, u32[]{:S(2)}, u32[]{:S(2)}) collective-permute-start(f32[104,512]{1,0:T(8,128)S(1)} %get-tuple-element.10), channel_id=1, source_target_pairs={{0,1},{1,2},{2,3},{4,5},{5,6},{6,7},{8,9},{9,10},{10,11},{12,13},{... | collective-permute-start | bytes 638984 | tf_op jit(solution)/shard_map/ppermute | solution.py:278
  14.7 7.7 %collective-permute-start.1 = (f32[104,512]{1,0:T(8,128)S(1)}, f32[104,512]{1,0:T(8,128)S(1)}, u32[]{:S(2)}, u32[]{:S(2)}) collective-permute-start(f32[104,512]{1,0:T(8,128)S(1)} %get-tuple-element.10), channel_id=1, source_target_pairs={{1,0},{2,1},{3,2},{5,4},{6,5},{7,6},{9,8},{10,9},{11,10},{13,12},{... | collective-permute-start | bytes 638984 | tf_op jit(solution)/shard_map/ppermute | solution.py:278
  22.4 18.0 %collective-permute-start.2 = (f32[3,104,512]{2,1,0:T(8,128)S(1)}, f32[3,104,512]{2,1,0:T(8,128)S(1)}, u32[]{:S(2)}, u32[]{:S(2)}) collective-permute-start(f32[3,104,512]{2,1,0:T(8,128)S(1)} %pad_maximum_fusion.mid_ref), channel_id=1, source_target_pairs={{0,4},{4,8},{8,12},{12,16},{16,20},{20,24},{24,28},{28,32},{32,36}... | collective-permute-start | bytes 1916936 | tf_op jit(solution)/shard_map/ppermute | solution.py:278
  27.4 13.1 %collective-permute-start.3 = (f32[3,104,512]{2,1,0:T(8,128)S(1)}, f32[3,104,512]{2,1,0:T(8,128)}, u32[]{:S(2)}, u32[]{:S(2)}) collective-permute-start(f32[3,104,512]{2,1,0:T(8,128)S(1)} %pad_maximum_fusion.mid_ref), channel_id=1, source_target_pairs={{4,0},{8,4},{12,8},{16,12},{20,16},{24,20},{28,24},{32,28},{36,32}... | collective-permute-start | bytes 1916936 | tf_op jit(solution)/shard_map/ppermute | solution.py:278
  29.3 11.2 %copy-start.10 = (s32[8,8]{1,0:T(8,128)S(1)}, s32[8,8]{1,0:T(8,128)}, u32[]{:S(2)}) copy-start(s32[8,8]{1,0:T(8,128)} %near_ref.1) | copy-start | bytes 772
  29.3 11.2 %copy-start.11 = (s32[8,8]{1,0:T(8,128)S(1)}, s32[8,8]{1,0:T(8,128)}, u32[]{:S(2)}) copy-start(s32[8,8]{1,0:T(8,128)} %far_ref.1) | copy-start | bytes 772
  29.3 11.2 %copy-start.12 = (f32[4]{0:T(128)S(1)}, f32[4]{0:T(128)}, u32[]{:S(2)}) copy-start(f32[4]{0:T(128)} %scale_ref.3) | copy-start | bytes 52
  29.4 11.2 %copy-start.13 = (s32[8]{0:T(128)S(1)}, s32[8]{0:T(128)}, u32[]{:S(2)}) copy-start(s32[8]{0:T(128)} %count_ref.1) | copy-start | bytes 100
  29.4 50.7 %all-to-all-start = ((f32[128,8,128]{2,1,0:T(8,128)}), f32[128,8,128]{2,1,0:T(8,128)S(1)}, u32[]{:S(2)}, u32[]{:S(2)}) async-start(f32[128,8,128]{2,1,0:T(8,128)} %get-tuple-element.9), calls=%async_computation | async-start | bytes 1048576 | tf_op jit(solution)/shard_map/all_to_all | solution.py:305
  39.6 40.5 %copy-start.1 = (f32[8,64,512]{2,1,0:T(8,128)S(1)}, f32[8,64,512]{2,1,0:T(8,128)}, u32[]{:S(2)}) copy-start(f32[8,64,512]{2,1,0:T(8,128)} %bases_ref.3) | copy-start | bytes 3145732
  40.5 39.7 %copy-start.3 = (f32[8,4096]{1,0:T(8,128)S(1)}, f32[8,4096]{1,0:T(8,128)}, u32[]{:S(2)}) copy-start(f32[8,4096]{1,0:T(8,128)} %p_ref.5) | copy-start | bytes 393220
  40.5 39.7 %copy-start.5 = (f32[1,64,512]{2,1,0:T(8,128)S(1)}, f32[1,64,512]{2,1,0:T(8,128)}, u32[]{:S(2)}) copy-start(f32[1,64,512]{2,1,0:T(8,128)} %param.19) | copy-start | bytes 393220
  40.5 39.7 %copy-start.6 = (f32[8,4096]{1,0:T(8,128)S(1)}, f32[8,4096]{1,0:T(8,128)}, u32[]{:S(2)}) copy-start(f32[8,4096]{1,0:T(8,128)} %res_ref.3) | copy-start | bytes 393220
  80.1 0.7 copy-start.14
  94.9 19.9 %copy-start.7 = (f32[8,4096]{1,0:T(8,128)S(1)}, f32[8,4096]{1,0:T(8,128)}, u32[]{:S(2)}) copy-start(f32[8,4096]{1,0:T(8,128)} %it_ref.1) | copy-start | bytes 393220

commit v2 on v1

v2 whole, which is shorter than its diff:
```python
import math

import jax
import jax.numpy as jnp
from jax import lax
from jax.experimental import pallas as pl
from jax.experimental.pallas import tpu as pltpu
from jax.sharding import PartitionSpec as P

F32 = jnp.float32
BF16 = jnp.bfloat16
EXACT = lax.Precision.HIGHEST
LN2 = math.log(2.0)
LOG2E = 1.0 / LN2
UNIT = math.sqrt(3.0) * LOG2E
VMEM = pl.BlockSpec(memory_space=pltpu.VMEM)
SMEM = pl.BlockSpec(memory_space=pltpu.SMEM)
HBM = pl.BlockSpec(memory_space=pltpu.HBM)
PART = 256


def params(mib, **kw):
    return pltpu.CompilerParams(vmem_limit_bytes=mib * 2**20, **kw)


def contract(a, b, dims, precision=None):
    return lax.dot_general(
        a, b, ((dims[0], dims[1]), ((), ())), precision=precision, preferred_element_type=F32
    )


def rounded(x):
    return x.astype(BF16).astype(F32)


def row_ids(shape):
    return lax.broadcasted_iota(jnp.int32, shape, 0)


def lane_ids(shape):
    return lax.broadcasted_iota(jnp.int32, shape, 1)


def features(xx, want_source, want_target):
    row = row_ids(xx.shape)
    high = rounded(xx)
    low = rounded(xx - high)
    held = high + low
    square = held * held
    square = square + pltpu.roll(square, 1, 0)
    norm = square + pltpu.roll(square, 2, 0)
    n0 = rounded(norm)
    rest = norm - n0
    n1 = rounded(rest)
    n2 = rest - n1
    zero = jnp.zeros_like(xx)
    out = []
    if want_source:
        parts = jnp.where(row < 4, high, low)
        tail = jnp.where(row == 0, n0, jnp.where(row == 1, n1, jnp.where(row == 2, n2, jnp.where(row < 6, 1.0, 0.0))))
        out.append(jnp.concatenate([parts, parts, tail, zero], axis=0).astype(BF16))
    if want_target:
        tail = jnp.where(row < 3, 1.0, jnp.where(row == 3, n0, jnp.where(row == 4, n1, jnp.where(row == 5, n2, 0.0))))
        out.append(jnp.concatenate([-2.0 * high, -2.0 * low, tail, zero], axis=0).astype(BF16))
    return out


def halves(w):
    high = rounded(w)
    return jnp.concatenate([high, w - high], axis=0).astype(BF16)


def kernel_of(z):
    z = jnp.maximum(z, 1e-30)
    v = z * lax.rsqrt(z)
    return (v + LOG2E) * jnp.exp2(-v)


def split(k):
    high = k.astype(BF16)
    return high, (k - high.astype(F32)).astype(BF16)


def gather_lanes(chunks, ids):
    lane = ids & 127
    chunk = ids >> 7
    picked = [None] * len(chunks)
    for s in range(len(chunks[0])):
        here = chunk == s
        for i, source in enumerate(chunks):
            got = jnp.take_along_axis(source[s](), lane, axis=1, mode="promise_in_bounds")
            picked[i] = got if s == 0 else jnp.where(here, got, picked[i])
    return picked


def upward_body(order_hbm, x_hbm, p_hbm, bases_hbm, transfer_hbm, skel_hbm, halo_ref, node_ref, own_ref, inv_ref, order_ref, xx, p_ref, bases_ref, transfer_ref, skel_ref, first, slot, tally, sems):
    leaf_dev, rank, leaf_pts = bases_ref.shape
    points = p_ref.shape[1]
    chunks = points // 128
    per_leaf = leaf_pts // 128
    moves = [
        pltpu.make_async_copy(source, target, sems.at[i])
        for i, (source, target) in enumerate(
            [
                (order_hbm, order_ref),
                (x_hbm, xx.at[0:4, :]),
                (x_hbm, xx.at[4:8, :]),
                (p_hbm, p_ref),
                (bases_hbm, bases_ref),
                (transfer_hbm, transfer_ref),
                (skel_hbm, skel_ref),
            ]
        )
    ]
    for move in moves:
        move.start()
    tally[...] = jnp.zeros_like(tally)
    for move in moves[:4]:
        move.wait()

    def loads(ref):
        return [lambda s=s: ref[:, s * 128 : (s + 1) * 128] for s in range(chunks)]

    def two_leaves(g, _):
        kept = []
        for h in range(2):
            leaf = 2 * g + h
            for j in range(per_leaf):
                c = leaf * per_leaf + j
                ids = order_ref[pl.ds(c, 1), :]
                got_x, got_p = gather_lanes([loads(xx), loads(p_ref)], jnp.broadcast_to(ids, (8, 128)))
                kept.append(got_x)
                halo_ref[pl.ds(pl.multiple_of(32 + leaf * 8, 8), 8), j * 128 : (j + 1) * 128] = got_p
                low = jnp.where(row_ids((128, 128)) == (ids & 127), 1.0, 0.0).astype(BF16)
                row = row_ids((chunks, 128)) == (ids >> 7)
                lane = lane_ids((chunks, 128))
                digit1 = jnp.where(row, (2 * c + (lane >> 6)).astype(F32), 0.0)
                digit0 = jnp.where(row, (lane & 63).astype(F32), 0.0)
                digits = jnp.concatenate([digit1, digit0], axis=0).astype(BF16)
                tally[...] += contract(digits, low, ((1,), (1,)))
            first[leaf] = kept[h * per_leaf]
        for j in range(per_leaf):
            both = jnp.where(row_ids((8, 128)) < 4, kept[j], kept[per_leaf + j])
            halo_ref[pl.ds(pl.multiple_of(g * 8, 8), 8), j * 128 : (j + 1) * 128] = both
        return 0

    lax.fori_loop(0, leaf_dev // 2, two_leaves, 0)
    inv_ref[...] = (64.0 * tally[0:chunks, :] + tally[chunks : 2 * chunks, :] + 0.5).astype(jnp.int32)
    for move in moves[4:]:
        move.wait()
    for leaf in range(leaf_dev):
        coef = contract(halo_ref[32 + leaf * 8 : 40 + leaf * 8, :], bases_ref[leaf], ((1,), (1,)), EXACT)
        halo_ref[96:104, leaf * rank : (leaf + 1) * rank] = coef
        slot[:, leaf * rank : (leaf + 1) * rank] = first[leaf][:, :rank]
    weights = contract(halo_ref[96:104, :], transfer_ref[...], ((1,), (1,)), EXACT)
    slots = [lambda s=s: slot[:, s * 128 : (s + 1) * 128] for s in range(leaf_dev * rank // 128)]
    ids = jnp.concatenate([skel_ref[...], skel_ref[...]], axis=1)
    (node_x,) = gather_lanes([slots], jnp.broadcast_to(ids, (8, 128)))
    tile = jnp.concatenate([weights, node_x[:, :rank]], axis=1)
    own_ref[...] = tile
    node_ref[...] = jnp.broadcast_to(tile[None], node_ref.shape)


def scale_rows(scale_ref, shape):
    row = row_ids(shape) & 3
    picked = jnp.where(row == 0, scale_ref[0], jnp.where(row == 1, scale_ref[1], jnp.where(row == 2, scale_ref[2], scale_ref[3])))
    return picked * UNIT


def prepare(ref, scale, base, src, wgt=None, tgt=None, coef=None):
    leaf_dev = ref.shape[0] // 13
    width = scale.shape[1]
    row = row_ids(scale.shape)
    for g in range(leaf_dev // 2):
        both = ref[g * 8 : g * 8 + 8, 0:width] * scale
        turned = pltpu.roll(both, 4, 0)
        for h in range(2):
            leaf = 2 * g + h
            xx = jnp.where(row < 4, both, turned) if h == 0 else jnp.where(row < 4, turned, both)
            made = features(xx, True, tgt is not None)
            src[base + leaf, :, 0:width] = made[0]
            if tgt is not None:
                tgt[leaf, :, 0:width] = made[1]
            if wgt is not None:
                wgt[base + leaf] = halves(ref[32 + leaf * 8 : 40 + leaf * 8, :] * LN2)
            if coef is not None:
                rank = coef.shape[2]
                coef[base + leaf] = halves(ref[96:104, leaf * rank : (leaf + 1) * rank] * LN2)


def list_pairs(near_ref, count_ref, keep, slot_of, idle, pairs):
    leaf_dev, slots = near_ref.shape

    def leaf_step(leaf, n):
        def entry(j, n):
            w = near_ref[leaf, j]
            pairs[n] = leaf * 128 + slot_of(w)
            return n + jnp.where(keep(w // leaf_dev), 1, 0)

        return lax.fori_loop(0, count_ref[leaf], entry, n)

    n = lax.fori_loop(0, leaf_dev, leaf_step, 0)
    for extra in range(3):
        pairs[n + extra] = idle
    return n


def near_pairs(pairs, n, src, tgt, wgt, out, z, high, low):
    parts = wgt.shape[2] // PART

    def where(p):
        return pairs[p] >> 7, pairs[p] & 127

    def distances(p, c, b):
        leaf, w = where(p)
        z[b] = contract(src[w, :, c * PART : (c + 1) * PART], tgt[leaf], ((0,), (0,)))

    def values(b):
        high[b], low[b] = split(kernel_of(z[b]))

    def product(p, c, b):
        _, w = where(p)
        weight = wgt[w, :, c * PART : (c + 1) * PART]
        got = jnp.dot(weight, high[b], preferred_element_type=F32)
        return got + jnp.dot(weight, low[b], preferred_element_type=F32)

    distances(0, 0, 0)
    distances(0, 1, 1)
    values(0)

    def two_pairs(g, _):
        for h in range(2):
            p = 2 * g + h
            got = None
            for c in range(parts):
                b = c % 2
                values(1 - b)
                mine = product(p, c, b)
                got = mine if got is None else got + mine
                distances(p + (c + 2) // parts, (c + 2) % parts, b)
            leaf, _ = where(p)
            out[leaf] += got[:8] + got[8:]
        return 0

    lax.fori_loop(0, (n + 1) // 2, two_pairs, 0)


def blank(src, wgt):
    src[src.shape[0] - 1] = jnp.zeros(src.shape[1:], BF16)
    wgt[wgt.shape[0] - 1] = jnp.zeros(wgt.shape[1:], BF16)


def close_body(near_ref, count_ref, place_ref, scale_ref, left_ref, mid_ref, right_ref, node_ref, own_ref, transfer_ref, out_ref, pushed_ref, pairs, src, tgt, wgt, z, high, low, node_src, node_wgt):
    leaf_dev, rhs, leaf_pts = out_ref.shape
    devices, _, _ = node_ref.shape
    rank = own_ref.shape[1] // 2
    scale = scale_rows(scale_ref, (8, leaf_pts))
    n = list_pairs(near_ref, count_ref, lambda k: (k >= 3) & (k < 6), lambda w: w - 3 * leaf_dev, 3 * leaf_dev, pairs)
    blank(src, wgt)
    prepare(left_ref, scale, 0, src, wgt)
    prepare(mid_ref, scale, leaf_dev, src, wgt, tgt)
    prepare(right_ref, scale, 2 * leaf_dev, src, wgt)
    out_ref[...] = jnp.zeros_like(out_ref)
    near_pairs(pairs, n, src, tgt, wgt, out_ref, z, high, low)

    tm_size = place_ref[2]
    lane = lane_ids((8, 128))

    def distant(e):
        far_a = jnp.abs(e // tm_size - place_ref[0]) > 1
        far_b = jnp.abs(e % tm_size - place_ref[1]) > 1
        return jnp.where(far_a | far_b, LN2, 0.0)

    def unpack(g, _):
        xs, ws = [], []
        for k in range(4):
            e = 8 * g + 2 * k
            one, two = node_ref[e], node_ref[e + 1]
            xs.append(jnp.where(lane < rank, pltpu.roll(one, rank, 1), two))
            ws.append(jnp.where(lane < rank, one * distant(e), pltpu.roll(two, rank, 1) * distant(e + 1)))
        at = pl.ds(pl.multiple_of(g * 512, 512), 512)
        node_src[:, at] = features(jnp.concatenate(xs, axis=1) * scale, True, False)[0]
        node_wgt[:, at] = halves(jnp.concatenate(ws, axis=1))
        return 0

    lax.fori_loop(0, devices // 8, unpack, 0, unroll=4)
    own_xx = pltpu.roll(own_ref[...], rank, 1) * scale[:, 0 : 2 * rank]
    target = features(own_xx, False, True)[0][:, :rank]
    total = jnp.zeros((16, rank), F32)
    step = 512
    for q in range(0, devices * rank, step):
        z_far = contract(target, node_src[:, q : q + step], ((0,), (0,)))
        k_high, k_low = split(kernel_of(z_far))
        weight = node_wgt[:, q : q + step]
        total = total + contract(weight, k_high, ((1,), (1,)))
        total = total + contract(weight, k_low, ((1,), (1,)))
    device_far = total[:8] + total[8:]
    pushed_ref[...] = jnp.dot(device_far, transfer_ref[...], precision=EXACT, preferred_element_type=F32)


def rest_body(near_ref, count_ref, far_ref, scale_ref, noise_ref, left_ref, mid_ref, right_ref, up_ref, down_ref, close_ref, pushed_ref, bases_ref, inv_ref, p_ref, res_ref, image_ref, sums_ref, pairs, src, tgt, wgt, coef, z, high, low, out, flat):
    leaf_dev, rank, leaf_pts = bases_ref.shape
    scale = scale_rows(scale_ref, (8, leaf_pts))
    n = list_pairs(near_ref, count_ref, lambda k: (k < 3) | (k >= 6), lambda w: w, 9 * leaf_dev, pairs)
    blank(src, wgt)
    for k in range(3):
        prepare(up_ref.at[k], scale, k * leaf_dev, src, wgt, None, coef)
        prepare(down_ref.at[k], scale, (6 + k) * leaf_dev, src, wgt, None, coef)
    prepare(left_ref, scale[:, :128], 3 * leaf_dev, src, None, None, coef)
    prepare(mid_ref, scale, 4 * leaf_dev, src, None, tgt, coef)
    prepare(right_ref, scale[:, :128], 5 * leaf_dev, src, None, None, coef)
    out[...] = close_ref[...]
    near_pairs(pairs, n, src, tgt, wgt, out, z, high, low)

    for leaf in range(leaf_dev):
        far = jnp.zeros((16, rank), F32)
        for j in range(far_ref.shape[1]):
            w = far_ref[leaf, j]
            z_far = contract(src[w, :, 0:rank], tgt[leaf, :, 0:rank], ((0,), (0,)))
            k_high, k_low = split(kernel_of(z_far))
            far = far + jnp.dot(coef[w], k_high, preferred_element_type=F32)
            far = far + jnp.dot(coef[w], k_low, preferred_element_type=F32)
        incoming = halves(far[:8] + far[8:] + pushed_ref[:, leaf * rank : (leaf + 1) * rank])
        base_high, base_low = split(bases_ref[leaf])
        got = jnp.dot(incoming, base_high, preferred_element_type=F32)
        got = got + jnp.dot(incoming, base_low, preferred_element_type=F32)
        flat[:, leaf * leaf_pts : (leaf + 1) * leaf_pts] = out[leaf] + got[:8] + got[8:]

    chunks = flat.shape[1] // 128
    row = row_ids((8, 128))
    lane = lane_ids((8, 128))
    source = [lambda s=s: flat[:, s * 128 : (s + 1) * 128] for s in range(chunks)]
    noise = jnp.zeros((8, 128), F32)
    for r in range(8):
        noise = jnp.where(row == r, noise_ref[r], noise)

    def place(g, sums):
        along, squares = sums
        for h in range(4):
            c = 4 * g + h
            at = pl.ds(pl.multiple_of(c * 128, 128), 128)
            ids = jnp.broadcast_to(inv_ref[pl.ds(c, 1), :], (8, 128))
            (part,) = gather_lanes([source], ids)
            image = part + noise * p_ref[:, at]
            image_ref[:, at] = image
            along, squares = along + res_ref[:, at] * image, squares + image * image
        return along, squares

    zero = jnp.zeros((8, 128), F32)
    along, squares = lax.fori_loop(0, chunks // 4, place, (zero, zero))
    along = jnp.sum(along, axis=1, keepdims=True)
    squares = jnp.sum(squares, axis=1, keepdims=True)
    both = jnp.where(lane == row, along, 0.0) + jnp.where(lane == row + 8, squares, 0.0)
    sums_ref[...] = jnp.broadcast_to(jnp.sum(both, axis=0, keepdims=True), sums_ref.shape)


def update_body(sums_ref, it_ref, p_ref, res_ref, image_ref, new_it_ref, new_res_ref):
    total = jnp.sum(sums_ref[...], axis=0, keepdims=True)
    row = row_ids((8, 128))
    lane = lane_ids((8, 128))
    along = jnp.sum(jnp.where(lane == row, total, 0.0), axis=1, keepdims=True)
    squares = jnp.sum(jnp.where(lane == row + 8, total, 0.0), axis=1, keepdims=True)
    alpha = along / (squares + 1e-06)
    new_it_ref[...] = it_ref[...] + alpha * p_ref[...]
    new_res_ref[...] = res_ref[...] - alpha * image_ref[...]


def shifted(x, axis, by):
    n = lax.axis_size(axis)
    return lax.ppermute(x, axis, [(i, i + by) for i in range(n) if 0 <= i + by < n])


def shards(coords, direction, iterate, residual, order, bases, transfer, near_list, near_count, far_list, device_skel, inv_scale, noise):
    leaf_dev, rank, leaf_pts = bases.shape
    rhs, points = direction.shape
    axes = ("leaf", "tm")
    devices = lax.axis_size("leaf") * lax.axis_size("tm")
    chunks = points // 128
    shape = jax.ShapeDtypeStruct
    halo, node, own, inverse = pl.pallas_call(
        upward_body,
        in_specs=[HBM] * 6,
        out_specs=[VMEM] * 4,
        out_shape=[
            shape((13 * leaf_dev, leaf_pts), F32),
            shape((devices, 8, 128), F32),
            shape((8, 128), F32),
            shape((chunks, 128), jnp.int32),
        ],
        scratch_shapes=[
            pltpu.VMEM((chunks, 128), jnp.int32),
            pltpu.VMEM((8, points), F32),
            pltpu.VMEM((rhs, points), F32),
            pltpu.VMEM(bases.shape, F32),
            pltpu.VMEM(transfer.shape[1:], F32),
            pltpu.VMEM(device_skel.shape, jnp.int32),
            pltpu.VMEM((leaf_dev, 8, 128), F32),
            pltpu.VMEM((8, leaf_dev * rank), F32),
            pltpu.VMEM((2 * chunks, 128), F32),
            pltpu.SemaphoreType.DMA((7,)),
        ],
        compiler_params=params(24),
        name="upward",
    )(order.reshape(chunks, 128), coords, direction, bases, transfer[0], device_skel)
    left = shifted(halo, "tm", 1)
    right = shifted(halo, "tm", -1)
    nodes = lax.all_to_all(node, axes, 0, 0)
    left, right, nodes = lax.optimization_barrier((left, right, nodes))
    row = jnp.stack([left, halo, right])
    up = shifted(row, "leaf", 1)
    down = shifted(row, "leaf", -1)
    place = jnp.stack([lax.axis_index("leaf"), lax.axis_index("tm"), lax.axis_size("tm")]).astype(jnp.int32)

    def pipeline(sources):
        return [
            pltpu.VMEM((sources + 1, 32, leaf_pts), BF16),
            pltpu.VMEM((leaf_dev, 32, leaf_pts), BF16),
            pltpu.VMEM((sources + 1, 16, leaf_pts), BF16),
        ]

    buffers = [
        pltpu.VMEM((2, PART, leaf_pts), F32),
        pltpu.VMEM((2, PART, leaf_pts), BF16),
        pltpu.VMEM((2, PART, leaf_pts), BF16),
    ]
    listed = pltpu.SMEM((near_list.size + 4,), jnp.int32)
    close, pushed = pl.pallas_call(
        close_body,
        in_specs=[SMEM] * 4 + [VMEM] * 6,
        out_specs=[VMEM] * 2,
        out_shape=[shape((leaf_dev, rhs, leaf_pts), F32), shape((rhs, leaf_dev * rank), F32)],
        scratch_shapes=[listed]
        + pipeline(3 * leaf_dev)
        + buffers
        + [pltpu.VMEM((32, devices * rank), BF16), pltpu.VMEM((16, devices * rank), BF16)],
        compiler_params=params(24),
        cost_estimate=pl.CostEstimate(flops=10**10, bytes_accessed=2**21, transcendentals=10**7),
        name="close",
    )(near_list, near_count, place, inv_scale, left, halo, right, nodes, own, transfer[0])
    image, sums = pl.pallas_call(
        rest_body,
        in_specs=[SMEM] * 5 + [VMEM] * 11,
        out_specs=[VMEM] * 2,
        out_shape=[shape((rhs, points), F32), shape((devices, 128), F32)],
        scratch_shapes=[listed]
        + pipeline(9 * leaf_dev)
        + [pltpu.VMEM((9 * leaf_dev, 16, rank), BF16)]
        + buffers
        + [pltpu.VMEM((leaf_dev, rhs, leaf_pts), F32), pltpu.VMEM((rhs, points), F32)],
        compiler_params=params(24),
        name="rest",
    )(near_list, near_count, far_list, inv_scale, noise, left, halo, right, up, down, close, pushed, bases, inverse, direction, residual)
    all_sums = lax.all_to_all(sums, axes, 0, 0, tiled=True)
    return pl.pallas_call(
        update_body,
        in_specs=[VMEM] * 5,
        out_specs=[VMEM] * 2,
        out_shape=[shape((rhs, points), F32)] * 2,
        compiler_params=params(24),
        name="update",
    )(all_sums, iterate, direction, residual, image)


def solution(mesh):
    whole = P(None, ("leaf", "tm"))
    first = P(("leaf", "tm"))
    return jax.shard_map(
        shards,
        mesh=mesh,
        in_specs=(whole,) * 4 + (first,) * 7 + (P(), P()),
        out_specs=(whole, whole),
        check_vma=False,
    )
```

time: 116 us -> 110 us (0.948)
  Pallas kernels: 59.4 us -> 45.9 us
  blocking collectives: 19.9 us -> 26.4 us
  waiting for transfers between devices: 6.4 us -> 8.6 us
    pallas_call x3, Pallas kernels: 58.6 us -> 45.1 us  [the longest x1 21.2 us: shards(): pl.pallas_call(rest_body, in_specs=[SMEM] * 5 + [VMEM] * 11, out_specs=[V...]
    all_to_all x1, blocking collectives: 19.9 us -> 26.4 us  [shards(): all_sums = lax.all_to_all(sums, axes, 0, 0, tiled=True)]
    all_to_all x1, waiting for transfers between devices: 0.01 us -> 2.3 us  [shards(): nodes = lax.all_to_all(node, axes, 0, 0)]
    all_to_all x1, starting transfers between devices: 10.2 us -> 11.5 us  [shards(): nodes = lax.all_to_all(node, axes, 0, 0)]
    unnamed x30 -> x32, local copies, waits for them, and re-layouts: 5.26 us -> 5.92 us
  transfers between devices with their start and end apart: 5 -> 5, of which waited for: 2 -> 2; matrix products, arithmetic and copies ran while one was open for 1% -> 0% of each run, Pallas kernels for 34% -> 17%
where the time goes in v2:
time: 110 us
  Pallas kernels  45.9 us (42%)
  blocking collectives  26.4 us (24%)
  starting transfers between devices  22.5 us (20%)
  waiting for transfers between devices  8.6 us (8%)
  local copies, waits for them, and re-layouts  5.92 us (5%)
    all_to_all x1, blocking collectives, shards(): all_sums = lax.all_to_all(sums, axes, 0, 0, tiled=True)  26.4 us
    pallas_call x1, Pallas kernels, shards(): pl.pallas_call(rest_body, in_specs=[SMEM] * 5 + [VMEM] * 11, out_specs=[V...  21.2 us
    pallas_call x1, Pallas kernels, shards(): pl.pallas_call(close_body, in_specs=[SMEM] * 4 + [VMEM] * 6, out_specs=[V...  18.6 us
    all_to_all x1, starting transfers between devices, shards(): nodes = lax.all_to_all(node, axes, 0, 0)  11.5 us
    ppermute x4, starting transfers between devices, shifted(): lax.ppermute(x, axis, [(i, i + by) for i in range(n) if 0 <= i + by < n])  11 us
    ppermute x4, waiting for transfers between devices, shifted(): lax.ppermute(x, axis, [(i, i + by) for i in range(n) if 0 <= i + by < n])  6.3 us
    unnamed x32, local copies, waits for them, and re-layouts  5.92 us
    pallas_call x1, Pallas kernels, shards(): pl.pallas_call(upward_body, in_specs=[HBM] * 6, out_specs=[VMEM] * 4, out...  5.34 us
  transfers between devices with their start and end apart: 5, of which 2 were waited for; matrix products, arithmetic and copies ran while one was open for 0% of the time, Pallas kernels for 17%

profile of v2, /device:TPU:1, one launch (start us, length us, event | category | flops | bytes accessed | tf_op | source)
XLA Modules:
  0.0 110.3 jit_solution(1703967326832267691)
XLA Ops:
  0.6 0.0 copy-start.12
  0.6 0.6 copy-done.12
  1.3 0.0 copy-start
  1.3 1.2 %copy-done = f32[8,64,512]{2,1,0:T(8,128)S(1)} copy-done((f32[8,64,512]{2,1,0:T(8,128)S(1)}, f32[8,64,512]{2,1,0:T(8,128)}, u32[]{:S(2)}) %copy-start) | copy-done | bytes 1048600
  2.5 0.0 copy-start.2
  2.5 0.9 copy-done.2
  3.4 0.0 copy-start.5
  3.4 0.9 copy-done.5
  4.3 0.0 copy-start.8
  4.3 0.8 copy-done.8
  5.2 0.0 copy-start.9
  5.2 0.7 copy-done.9
  5.9 5.3 %upward.1 = (f32[104,512]{1,0:T(8,128)S(1)}, f32[128,8,128]{2,1,0:T(8,128)}, f32[8,128]{1,0:T(8,128)S(1)}, s32[32,128]{1,0:T(8,128)S(1)}) custom-call(s32[32,128]{1,0:T(8,128)S(1)} %bitcast.18, f32[4,4096]{1,0:T(4,128)S(1)} %copy-done.8, f32[8,4096]{1,0:T(8,128)S(1)} %copy-done.2, f32[8,64,512]{2,1,0:T(8,128)S(1)} %copy-done, f32[64,512]{1,0:T(8,128)S(1)} %bitcast.15, ...), custom_call_target="tpu_custom_call" | custom-call | tf_op jit(solution)/shard_map/upward/pallas_call | solution.py:380
  11.2 11.5 %all-to-all-start = ((f32[128,8,128]{2,1,0:T(8,128)}), f32[128,8,128]{2,1,0:T(8,128)S(1)}, u32[]{:S(2)}, u32[]{:S(2)}) async-start(f32[128,8,128]{2,1,0:T(8,128)} %get-tuple-element.14), calls=%async_computation | async-start | bytes 1048576 | tf_op jit(solution)/shard_map/all_to_all | solution.py:407
  22.7 1.3 %collective-permute-start.1 = (f32[104,512]{1,0:T(8,128)S(1)}, f32[104,512]{1,0:T(8,128)S(1)}, u32[]{:S(2)}, u32[]{:S(2)}) collective-permute-start(f32[104,512]{1,0:T(8,128)S(1)} %get-tuple-element.13.mid_ref), channel_id=1, source_target_pairs={{1,0},{2,1},{3,2},{5,4},{6,5},{7,6},{9,8},{10,9},{11,10},{13,12},{... | collective-permute-start | bytes 638984 | tf_op jit(solution)/shard_map/ppermute | solution.py:370
  24.0 4.0 %collective-permute-start = (f32[104,512]{1,0:T(8,128)S(1)}, f32[104,512]{1,0:T(8,128)S(1)}, u32[]{:S(2)}, u32[]{:S(2)}) collective-permute-start(f32[104,512]{1,0:T(8,128)S(1)} %get-tuple-element.13.mid_ref), channel_id=1, source_target_pairs={{0,1},{1,2},{2,3},{4,5},{5,6},{6,7},{8,9},{9,10},{10,11},{12,13},{... | collective-permute-start | bytes 638984 | tf_op jit(solution)/shard_map/ppermute | solution.py:370
  28.1 0.1 pad_add_fusion.place_ref
  28.1 6.3 %collective-permute-done.1.right_ref = f32[104,512]{1,0:T(8,128)S(1)} collective-permute-done((f32[104,512]{1,0:T(8,128)S(1)}, f32[104,512]{1,0:T(8,128)S(1)}, u32[]{:S(2)}, u32[]{:S(2)}) %collective-permute-start.1) | collective-permute-done | bytes 213024 | tf_op jit(solution)/shard_map/ppermute | solution.py:370
  34.4 0.0 collective-permute-done.left_ref
  34.4 2.3 %all-to-all-done.node_ref = f32[128,8,128]{2,1,0:T(8,128)S(1)} async-done(((f32[128,8,128]{2,1,0:T(8,128)}), f32[128,8,128]{2,1,0:T(8,128)S(1)}, u32[]{:S(2)}, u32[]{:S(2)}) %all-to-all-start) | async-done | bytes 524320 | tf_op jit(solution)/shard_map/all_to_all | solution.py:407
  36.7 0.0 copy-start.6
  36.7 0.0 copy-start.10
  36.8 0.0 copy-start.13
  36.8 0.0 copy-start.14
  36.8 2.4 %collective-permute-start.3 = (f32[3,104,512]{2,1,0:T(8,128)S(1)}, f32[3,104,512]{2,1,0:T(8,128)S(1)}, u32[]{:S(2)}, u32[]{:S(2)}) collective-permute-start(f32[3,104,512]{2,1,0:T(8,128)S(1)} %pad_maximum_fusion), channel_id=1, source_target_pairs={{4,0},{8,4},{12,8},{16,12},{20,16},{24,20},{28,24},{32,28},{36,32}... | collective-permute-start | bytes 1916936 | tf_op jit(solution)/shard_map/ppermute | solution.py:370
  39.2 3.3 %collective-permute-start.2 = (f32[3,104,512]{2,1,0:T(8,128)S(1)}, f32[3,104,512]{2,1,0:T(8,128)S(1)}, u32[]{:S(2)}, u32[]{:S(2)}) collective-permute-start(f32[3,104,512]{2,1,0:T(8,128)S(1)} %pad_maximum_fusion), channel_id=1, source_target_pairs={{0,4},{4,8},{8,12},{12,16},{16,20},{20,24},{24,28},{28,32},{32,36}... | collective-permute-start | bytes 1916936 | tf_op jit(solution)/shard_map/ppermute | solution.py:370
  42.5 0.0 copy-done.6
  42.5 0.0 copy-done.10
  42.5 0.0 copy-done.13
  42.5 0.0 copy-done.14
  42.5 0.0 copy-start.1
  42.6 0.0 copy-start.3
  42.6 0.0 copy-start.4
  42.6 18.6 %close.1 = (f32[8,8,512]{2,1,0:T(8,128)S(1)}, f32[8,512]{1,0:T(8,128)S(1)}) custom-call(s32[8,8]{1,0:T(8,128)S(1)} %copy-done.10, s32[8]{0:T(128)S(1)} %copy-done.13, s32[3]{0:T(128)S(1)} %pad_add_fusion.place_ref, f32[4]{0:T(128)S(1)} %copy-done.14, f32[104,512]{1,0:T(8,128)S(1)} %collective-permute-done.left_ref, ...), custom_call_target="tpu_custom_call" | custom-call | flops 10000000000 | bytes 2097152 | tf_op jit(solution)/shard_map/close/pallas_call | solution.py:427
  61.2 0.0 copy-start.11
  61.2 0.0 collective-permute-done.3.down_ref
  61.2 0.0 collective-permute-done.2.up_ref
  61.2 0.0 copy-start.15
  61.2 0.0 copy-done.1
  61.2 0.0 copy-done.3
  61.2 0.0 copy-done.4
  61.2 0.6 copy-done.11
  61.9 0.0 copy-done.15
  61.9 21.2 %rest.1 = (f32[8,4096]{1,0:T(8,128)S(1)}, f32[128,128]{1,0:T(8,128)S(1)}) custom-call(s32[8,8]{1,0:T(8,128)S(1)} %copy-done.10, s32[8]{0:T(128)S(1)} %copy-done.13, s32[8,8]{1,0:T(8,128)S(1)} %copy-done.11, f32[4]{0:T(128)S(1)} %copy-done.14, f32[8]{0:T(128)S(1)} %copy-done.15, f32[104,512]{1,0:T(8,128)S(1)} %collective-permute-done.left_ref, ...), custom_call_target="tpu_custom_call" | custom-call | tf_op jit(solution)/shard_map/rest/pallas_call | solution.py:440
  83.0 0.0 copy-start.7
  83.0 26.4 %all_to_all.16 = f32[128,1,128]{2,1,0:T(1,128)S(1)} all-to-all(f32[128,1,128]{2,1,0:T(1,128)S(1)} %bitcast.17), channel_id=1, replica_groups=mesh['leaf'=32,'tm'=4] {'leaf','tm'}, dimensions={0} | all-to-all | bytes 131072 | tf_op jit(solution)/shard_map/all_to_all | solution.py:453
  109.4 0.0 copy-done.7
  109.4 0.8 update.1
  (1 shorter events, 0.0 us)
Async XLA Ops:
  0.6 0.7 copy-start.12
  1.3 1.2 %copy-start = (f32[8,64,512]{2,1,0:T(8,128)S(1)}, f32[8,64,512]{2,1,0:T(8,128)}, u32[]{:S(2)}) copy-start(f32[8,64,512]{2,1,0:T(8,128)} %bases_ref.1) | copy-start | bytes 3145732
  2.5 0.9 copy-start.2
  3.4 0.9 copy-start.5
  4.3 0.8 copy-start.8
  5.2 0.7 copy-start.9
  11.2 25.5 %all-to-all-start = ((f32[128,8,128]{2,1,0:T(8,128)}), f32[128,8,128]{2,1,0:T(8,128)S(1)}, u32[]{:S(2)}, u32[]{:S(2)}) async-start(f32[128,8,128]{2,1,0:T(8,128)} %get-tuple-element.14), calls=%async_computation | async-start | bytes 1048576 | tf_op jit(solution)/shard_map/all_to_all | solution.py:407
  22.7 11.7 %collective-permute-start.1 = (f32[104,512]{1,0:T(8,128)S(1)}, f32[104,512]{1,0:T(8,128)S(1)}, u32[]{:S(2)}, u32[]{:S(2)}) collective-permute-start(f32[104,512]{1,0:T(8,128)S(1)} %get-tuple-element.13.mid_ref), channel_id=1, source_target_pairs={{1,0},{2,1},{3,2},{5,4},{6,5},{7,6},{9,8},{10,9},{11,10},{13,12},{... | collective-permute-start | bytes 638984 | tf_op jit(solution)/shard_map/ppermute | solution.py:370
  24.0 10.4 %collective-permute-start = (f32[104,512]{1,0:T(8,128)S(1)}, f32[104,512]{1,0:T(8,128)S(1)}, u32[]{:S(2)}, u32[]{:S(2)}) collective-permute-start(f32[104,512]{1,0:T(8,128)S(1)} %get-tuple-element.13.mid_ref), channel_id=1, source_target_pairs={{0,1},{1,2},{2,3},{4,5},{5,6},{6,7},{8,9},{9,10},{10,11},{12,13},{... | collective-permute-start | bytes 638984 | tf_op jit(solution)/shard_map/ppermute | solution.py:370
  36.7 5.8 %copy-start.6 = (f32[1,64,512]{2,1,0:T(8,128)S(1)}, f32[1,64,512]{2,1,0:T(8,128)}, u32[]{:S(2)}) copy-start(f32[1,64,512]{2,1,0:T(8,128)} %param.19) | copy-start | bytes 393220
  36.7 5.8 %copy-start.10 = (s32[8,8]{1,0:T(8,128)S(1)}, s32[8,8]{1,0:T(8,128)}, u32[]{:S(2)}) copy-start(s32[8,8]{1,0:T(8,128)} %near_ref.3) | copy-start | bytes 772
  36.8 5.8 %copy-start.13 = (s32[8]{0:T(128)S(1)}, s32[8]{0:T(128)}, u32[]{:S(2)}) copy-start(s32[8]{0:T(128)} %count_ref.3) | copy-start | bytes 100
  36.8 5.8 %copy-start.14 = (f32[4]{0:T(128)S(1)}, f32[4]{0:T(128)}, u32[]{:S(2)}) copy-start(f32[4]{0:T(128)} %scale_ref.3) | copy-start | bytes 52
  36.8 24.4 %collective-permute-start.3 = (f32[3,104,512]{2,1,0:T(8,128)S(1)}, f32[3,104,512]{2,1,0:T(8,128)S(1)}, u32[]{:S(2)}, u32[]{:S(2)}) collective-permute-start(f32[3,104,512]{2,1,0:T(8,128)S(1)} %pad_maximum_fusion), channel_id=1, source_target_pairs={{4,0},{8,4},{12,8},{16,12},{20,16},{24,20},{28,24},{32,28},{36,32}... | collective-permute-start | bytes 1916936 | tf_op jit(solution)/shard_map/ppermute | solution.py:370
  39.2 21.9 %collective-permute-start.2 = (f32[3,104,512]{2,1,0:T(8,128)S(1)}, f32[3,104,512]{2,1,0:T(8,128)S(1)}, u32[]{:S(2)}, u32[]{:S(2)}) collective-permute-start(f32[3,104,512]{2,1,0:T(8,128)S(1)} %pad_maximum_fusion), channel_id=1, source_target_pairs={{0,4},{4,8},{8,12},{12,16},{16,20},{20,24},{24,28},{28,32},{32,36}... | collective-permute-start | bytes 1916936 | tf_op jit(solution)/shard_map/ppermute | solution.py:370
  42.5 18.7 %copy-start.1 = (f32[8,64,512]{2,1,0:T(8,128)S(1)}, f32[8,64,512]{2,1,0:T(8,128)}, u32[]{:S(2)}) copy-start(f32[8,64,512]{2,1,0:T(8,128)} %bases_ref.1) | copy-start | bytes 3145732
  42.6 18.7 %copy-start.3 = (f32[8,4096]{1,0:T(8,128)S(1)}, f32[8,4096]{1,0:T(8,128)}, u32[]{:S(2)}) copy-start(f32[8,4096]{1,0:T(8,128)} %p_ref.3) | copy-start | bytes 393220
  42.6 18.7 %copy-start.4 = (f32[8,4096]{1,0:T(8,128)S(1)}, f32[8,4096]{1,0:T(8,128)}, u32[]{:S(2)}) copy-start(f32[8,4096]{1,0:T(8,128)} %res_ref.3) | copy-start | bytes 393220
  61.2 0.7 copy-start.11
  61.2 0.7 copy-start.15
  83.0 26.4 %copy-start.7 = (f32[8,4096]{1,0:T(8,128)S(1)}, f32[8,4096]{1,0:T(8,128)}, u32[]{:S(2)}) copy-start(f32[8,4096]{1,0:T(8,128)} %it_ref.1) | copy-start | bytes 393220

commit v3 on v2

--- a/solution.py
+++ b/solution.py
@@ -1,3 +1,4 @@
+import functools
 import math
 
 import jax
@@ -13,9 +14,10 @@
 LN2 = math.log(2.0)
 LOG2E = 1.0 / LN2
 UNIT = math.sqrt(3.0) * LOG2E
+FACTOR = -LN2 * math.e
 VMEM = pl.BlockSpec(memory_space=pltpu.VMEM)
 SMEM = pl.BlockSpec(memory_space=pltpu.SMEM)
-HBM = pl.BlockSpec(memory_space=pltpu.HBM)
+ANY = pl.BlockSpec(memory_space=pl.ANY)
 PART = 256
 
 
@@ -72,8 +74,8 @@
 
 def kernel_of(z):
     z = jnp.maximum(z, 1e-30)
-    v = z * lax.rsqrt(z)
-    return (v + LOG2E) * jnp.exp2(-v)
+    q = -LOG2E - z * lax.rsqrt(z)
+    return q * jnp.exp2(q)
 
 
 def split(k):
@@ -93,7 +95,7 @@
     return picked
 
 
-def upward_body(order_hbm, x_hbm, p_hbm, bases_hbm, transfer_hbm, skel_hbm, halo_ref, node_ref, own_ref, inv_ref, order_ref, xx, p_ref, bases_ref, transfer_ref, skel_ref, first, slot, tally, sems):
+def gather_body(order_hbm, x_hbm, p_hbm, bases_hbm, halo_ref, first_ref, order_ref, xx, p_ref, bases_ref, sems):
     leaf_dev, rank, leaf_pts = bases_ref.shape
     points = p_ref.shape[1]
     chunks = points // 128
@@ -107,14 +109,11 @@
                 (x_hbm, xx.at[4:8, :]),
                 (p_hbm, p_ref),
                 (bases_hbm, bases_ref),
-                (transfer_hbm, transfer_ref),
-                (skel_hbm, skel_ref),
             ]
         )
     ]
     for move in moves:
         move.start()
-    tally[...] = jnp.zeros_like(tally)
     for move in moves[:4]:
         move.wait()
 
@@ -126,32 +125,29 @@
         for h in range(2):
             leaf = 2 * g + h
             for j in range(per_leaf):
-                c = leaf * per_leaf + j
-                ids = order_ref[pl.ds(c, 1), :]
+                ids = order_ref[pl.ds(leaf * per_leaf + j, 1), :]
                 got_x, got_p = gather_lanes([loads(xx), loads(p_ref)], jnp.broadcast_to(ids, (8, 128)))
                 kept.append(got_x)
                 halo_ref[pl.ds(pl.multiple_of(32 + leaf * 8, 8), 8), j * 128 : (j + 1) * 128] = got_p
-                low = jnp.where(row_ids((128, 128)) == (ids & 127), 1.0, 0.0).astype(BF16)
-                row = row_ids((chunks, 128)) == (ids >> 7)
-                lane = lane_ids((chunks, 128))
-                digit1 = jnp.where(row, (2 * c + (lane >> 6)).astype(F32), 0.0)
-                digit0 = jnp.where(row, (lane & 63).astype(F32), 0.0)
-                digits = jnp.concatenate([digit1, digit0], axis=0).astype(BF16)
-                tally[...] += contract(digits, low, ((1,), (1,)))
-            first[leaf] = kept[h * per_leaf]
+            first_ref[leaf] = kept[h * per_leaf]
         for j in range(per_leaf):
             both = jnp.where(row_ids((8, 128)) < 4, kept[j], kept[per_leaf + j])
             halo_ref[pl.ds(pl.multiple_of(g * 8, 8), 8), j * 128 : (j + 1) * 128] = both
         return 0
 
     lax.fori_loop(0, leaf_dev // 2, two_leaves, 0)
-    inv_ref[...] = (64.0 * tally[0:chunks, :] + tally[chunks : 2 * chunks, :] + 0.5).astype(jnp.int32)
-    for move in moves[4:]:
-        move.wait()
+    moves[4].wait()
     for leaf in range(leaf_dev):
         coef = contract(halo_ref[32 + leaf * 8 : 40 + leaf * 8, :], bases_ref[leaf], ((1,), (1,)), EXACT)
         halo_ref[96:104, leaf * rank : (leaf + 1) * rank] = coef
-        slot[:, leaf * rank : (leaf + 1) * rank] = first[leaf][:, :rank]
+
+
+def node_body(order_ref, halo_ref, first_ref, transfer_ref, skel_ref, node_ref, own_ref, inv_ref, slot):
+    chunks = order_ref.shape[0]
+    rank = transfer_ref.shape[0]
+    leaf_dev = first_ref.shape[0]
+    for leaf in range(leaf_dev):
+        slot[:, leaf * rank : (leaf + 1) * rank] = first_ref[leaf][:, :rank]
     weights = contract(halo_ref[96:104, :], transfer_ref[...], ((1,), (1,)), EXACT)
     slots = [lambda s=s: slot[:, s * 128 : (s + 1) * 128] for s in range(leaf_dev * rank // 128)]
     ids = jnp.concatenate([skel_ref[...], skel_ref[...]], axis=1)
@@ -159,6 +155,17 @@
     tile = jnp.concatenate([weights, node_x[:, :rank]], axis=1)
     own_ref[...] = tile
     node_ref[...] = jnp.broadcast_to(tile[None], node_ref.shape)
+    tally = jnp.zeros((2 * chunks, 128), F32)
+    for c in range(chunks):
+        ids = order_ref[c : c + 1, :]
+        low = jnp.where(row_ids((128, 128)) == (ids & 127), 1.0, 0.0).astype(BF16)
+        row = row_ids((chunks, 128)) == (ids >> 7)
+        lane = lane_ids((chunks, 128))
+        digit1 = jnp.where(row, (2 * c + (lane >> 6)).astype(F32), 0.0)
+        digit0 = jnp.where(row, (lane & 63).astype(F32), 0.0)
+        digits = jnp.concatenate([digit1, digit0], axis=0).astype(BF16)
+        tally = tally + contract(digits, low, ((1,), (1,)))
+    inv_ref[...] = (64.0 * tally[0:chunks] + tally[chunks : 2 * chunks] + 0.5).astype(jnp.int32)
 
 
 def scale_rows(scale_ref, shape):
@@ -182,10 +189,10 @@
             if tgt is not None:
                 tgt[leaf, :, 0:width] = made[1]
             if wgt is not None:
-                wgt[base + leaf] = halves(ref[32 + leaf * 8 : 40 + leaf * 8, :] * LN2)
+                wgt[base + leaf] = halves(ref[32 + leaf * 8 : 40 + leaf * 8, :] * FACTOR)
             if coef is not None:
                 rank = coef.shape[2]
-                coef[base + leaf] = halves(ref[96:104, leaf * rank : (leaf + 1) * rank] * LN2)
+                coef[base + leaf] = halves(ref[96:104, leaf * rank : (leaf + 1) * rank] * FACTOR)
 
 
 def list_pairs(near_ref, count_ref, keep, slot_of, idle, pairs):
@@ -250,7 +257,7 @@
     wgt[wgt.shape[0] - 1] = jnp.zeros(wgt.shape[1:], BF16)
 
 
-def close_body(near_ref, count_ref, place_ref, scale_ref, left_ref, mid_ref, right_ref, node_ref, own_ref, transfer_ref, out_ref, pushed_ref, pairs, src, tgt, wgt, z, high, low, node_src, node_wgt):
+def close_body(tm_size, near_ref, count_ref, place_ref, scale_ref, left_ref, mid_ref, right_ref, node_ref, own_ref, transfer_ref, out_ref, pushed_ref, pairs, src, tgt, wgt, z, high, low, node_src, node_wgt):
     leaf_dev, rhs, leaf_pts = out_ref.shape
     devices, _, _ = node_ref.shape
     rank = own_ref.shape[1] // 2
@@ -263,13 +270,12 @@
     out_ref[...] = jnp.zeros_like(out_ref)
     near_pairs(pairs, n, src, tgt, wgt, out_ref, z, high, low)
 
-    tm_size = place_ref[2]
     lane = lane_ids((8, 128))
 
     def distant(e):
         far_a = jnp.abs(e // tm_size - place_ref[0]) > 1
         far_b = jnp.abs(e % tm_size - place_ref[1]) > 1
-        return jnp.where(far_a | far_b, LN2, 0.0)
+        return jnp.where(far_a | far_b, FACTOR, 0.0)
 
     def unpack(g, _):
         xs, ws = [], []
@@ -298,7 +304,7 @@
     pushed_ref[...] = jnp.dot(device_far, transfer_ref[...], precision=EXACT, preferred_element_type=F32)
 
 
-def rest_body(near_ref, count_ref, far_ref, scale_ref, noise_ref, left_ref, mid_ref, right_ref, up_ref, down_ref, close_ref, pushed_ref, bases_ref, inv_ref, p_ref, res_ref, image_ref, sums_ref, pairs, src, tgt, wgt, coef, z, high, low, out, flat):
+def rest_body(near_ref, count_ref, far_ref, scale_ref, noise_ref, left_ref, mid_ref, right_ref, up_ref, down_ref, close_ref, pushed_ref, bases_ref, inv_ref, p_ref, res_ref, image_ref, sums_ref, pairs, src, tgt, wgt, coef, z, high, low, out, flat, far_src, far_wgt):
     leaf_dev, rank, leaf_pts = bases_ref.shape
     scale = scale_rows(scale_ref, (8, leaf_pts))
     n = list_pairs(near_ref, count_ref, lambda k: (k < 3) | (k >= 6), lambda w: w, 9 * leaf_dev, pairs)
@@ -313,13 +319,14 @@
     near_pairs(pairs, n, src, tgt, wgt, out, z, high, low)
 
     for leaf in range(leaf_dev):
-        far = jnp.zeros((16, rank), F32)
         for j in range(far_ref.shape[1]):
             w = far_ref[leaf, j]
-            z_far = contract(src[w, :, 0:rank], tgt[leaf, :, 0:rank], ((0,), (0,)))
-            k_high, k_low = split(kernel_of(z_far))
-            far = far + jnp.dot(coef[w], k_high, preferred_element_type=F32)
-            far = far + jnp.dot(coef[w], k_low, preferred_element_type=F32)
+            at = slice(j * rank, (j + 1) * rank)
+            far_src[leaf, :, at] = src[w, :, 0:rank]
+            far_wgt[leaf, :, at] = coef[w]
+    for leaf in range(leaf_dev):
+        k_high, k_low = split(kernel_of(contract(tgt[leaf, :, 0:rank], far_src[leaf], ((0,), (0,)))))
+        far = contract(far_wgt[leaf], k_high, ((1,), (1,))) + contract(far_wgt[leaf], k_low, ((1,), (1,)))
         incoming = halves(far[:8] + far[8:] + pushed_ref[:, leaf * rank : (leaf + 1) * rank])
         base_high, base_low = split(bases_ref[leaf])
         got = jnp.dot(incoming, base_high, preferred_element_type=F32)
@@ -377,31 +384,32 @@
     devices = lax.axis_size("leaf") * lax.axis_size("tm")
     chunks = points // 128
     shape = jax.ShapeDtypeStruct
-    halo, node, own, inverse = pl.pallas_call(
-        upward_body,
-        in_specs=[HBM] * 6,
-        out_specs=[VMEM] * 4,
-        out_shape=[
-            shape((13 * leaf_dev, leaf_pts), F32),
-            shape((devices, 8, 128), F32),
-            shape((8, 128), F32),
-            shape((chunks, 128), jnp.int32),
-        ],
+    by_row = order.reshape(chunks, 128)
+    halo, first = pl.pallas_call(
+        gather_body,
+        in_specs=[ANY] * 4,
+        out_specs=[VMEM] * 2,
+        out_shape=[shape((13 * leaf_dev, leaf_pts), F32), shape((leaf_dev, 8, 128), F32)],
         scratch_shapes=[
             pltpu.VMEM((chunks, 128), jnp.int32),
             pltpu.VMEM((8, points), F32),
             pltpu.VMEM((rhs, points), F32),
             pltpu.VMEM(bases.shape, F32),
-            pltpu.VMEM(transfer.shape[1:], F32),
-            pltpu.VMEM(device_skel.shape, jnp.int32),
-            pltpu.VMEM((leaf_dev, 8, 128), F32),
-            pltpu.VMEM((8, leaf_dev * rank), F32),
-            pltpu.VMEM((2 * chunks, 128), F32),
-            pltpu.SemaphoreType.DMA((7,)),
+            pltpu.SemaphoreType.DMA((5,)),
         ],
+        compiler_params=params(60),
+        name="gather",
+    )(by_row, coords, direction, bases)
+    node, own, inverse = pl.pallas_call(
+        node_body,
+        in_specs=[VMEM] * 5,
+        out_specs=[VMEM] * 3,
+        out_shape=[shape((devices, 8, 128), F32), shape((8, 128), F32), shape((chunks, 128), jnp.int32)],
+        scratch_shapes=[pltpu.VMEM((8, leaf_dev * rank), F32)],
         compiler_params=params(24),
-        name="upward",
-    )(order.reshape(chunks, 128), coords, direction, bases, transfer[0], device_skel)
+        cost_estimate=pl.CostEstimate(flops=10**9, bytes_accessed=2**20, transcendentals=0),
+        name="node",
+    )(by_row, halo, first, transfer[0], device_skel)
     left = shifted(halo, "tm", 1)
     right = shifted(halo, "tm", -1)
     nodes = lax.all_to_all(node, axes, 0, 0)
@@ -409,7 +417,7 @@
     row = jnp.stack([left, halo, right])
     up = shifted(row, "leaf", 1)
     down = shifted(row, "leaf", -1)
-    place = jnp.stack([lax.axis_index("leaf"), lax.axis_index("tm"), lax.axis_size("tm")]).astype(jnp.int32)
+    place = jnp.stack([lax.axis_index("leaf"), lax.axis_index("tm")]).astype(jnp.int32)
 
     def pipeline(sources):
         return [
@@ -425,7 +433,7 @@
     ]
     listed = pltpu.SMEM((near_list.size + 4,), jnp.int32)
     close, pushed = pl.pallas_call(
-        close_body,
+        functools.partial(close_body, lax.axis_size("tm")),
         in_specs=[SMEM] * 4 + [VMEM] * 6,
         out_specs=[VMEM] * 2,
         out_shape=[shape((leaf_dev, rhs, leaf_pts), F32), shape((rhs, leaf_dev * rank), F32)],
@@ -446,7 +454,12 @@
         + pipeline(9 * leaf_dev)
         + [pltpu.VMEM((9 * leaf_dev, 16, rank), BF16)]
         + buffers
-        + [pltpu.VMEM((leaf_dev, rhs, leaf_pts), F32), pltpu.VMEM((rhs, points), F32)],
+        + [
+            pltpu.VMEM((leaf_dev, rhs, leaf_pts), F32),
+            pltpu.VMEM((rhs, points), F32),
+            pltpu.VMEM((leaf_dev, 32, far_list.shape[1] * rank), BF16),
+            pltpu.VMEM((leaf_dev, 16, far_list.shape[1] * rank), BF16),
+        ],
         compiler_params=params(24),
         name="rest",
     )(near_list, near_count, far_list, inv_scale, noise, left, halo, right, up, down, close, pushed, bases, inverse, direction, residual)

time: 110 us -> 107 us (0.973)
  blocking collectives: 26.4 us -> 22.1 us
  Pallas kernels: 45.9 us -> 49.1 us
  local copies, waits for them, and re-layouts: 5.92 us -> 3.02 us
    all_to_all x1, blocking collectives: 26.4 us -> 22.1 us  [shards(): all_sums = lax.all_to_all(sums, axes, 0, 0, tiled=True)]
    pallas_call x2 -> x3, Pallas kernels: 23.9 us -> 27.2 us  [the longest x1 20.4 us: shards(): pl.pallas_call(functools.partial(close_body, lax.axis_size('tm')), in_spe...]
    unnamed x32 -> x30, local copies, waits for them, and re-layouts: 5.92 us -> 3.02 us
  transfers between devices with their start and end apart: 5 -> 5, of which waited for: 2 -> 2; matrix products, arithmetic and copies ran while one was open for 0% -> 0% of each run, Pallas kernels for 17% -> 19%
where the time goes in v3:
time: 107 us; the launch traced here: 106 us
  Pallas kernels  49.1 us (46%)
  starting transfers between devices  22.3 us (21%)
  blocking collectives  22.1 us (21%)
  waiting for transfers between devices  8.59 us (8%)
  local copies, waits for them, and re-layouts  3.02 us (3%)
    all_to_all x1, blocking collectives, shards(): all_sums = lax.all_to_all(sums, axes, 0, 0, tiled=True)  22.1 us
    pallas_call x1, Pallas kernels, shards(): pl.pallas_call(rest_body, in_specs=[SMEM] * 5 + [VMEM] * 11, out_specs=[V...  21.1 us
    pallas_call x1, Pallas kernels, shards(): pl.pallas_call(functools.partial(close_body, lax.axis_size('tm')), in_spe...  20.4 us
    all_to_all x1, starting transfers between devices, shards(): nodes = lax.all_to_all(node, axes, 0, 0)  11.5 us
    ppermute x4, starting transfers between devices, shifted(): lax.ppermute(x, axis, [(i, i + by) for i in range(n) if 0 <= i + by < n])  10.9 us
    ppermute x4, waiting for transfers between devices, shifted(): lax.ppermute(x, axis, [(i, i + by) for i in range(n) if 0 <= i + by < n])  6.29 us
    pallas_call x1, Pallas kernels, shards(): pl.pallas_call(gather_body, in_specs=[ANY] * 4, out_specs=[VMEM] * 2, out...  5.29 us
    unnamed x30, local copies, waits for them, and re-layouts  3.02 us
  transfers between devices with their start and end apart: 5, of which 2 were waited for; matrix products, arithmetic and copies ran while one was open for 0% of the time, Pallas kernels for 19%

profile of v3, /device:TPU:1, one launch (start us, length us, event | category | flops | bytes accessed | tf_op | source)
XLA Modules:
  0.0 106.2 jit_solution(12803468449277697613)
XLA Ops:
  0.6 0.0 copy-start.6
  0.6 0.0 copy-start.12
  0.6 5.3 %gather.1 = (f32[104,512]{1,0:T(8,128)}, f32[8,8,128]{2,1,0:T(8,128)}) custom-call(s32[32,128]{1,0:T(8,128)} %bitcast.16, f32[4,4096]{1,0:T(4,128)} %x_hbm.1, f32[8,4096]{1,0:T(8,128)} %p_ref.3, f32[8,64,512]{2,1,0:T(8,128)} %bases_ref.1), custom_call_target="tpu_custom_call" | custom-call | tf_op jit(solution)/shard_map/gather/pallas_call | solution.py:388
  5.9 0.0 copy-start.14
  6.0 0.0 copy-done.6
  6.0 0.0 copy-done.12
  6.0 0.6 copy-done.14
  6.6 0.0 copy-start.2
  6.6 0.9 copy-done.2
  7.5 0.0 copy-start.13
  7.5 0.8 copy-done.13
  8.3 1.5 %node.1 = (f32[128,8,128]{2,1,0:T(8,128)}, f32[8,128]{1,0:T(8,128)S(1)}, s32[32,128]{1,0:T(8,128)S(1)}) custom-call(s32[32,128]{1,0:T(8,128)S(1)} %bitcast.17, f32[104,512]{1,0:T(8,128)S(1)} %copy-done.2, f32[8,8,128]{2,1,0:T(8,128)S(1)} %copy-done.13, f32[64,512]{1,0:T(8,128)S(1)} %bitcast.18, s32[1,64]{1,0:T(1,128)S(1)} %copy-done.14), custom_call_target="tpu_custom_call" | custom-call | flops 1000000000 | bytes 1048576 | tf_op jit(solution)/shard_map/node/pallas_call | solution.py:403
  9.8 0.0 copy-start.3
  9.8 11.5 %all-to-all-start = ((f32[128,8,128]{2,1,0:T(8,128)}), f32[128,8,128]{2,1,0:T(8,128)S(1)}, u32[]{:S(2)}, u32[]{:S(2)}) async-start(f32[128,8,128]{2,1,0:T(8,128)} %get-tuple-element.16), calls=%async_computation | async-start | bytes 1048576 | tf_op jit(solution)/shard_map/all_to_all | solution.py:415
  21.3 0.0 copy-done.3
  21.3 1.3 %collective-permute-start.1 = (f32[104,512]{1,0:T(8,128)S(1)}, f32[104,512]{1,0:T(8,128)S(1)}, u32[]{:S(2)}, u32[]{:S(2)}) collective-permute-start(f32[104,512]{1,0:T(8,128)S(1)} %copy-done.3), channel_id=1, source_target_pairs={{1,0},{2,1},{3,2},{5,4},{6,5},{7,6},{9,8},{10,9},{11,10},{13,12},{... | collective-permute-start | bytes 638984 | tf_op jit(solution)/shard_map/ppermute | solution.py:377
  22.6 4.0 %collective-permute-start = (f32[104,512]{1,0:T(8,128)S(1)}, f32[104,512]{1,0:T(8,128)S(1)}, u32[]{:S(2)}, u32[]{:S(2)}) collective-permute-start(f32[104,512]{1,0:T(8,128)S(1)} %copy-done.3), channel_id=1, source_target_pairs={{0,1},{1,2},{2,3},{4,5},{5,6},{6,7},{8,9},{9,10},{10,11},{12,13},{... | collective-permute-start | bytes 638984 | tf_op jit(solution)/shard_map/ppermute | solution.py:377
  26.6 0.1 pad_add_fusion.place_ref
  26.7 6.3 %collective-permute-done.1.right_ref = f32[104,512]{1,0:T(8,128)S(1)} collective-permute-done((f32[104,512]{1,0:T(8,128)S(1)}, f32[104,512]{1,0:T(8,128)S(1)}, u32[]{:S(2)}, u32[]{:S(2)}) %collective-permute-start.1) | collective-permute-done | bytes 213024 | tf_op jit(solution)/shard_map/ppermute | solution.py:377
  33.0 0.0 collective-permute-done.left_ref
  33.0 2.3 %all-to-all-done.node_ref = f32[128,8,128]{2,1,0:T(8,128)S(1)} async-done(((f32[128,8,128]{2,1,0:T(8,128)}), f32[128,8,128]{2,1,0:T(8,128)S(1)}, u32[]{:S(2)}, u32[]{:S(2)}) %all-to-all-start) | async-done | bytes 524320 | tf_op jit(solution)/shard_map/all_to_all | solution.py:415
  35.3 0.0 copy-start.7
  35.3 0.0 copy-start.9
  35.3 0.0 copy-start.10
  35.3 2.3 %collective-permute-start.3 = (f32[3,104,512]{2,1,0:T(8,128)S(1)}, f32[3,104,512]{2,1,0:T(8,128)S(1)}, u32[]{:S(2)}, u32[]{:S(2)}) collective-permute-start(f32[3,104,512]{2,1,0:T(8,128)S(1)} %pad_maximum_fusion), channel_id=1, source_target_pairs={{4,0},{8,4},{12,8},{16,12},{20,16},{24,20},{28,24},{32,28},{36,32}... | collective-permute-start | bytes 1916936 | tf_op jit(solution)/shard_map/ppermute | solution.py:377
  37.7 3.3 %collective-permute-start.2 = (f32[3,104,512]{2,1,0:T(8,128)S(1)}, f32[3,104,512]{2,1,0:T(8,128)S(1)}, u32[]{:S(2)}, u32[]{:S(2)}) collective-permute-start(f32[3,104,512]{2,1,0:T(8,128)S(1)} %pad_maximum_fusion), channel_id=1, source_target_pairs={{0,4},{4,8},{8,12},{12,16},{16,20},{20,24},{24,28},{28,32},{32,36}... | collective-permute-start | bytes 1916936 | tf_op jit(solution)/shard_map/ppermute | solution.py:377
  40.9 0.0 copy-done.7
  40.9 0.0 copy-done.9
  40.9 0.0 copy-done.10
  41.0 0.0 copy-start
  41.0 0.0 copy-start.1
  41.0 0.0 copy-start.4
  41.0 20.4 %close.1 = (f32[8,8,512]{2,1,0:T(8,128)S(1)}, f32[8,512]{1,0:T(8,128)S(1)}) custom-call(s32[8,8]{1,0:T(8,128)S(1)} %copy-done.7, s32[8]{0:T(128)S(1)} %copy-done.9, s32[2]{0:T(128)S(1)} %pad_add_fusion.place_ref, f32[4]{0:T(128)S(1)} %copy-done.10, f32[104,512]{1,0:T(8,128)S(1)} %collective-permute-done.left_ref, f32[104,512]{1,0:T(8,128)S(1)} %copy-done.3, ...), custom_call_target="tpu_custom_call" | custom-call | flops 10000000000 | bytes 2097152 | tf_op jit(solution)/shard_map/close/pallas_call | solution.py:435
  61.4 0.0 copy-start.8
  61.4 0.0 collective-permute-done.3.down_ref
  61.4 0.0 collective-permute-done.2.up_ref
  61.4 0.0 copy-start.11
  61.4 0.0 copy-done
  61.4 0.0 copy-done.1
  61.4 0.0 copy-done.4
  61.4 0.6 copy-done.8
  62.1 0.0 copy-done.11
  62.1 21.1 %rest.1 = (f32[8,4096]{1,0:T(8,128)S(1)}, f32[128,128]{1,0:T(8,128)S(1)}) custom-call(s32[8,8]{1,0:T(8,128)S(1)} %copy-done.7, s32[8]{0:T(128)S(1)} %copy-done.9, s32[8,8]{1,0:T(8,128)S(1)} %copy-done.8, f32[4]{0:T(128)S(1)} %copy-done.10, f32[8]{0:T(128)S(1)} %copy-done.11, f32[104,512]{1,0:T(8,128)S(1)} %collective-permute-done.left_ref, ...), custom_call_target="tpu_custom_call" | custom-call | tf_op jit(solution)/shard_map/rest/pallas_call | solution.py:448
  83.2 0.0 copy-start.5
  83.2 22.1 %all_to_all.16 = f32[128,1,128]{2,1,0:T(1,128)S(1)} all-to-all(f32[128,1,128]{2,1,0:T(1,128)S(1)} %bitcast.15), channel_id=1, replica_groups=mesh['leaf'=32,'tm'=4] {'leaf','tm'}, dimensions={0} | all-to-all | bytes 131072 | tf_op jit(solution)/shard_map/all_to_all | solution.py:466
  105.4 0.0 copy-done.5
  105.4 0.8 update.1
  (1 shorter events, 0.0 us)
Async XLA Ops:
  0.6 5.3 %copy-start.6 = (s32[4096]{0:T(1024)S(1)}, s32[4096]{0:T(1024)}, u32[]{:S(2)}) copy-start(s32[4096]{0:T(1024)} %param.17) | copy-start | bytes 49156
  0.6 5.3 %copy-start.12 = (f32[1,64,512]{2,1,0:T(8,128)S(1)}, f32[1,64,512]{2,1,0:T(8,128)}, u32[]{:S(2)}) copy-start(f32[1,64,512]{2,1,0:T(8,128)} %param.19) | copy-start | bytes 393220
  5.9 0.7 copy-start.14
  6.6 0.9 copy-start.2
  7.5 0.8 copy-start.13
  9.8 11.5 %copy-start.3 = (f32[104,512]{1,0:T(8,128)S(1)}, f32[104,512]{1,0:T(8,128)}, u32[]{:S(2)}) copy-start(f32[104,512]{1,0:T(8,128)} %get-tuple-element.14.halo_ref.mid_ref) | copy-start | bytes 638980
  9.8 25.5 %all-to-all-start = ((f32[128,8,128]{2,1,0:T(8,128)}), f32[128,8,128]{2,1,0:T(8,128)S(1)}, u32[]{:S(2)}, u32[]{:S(2)}) async-start(f32[128,8,128]{2,1,0:T(8,128)} %get-tuple-element.16), calls=%async_computation | async-start | bytes 1048576 | tf_op jit(solution)/shard_map/all_to_all | solution.py:415
  21.3 11.7 %collective-permute-start.1 = (f32[104,512]{1,0:T(8,128)S(1)}, f32[104,512]{1,0:T(8,128)S(1)}, u32[]{:S(2)}, u32[]{:S(2)}) collective-permute-start(f32[104,512]{1,0:T(8,128)S(1)} %copy-done.3), channel_id=1, source_target_pairs={{1,0},{2,1},{3,2},{5,4},{6,5},{7,6},{9,8},{10,9},{11,10},{13,12},{... | collective-permute-start | bytes 638984 | tf_op jit(solution)/shard_map/ppermute | solution.py:377
  22.6 10.4 %collective-permute-start = (f32[104,512]{1,0:T(8,128)S(1)}, f32[104,512]{1,0:T(8,128)S(1)}, u32[]{:S(2)}, u32[]{:S(2)}) collective-permute-start(f32[104,512]{1,0:T(8,128)S(1)} %copy-done.3), channel_id=1, source_target_pairs={{0,1},{1,2},{2,3},{4,5},{5,6},{6,7},{8,9},{9,10},{10,11},{12,13},{... | collective-permute-start | bytes 638984 | tf_op jit(solution)/shard_map/ppermute | solution.py:377
  35.3 5.7 %copy-start.7 = (s32[8,8]{1,0:T(8,128)S(1)}, s32[8,8]{1,0:T(8,128)}, u32[]{:S(2)}) copy-start(s32[8,8]{1,0:T(8,128)} %near_ref.3) | copy-start | bytes 772
  35.3 5.6 %copy-start.9 = (s32[8]{0:T(128)S(1)}, s32[8]{0:T(128)}, u32[]{:S(2)}) copy-start(s32[8]{0:T(128)} %count_ref.3) | copy-start | bytes 100
  35.3 5.6 %copy-start.10 = (f32[4]{0:T(128)S(1)}, f32[4]{0:T(128)}, u32[]{:S(2)}) copy-start(f32[4]{0:T(128)} %scale_ref.3) | copy-start | bytes 52
  35.3 26.0 %collective-permute-start.3 = (f32[3,104,512]{2,1,0:T(8,128)S(1)}, f32[3,104,512]{2,1,0:T(8,128)S(1)}, u32[]{:S(2)}, u32[]{:S(2)}) collective-permute-start(f32[3,104,512]{2,1,0:T(8,128)S(1)} %pad_maximum_fusion), channel_id=1, source_target_pairs={{4,0},{8,4},{12,8},{16,12},{20,16},{24,20},{28,24},{32,28},{36,32}... | collective-permute-start | bytes 1916936 | tf_op jit(solution)/shard_map/ppermute | solution.py:377
  37.7 23.7 %collective-permute-start.2 = (f32[3,104,512]{2,1,0:T(8,128)S(1)}, f32[3,104,512]{2,1,0:T(8,128)S(1)}, u32[]{:S(2)}, u32[]{:S(2)}) collective-permute-start(f32[3,104,512]{2,1,0:T(8,128)S(1)} %pad_maximum_fusion), channel_id=1, source_target_pairs={{0,4},{4,8},{8,12},{12,16},{16,20},{20,24},{24,28},{28,32},{32,36}... | collective-permute-start | bytes 1916936 | tf_op jit(solution)/shard_map/ppermute | solution.py:377
  41.0 20.5 %copy-start = (f32[8,64,512]{2,1,0:T(8,128)S(1)}, f32[8,64,512]{2,1,0:T(8,128)}, u32[]{:S(2)}) copy-start(f32[8,64,512]{2,1,0:T(8,128)} %bases_ref.1) | copy-start | bytes 3145732
  41.0 20.5 %copy-start.1 = (f32[8,4096]{1,0:T(8,128)S(1)}, f32[8,4096]{1,0:T(8,128)}, u32[]{:S(2)}) copy-start(f32[8,4096]{1,0:T(8,128)} %p_ref.3) | copy-start | bytes 393220
  41.0 20.5 %copy-start.4 = (f32[8,4096]{1,0:T(8,128)S(1)}, f32[8,4096]{1,0:T(8,128)}, u32[]{:S(2)}) copy-start(f32[8,4096]{1,0:T(8,128)} %res_ref.3) | copy-start | bytes 393220
  61.4 0.7 copy-start.8
  61.4 0.7 copy-start.11
  83.2 22.1 %copy-start.5 = (f32[8,4096]{1,0:T(8,128)S(1)}, f32[8,4096]{1,0:T(8,128)}, u32[]{:S(2)}) copy-start(f32[8,4096]{1,0:T(8,128)} %it_ref.1) | copy-start | bytes 393220

commit v4 on v3

--- a/solution.py
+++ b/solution.py
@@ -195,28 +195,34 @@
                 coef[base + leaf] = halves(ref[96:104, leaf * rank : (leaf + 1) * rank] * FACTOR)
 
 
-def list_pairs(near_ref, count_ref, keep, slot_of, idle, pairs):
+def list_pairs(near_ref, count_ref, inside, outside, sizes):
     leaf_dev, slots = near_ref.shape
 
-    def leaf_step(leaf, n):
-        def entry(j, n):
+    def leaf_step(leaf, sums):
+        def entry(j, sums):
             w = near_ref[leaf, j]
-            pairs[n] = leaf * 128 + slot_of(w)
-            return n + jnp.where(keep(w // leaf_dev), 1, 0)
-
-        return lax.fori_loop(0, count_ref[leaf], entry, n)
-
-    n = lax.fori_loop(0, leaf_dev, leaf_step, 0)
+            here = jnp.where(w // leaf_dev == 4, 1, 0)
+            code = leaf * 128 + w
+            inside[sums[0]] = code
+            outside[sums[1]] = code
+            return sums[0] + here, sums[1] + 1 - here
+
+        return lax.fori_loop(0, count_ref[leaf], entry, sums)
+
+    sums = lax.fori_loop(0, leaf_dev, leaf_step, (0, 0))
+    idle = 9 * leaf_dev
     for extra in range(3):
-        pairs[n + extra] = idle
-    return n
-
-
-def near_pairs(pairs, n, src, tgt, wgt, out, z, high, low):
+        inside[sums[0] + extra] = idle
+        outside[sums[1] + extra] = idle
+    sizes[0], sizes[1] = sums
+    return sums[0]
+
+
+def near_pairs(pairs, n, first, src, tgt, wgt, out, z, high, low):
     parts = wgt.shape[2] // PART
 
     def where(p):
-        return pairs[p] >> 7, pairs[p] & 127
+        return pairs[p] >> 7, (pairs[p] & 127) - first
 
     def distances(p, c, b):
         leaf, w = where(p)
@@ -252,24 +258,21 @@
     lax.fori_loop(0, (n + 1) // 2, two_pairs, 0)
 
 
-def blank(src, wgt):
-    src[src.shape[0] - 1] = jnp.zeros(src.shape[1:], BF16)
-    wgt[wgt.shape[0] - 1] = jnp.zeros(wgt.shape[1:], BF16)
-
-
-def close_body(tm_size, near_ref, count_ref, place_ref, scale_ref, left_ref, mid_ref, right_ref, node_ref, own_ref, transfer_ref, out_ref, pushed_ref, pairs, src, tgt, wgt, z, high, low, node_src, node_wgt):
+def inside_body(near_ref, count_ref, scale_ref, halo_ref, out_ref, pairs_ref, sizes_ref, pairs, src, tgt, wgt, z, high, low):
     leaf_dev, rhs, leaf_pts = out_ref.shape
-    devices, _, _ = node_ref.shape
+    n = list_pairs(near_ref, count_ref, pairs, pairs_ref, sizes_ref)
+    for extra in range(3):
+        pairs[n + extra] = 5 * leaf_dev
+    prepare(halo_ref, scale_rows(scale_ref, (8, leaf_pts)), 0, src, wgt, tgt)
+    src[leaf_dev] = jnp.zeros(src.shape[1:], BF16)
+    wgt[leaf_dev] = jnp.zeros(wgt.shape[1:], BF16)
+    out_ref[...] = jnp.zeros_like(out_ref)
+    near_pairs(pairs, n, 4 * leaf_dev, src, tgt, wgt, out_ref, z, high, low)
+
+
+def node_field(tm_size, place_ref, scale, node_ref, own_ref, transfer_ref, node_src, node_wgt):
+    devices = node_ref.shape[0]
     rank = own_ref.shape[1] // 2
-    scale = scale_rows(scale_ref, (8, leaf_pts))
-    n = list_pairs(near_ref, count_ref, lambda k: (k >= 3) & (k < 6), lambda w: w - 3 * leaf_dev, 3 * leaf_dev, pairs)
-    blank(src, wgt)
-    prepare(left_ref, scale, 0, src, wgt)
-    prepare(mid_ref, scale, leaf_dev, src, wgt, tgt)
-    prepare(right_ref, scale, 2 * leaf_dev, src, wgt)
-    out_ref[...] = jnp.zeros_like(out_ref)
-    near_pairs(pairs, n, src, tgt, wgt, out_ref, z, high, low)
-
     lane = lane_ids((8, 128))
 
     def distant(e):
@@ -300,23 +303,24 @@
         weight = node_wgt[:, q : q + step]
         total = total + contract(weight, k_high, ((1,), (1,)))
         total = total + contract(weight, k_low, ((1,), (1,)))
-    device_far = total[:8] + total[8:]
-    pushed_ref[...] = jnp.dot(device_far, transfer_ref[...], precision=EXACT, preferred_element_type=F32)
-
-
-def rest_body(near_ref, count_ref, far_ref, scale_ref, noise_ref, left_ref, mid_ref, right_ref, up_ref, down_ref, close_ref, pushed_ref, bases_ref, inv_ref, p_ref, res_ref, image_ref, sums_ref, pairs, src, tgt, wgt, coef, z, high, low, out, flat, far_src, far_wgt):
+    return jnp.dot(total[:8] + total[8:], transfer_ref[...], precision=EXACT, preferred_element_type=F32)
+
+
+def rest_body(tm_size, pairs_ref, sizes_ref, far_ref, place_ref, scale_ref, noise_ref, left_ref, mid_ref, right_ref, up_ref, down_ref, inside_ref, node_ref, own_ref, transfer_ref, bases_ref, inv_ref, p_ref, res_ref, image_ref, sums_ref, src, tgt, wgt, coef, z, high, low, out, flat, far_src, far_wgt, node_src, node_wgt):
     leaf_dev, rank, leaf_pts = bases_ref.shape
     scale = scale_rows(scale_ref, (8, leaf_pts))
-    n = list_pairs(near_ref, count_ref, lambda k: (k < 3) | (k >= 6), lambda w: w, 9 * leaf_dev, pairs)
-    blank(src, wgt)
+    pushed = node_field(tm_size, place_ref, scale, node_ref, own_ref, transfer_ref, node_src, node_wgt)
+    idle = 9 * leaf_dev
+    src[idle] = jnp.zeros(src.shape[1:], BF16)
+    wgt[idle] = jnp.zeros(wgt.shape[1:], BF16)
     for k in range(3):
         prepare(up_ref.at[k], scale, k * leaf_dev, src, wgt, None, coef)
         prepare(down_ref.at[k], scale, (6 + k) * leaf_dev, src, wgt, None, coef)
-    prepare(left_ref, scale[:, :128], 3 * leaf_dev, src, None, None, coef)
+    prepare(left_ref, scale, 3 * leaf_dev, src, wgt, None, coef)
     prepare(mid_ref, scale, 4 * leaf_dev, src, None, tgt, coef)
-    prepare(right_ref, scale[:, :128], 5 * leaf_dev, src, None, None, coef)
-    out[...] = close_ref[...]
-    near_pairs(pairs, n, src, tgt, wgt, out, z, high, low)
+    prepare(right_ref, scale, 5 * leaf_dev, src, wgt, None, coef)
+    out[...] = inside_ref[...]
+    near_pairs(pairs_ref, sizes_ref[1], 0, src, tgt, wgt, out, z, high, low)
 
     for leaf in range(leaf_dev):
         for j in range(far_ref.shape[1]):
@@ -327,7 +331,7 @@
     for leaf in range(leaf_dev):
         k_high, k_low = split(kernel_of(contract(tgt[leaf, :, 0:rank], far_src[leaf], ((0,), (0,)))))
         far = contract(far_wgt[leaf], k_high, ((1,), (1,))) + contract(far_wgt[leaf], k_low, ((1,), (1,)))
-        incoming = halves(far[:8] + far[8:] + pushed_ref[:, leaf * rank : (leaf + 1) * rank])
+        incoming = halves(far[:8] + far[8:] + pushed[:, leaf * rank : (leaf + 1) * rank])
         base_high, base_low = split(bases_ref[leaf])
         got = jnp.dot(incoming, base_high, preferred_element_type=F32)
         got = got + jnp.dot(incoming, base_low, preferred_element_type=F32)
@@ -412,12 +416,6 @@
     )(by_row, halo, first, transfer[0], device_skel)
     left = shifted(halo, "tm", 1)
     right = shifted(halo, "tm", -1)
-    nodes = lax.all_to_all(node, axes, 0, 0)
-    left, right, nodes = lax.optimization_barrier((left, right, nodes))
-    row = jnp.stack([left, halo, right])
-    up = shifted(row, "leaf", 1)
-    down = shifted(row, "leaf", -1)
-    place = jnp.stack([lax.axis_index("leaf"), lax.axis_index("tm")]).astype(jnp.int32)
 
     def pipeline(sources):
         return [
@@ -431,27 +429,30 @@
         pltpu.VMEM((2, PART, leaf_pts), BF16),
         pltpu.VMEM((2, PART, leaf_pts), BF16),
     ]
-    listed = pltpu.SMEM((near_list.size + 4,), jnp.int32)
-    close, pushed = pl.pallas_call(
-        functools.partial(close_body, lax.axis_size("tm")),
-        in_specs=[SMEM] * 4 + [VMEM] * 6,
-        out_specs=[VMEM] * 2,
-        out_shape=[shape((leaf_dev, rhs, leaf_pts), F32), shape((rhs, leaf_dev * rank), F32)],
-        scratch_shapes=[listed]
-        + pipeline(3 * leaf_dev)
-        + buffers
-        + [pltpu.VMEM((32, devices * rank), BF16), pltpu.VMEM((16, devices * rank), BF16)],
+    entries = near_list.size + 4
+    inside, pairs, sizes = pl.pallas_call(
+        inside_body,
+        in_specs=[SMEM] * 3 + [VMEM],
+        out_specs=[VMEM, SMEM, SMEM],
+        out_shape=[shape((leaf_dev, rhs, leaf_pts), F32), shape((entries,), jnp.int32), shape((2,), jnp.int32)],
+        scratch_shapes=[pltpu.SMEM((entries,), jnp.int32)] + pipeline(leaf_dev) + buffers,
         compiler_params=params(24),
         cost_estimate=pl.CostEstimate(flops=10**10, bytes_accessed=2**21, transcendentals=10**7),
-        name="close",
-    )(near_list, near_count, place, inv_scale, left, halo, right, nodes, own, transfer[0])
+        name="inside",
+    )(near_list, near_count, inv_scale, halo)
+    left, right, inside, node = lax.optimization_barrier((left, right, inside, node))
+    nodes = lax.all_to_all(node, axes, 0, 0)
+    row = jnp.stack([left, halo, right])
+    up = shifted(row, "leaf", 1)
+    down = shifted(row, "leaf", -1)
+    place = jnp.stack([lax.axis_index("leaf"), lax.axis_index("tm")]).astype(jnp.int32)
+
     image, sums = pl.pallas_call(
-        rest_body,
-        in_specs=[SMEM] * 5 + [VMEM] * 11,
+        functools.partial(rest_body, lax.axis_size("tm")),
+        in_specs=[SMEM] * 6 + [VMEM] * 13,
         out_specs=[VMEM] * 2,
         out_shape=[shape((rhs, points), F32), shape((devices, 128), F32)],
-        scratch_shapes=[listed]
-        + pipeline(9 * leaf_dev)
+        scratch_shapes=pipeline(9 * leaf_dev)
         + [pltpu.VMEM((9 * leaf_dev, 16, rank), BF16)]
         + buffers
         + [
@@ -459,10 +460,12 @@
             pltpu.VMEM((rhs, points), F32),
             pltpu.VMEM((leaf_dev, 32, far_list.shape[1] * rank), BF16),
             pltpu.VMEM((leaf_dev, 16, far_list.shape[1] * rank), BF16),
+            pltpu.VMEM((32, devices * rank), BF16),
+            pltpu.VMEM((16, devices * rank), BF16),
         ],
         compiler_params=params(24),
         name="rest",
-    )(near_list, near_count, far_list, inv_scale, noise, left, halo, right, up, down, close, pushed, bases, inverse, direction, residual)
+    )(pairs, sizes, far_list, place, inv_scale, noise, left, halo, right, up, down, inside, nodes, own, transfer[0], bases, inverse, direction, residual)
     all_sums = lax.all_to_all(sums, axes, 0, 0, tiled=True)
     return pl.pallas_call(
         update_body,

time: 107 us -> 109 us (1.019)
  blocking collectives: 22.1 us -> 16.4 us
  waiting for transfers between devices: 8.59 us -> 13.9 us
  Pallas kernels: 49.1 us -> 51.5 us
    all_to_all x1, waiting for transfers between devices: 2.3 us -> 13.9 us  [shards(): nodes = lax.all_to_all(node, axes, 0, 0)]
    ppermute x4, waiting for transfers between devices: 6.29 us -> 0.01 us  [shifted(): lax.ppermute(x, axis, [(i, i + by) for i in range(n) if 0 <= i + by < n])]
    all_to_all x1, blocking collectives: 22.1 us -> 16.4 us  [shards(): all_sums = lax.all_to_all(sums, axes, 0, 0, tiled=True)]
    pallas_call x2, Pallas kernels: 41.5 us -> 44 us  [the longest x1 32.7 us: shards(): pl.pallas_call(functools.partial(rest_body, lax.axis_size('tm')), in_spec...]
    all_to_all x1, starting transfers between devices: 11.5 us -> 10.1 us  [shards(): nodes = lax.all_to_all(node, axes, 0, 0)]
  transfers between devices with their start and end apart: 5 -> 5, of which waited for: 2 -> 1; matrix products, arithmetic and copies ran while one was open for 0% -> 0% of each run, Pallas kernels for 19% -> 12%
where the time goes in v4:
time: 109 us; the launch traced here: 107 us
  Pallas kernels  51.5 us (47%)
  starting transfers between devices  21.5 us (20%)
  blocking collectives  16.4 us (15%)
  waiting for transfers between devices  13.9 us (13%)
  local copies, waits for them, and re-layouts  2.2 us (2%)
    pallas_call x1, Pallas kernels, shards(): pl.pallas_call(functools.partial(rest_body, lax.axis_size('tm')), in_spec...  32.7 us
    all_to_all x1, blocking collectives, shards(): all_sums = lax.all_to_all(sums, axes, 0, 0, tiled=True)  16.4 us
    all_to_all x1, waiting for transfers between devices, shards(): nodes = lax.all_to_all(node, axes, 0, 0)  13.9 us
    ppermute x4, starting transfers between devices, shifted(): lax.ppermute(x, axis, [(i, i + by) for i in range(n) if 0 <= i + by < n])  11.4 us
    pallas_call x1, Pallas kernels, shards(): pl.pallas_call(inside_body, in_specs=[SMEM] * 3 + [VMEM], out_specs=[VMEM...  11.2 us
    all_to_all x1, starting transfers between devices, shards(): nodes = lax.all_to_all(node, axes, 0, 0)  10.1 us
    pallas_call x1, Pallas kernels, shards(): pl.pallas_call(gather_body, in_specs=[ANY] * 4, out_specs=[VMEM] * 2, out...  5.25 us
    unnamed x30, local copies, waits for them, and re-layouts  2.2 us
  transfers between devices with their start and end apart: 5, of which 1 were waited for; matrix products, arithmetic and copies ran while one was open for 0% of the time, Pallas kernels for 12%

profile of v4, /device:TPU:1, one launch (start us, length us, event | category | flops | bytes accessed | tf_op | source)
XLA Modules:
  0.0 107.4 jit_solution(14514529859614482521)
XLA Ops:
  0.6 0.0 copy-start.12
  0.6 5.2 %gather.1 = (f32[104,512]{1,0:T(8,128)}, f32[8,8,128]{2,1,0:T(8,128)}) custom-call(s32[32,128]{1,0:T(8,128)} %bitcast.18, f32[4,4096]{1,0:T(4,128)} %x_hbm.1, f32[8,4096]{1,0:T(8,128)} %p_ref.3, f32[8,64,512]{2,1,0:T(8,128)} %bases_ref.1), custom_call_target="tpu_custom_call" | custom-call | tf_op jit(solution)/shard_map/gather/pallas_call | solution.py:392
  5.9 0.0 copy-start.9
  5.9 0.0 copy-start.13
  5.9 4.0 %collective-permute-start = (f32[104,512]{1,0:T(8,128)}, f32[104,512]{1,0:T(8,128)S(1)}, u32[]{:S(2)}, u32[]{:S(2)}) collective-permute-start(f32[104,512]{1,0:T(8,128)} %get-tuple-element.16.halo_ref.mid_ref), channel_id=1, source_target_pairs={{0,1},{1,2},{2,3},{4,5},{5,6},{6,7},{8,9},{9,10},{10,11},{12,13},{... | collective-permute-start | bytes 638984 | tf_op jit(solution)/shard_map/ppermute | solution.py:381
  9.9 1.3 %collective-permute-start.1 = (f32[104,512]{1,0:T(8,128)}, f32[104,512]{1,0:T(8,128)S(1)}, u32[]{:S(2)}, u32[]{:S(2)}) collective-permute-start(f32[104,512]{1,0:T(8,128)} %get-tuple-element.16.halo_ref.mid_ref), channel_id=1, source_target_pairs={{1,0},{2,1},{3,2},{5,4},{6,5},{7,6},{9,8},{10,9},{11,10},{13,12},{... | collective-permute-start | bytes 638984 | tf_op jit(solution)/shard_map/ppermute | solution.py:381
  11.2 0.0 copy-done.12
  11.2 0.0 copy-done.9
  11.2 0.0 copy-done.13
  11.2 0.0 copy-start.2
  11.2 0.9 copy-done.2
  12.2 0.0 copy-start.3
  12.2 0.0 copy-start.5
  12.2 0.0 copy-start.7
  12.2 0.0 copy-start.11
  12.2 11.2 %inside.1 = (f32[8,8,512]{2,1,0:T(8,128)S(1)}, s32[68]{0:T(128)S(1)}, s32[2]{0:T(128)S(1)}) custom-call(s32[8,8]{1,0:T(8,128)S(1)} %copy-done.12, s32[8]{0:T(128)S(1)} %copy-done.13, f32[4]{0:T(128)S(1)} %copy-done.9, f32[104,512]{1,0:T(8,128)S(1)} %copy-done.2), custom_call_target="tpu_custom_call" | custom-call | flops 10000000000 | bytes 2097152 | tf_op jit(solution)/shard_map/inside/pallas_call | solution.py:433
  23.4 0.0 copy-start.14
  23.4 0.0 copy-done.3
  23.4 0.0 copy-done.5
  23.4 0.0 copy-done.7
  23.5 0.0 copy-done.11
  23.5 0.6 copy-done.14
  24.1 1.5 %node.1 = (f32[128,8,128]{2,1,0:T(8,128)}, f32[8,128]{1,0:T(8,128)S(1)}, s32[32,128]{1,0:T(8,128)S(1)}) custom-call(s32[32,128]{1,0:T(8,128)S(1)} %bitcast.19, f32[104,512]{1,0:T(8,128)S(1)} %copy-done.3, f32[8,8,128]{2,1,0:T(8,128)S(1)} %copy-done.11, f32[64,512]{1,0:T(8,128)S(1)} %bitcast.15, s32[1,64]{1,0:T(1,128)S(1)} %copy-done.14), custom_call_target="tpu_custom_call" | custom-call | flops 1000000000 | bytes 1048576 | tf_op jit(solution)/shard_map/node/pallas_call | solution.py:407
  25.6 0.0 collective-permute-done.left_ref
  25.6 0.0 collective-permute-done.1.right_ref
  25.6 0.0 copy-start
  25.6 0.9 pad_maximum_fusion
  26.5 0.0 copy-start.1
  26.5 0.0 copy-start.4
  26.5 3.2 %collective-permute-start.2 = (f32[3,104,512]{2,1,0:T(8,128)}, f32[3,104,512]{2,1,0:T(8,128)S(1)}, u32[]{:S(2)}, u32[]{:S(2)}) collective-permute-start(f32[3,104,512]{2,1,0:T(8,128)} %pad_maximum_fusion), channel_id=1, source_target_pairs={{0,4},{4,8},{8,12},{12,16},{16,20},{20,24},{24,28},{28,32},{32,36}... | collective-permute-start | bytes 1916936 | tf_op jit(solution)/shard_map/ppermute | solution.py:381
  29.6 3.0 %collective-permute-start.3 = (f32[3,104,512]{2,1,0:T(8,128)}, f32[3,104,512]{2,1,0:T(8,128)}, u32[]{:S(2)}, u32[]{:S(2)}) collective-permute-start(f32[3,104,512]{2,1,0:T(8,128)} %pad_maximum_fusion), channel_id=1, source_target_pairs={{4,0},{8,4},{12,8},{16,12},{20,16},{24,20},{28,24},{32,28},{36,32}... | collective-permute-start | bytes 1916936 | tf_op jit(solution)/shard_map/ppermute | solution.py:381
  32.7 10.1 %all-to-all-start = ((f32[128,8,128]{2,1,0:T(8,128)}), f32[128,8,128]{2,1,0:T(8,128)S(1)}, u32[]{:S(2)}, u32[]{:S(2)}) async-start(f32[128,8,128]{2,1,0:T(8,128)} %get-tuple-element.25), calls=%async_computation | async-start | bytes 1048576 | tf_op jit(solution)/shard_map/all_to_all | solution.py:444
  42.7 0.1 pad_add_fusion.place_ref
  42.8 0.0 copy-start.8
  42.8 13.9 %all-to-all-done.node_ref = f32[128,8,128]{2,1,0:T(8,128)S(1)} async-done(((f32[128,8,128]{2,1,0:T(8,128)}), f32[128,8,128]{2,1,0:T(8,128)S(1)}, u32[]{:S(2)}, u32[]{:S(2)}) %all-to-all-start) | async-done | bytes 524320 | tf_op jit(solution)/shard_map/all_to_all | solution.py:444
  56.7 0.0 collective-permute-done.2.up_ref
  56.7 0.0 collective-permute-done.3.down_ref
  56.7 0.0 copy-start.10
  56.7 0.0 copy-done
  56.7 0.0 copy-done.1
  56.7 0.0 copy-done.4
  56.7 0.0 copy-done.8
  56.8 0.6 copy-done.10
  57.4 32.7 %rest.1 = (f32[8,4096]{1,0:T(8,128)S(1)}, f32[128,128]{1,0:T(8,128)S(1)}) custom-call(s32[68]{0:T(128)S(1)} %get-tuple-element.17.pairs_ref, s32[2]{0:T(128)S(1)} %get-tuple-element.18.sizes_ref, s32[8,8]{1,0:T(8,128)S(1)} %copy-done.8, s32[2]{0:T(128)S(1)} %pad_add_fusion.place_ref, f32[4]{0:T(128)S(1)} %copy-done.9, f32[8]{0:T(128)S(1)} %copy-done.10, ...), custom_call_target="tpu_custom_call" | custom-call | tf_op jit(solution)/shard_map/rest/pallas_call | solution.py:450
  90.1 0.0 copy-start.6
  90.1 16.4 %all_to_all.16 = f32[128,1,128]{2,1,0:T(1,128)S(1)} all-to-all(f32[128,1,128]{2,1,0:T(1,128)S(1)} %bitcast.17), channel_id=1, replica_groups=mesh['leaf'=32,'tm'=4] {'leaf','tm'}, dimensions={0} | all-to-all | bytes 131072 | tf_op jit(solution)/shard_map/all_to_all | solution.py:469
  106.5 0.0 copy-done.6
  106.5 0.8 update.1
Async XLA Ops:
  0.6 10.6 %copy-start.12 = (s32[8,8]{1,0:T(8,128)S(1)}, s32[8,8]{1,0:T(8,128)}, u32[]{:S(2)}) copy-start(s32[8,8]{1,0:T(8,128)} %near_ref.1) | copy-start | bytes 772
  5.9 5.3 %copy-start.9 = (f32[4]{0:T(128)S(1)}, f32[4]{0:T(128)}, u32[]{:S(2)}) copy-start(f32[4]{0:T(128)} %scale_ref.3) | copy-start | bytes 52
  5.9 5.3 %copy-start.13 = (s32[8]{0:T(128)S(1)}, s32[8]{0:T(128)}, u32[]{:S(2)}) copy-start(s32[8]{0:T(128)} %count_ref.1) | copy-start | bytes 100
  5.9 19.6 %collective-permute-start = (f32[104,512]{1,0:T(8,128)}, f32[104,512]{1,0:T(8,128)S(1)}, u32[]{:S(2)}, u32[]{:S(2)}) collective-permute-start(f32[104,512]{1,0:T(8,128)} %get-tuple-element.16.halo_ref.mid_ref), channel_id=1, source_target_pairs={{0,1},{1,2},{2,3},{4,5},{5,6},{6,7},{8,9},{9,10},{10,11},{12,13},{... | collective-permute-start | bytes 638984 | tf_op jit(solution)/shard_map/ppermute | solution.py:381
  9.9 15.7 %collective-permute-start.1 = (f32[104,512]{1,0:T(8,128)}, f32[104,512]{1,0:T(8,128)S(1)}, u32[]{:S(2)}, u32[]{:S(2)}) collective-permute-start(f32[104,512]{1,0:T(8,128)} %get-tuple-element.16.halo_ref.mid_ref), channel_id=1, source_target_pairs={{1,0},{2,1},{3,2},{5,4},{6,5},{7,6},{9,8},{10,9},{11,10},{13,12},{... | collective-permute-start | bytes 638984 | tf_op jit(solution)/shard_map/ppermute | solution.py:381
  11.2 0.9 copy-start.2
  12.2 11.3 %copy-start.3 = (f32[104,512]{1,0:T(8,128)S(1)}, f32[104,512]{1,0:T(8,128)}, u32[]{:S(2)}) copy-start(f32[104,512]{1,0:T(8,128)} %get-tuple-element.16.halo_ref.mid_ref) | copy-start | bytes 638980
  12.2 11.3 %copy-start.5 = (f32[1,64,512]{2,1,0:T(8,128)S(1)}, f32[1,64,512]{2,1,0:T(8,128)}, u32[]{:S(2)}) copy-start(f32[1,64,512]{2,1,0:T(8,128)} %param.19) | copy-start | bytes 393220
  12.2 11.3 %copy-start.7 = (s32[4096]{0:T(1024)S(1)}, s32[4096]{0:T(1024)}, u32[]{:S(2)}) copy-start(s32[4096]{0:T(1024)} %param.17) | copy-start | bytes 49156
  12.2 11.3 %copy-start.11 = (f32[8,8,128]{2,1,0:T(8,128)S(1)}, f32[8,8,128]{2,1,0:T(8,128)}, u32[]{:S(2)}) copy-start(f32[8,8,128]{2,1,0:T(8,128)} %get-tuple-element.20.first_ref) | copy-start | bytes 98308
  23.4 0.7 copy-start.14
  25.6 31.2 %copy-start = (f32[8,64,512]{2,1,0:T(8,128)S(1)}, f32[8,64,512]{2,1,0:T(8,128)}, u32[]{:S(2)}) copy-start(f32[8,64,512]{2,1,0:T(8,128)} %bases_ref.1) | copy-start | bytes 3145732
  26.5 30.2 %copy-start.1 = (f32[8,4096]{1,0:T(8,128)S(1)}, f32[8,4096]{1,0:T(8,128)}, u32[]{:S(2)}) copy-start(f32[8,4096]{1,0:T(8,128)} %p_ref.3) | copy-start | bytes 393220
  26.5 30.3 %copy-start.4 = (f32[8,4096]{1,0:T(8,128)S(1)}, f32[8,4096]{1,0:T(8,128)}, u32[]{:S(2)}) copy-start(f32[8,4096]{1,0:T(8,128)} %res_ref.3) | copy-start | bytes 393220
  26.5 30.2 %collective-permute-start.2 = (f32[3,104,512]{2,1,0:T(8,128)}, f32[3,104,512]{2,1,0:T(8,128)S(1)}, u32[]{:S(2)}, u32[]{:S(2)}) collective-permute-start(f32[3,104,512]{2,1,0:T(8,128)} %pad_maximum_fusion), channel_id=1, source_target_pairs={{0,4},{4,8},{8,12},{12,16},{16,20},{20,24},{24,28},{28,32},{32,36}... | collective-permute-start | bytes 1916936 | tf_op jit(solution)/shard_map/ppermute | solution.py:381
  29.6 27.1 %collective-permute-start.3 = (f32[3,104,512]{2,1,0:T(8,128)}, f32[3,104,512]{2,1,0:T(8,128)}, u32[]{:S(2)}, u32[]{:S(2)}) collective-permute-start(f32[3,104,512]{2,1,0:T(8,128)} %pad_maximum_fusion), channel_id=1, source_target_pairs={{4,0},{8,4},{12,8},{16,12},{20,16},{24,20},{28,24},{32,28},{36,32}... | collective-permute-start | bytes 1916936 | tf_op jit(solution)/shard_map/ppermute | solution.py:381
  32.7 24.0 %all-to-all-start = ((f32[128,8,128]{2,1,0:T(8,128)}), f32[128,8,128]{2,1,0:T(8,128)S(1)}, u32[]{:S(2)}, u32[]{:S(2)}) async-start(f32[128,8,128]{2,1,0:T(8,128)} %get-tuple-element.25), calls=%async_computation | async-start | bytes 1048576 | tf_op jit(solution)/shard_map/all_to_all | solution.py:444
  42.8 13.9 %copy-start.8 = (s32[8,8]{1,0:T(8,128)S(1)}, s32[8,8]{1,0:T(8,128)}, u32[]{:S(2)}) copy-start(s32[8,8]{1,0:T(8,128)} %far_ref.1) | copy-start | bytes 772
  56.7 0.7 copy-start.10
  90.1 16.4 %copy-start.6 = (f32[8,4096]{1,0:T(8,128)S(1)}, f32[8,4096]{1,0:T(8,128)}, u32[]{:S(2)}) copy-start(f32[8,4096]{1,0:T(8,128)} %it_ref.1) | copy-start | bytes 393220

commit v5 on v4

--- a/solution.py
+++ b/solution.py
@@ -142,7 +142,7 @@
         halo_ref[96:104, leaf * rank : (leaf + 1) * rank] = coef
 
 
-def node_body(order_ref, halo_ref, first_ref, transfer_ref, skel_ref, node_ref, own_ref, inv_ref, slot):
+def node_work(order_ref, halo_ref, first_ref, transfer_ref, skel_ref, node_ref, own_ref, inv_ref, slot):
     chunks = order_ref.shape[0]
     rank = transfer_ref.shape[0]
     leaf_dev = first_ref.shape[0]
@@ -258,15 +258,19 @@
     lax.fori_loop(0, (n + 1) // 2, two_pairs, 0)
 
 
-def inside_body(near_ref, count_ref, scale_ref, halo_ref, out_ref, pairs_ref, sizes_ref, pairs, src, tgt, wgt, z, high, low):
+def inside_body(near_ref, count_ref, scale_ref, halo_hbm, first_ref, order_ref, transfer_ref, skel_ref, out_ref, node_ref, own_ref, inv_ref, pairs_ref, sizes_ref, pairs, halo_ref, slot, src, tgt, wgt, z, high, low, sem):
     leaf_dev, rhs, leaf_pts = out_ref.shape
+    move = pltpu.make_async_copy(halo_hbm, halo_ref, sem)
+    move.start()
     n = list_pairs(near_ref, count_ref, pairs, pairs_ref, sizes_ref)
     for extra in range(3):
         pairs[n + extra] = 5 * leaf_dev
-    prepare(halo_ref, scale_rows(scale_ref, (8, leaf_pts)), 0, src, wgt, tgt)
     src[leaf_dev] = jnp.zeros(src.shape[1:], BF16)
     wgt[leaf_dev] = jnp.zeros(wgt.shape[1:], BF16)
     out_ref[...] = jnp.zeros_like(out_ref)
+    move.wait()
+    node_work(order_ref, halo_ref, first_ref, transfer_ref, skel_ref, node_ref, own_ref, inv_ref, slot)
+    prepare(halo_ref, scale_rows(scale_ref, (8, leaf_pts)), 0, src, wgt, tgt)
     near_pairs(pairs, n, 4 * leaf_dev, src, tgt, wgt, out_ref, z, high, low)
 
 
@@ -306,22 +310,33 @@
     return jnp.dot(total[:8] + total[8:], transfer_ref[...], precision=EXACT, preferred_element_type=F32)
 
 
-def rest_body(tm_size, pairs_ref, sizes_ref, far_ref, place_ref, scale_ref, noise_ref, left_ref, mid_ref, right_ref, up_ref, down_ref, inside_ref, node_ref, own_ref, transfer_ref, bases_ref, inv_ref, p_ref, res_ref, image_ref, sums_ref, src, tgt, wgt, coef, z, high, low, out, flat, far_src, far_wgt, node_src, node_wgt):
-    leaf_dev, rank, leaf_pts = bases_ref.shape
+def outside_body(pairs_ref, sizes_ref, scale_ref, left_ref, mid_ref, right_ref, up_ref, down_ref, inside_ref, out_ref, src, tgt, wgt, z, high, low):
+    leaf_dev, rhs, leaf_pts = out_ref.shape
     scale = scale_rows(scale_ref, (8, leaf_pts))
-    pushed = node_field(tm_size, place_ref, scale, node_ref, own_ref, transfer_ref, node_src, node_wgt)
     idle = 9 * leaf_dev
     src[idle] = jnp.zeros(src.shape[1:], BF16)
     wgt[idle] = jnp.zeros(wgt.shape[1:], BF16)
     for k in range(3):
-        prepare(up_ref.at[k], scale, k * leaf_dev, src, wgt, None, coef)
-        prepare(down_ref.at[k], scale, (6 + k) * leaf_dev, src, wgt, None, coef)
-    prepare(left_ref, scale, 3 * leaf_dev, src, wgt, None, coef)
-    prepare(mid_ref, scale, 4 * leaf_dev, src, None, tgt, coef)
-    prepare(right_ref, scale, 5 * leaf_dev, src, wgt, None, coef)
-    out[...] = inside_ref[...]
-    near_pairs(pairs_ref, sizes_ref[1], 0, src, tgt, wgt, out, z, high, low)
-
+        prepare(up_ref.at[k], scale, k * leaf_dev, src, wgt)
+        prepare(down_ref.at[k], scale, (6 + k) * leaf_dev, src, wgt)
+    prepare(left_ref, scale, 3 * leaf_dev, src, wgt)
+    prepare(mid_ref, scale, 4 * leaf_dev, src, None, tgt)
+    prepare(right_ref, scale, 5 * leaf_dev, src, wgt)
+    out_ref[...] = inside_ref[...]
+    near_pairs(pairs_ref, sizes_ref[1], 0, src, tgt, wgt, out_ref, z, high, low)
+
+
+def tail_body(tm_size, far_ref, place_ref, scale_ref, noise_ref, left_ref, mid_ref, right_ref, up_ref, down_ref, near_ref, node_ref, own_ref, transfer_ref, bases_ref, inv_ref, p_ref, res_ref, image_ref, sums_ref, src, tgt, coef, flat, far_src, far_wgt, node_src, node_wgt):
+    leaf_dev, rank, leaf_pts = bases_ref.shape
+    scale = scale_rows(scale_ref, (8, 4 * 128))
+    pushed = node_field(tm_size, place_ref, scale, node_ref, own_ref, transfer_ref, node_src, node_wgt)
+    brief = scale[:, :128]
+    for k in range(3):
+        prepare(up_ref.at[k], brief, k * leaf_dev, src, None, None, coef)
+        prepare(down_ref.at[k], brief, (6 + k) * leaf_dev, src, None, None, coef)
+    prepare(left_ref, brief, 3 * leaf_dev, src, None, None, coef)
+    prepare(mid_ref, brief, 4 * leaf_dev, src, None, tgt, coef)
+    prepare(right_ref, brief, 5 * leaf_dev, src, None, None, coef)
     for leaf in range(leaf_dev):
         for j in range(far_ref.shape[1]):
             w = far_ref[leaf, j]
@@ -335,7 +350,7 @@
         base_high, base_low = split(bases_ref[leaf])
         got = jnp.dot(incoming, base_high, preferred_element_type=F32)
         got = got + jnp.dot(incoming, base_low, preferred_element_type=F32)
-        flat[:, leaf * leaf_pts : (leaf + 1) * leaf_pts] = out[leaf] + got[:8] + got[8:]
+        flat[:, leaf * leaf_pts : (leaf + 1) * leaf_pts] = near_ref[leaf] + got[:8] + got[8:]
 
     chunks = flat.shape[1] // 128
     row = row_ids((8, 128))
@@ -404,16 +419,6 @@
         compiler_params=params(60),
         name="gather",
     )(by_row, coords, direction, bases)
-    node, own, inverse = pl.pallas_call(
-        node_body,
-        in_specs=[VMEM] * 5,
-        out_specs=[VMEM] * 3,
-        out_shape=[shape((devices, 8, 128), F32), shape((8, 128), F32), shape((chunks, 128), jnp.int32)],
-        scratch_shapes=[pltpu.VMEM((8, leaf_dev * rank), F32)],
-        compiler_params=params(24),
-        cost_estimate=pl.CostEstimate(flops=10**9, bytes_accessed=2**20, transcendentals=0),
-        name="node",
-    )(by_row, halo, first, transfer[0], device_skel)
     left = shifted(halo, "tm", 1)
     right = shifted(halo, "tm", -1)
 
@@ -430,16 +435,30 @@
         pltpu.VMEM((2, PART, leaf_pts), BF16),
     ]
     entries = near_list.size + 4
-    inside, pairs, sizes = pl.pallas_call(
+    inside, node, own, inverse, pairs, sizes = pl.pallas_call(
         inside_body,
-        in_specs=[SMEM] * 3 + [VMEM],
-        out_specs=[VMEM, SMEM, SMEM],
-        out_shape=[shape((leaf_dev, rhs, leaf_pts), F32), shape((entries,), jnp.int32), shape((2,), jnp.int32)],
-        scratch_shapes=[pltpu.SMEM((entries,), jnp.int32)] + pipeline(leaf_dev) + buffers,
+        in_specs=[SMEM] * 3 + [ANY] + [VMEM] * 4,
+        out_specs=[VMEM] * 4 + [SMEM] * 2,
+        out_shape=[
+            shape((leaf_dev, rhs, leaf_pts), F32),
+            shape((devices, 8, 128), F32),
+            shape((8, 128), F32),
+            shape((chunks, 128), jnp.int32),
+            shape((entries,), jnp.int32),
+            shape((2,), jnp.int32),
+        ],
+        scratch_shapes=[
+            pltpu.SMEM((entries,), jnp.int32),
+            pltpu.VMEM(halo.shape, F32),
+            pltpu.VMEM((8, leaf_dev * rank), F32),
+        ]
+        + pipeline(leaf_dev)
+        + buffers
+        + [pltpu.SemaphoreType.DMA(())],
         compiler_params=params(24),
         cost_estimate=pl.CostEstimate(flops=10**10, bytes_accessed=2**21, transcendentals=10**7),
         name="inside",
-    )(near_list, near_count, inv_scale, halo)
+    )(near_list, near_count, inv_scale, halo, first, by_row, transfer[0], device_skel)
     left, right, inside, node = lax.optimization_barrier((left, right, inside, node))
     nodes = lax.all_to_all(node, axes, 0, 0)
     row = jnp.stack([left, halo, right])
@@ -447,16 +466,25 @@
     down = shifted(row, "leaf", -1)
     place = jnp.stack([lax.axis_index("leaf"), lax.axis_index("tm")]).astype(jnp.int32)
 
+    near = pl.pallas_call(
+        outside_body,
+        in_specs=[SMEM] * 3 + [VMEM] * 6,
+        out_specs=VMEM,
+        out_shape=shape((leaf_dev, rhs, leaf_pts), F32),
+        scratch_shapes=pipeline(9 * leaf_dev) + buffers,
+        compiler_params=params(24),
+        cost_estimate=pl.CostEstimate(flops=3 * 10**10, bytes_accessed=2**21, transcendentals=3 * 10**7),
+        name="outside",
+    )(pairs, sizes, inv_scale, left, halo, right, up, down, inside)
     image, sums = pl.pallas_call(
-        functools.partial(rest_body, lax.axis_size("tm")),
-        in_specs=[SMEM] * 6 + [VMEM] * 13,
+        functools.partial(tail_body, lax.axis_size("tm")),
+        in_specs=[SMEM] * 4 + [VMEM] * 13,
         out_specs=[VMEM] * 2,
         out_shape=[shape((rhs, points), F32), shape((devices, 128), F32)],
-        scratch_shapes=pipeline(9 * leaf_dev)
-        + [pltpu.VMEM((9 * leaf_dev, 16, rank), BF16)]
-        + buffers
-        + [
-            pltpu.VMEM((leaf_dev, rhs, leaf_pts), F32),
+        scratch_shapes=[
+            pltpu.VMEM((9 * leaf_dev, 32, 128), BF16),
+            pltpu.VMEM((leaf_dev, 32, 128), BF16),
+            pltpu.VMEM((9 * leaf_dev, 16, rank), BF16),
             pltpu.VMEM((rhs, points), F32),
             pltpu.VMEM((leaf_dev, 32, far_list.shape[1] * rank), BF16),
             pltpu.VMEM((leaf_dev, 16, far_list.shape[1] * rank), BF16),
@@ -464,8 +492,8 @@
             pltpu.VMEM((16, devices * rank), BF16),
         ],
         compiler_params=params(24),
-        name="rest",
-    )(pairs, sizes, far_list, place, inv_scale, noise, left, halo, right, up, down, inside, nodes, own, transfer[0], bases, inverse, direction, residual)
+        name="tail",
+    )(far_list, place, inv_scale, noise, left, halo, right, up, down, near, nodes, own, transfer[0], bases, inverse, direction, residual)
     all_sums = lax.all_to_all(sums, axes, 0, 0, tiled=True)
     return pl.pallas_call(
         update_body,

time: 109 us -> 105 us (0.963)
  waiting for transfers between devices: 13.9 us -> 0.01 us
  blocking collectives: 16.4 us -> 26.6 us
  Pallas kernels: 51.5 us -> 45.3 us
  local copies, waits for them, and re-layouts: 2.2 us -> 5.98 us
  starting transfers between devices: 21.5 us -> 23.7 us
    all_to_all x1, waiting for transfers between devices: 13.9 us -> 0.01 us  [shards(): nodes = lax.all_to_all(node, axes, 0, 0)]
    all_to_all x1, blocking collectives: 16.4 us -> 26.6 us  [shards(): all_sums = lax.all_to_all(sums, axes, 0, 0, tiled=True)]
    pallas_call x3, Pallas kernels: 45.4 us -> 39.2 us  [the longest x1 20.1 us: shards(): pl.pallas_call(outside_body, in_specs=[SMEM] * 3 + [VMEM] * 6, out_specs=...]
    unnamed x30 -> x36, local copies, waits for them, and re-layouts: 2.2 us -> 5.98 us
    all_to_all x1, starting transfers between devices: 10.1 us -> 12.3 us  [shards(): nodes = lax.all_to_all(node, axes, 0, 0)]
  transfers between devices with their start and end apart: 5 -> 5, of which waited for: 1 -> 0; matrix products, arithmetic and copies ran while one was open for 0% -> 0% of each run, Pallas kernels for 12% -> 29%
where the time goes in v5:
time: 105 us; the launch traced here: 103 us
  Pallas kernels  45.3 us (43%)
  blocking collectives  26.6 us (25%)
  starting transfers between devices  23.7 us (23%)
  local copies, waits for them, and re-layouts  5.98 us (6%)
    all_to_all x1, blocking collectives, shards(): all_sums = lax.all_to_all(sums, axes, 0, 0, tiled=True)  26.6 us
    pallas_call x1, Pallas kernels, shards(): pl.pallas_call(outside_body, in_specs=[SMEM] * 3 + [VMEM] * 6, out_specs=...  20.1 us
    all_to_all x1, starting transfers between devices, shards(): nodes = lax.all_to_all(node, axes, 0, 0)  12.3 us
    ppermute x4, starting transfers between devices, shifted(): lax.ppermute(x, axis, [(i, i + by) for i in range(n) if 0 <= i + by < n])  11.3 us
    pallas_call x1, Pallas kernels, shards(): pl.pallas_call(inside_body, in_specs=[SMEM] * 3 + [ANY] + [VMEM] * 4, out...  10.3 us
    pallas_call x1, Pallas kernels, shards(): pl.pallas_call(functools.partial(tail_body, lax.axis_size('tm')), in_spec...  8.77 us
    unnamed x36, local copies, waits for them, and re-layouts  5.98 us
    pallas_call x1, Pallas kernels, shards(): pl.pallas_call(gather_body, in_specs=[ANY] * 4, out_specs=[VMEM] * 2, out...  5.29 us
  transfers between devices with their start and end apart: 5, of which 0 were waited for; matrix products, arithmetic and copies ran while one was open for 0% of the time, Pallas kernels for 29%

profile of v5, /device:TPU:1, one launch (start us, length us, event | category | flops | bytes accessed | tf_op | source)
XLA Modules:
  0.0 103.5 jit_solution(13530807988349014216)
XLA Ops:
  0.6 0.0 copy-start.8
  0.6 0.0 copy-start.10
  0.6 5.3 %gather.1 = (f32[104,512]{1,0:T(8,128)}, f32[8,8,128]{2,1,0:T(8,128)}) custom-call(s32[32,128]{1,0:T(8,128)} %bitcast.18, f32[4,4096]{1,0:T(4,128)} %x_hbm.1, f32[8,4096]{1,0:T(8,128)} %p_ref.3, f32[8,64,512]{2,1,0:T(8,128)} %bases_ref.1), custom_call_target="tpu_custom_call" | custom-call | tf_op jit(solution)/shard_map/gather/pallas_call | solution.py:407
  5.9 0.0 copy-start.15
  6.0 4.0 %collective-permute-start = (f32[104,512]{1,0:T(8,128)}, f32[104,512]{1,0:T(8,128)S(1)}, u32[]{:S(2)}, u32[]{:S(2)}) collective-permute-start(f32[104,512]{1,0:T(8,128)} %get-tuple-element.16.halo_hbm.mid_ref), channel_id=1, source_target_pairs={{0,1},{1,2},{2,3},{4,5},{5,6},{6,7},{8,9},{9,10},{10,11},{12,13},{... | collective-permute-start | bytes 638984 | tf_op jit(solution)/shard_map/ppermute | solution.py:396
  9.9 1.3 %collective-permute-start.1 = (f32[104,512]{1,0:T(8,128)}, f32[104,512]{1,0:T(8,128)S(1)}, u32[]{:S(2)}, u32[]{:S(2)}) collective-permute-start(f32[104,512]{1,0:T(8,128)} %get-tuple-element.16.halo_hbm.mid_ref), channel_id=1, source_target_pairs={{1,0},{2,1},{3,2},{5,4},{6,5},{7,6},{9,8},{10,9},{11,10},{13,12},{... | collective-permute-start | bytes 638984 | tf_op jit(solution)/shard_map/ppermute | solution.py:396
  11.2 0.0 copy-start.12
  11.2 0.0 copy-start.16
  11.2 0.0 copy-start.17
  11.3 0.0 copy-done.8
  11.3 0.0 copy-done.10
  11.3 0.0 copy-done.15
  11.3 0.6 copy-done.12
  11.9 0.0 copy-done.16
  11.9 0.0 copy-done.17
  11.9 0.0 copy-start.2
  11.9 0.9 copy-done.2
  12.8 0.0 copy-start.14
  12.8 0.8 copy-done.14
  13.6 10.3 %inside.1 = (f32[8,8,512]{2,1,0:T(8,128)S(1)}, f32[128,8,128]{2,1,0:T(8,128)}, f32[8,128]{1,0:T(8,128)S(1)}, s32[32,128]{1,0:T(8,128)S(1)}, s32[68]{0:T(128)S(1)}, /*index=5*/s32[2]{0:T(128)S(1)}) custom-call(s32[8,8]{1,0:T(8,128)S(1)} %copy-done.15, s32[8]{0:T(128)S(1)} %copy-done.16, f32[4]{0:T(128)S(1)} %copy-done.12, f32[104,512]{1,0:T(8,128)S(1)} %copy-done.2, ...), custom_call_target="tpu_custom_call" | custom-call | flops 10000000000 | bytes 2097152 | tf_op jit(solution)/shard_map/inside/pallas_call | solution.py:438
  23.9 0.0 collective-permute-done.left_ref
  23.9 0.0 collective-permute-done.1.right_ref
  24.0 0.9 pad_maximum_fusion
  24.9 4.2 %collective-permute-start.2 = (f32[3,104,512]{2,1,0:T(8,128)}, f32[3,104,512]{2,1,0:T(8,128)S(1)}, u32[]{:S(2)}, u32[]{:S(2)}) collective-permute-start(f32[3,104,512]{2,1,0:T(8,128)} %pad_maximum_fusion), channel_id=1, source_target_pairs={{0,4},{4,8},{8,12},{12,16},{16,20},{20,24},{24,28},{28,32},{32,36}... | collective-permute-start | bytes 1916936 | tf_op jit(solution)/shard_map/ppermute | solution.py:396
  29.0 1.9 %collective-permute-start.3 = (f32[3,104,512]{2,1,0:T(8,128)}, f32[3,104,512]{2,1,0:T(8,128)S(1)}, u32[]{:S(2)}, u32[]{:S(2)}) collective-permute-start(f32[3,104,512]{2,1,0:T(8,128)} %pad_maximum_fusion), channel_id=1, source_target_pairs={{4,0},{8,4},{12,8},{16,12},{20,16},{24,20},{28,24},{32,28},{36,32}... | collective-permute-start | bytes 1916936 | tf_op jit(solution)/shard_map/ppermute | solution.py:396
  31.0 0.1 pad_add_fusion.place_ref
  31.0 0.0 copy-start.3
  31.0 12.3 %all-to-all-start = ((f32[128,8,128]{2,1,0:T(8,128)}), f32[128,8,128]{2,1,0:T(8,128)S(1)}, u32[]{:S(2)}, u32[]{:S(2)}) async-start(f32[128,8,128]{2,1,0:T(8,128)} %get-tuple-element.25), calls=%async_computation | async-start | bytes 1048576 | tf_op jit(solution)/shard_map/all_to_all | solution.py:463
  43.4 0.0 collective-permute-done.2.up_ref
  43.4 0.0 collective-permute-done.3.down_ref
  43.4 0.0 copy-start.4
  43.4 0.8 copy-done.4
  44.3 0.0 copy-done.3
  44.3 1.1 %copy-done.5 = f32[3,104,512]{2,1,0:T(8,128)S(1)} copy-done((f32[3,104,512]{2,1,0:T(8,128)S(1)}, f32[3,104,512]{2,1,0:T(8,128)}, u32[]{:S(2)}) %copy-start.5) | copy-done | bytes 639000
  45.4 20.1 %outside.1.near_ref = f32[8,8,512]{2,1,0:T(8,128)S(1)} custom-call(s32[68]{0:T(128)S(1)} %get-tuple-element.22.pairs_ref, s32[2]{0:T(128)S(1)} %get-tuple-element.23.sizes_ref, f32[4]{0:T(128)S(1)} %copy-done.12, f32[104,512]{1,0:T(8,128)S(1)} %collective-permute-done.left_ref, f32[104,512]{1,0:T(8,128)S(1)} %copy-done.3, ...), custom_call_target="tpu_custom_call" | custom-call | flops 30000001024 | bytes 2097152 | tf_op jit(solution)/shard_map/outside/pallas_call | solution.py:469
  65.5 0.0 all-to-all-done.node_ref
  65.5 0.0 copy-start.13
  65.5 0.0 copy-done
  65.5 0.0 copy-done.1
  65.5 0.0 copy-done.7
  65.5 0.0 copy-done.11
  65.6 0.6 copy-done.13
  66.2 1.1 %copy-done.6 = f32[3,104,512]{2,1,0:T(8,128)S(1)} copy-done((f32[3,104,512]{2,1,0:T(8,128)S(1)}, f32[3,104,512]{2,1,0:T(8,128)}, u32[]{:S(2)}) %copy-start.6) | copy-done | bytes 639000
  67.2 8.8 %tail.1 = (f32[8,4096]{1,0:T(8,128)S(1)}, f32[128,128]{1,0:T(8,128)S(1)}) custom-call(s32[8,8]{1,0:T(8,128)S(1)} %copy-done.11, s32[2]{0:T(128)S(1)} %pad_add_fusion.place_ref, f32[4]{0:T(128)S(1)} %copy-done.12, f32[8]{0:T(128)S(1)} %copy-done.13, f32[104,512]{1,0:T(8,128)S(1)} %collective-permute-done.left_ref, f32[104,512]{1,0:T(8,128)S(1)} %copy-done.3, ...), custom_call_target="tpu_custom_call" | custom-call | tf_op jit(solution)/shard_map/tail/pallas_call | solution.py:479
  76.0 0.0 copy-start.9
  76.0 26.6 %all_to_all.16 = f32[128,1,128]{2,1,0:T(1,128)S(1)} all-to-all(f32[128,1,128]{2,1,0:T(1,128)S(1)} %bitcast.17), channel_id=1, replica_groups=mesh['leaf'=32,'tm'=4] {'leaf','tm'}, dimensions={0} | all-to-all | bytes 131072 | tf_op jit(solution)/shard_map/all_to_all | solution.py:497
  102.7 0.0 copy-done.9
  102.7 0.8 update.1
  (6 shorter events, 0.0 us)
Async XLA Ops:
  0.6 10.6 %copy-start.8 = (f32[1,64,512]{2,1,0:T(8,128)S(1)}, f32[1,64,512]{2,1,0:T(8,128)}, u32[]{:S(2)}) copy-start(f32[1,64,512]{2,1,0:T(8,128)} %param.19) | copy-start | bytes 393220
  0.6 10.6 %copy-start.10 = (s32[4096]{0:T(1024)S(1)}, s32[4096]{0:T(1024)}, u32[]{:S(2)}) copy-start(s32[4096]{0:T(1024)} %param.17) | copy-start | bytes 49156
  5.9 5.3 %copy-start.15 = (s32[8,8]{1,0:T(8,128)S(1)}, s32[8,8]{1,0:T(8,128)}, u32[]{:S(2)}) copy-start(s32[8,8]{1,0:T(8,128)} %near_ref.1) | copy-start | bytes 772
  6.0 18.0 %collective-permute-start = (f32[104,512]{1,0:T(8,128)}, f32[104,512]{1,0:T(8,128)S(1)}, u32[]{:S(2)}, u32[]{:S(2)}) collective-permute-start(f32[104,512]{1,0:T(8,128)} %get-tuple-element.16.halo_hbm.mid_ref), channel_id=1, source_target_pairs={{0,1},{1,2},{2,3},{4,5},{5,6},{6,7},{8,9},{9,10},{10,11},{12,13},{... | collective-permute-start | bytes 638984 | tf_op jit(solution)/shard_map/ppermute | solution.py:396
  9.9 14.0 %collective-permute-start.1 = (f32[104,512]{1,0:T(8,128)}, f32[104,512]{1,0:T(8,128)S(1)}, u32[]{:S(2)}, u32[]{:S(2)}) collective-permute-start(f32[104,512]{1,0:T(8,128)} %get-tuple-element.16.halo_hbm.mid_ref), channel_id=1, source_target_pairs={{1,0},{2,1},{3,2},{5,4},{6,5},{7,6},{9,8},{10,9},{11,10},{13,12},{... | collective-permute-start | bytes 638984 | tf_op jit(solution)/shard_map/ppermute | solution.py:396
  11.2 0.7 copy-start.12
  11.2 0.7 copy-start.16
  11.2 0.7 copy-start.17
  11.9 0.9 copy-start.2
  12.8 0.8 copy-start.14
  24.9 18.5 %collective-permute-start.2 = (f32[3,104,512]{2,1,0:T(8,128)}, f32[3,104,512]{2,1,0:T(8,128)S(1)}, u32[]{:S(2)}, u32[]{:S(2)}) collective-permute-start(f32[3,104,512]{2,1,0:T(8,128)} %pad_maximum_fusion), channel_id=1, source_target_pairs={{0,4},{4,8},{8,12},{12,16},{16,20},{20,24},{24,28},{28,32},{32,36}... | collective-permute-start | bytes 1916936 | tf_op jit(solution)/shard_map/ppermute | solution.py:396
  29.0 14.4 %collective-permute-start.3 = (f32[3,104,512]{2,1,0:T(8,128)}, f32[3,104,512]{2,1,0:T(8,128)S(1)}, u32[]{:S(2)}, u32[]{:S(2)}) collective-permute-start(f32[3,104,512]{2,1,0:T(8,128)} %pad_maximum_fusion), channel_id=1, source_target_pairs={{4,0},{8,4},{12,8},{16,12},{20,16},{24,20},{28,24},{32,28},{36,32}... | collective-permute-start | bytes 1916936 | tf_op jit(solution)/shard_map/ppermute | solution.py:396
  31.0 13.2 %copy-start.3 = (f32[104,512]{1,0:T(8,128)S(1)}, f32[104,512]{1,0:T(8,128)}, u32[]{:S(2)}) copy-start(f32[104,512]{1,0:T(8,128)} %get-tuple-element.16.halo_hbm.mid_ref) | copy-start | bytes 638980
  31.0 34.4 %all-to-all-start = ((f32[128,8,128]{2,1,0:T(8,128)}), f32[128,8,128]{2,1,0:T(8,128)S(1)}, u32[]{:S(2)}, u32[]{:S(2)}) async-start(f32[128,8,128]{2,1,0:T(8,128)} %get-tuple-element.25), calls=%async_computation | async-start | bytes 1048576 | tf_op jit(solution)/shard_map/all_to_all | solution.py:463
  43.4 0.9 copy-start.4
  44.3 1.1 %copy-start.5 = (f32[3,104,512]{2,1,0:T(8,128)S(1)}, f32[3,104,512]{2,1,0:T(8,128)}, u32[]{:S(2)}) copy-start(f32[3,104,512]{2,1,0:T(8,128)} %copy-done.4) | copy-start | bytes 1916932
  45.4 20.2 %copy-start = (f32[8,64,512]{2,1,0:T(8,128)S(1)}, f32[8,64,512]{2,1,0:T(8,128)}, u32[]{:S(2)}) copy-start(f32[8,64,512]{2,1,0:T(8,128)} %bases_ref.1) | copy-start | bytes 3145732
  45.4 20.2 %copy-start.1 = (f32[8,4096]{1,0:T(8,128)S(1)}, f32[8,4096]{1,0:T(8,128)}, u32[]{:S(2)}) copy-start(f32[8,4096]{1,0:T(8,128)} %p_ref.3) | copy-start | bytes 393220
  45.4 20.2 %copy-start.7 = (f32[8,4096]{1,0:T(8,128)S(1)}, f32[8,4096]{1,0:T(8,128)}, u32[]{:S(2)}) copy-start(f32[8,4096]{1,0:T(8,128)} %res_ref.3) | copy-start | bytes 393220
  45.4 20.2 %copy-start.11 = (s32[8,8]{1,0:T(8,128)S(1)}, s32[8,8]{1,0:T(8,128)}, u32[]{:S(2)}) copy-start(s32[8,8]{1,0:T(8,128)} %far_ref.1) | copy-start | bytes 772
  65.5 0.7 copy-start.13
  66.2 1.1 %copy-start.6 = (f32[3,104,512]{2,1,0:T(8,128)S(1)}, f32[3,104,512]{2,1,0:T(8,128)}, u32[]{:S(2)}) copy-start(f32[3,104,512]{2,1,0:T(8,128)} %copy-done.4) | copy-start | bytes 1916932
  76.0 26.6 %copy-start.9 = (f32[8,4096]{1,0:T(8,128)S(1)}, f32[8,4096]{1,0:T(8,128)}, u32[]{:S(2)}) copy-start(f32[8,4096]{1,0:T(8,128)} %it_ref.1) | copy-start | bytes 393220

commit v6 on v5

--- a/solution.py
+++ b/solution.py
@@ -19,6 +19,7 @@
 SMEM = pl.BlockSpec(memory_space=pltpu.SMEM)
 ANY = pl.BlockSpec(memory_space=pl.ANY)
 PART = 256
+FIRST_PAIRS = 10
 
 
 def params(mib, **kw):
@@ -95,7 +96,7 @@
     return picked
 
 
-def gather_body(order_hbm, x_hbm, p_hbm, bases_hbm, halo_ref, first_ref, order_ref, xx, p_ref, bases_ref, sems):
+def gather_body(order_hbm, x_hbm, p_hbm, bases_hbm, halo_ref, order_ref, xx, p_ref, bases_ref, sems):
     leaf_dev, rank, leaf_pts = bases_ref.shape
     points = p_ref.shape[1]
     chunks = points // 128
@@ -129,7 +130,6 @@
                 got_x, got_p = gather_lanes([loads(xx), loads(p_ref)], jnp.broadcast_to(ids, (8, 128)))
                 kept.append(got_x)
                 halo_ref[pl.ds(pl.multiple_of(32 + leaf * 8, 8), 8), j * 128 : (j + 1) * 128] = got_p
-            first_ref[leaf] = kept[h * per_leaf]
         for j in range(per_leaf):
             both = jnp.where(row_ids((8, 128)) < 4, kept[j], kept[per_leaf + j])
             halo_ref[pl.ds(pl.multiple_of(g * 8, 8), 8), j * 128 : (j + 1) * 128] = both
@@ -142,12 +142,16 @@
         halo_ref[96:104, leaf * rank : (leaf + 1) * rank] = coef
 
 
-def node_work(order_ref, halo_ref, first_ref, transfer_ref, skel_ref, node_ref, own_ref, inv_ref, slot):
+def node_work(order_ref, halo_ref, transfer_ref, skel_ref, node_ref, own_ref, inv_ref, slot):
     chunks = order_ref.shape[0]
     rank = transfer_ref.shape[0]
-    leaf_dev = first_ref.shape[0]
-    for leaf in range(leaf_dev):
-        slot[:, leaf * rank : (leaf + 1) * rank] = first_ref[leaf][:, :rank]
+    leaf_dev = halo_ref.shape[0] // 13
+    upper = row_ids((8, 128)) < 4
+    for g in range(leaf_dev // 2):
+        both = halo_ref[g * 8 : g * 8 + 8, 0:128]
+        turned = pltpu.roll(both, 4, 0)
+        slot[:, 2 * g * rank : (2 * g + 1) * rank] = jnp.where(upper, both, turned)[:, :rank]
+        slot[:, (2 * g + 1) * rank : (2 * g + 2) * rank] = jnp.where(upper, turned, both)[:, :rank]
     weights = contract(halo_ref[96:104, :], transfer_ref[...], ((1,), (1,)), EXACT)
     slots = [lambda s=s: slot[:, s * 128 : (s + 1) * 128] for s in range(leaf_dev * rank // 128)]
     ids = jnp.concatenate([skel_ref[...], skel_ref[...]], axis=1)
@@ -201,7 +205,7 @@
     def leaf_step(leaf, sums):
         def entry(j, sums):
             w = near_ref[leaf, j]
-            here = jnp.where(w // leaf_dev == 4, 1, 0)
+            here = jnp.where((w // leaf_dev == 4) & (sums[0] < FIRST_PAIRS), 1, 0)
             code = leaf * 128 + w
             inside[sums[0]] = code
             outside[sums[1]] = code
@@ -258,7 +262,7 @@
     lax.fori_loop(0, (n + 1) // 2, two_pairs, 0)
 
 
-def inside_body(near_ref, count_ref, scale_ref, halo_hbm, first_ref, order_ref, transfer_ref, skel_ref, out_ref, node_ref, own_ref, inv_ref, pairs_ref, sizes_ref, pairs, halo_ref, slot, src, tgt, wgt, z, high, low, sem):
+def inside_body(near_ref, count_ref, scale_ref, halo_hbm, order_ref, transfer_ref, skel_ref, out_ref, node_ref, own_ref, inv_ref, pairs_ref, sizes_ref, pairs, halo_ref, slot, src, tgt, wgt, z, high, low, sem):
     leaf_dev, rhs, leaf_pts = out_ref.shape
     move = pltpu.make_async_copy(halo_hbm, halo_ref, sem)
     move.start()
@@ -269,7 +273,7 @@
     wgt[leaf_dev] = jnp.zeros(wgt.shape[1:], BF16)
     out_ref[...] = jnp.zeros_like(out_ref)
     move.wait()
-    node_work(order_ref, halo_ref, first_ref, transfer_ref, skel_ref, node_ref, own_ref, inv_ref, slot)
+    node_work(order_ref, halo_ref, transfer_ref, skel_ref, node_ref, own_ref, inv_ref, slot)
     prepare(halo_ref, scale_rows(scale_ref, (8, leaf_pts)), 0, src, wgt, tgt)
     near_pairs(pairs, n, 4 * leaf_dev, src, tgt, wgt, out_ref, z, high, low)
 
@@ -320,7 +324,7 @@
         prepare(up_ref.at[k], scale, k * leaf_dev, src, wgt)
         prepare(down_ref.at[k], scale, (6 + k) * leaf_dev, src, wgt)
     prepare(left_ref, scale, 3 * leaf_dev, src, wgt)
-    prepare(mid_ref, scale, 4 * leaf_dev, src, None, tgt)
+    prepare(mid_ref, scale, 4 * leaf_dev, src, wgt, tgt)
     prepare(right_ref, scale, 5 * leaf_dev, src, wgt)
     out_ref[...] = inside_ref[...]
     near_pairs(pairs_ref, sizes_ref[1], 0, src, tgt, wgt, out_ref, z, high, low)
@@ -404,11 +408,11 @@
     chunks = points // 128
     shape = jax.ShapeDtypeStruct
     by_row = order.reshape(chunks, 128)
-    halo, first = pl.pallas_call(
+    halo = pl.pallas_call(
         gather_body,
         in_specs=[ANY] * 4,
-        out_specs=[VMEM] * 2,
-        out_shape=[shape((13 * leaf_dev, leaf_pts), F32), shape((leaf_dev, 8, 128), F32)],
+        out_specs=VMEM,
+        out_shape=shape((13 * leaf_dev, leaf_pts), F32),
         scratch_shapes=[
             pltpu.VMEM((chunks, 128), jnp.int32),
             pltpu.VMEM((8, points), F32),
@@ -437,7 +441,7 @@
     entries = near_list.size + 4
     inside, node, own, inverse, pairs, sizes = pl.pallas_call(
         inside_body,
-        in_specs=[SMEM] * 3 + [ANY] + [VMEM] * 4,
+        in_specs=[SMEM] * 3 + [ANY] + [VMEM] * 3,
         out_specs=[VMEM] * 4 + [SMEM] * 2,
         out_shape=[
             shape((leaf_dev, rhs, leaf_pts), F32),
@@ -455,10 +459,10 @@
         + pipeline(leaf_dev)
         + buffers
         + [pltpu.SemaphoreType.DMA(())],
-        compiler_params=params(24),
+        compiler_params=params(58),
         cost_estimate=pl.CostEstimate(flops=10**10, bytes_accessed=2**21, transcendentals=10**7),
         name="inside",
-    )(near_list, near_count, inv_scale, halo, first, by_row, transfer[0], device_skel)
+    )(near_list, near_count, inv_scale, halo, by_row, transfer[0], device_skel)
     left, right, inside, node = lax.optimization_barrier((left, right, inside, node))
     nodes = lax.all_to_all(node, axes, 0, 0)
     row = jnp.stack([left, halo, right])
@@ -472,7 +476,7 @@
         out_specs=VMEM,
         out_shape=shape((leaf_dev, rhs, leaf_pts), F32),
         scratch_shapes=pipeline(9 * leaf_dev) + buffers,
-        compiler_params=params(24),
+        compiler_params=params(14),
         cost_estimate=pl.CostEstimate(flops=3 * 10**10, bytes_accessed=2**21, transcendentals=3 * 10**7),
         name="outside",
     )(pairs, sizes, inv_scale, left, halo, right, up, down, inside)
@@ -491,7 +495,7 @@
             pltpu.VMEM((32, devices * rank), BF16),
             pltpu.VMEM((16, devices * rank), BF16),
         ],
-        compiler_params=params(24),
+        compiler_params=params(14),
         name="tail",
     )(far_list, place, inv_scale, noise, left, halo, right, up, down, near, nodes, own, transfer[0], bases, inverse, direction, residual)
     all_sums = lax.all_to_all(sums, axes, 0, 0, tiled=True)
@@ -500,7 +504,7 @@
         in_specs=[VMEM] * 5,
         out_specs=[VMEM] * 2,
         out_shape=[shape((rhs, points), F32)] * 2,
-        compiler_params=params(24),
+        compiler_params=params(8),
         name="update",
     )(all_sums, iterate, direction, residual, image)
 

time: 105 us -> 100 us (0.952); the launches traced: 103 us -> 99.6 us
  local copies, waits for them, and re-layouts: 5.98 us -> 4.33 us
    pallas_call x2, Pallas kernels: 15.6 us -> 13.8 us  [the longest x1 8.6 us: shards(): pl.pallas_call(inside_body, in_specs=[SMEM] * 3 + [ANY] + [VMEM] * 3, out...]
    unnamed x36 -> x34, local copies, waits for them, and re-layouts: 5.98 us -> 4.33 us
  transfers between devices with their start and end apart: 5 -> 5, of which waited for: 0 -> 0; matrix products, arithmetic and copies ran while one was open for 0% -> 0% of each run, Pallas kernels for 29% -> 30%
where the time goes in v6:
time: 100 us; the launch traced here: 99.6 us
  Pallas kernels  44.5 us (44%)
  blocking collectives  25.9 us (26%)
  starting transfers between devices  22.9 us (23%)
  local copies, waits for them, and re-layouts  4.33 us (4%)
    all_to_all x1, blocking collectives, shards(): all_sums = lax.all_to_all(sums, axes, 0, 0, tiled=True)  25.9 us
    pallas_call x1, Pallas kernels, shards(): pl.pallas_call(outside_body, in_specs=[SMEM] * 3 + [VMEM] * 6, out_specs=...  21.1 us
    all_to_all x1, starting transfers between devices, shards(): nodes = lax.all_to_all(node, axes, 0, 0)  11.6 us
    ppermute x4, starting transfers between devices, shifted(): lax.ppermute(x, axis, [(i, i + by) for i in range(n) if 0 <= i + by < n])  11.3 us
    pallas_call x1, Pallas kernels, shards(): pl.pallas_call(functools.partial(tail_body, lax.axis_size('tm')), in_spec...  8.77 us
    pallas_call x1, Pallas kernels, shards(): pl.pallas_call(inside_body, in_specs=[SMEM] * 3 + [ANY] + [VMEM] * 3, out...  8.6 us
    pallas_call x1, Pallas kernels, shards(): pl.pallas_call(gather_body, in_specs=[ANY] * 4, out_specs=VMEM, out_shape...  5.25 us
    unnamed x34, local copies, waits for them, and re-layouts  4.33 us
  transfers between devices with their start and end apart: 5, of which 0 were waited for; matrix products, arithmetic and copies ran while one was open for 0% of the time, Pallas kernels for 30%

profile of v6, /device:TPU:1, one launch (start us, length us, event | category | flops | bytes accessed | tf_op | source)
XLA Modules:
  0.0 99.6 jit_solution(7465784485006700478)
XLA Ops:
  0.6 5.2 %gather.1.halo_hbm.mid_ref = f32[104,512]{1,0:T(8,128)} custom-call(s32[32,128]{1,0:T(8,128)} %bitcast.18, f32[4,4096]{1,0:T(4,128)} %x_hbm.1, f32[8,4096]{1,0:T(8,128)} %p_ref.3, f32[8,64,512]{2,1,0:T(8,128)} %bases_ref.1), custom_call_target="tpu_custom_call" | custom-call | tf_op jit(solution)/shard_map/gather/pallas_call | solution.py:411
  5.9 4.0 %collective-permute-start = (f32[104,512]{1,0:T(8,128)}, f32[104,512]{1,0:T(8,128)S(1)}, u32[]{:S(2)}, u32[]{:S(2)}) collective-permute-start(f32[104,512]{1,0:T(8,128)} %gather.1.halo_hbm.mid_ref), channel_id=1, source_target_pairs={{0,1},{1,2},{2,3},{4,5},{5,6},{6,7},{8,9},{9,10},{10,11},{12,13},{... | collective-permute-start | bytes 638984 | tf_op jit(solution)/shard_map/ppermute | solution.py:400
  9.8 1.3 %collective-permute-start.1 = (f32[104,512]{1,0:T(8,128)}, f32[104,512]{1,0:T(8,128)S(1)}, u32[]{:S(2)}, u32[]{:S(2)}) collective-permute-start(f32[104,512]{1,0:T(8,128)} %gather.1.halo_hbm.mid_ref), channel_id=1, source_target_pairs={{1,0},{2,1},{3,2},{5,4},{6,5},{7,6},{9,8},{10,9},{11,10},{13,12},{... | collective-permute-start | bytes 638984 | tf_op jit(solution)/shard_map/ppermute | solution.py:400
  11.1 0.0 copy-start.1
  11.2 8.6 %inside.1 = (f32[8,8,512]{2,1,0:T(8,128)}, f32[128,8,128]{2,1,0:T(8,128)}, f32[8,128]{1,0:T(8,128)}, s32[32,128]{1,0:T(8,128)}, s32[68]{0:T(128)}, /*index=5*/s32[2]{0:T(128)}) custom-call(s32[8,8]{1,0:T(8,128)} %near_ref.1, s32[8]{0:T(128)} %count_ref.1, f32[4]{0:T(128)} %scale_ref.5, f32[104,512]{1,0:T(8,128)} %gather.1.halo_hbm.mid_ref, ...), custom_call_target="tpu_custom_call" | custom-call | flops 10000000000 | bytes 2097152 | tf_op jit(solution)/shard_map/inside/pallas_call | solution.py:442
  19.8 0.0 collective-permute-done.left_ref
  19.8 0.0 collective-permute-done.1.right_ref
  19.8 0.0 copy-done.1
  19.8 0.9 pad_maximum_fusion
  20.7 4.1 %collective-permute-start.2 = (f32[3,104,512]{2,1,0:T(8,128)}, f32[3,104,512]{2,1,0:T(8,128)S(1)}, u32[]{:S(2)}, u32[]{:S(2)}) collective-permute-start(f32[3,104,512]{2,1,0:T(8,128)} %pad_maximum_fusion), channel_id=1, source_target_pairs={{0,4},{4,8},{8,12},{12,16},{16,20},{20,24},{24,28},{28,32},{32,36}... | collective-permute-start | bytes 1916936 | tf_op jit(solution)/shard_map/ppermute | solution.py:400
  24.8 1.9 %collective-permute-start.3 = (f32[3,104,512]{2,1,0:T(8,128)}, f32[3,104,512]{2,1,0:T(8,128)S(1)}, u32[]{:S(2)}, u32[]{:S(2)}) collective-permute-start(f32[3,104,512]{2,1,0:T(8,128)} %pad_maximum_fusion), channel_id=1, source_target_pairs={{4,0},{8,4},{12,8},{16,12},{20,16},{24,20},{28,24},{32,28},{36,32}... | collective-permute-start | bytes 1916936 | tf_op jit(solution)/shard_map/ppermute | solution.py:400
  26.8 0.1 pad_add_fusion.place_ref
  26.8 0.0 copy-start.14
  26.8 11.6 %all-to-all-start = ((f32[128,8,128]{2,1,0:T(8,128)}), f32[128,8,128]{2,1,0:T(8,128)S(1)}, u32[]{:S(2)}, u32[]{:S(2)}) async-start(f32[128,8,128]{2,1,0:T(8,128)} %get-tuple-element.21), calls=%async_computation | async-start | bytes 1048576 | tf_op jit(solution)/shard_map/all_to_all | solution.py:467
  38.5 0.0 collective-permute-done.2.up_ref
  38.5 0.0 collective-permute-done.3.down_ref
  38.5 0.0 copy-start.3
  38.5 0.9 copy-done.3
  39.3 0.0 copy-start.12
  39.3 0.0 copy-start.15
  39.3 0.0 copy-start.16
  39.4 0.0 copy-done.14
  39.4 0.6 copy-done.12
  40.0 0.0 copy-done.15
  40.0 0.0 copy-done.16
  40.0 0.0 copy-start.4
  40.0 1.1 %copy-done.4 = f32[3,104,512]{2,1,0:T(8,128)S(1)} copy-done((f32[3,104,512]{2,1,0:T(8,128)S(1)}, f32[3,104,512]{2,1,0:T(8,128)}, u32[]{:S(2)}) %copy-start.4) | copy-done | bytes 639000
  41.1 0.0 copy-start
  41.1 0.0 copy-start.9
  41.1 0.0 copy-start.10
  41.2 0.0 copy-start.11
  41.2 21.1 %outside.1.near_ref = f32[8,8,512]{2,1,0:T(8,128)S(1)} custom-call(s32[68]{0:T(128)S(1)} %copy-done.15, s32[2]{0:T(128)S(1)} %copy-done.16, f32[4]{0:T(128)S(1)} %copy-done.12, f32[104,512]{1,0:T(8,128)S(1)} %collective-permute-done.left_ref, f32[104,512]{1,0:T(8,128)S(1)} %copy-done.1, f32[104,512]{1,0:T(8,128)S(1)} %collective-permute-done.1.right_ref, ...), custom_call_target="tpu_custom_call" | custom-call | flops 30000001024 | bytes 2097152 | tf_op jit(solution)/shard_map/outside/pallas_call | solution.py:473
  62.3 0.0 all-to-all-done.node_ref
  62.3 0.0 copy-start.13
  62.3 0.0 copy-done
  62.3 0.0 copy-done.2
  62.3 0.0 copy-done.6
  62.3 0.0 copy-done.7
  62.3 0.0 copy-done.9
  62.3 0.0 copy-done.10
  62.3 0.0 copy-done.11
  62.4 0.6 copy-done.13
  62.9 1.1 %copy-done.5 = f32[3,104,512]{2,1,0:T(8,128)S(1)} copy-done((f32[3,104,512]{2,1,0:T(8,128)S(1)}, f32[3,104,512]{2,1,0:T(8,128)}, u32[]{:S(2)}) %copy-start.5) | copy-done | bytes 639000
  64.0 8.8 %tail.1 = (f32[8,4096]{1,0:T(8,128)S(1)}, f32[128,128]{1,0:T(8,128)S(1)}) custom-call(s32[8,8]{1,0:T(8,128)S(1)} %copy-done.10, s32[2]{0:T(128)S(1)} %pad_add_fusion.place_ref, f32[4]{0:T(128)S(1)} %copy-done.12, f32[8]{0:T(128)S(1)} %copy-done.13, f32[104,512]{1,0:T(8,128)S(1)} %collective-permute-done.left_ref, f32[104,512]{1,0:T(8,128)S(1)} %copy-done.1, ...), custom_call_target="tpu_custom_call" | custom-call | tf_op jit(solution)/shard_map/tail/pallas_call | solution.py:483
  72.8 0.0 copy-start.8
  72.8 25.9 %all_to_all.16 = f32[128,1,128]{2,1,0:T(1,128)S(1)} all-to-all(f32[128,1,128]{2,1,0:T(1,128)S(1)} %bitcast.17), channel_id=1, replica_groups=mesh['leaf'=32,'tm'=4] {'leaf','tm'}, dimensions={0} | all-to-all | bytes 131072 | tf_op jit(solution)/shard_map/all_to_all | solution.py:501
  98.7 0.0 copy-done.8
  98.7 0.8 update.1
  (4 shorter events, 0.0 us)
Async XLA Ops:
  5.9 13.9 %collective-permute-start = (f32[104,512]{1,0:T(8,128)}, f32[104,512]{1,0:T(8,128)S(1)}, u32[]{:S(2)}, u32[]{:S(2)}) collective-permute-start(f32[104,512]{1,0:T(8,128)} %gather.1.halo_hbm.mid_ref), channel_id=1, source_target_pairs={{0,1},{1,2},{2,3},{4,5},{5,6},{6,7},{8,9},{9,10},{10,11},{12,13},{... | collective-permute-start | bytes 638984 | tf_op jit(solution)/shard_map/ppermute | solution.py:400
  9.8 9.9 %collective-permute-start.1 = (f32[104,512]{1,0:T(8,128)}, f32[104,512]{1,0:T(8,128)S(1)}, u32[]{:S(2)}, u32[]{:S(2)}) collective-permute-start(f32[104,512]{1,0:T(8,128)} %gather.1.halo_hbm.mid_ref), channel_id=1, source_target_pairs={{1,0},{2,1},{3,2},{5,4},{6,5},{7,6},{9,8},{10,9},{11,10},{13,12},{... | collective-permute-start | bytes 638984 | tf_op jit(solution)/shard_map/ppermute | solution.py:400
  11.1 8.6 %copy-start.1 = (f32[104,512]{1,0:T(8,128)S(1)}, f32[104,512]{1,0:T(8,128)}, u32[]{:S(2)}) copy-start(f32[104,512]{1,0:T(8,128)} %gather.1.halo_hbm.mid_ref) | copy-start | bytes 638980
  20.7 17.8 %collective-permute-start.2 = (f32[3,104,512]{2,1,0:T(8,128)}, f32[3,104,512]{2,1,0:T(8,128)S(1)}, u32[]{:S(2)}, u32[]{:S(2)}) collective-permute-start(f32[3,104,512]{2,1,0:T(8,128)} %pad_maximum_fusion), channel_id=1, source_target_pairs={{0,4},{4,8},{8,12},{12,16},{16,20},{20,24},{24,28},{28,32},{32,36}... | collective-permute-start | bytes 1916936 | tf_op jit(solution)/shard_map/ppermute | solution.py:400
  24.8 13.7 %collective-permute-start.3 = (f32[3,104,512]{2,1,0:T(8,128)}, f32[3,104,512]{2,1,0:T(8,128)S(1)}, u32[]{:S(2)}, u32[]{:S(2)}) collective-permute-start(f32[3,104,512]{2,1,0:T(8,128)} %pad_maximum_fusion), channel_id=1, source_target_pairs={{4,0},{8,4},{12,8},{16,12},{20,16},{24,20},{28,24},{32,28},{36,32}... | collective-permute-start | bytes 1916936 | tf_op jit(solution)/shard_map/ppermute | solution.py:400
  26.8 12.5 %copy-start.14 = (f32[8,8,512]{2,1,0:T(8,128)S(1)}, f32[8,8,512]{2,1,0:T(8,128)}, u32[]{:S(2)}) copy-start(f32[8,8,512]{2,1,0:T(8,128)} %get-tuple-element.20.inside_ref) | copy-start | bytes 393220
  26.8 35.4 %all-to-all-start = ((f32[128,8,128]{2,1,0:T(8,128)}), f32[128,8,128]{2,1,0:T(8,128)S(1)}, u32[]{:S(2)}, u32[]{:S(2)}) async-start(f32[128,8,128]{2,1,0:T(8,128)} %get-tuple-element.21), calls=%async_computation | async-start | bytes 1048576 | tf_op jit(solution)/shard_map/all_to_all | solution.py:467
  38.5 0.9 copy-start.3
  39.3 0.7 copy-start.12
  39.3 0.7 copy-start.15
  39.3 0.7 copy-start.16
  40.0 1.1 %copy-start.4 = (f32[3,104,512]{2,1,0:T(8,128)S(1)}, f32[3,104,512]{2,1,0:T(8,128)}, u32[]{:S(2)}) copy-start(f32[3,104,512]{2,1,0:T(8,128)} %copy-done.3) | copy-start | bytes 1916932
  41.1 21.2 %copy-start = (f32[8,64,512]{2,1,0:T(8,128)S(1)}, f32[8,64,512]{2,1,0:T(8,128)}, u32[]{:S(2)}) copy-start(f32[8,64,512]{2,1,0:T(8,128)} %bases_ref.1) | copy-start | bytes 3145732
  41.1 21.2 %copy-start.2 = (f32[8,4096]{1,0:T(8,128)S(1)}, f32[8,4096]{1,0:T(8,128)}, u32[]{:S(2)}) copy-start(f32[8,4096]{1,0:T(8,128)} %p_ref.3) | copy-start | bytes 393220
  41.1 21.2 %copy-start.6 = (f32[8,4096]{1,0:T(8,128)S(1)}, f32[8,4096]{1,0:T(8,128)}, u32[]{:S(2)}) copy-start(f32[8,4096]{1,0:T(8,128)} %res_ref.3) | copy-start | bytes 393220
  41.1 21.2 %copy-start.7 = (f32[1,64,512]{2,1,0:T(8,128)S(1)}, f32[1,64,512]{2,1,0:T(8,128)}, u32[]{:S(2)}) copy-start(f32[1,64,512]{2,1,0:T(8,128)} %param.19) | copy-start | bytes 393220
  41.1 21.2 %copy-start.9 = (s32[32,128]{1,0:T(8,128)S(1)}, s32[32,128]{1,0:T(8,128)}, u32[]{:S(2)}) copy-start(s32[32,128]{1,0:T(8,128)} %get-tuple-element.23.inv_ref) | copy-start | bytes 49156
  41.1 21.2 %copy-start.10 = (s32[8,8]{1,0:T(8,128)S(1)}, s32[8,8]{1,0:T(8,128)}, u32[]{:S(2)}) copy-start(s32[8,8]{1,0:T(8,128)} %far_ref.1) | copy-start | bytes 772
  41.2 21.2 %copy-start.11 = (f32[8,128]{1,0:T(8,128)S(1)}, f32[8,128]{1,0:T(8,128)}, u32[]{:S(2)}) copy-start(f32[8,128]{1,0:T(8,128)} %get-tuple-element.22.own_ref) | copy-start | bytes 12292
  62.3 0.7 copy-start.13
  62.9 1.1 %copy-start.5 = (f32[3,104,512]{2,1,0:T(8,128)S(1)}, f32[3,104,512]{2,1,0:T(8,128)}, u32[]{:S(2)}) copy-start(f32[3,104,512]{2,1,0:T(8,128)} %copy-done.3) | copy-start | bytes 1916932
  72.8 25.9 %copy-start.8 = (f32[8,4096]{1,0:T(8,128)S(1)}, f32[8,4096]{1,0:T(8,128)}, u32[]{:S(2)}) copy-start(f32[8,4096]{1,0:T(8,128)} %it_ref.1) | copy-start | bytes 393220

commit v7 on v6

--- a/solution.py
+++ b/solution.py
@@ -314,33 +314,21 @@
     return jnp.dot(total[:8] + total[8:], transfer_ref[...], precision=EXACT, preferred_element_type=F32)
 
 
-def outside_body(pairs_ref, sizes_ref, scale_ref, left_ref, mid_ref, right_ref, up_ref, down_ref, inside_ref, out_ref, src, tgt, wgt, z, high, low):
+def outside_body(pairs_ref, sizes_ref, far_ref, scale_ref, left_ref, mid_ref, right_ref, up_ref, down_ref, inside_ref, out_ref, far_out_ref, src, tgt, wgt, coef, far_src, far_wgt, z, high, low):
     leaf_dev, rhs, leaf_pts = out_ref.shape
+    rank = coef.shape[2]
     scale = scale_rows(scale_ref, (8, leaf_pts))
     idle = 9 * leaf_dev
     src[idle] = jnp.zeros(src.shape[1:], BF16)
     wgt[idle] = jnp.zeros(wgt.shape[1:], BF16)
     for k in range(3):
-        prepare(up_ref.at[k], scale, k * leaf_dev, src, wgt)
-        prepare(down_ref.at[k], scale, (6 + k) * leaf_dev, src, wgt)
-    prepare(left_ref, scale, 3 * leaf_dev, src, wgt)
-    prepare(mid_ref, scale, 4 * leaf_dev, src, wgt, tgt)
-    prepare(right_ref, scale, 5 * leaf_dev, src, wgt)
+        prepare(up_ref.at[k], scale, k * leaf_dev, src, wgt, None, coef)
+        prepare(down_ref.at[k], scale, (6 + k) * leaf_dev, src, wgt, None, coef)
+    prepare(left_ref, scale, 3 * leaf_dev, src, wgt, None, coef)
+    prepare(mid_ref, scale, 4 * leaf_dev, src, wgt, tgt, coef)
+    prepare(right_ref, scale, 5 * leaf_dev, src, wgt, None, coef)
     out_ref[...] = inside_ref[...]
     near_pairs(pairs_ref, sizes_ref[1], 0, src, tgt, wgt, out_ref, z, high, low)
-
-
-def tail_body(tm_size, far_ref, place_ref, scale_ref, noise_ref, left_ref, mid_ref, right_ref, up_ref, down_ref, near_ref, node_ref, own_ref, transfer_ref, bases_ref, inv_ref, p_ref, res_ref, image_ref, sums_ref, src, tgt, coef, flat, far_src, far_wgt, node_src, node_wgt):
-    leaf_dev, rank, leaf_pts = bases_ref.shape
-    scale = scale_rows(scale_ref, (8, 4 * 128))
-    pushed = node_field(tm_size, place_ref, scale, node_ref, own_ref, transfer_ref, node_src, node_wgt)
-    brief = scale[:, :128]
-    for k in range(3):
-        prepare(up_ref.at[k], brief, k * leaf_dev, src, None, None, coef)
-        prepare(down_ref.at[k], brief, (6 + k) * leaf_dev, src, None, None, coef)
-    prepare(left_ref, brief, 3 * leaf_dev, src, None, None, coef)
-    prepare(mid_ref, brief, 4 * leaf_dev, src, None, tgt, coef)
-    prepare(right_ref, brief, 5 * leaf_dev, src, None, None, coef)
     for leaf in range(leaf_dev):
         for j in range(far_ref.shape[1]):
             w = far_ref[leaf, j]
@@ -350,7 +338,15 @@
     for leaf in range(leaf_dev):
         k_high, k_low = split(kernel_of(contract(tgt[leaf, :, 0:rank], far_src[leaf], ((0,), (0,)))))
         far = contract(far_wgt[leaf], k_high, ((1,), (1,))) + contract(far_wgt[leaf], k_low, ((1,), (1,)))
-        incoming = halves(far[:8] + far[8:] + pushed[:, leaf * rank : (leaf + 1) * rank])
+        far_out_ref[leaf] = far[:8] + far[8:]
+
+
+def tail_body(tm_size, place_ref, scale_ref, noise_ref, near_ref, far_ref, node_ref, own_ref, transfer_ref, bases_ref, inv_ref, p_ref, res_ref, image_ref, sums_ref, flat, node_src, node_wgt):
+    leaf_dev, rank, leaf_pts = bases_ref.shape
+    scale = scale_rows(scale_ref, (8, 4 * 128))
+    pushed = node_field(tm_size, place_ref, scale, node_ref, own_ref, transfer_ref, node_src, node_wgt)
+    for leaf in range(leaf_dev):
+        incoming = halves(far_ref[leaf] + pushed[:, leaf * rank : (leaf + 1) * rank])
         base_high, base_low = split(bases_ref[leaf])
         got = jnp.dot(incoming, base_high, preferred_element_type=F32)
         got = got + jnp.dot(incoming, base_low, preferred_element_type=F32)
@@ -470,34 +466,35 @@
     down = shifted(row, "leaf", -1)
     place = jnp.stack([lax.axis_index("leaf"), lax.axis_index("tm")]).astype(jnp.int32)
 
-    near = pl.pallas_call(
+    near, far = pl.pallas_call(
         outside_body,
-        in_specs=[SMEM] * 3 + [VMEM] * 6,
-        out_specs=VMEM,
-        out_shape=shape((leaf_dev, rhs, leaf_pts), F32),
-        scratch_shapes=pipeline(9 * leaf_dev) + buffers,
+        in_specs=[SMEM] * 4 + [VMEM] * 6,
+        out_specs=[VMEM] * 2,
+        out_shape=[shape((leaf_dev, rhs, leaf_pts), F32), shape((leaf_dev, rhs, rank), F32)],
+        scratch_shapes=pipeline(9 * leaf_dev)
+        + [
+            pltpu.VMEM((9 * leaf_dev, 16, rank), BF16),
+            pltpu.VMEM((leaf_dev, 32, far_list.shape[1] * rank), BF16),
+            pltpu.VMEM((leaf_dev, 16, far_list.shape[1] * rank), BF16),
+        ]
+        + buffers,
         compiler_params=params(14),
         cost_estimate=pl.CostEstimate(flops=3 * 10**10, bytes_accessed=2**21, transcendentals=3 * 10**7),
         name="outside",
-    )(pairs, sizes, inv_scale, left, halo, right, up, down, inside)
+    )(pairs, sizes, far_list, inv_scale, left, halo, right, up, down, inside)
     image, sums = pl.pallas_call(
         functools.partial(tail_body, lax.axis_size("tm")),
-        in_specs=[SMEM] * 4 + [VMEM] * 13,
+        in_specs=[SMEM] * 3 + [VMEM] * 9,
         out_specs=[VMEM] * 2,
         out_shape=[shape((rhs, points), F32), shape((devices, 128), F32)],
         scratch_shapes=[
-            pltpu.VMEM((9 * leaf_dev, 32, 128), BF16),
-            pltpu.VMEM((leaf_dev, 32, 128), BF16),
-            pltpu.VMEM((9 * leaf_dev, 16, rank), BF16),
             pltpu.VMEM((rhs, points), F32),
-            pltpu.VMEM((leaf_dev, 32, far_list.shape[1] * rank), BF16),
-            pltpu.VMEM((leaf_dev, 16, far_list.shape[1] * rank), BF16),
             pltpu.VMEM((32, devices * rank), BF16),
             pltpu.VMEM((16, devices * rank), BF16),
         ],
-        compiler_params=params(14),
+        compiler_params=params(10),
         name="tail",
-    )(far_list, place, inv_scale, noise, left, halo, right, up, down, near, nodes, own, transfer[0], bases, inverse, direction, residual)
+    )(place, inv_scale, noise, near, far, nodes, own, transfer[0], bases, inverse, direction, residual)
     all_sums = lax.all_to_all(sums, axes, 0, 0, tiled=True)
     return pl.pallas_call(
         update_body,

time: 100 us -> 99.3 us (level)
  Pallas kernels: 44.5 us -> 48.2 us
  blocking collectives: 25.9 us -> 22.2 us
    pallas_call x1, Pallas kernels: 21.1 us -> 27.3 us  [shards(): pl.pallas_call(outside_body, in_specs=[SMEM] * 4 + [VMEM] * 6, out_specs=...]
    all_to_all x1, blocking collectives: 25.9 us -> 22.2 us  [shards(): all_sums = lax.all_to_all(sums, axes, 0, 0, tiled=True)]
    pallas_call x1, Pallas kernels: 8.77 us -> 6.17 us  [shards(): pl.pallas_call(functools.partial(tail_body, lax.axis_size('tm')), in_spec...]
    unnamed x34 -> x32, local copies, waits for them, and re-layouts: 4.33 us -> 4.17 us
  transfers between devices with their start and end apart: 5 -> 5, of which waited for: 0 -> 0; matrix products, arithmetic and copies ran while one was open for 0% -> 0% of each run, Pallas kernels for 30% -> 36%
where the time goes in v7:
time: 99.3 us
  Pallas kernels  48.2 us (49%)
  starting transfers between devices  22.8 us (23%)
  blocking collectives  22.2 us (22%)
  local copies, waits for them, and re-layouts  4.17 us (4%)
    pallas_call x1, Pallas kernels, shards(): pl.pallas_call(outside_body, in_specs=[SMEM] * 4 + [VMEM] * 6, out_specs=...  27.3 us
    all_to_all x1, blocking collectives, shards(): all_sums = lax.all_to_all(sums, axes, 0, 0, tiled=True)  22.2 us
    all_to_all x1, starting transfers between devices, shards(): nodes = lax.all_to_all(node, axes, 0, 0)  11.6 us
    ppermute x4, starting transfers between devices, shifted(): lax.ppermute(x, axis, [(i, i + by) for i in range(n) if 0 <= i + by < n])  11.1 us
    pallas_call x1, Pallas kernels, shards(): pl.pallas_call(inside_body, in_specs=[SMEM] * 3 + [ANY] + [VMEM] * 3, out...  8.72 us
    pallas_call x1, Pallas kernels, shards(): pl.pallas_call(functools.partial(tail_body, lax.axis_size('tm')), in_spec...  6.17 us
    pallas_call x1, Pallas kernels, shards(): pl.pallas_call(gather_body, in_specs=[ANY] * 4, out_specs=VMEM, out_shape...  5.25 us
    unnamed x32, local copies, waits for them, and re-layouts  4.17 us
  transfers between devices with their start and end apart: 5, of which 0 were waited for; matrix products, arithmetic and copies ran while one was open for 0% of the time, Pallas kernels for 36%

profile of v7, /device:TPU:1, one launch (start us, length us, event | category | flops | bytes accessed | tf_op | source)
XLA Modules:
  0.0 99.3 jit_solution(17961643338421812626)
XLA Ops:
  0.6 5.2 %gather.1.halo_hbm.mid_ref = f32[104,512]{1,0:T(8,128)} custom-call(s32[32,128]{1,0:T(8,128)} %bitcast.18, f32[4,4096]{1,0:T(4,128)} %x_hbm.1, f32[8,4096]{1,0:T(8,128)} %p_ref.3, f32[8,64,512]{2,1,0:T(8,128)} %bases_ref.1), custom_call_target="tpu_custom_call" | custom-call | tf_op jit(solution)/shard_map/gather/pallas_call | solution.py:407
  5.9 4.0 %collective-permute-start = (f32[104,512]{1,0:T(8,128)}, f32[104,512]{1,0:T(8,128)S(1)}, u32[]{:S(2)}, u32[]{:S(2)}) collective-permute-start(f32[104,512]{1,0:T(8,128)} %gather.1.halo_hbm.mid_ref), channel_id=1, source_target_pairs={{0,1},{1,2},{2,3},{4,5},{5,6},{6,7},{8,9},{9,10},{10,11},{12,13},{... | collective-permute-start | bytes 638984 | tf_op jit(solution)/shard_map/ppermute | solution.py:396
  9.8 1.3 %collective-permute-start.1 = (f32[104,512]{1,0:T(8,128)}, f32[104,512]{1,0:T(8,128)S(1)}, u32[]{:S(2)}, u32[]{:S(2)}) collective-permute-start(f32[104,512]{1,0:T(8,128)} %gather.1.halo_hbm.mid_ref), channel_id=1, source_target_pairs={{1,0},{2,1},{3,2},{5,4},{6,5},{7,6},{9,8},{10,9},{11,10},{13,12},{... | collective-permute-start | bytes 638984 | tf_op jit(solution)/shard_map/ppermute | solution.py:396
  11.1 0.0 copy-start.2
  11.2 8.7 %inside.1 = (f32[8,8,512]{2,1,0:T(8,128)}, f32[128,8,128]{2,1,0:T(8,128)}, f32[8,128]{1,0:T(8,128)}, s32[32,128]{1,0:T(8,128)}, s32[68]{0:T(128)}, /*index=5*/s32[2]{0:T(128)}) custom-call(s32[8,8]{1,0:T(8,128)} %near_ref.1, s32[8]{0:T(128)} %count_ref.1, f32[4]{0:T(128)} %scale_ref.5, f32[104,512]{1,0:T(8,128)} %gather.1.halo_hbm.mid_ref, ...), custom_call_target="tpu_custom_call" | custom-call | flops 10000000000 | bytes 2097152 | tf_op jit(solution)/shard_map/inside/pallas_call | solution.py:438
  19.9 0.0 collective-permute-done.left_ref
  19.9 0.0 collective-permute-done.1.right_ref
  19.9 0.0 copy-done.2
  19.9 0.9 pad_maximum_fusion
  20.8 4.0 %collective-permute-start.2 = (f32[3,104,512]{2,1,0:T(8,128)}, f32[3,104,512]{2,1,0:T(8,128)S(1)}, u32[]{:S(2)}, u32[]{:S(2)}) collective-permute-start(f32[3,104,512]{2,1,0:T(8,128)} %pad_maximum_fusion), channel_id=1, source_target_pairs={{0,4},{4,8},{8,12},{12,16},{16,20},{20,24},{24,28},{28,32},{32,36}... | collective-permute-start | bytes 1916936 | tf_op jit(solution)/shard_map/ppermute | solution.py:396
  24.8 1.9 %collective-permute-start.3 = (f32[3,104,512]{2,1,0:T(8,128)}, f32[3,104,512]{2,1,0:T(8,128)S(1)}, u32[]{:S(2)}, u32[]{:S(2)}) collective-permute-start(f32[3,104,512]{2,1,0:T(8,128)} %pad_maximum_fusion), channel_id=1, source_target_pairs={{4,0},{8,4},{12,8},{16,12},{20,16},{24,20},{28,24},{32,28},{36,32}... | collective-permute-start | bytes 1916936 | tf_op jit(solution)/shard_map/ppermute | solution.py:396
  26.8 0.1 pad_add_fusion.place_ref
  26.8 0.0 copy-start.12
  26.8 11.6 %all-to-all-start = ((f32[128,8,128]{2,1,0:T(8,128)}), f32[128,8,128]{2,1,0:T(8,128)S(1)}, u32[]{:S(2)}, u32[]{:S(2)}) async-start(f32[128,8,128]{2,1,0:T(8,128)} %get-tuple-element.25), calls=%async_computation | async-start | bytes 1048576 | tf_op jit(solution)/shard_map/all_to_all | solution.py:463
  38.5 0.0 collective-permute-done.2.up_ref
  38.5 0.0 collective-permute-done.3.down_ref
  38.5 0.0 copy-start.10
  38.5 0.9 copy-done.10
  39.4 0.0 copy-start.8
  39.4 0.0 copy-start.14
  39.4 0.0 copy-start.15
  39.4 0.0 copy-done.12
  39.4 0.6 copy-done.8
  40.0 0.0 copy-done.14
  40.0 0.0 copy-done.15
  40.1 0.0 copy-start.11
  40.1 1.1 %copy-done.11 = f32[3,104,512]{2,1,0:T(8,128)S(1)} copy-done((f32[3,104,512]{2,1,0:T(8,128)S(1)}, f32[3,104,512]{2,1,0:T(8,128)}, u32[]{:S(2)}) %copy-start.11) | copy-done | bytes 639000
  41.1 0.0 copy-start.13
  41.1 0.9 copy-done.13
  42.0 0.0 copy-start
  42.0 0.0 copy-start.1
  42.0 0.0 copy-start.3
  42.1 0.0 copy-start.6
  42.1 27.3 %outside.1 = (f32[8,8,512]{2,1,0:T(8,128)S(1)}, f32[8,8,64]{2,1,0:T(8,128)S(1)}) custom-call(s32[68]{0:T(128)S(1)} %copy-done.14, s32[2]{0:T(128)S(1)} %copy-done.15, s32[8,8]{1,0:T(8,128)S(1)} %copy-done.12, f32[4]{0:T(128)S(1)} %copy-done.8, f32[104,512]{1,0:T(8,128)S(1)} %collective-permute-done.left_ref, f32[104,512]{1,0:T(8,128)S(1)} %copy-done.2, ...), custom_call_target="tpu_custom_call" | custom-call | flops 30000001024 | bytes 2097152 | tf_op jit(solution)/shard_map/outside/pallas_call | solution.py:469
  69.3 0.0 all-to-all-done.node_ref
  69.3 0.0 copy-start.9
  69.4 0.0 copy-done
  69.4 0.0 copy-done.1
  69.4 0.0 copy-done.3
  69.4 0.0 copy-done.4
  69.4 0.0 copy-done.6
  69.4 0.6 copy-done.7
  70.0 0.0 copy-done.9
  70.0 6.2 %tail.1 = (f32[8,4096]{1,0:T(8,128)S(1)}, f32[128,128]{1,0:T(8,128)S(1)}) custom-call(s32[2]{0:T(128)S(1)} %pad_add_fusion.place_ref, f32[4]{0:T(128)S(1)} %copy-done.8, f32[8]{0:T(128)S(1)} %copy-done.9, f32[8,8,512]{2,1,0:T(8,128)S(1)} %get-tuple-element.23.near_ref, f32[8,8,64]{2,1,0:T(8,128)S(1)} %get-tuple-element.24.far_ref, ...), custom_call_target="tpu_custom_call" | custom-call | tf_op jit(solution)/shard_map/tail/pallas_call | solution.py:485
  76.2 0.0 copy-start.5
  76.2 22.2 %all_to_all.16 = f32[128,1,128]{2,1,0:T(1,128)S(1)} all-to-all(f32[128,1,128]{2,1,0:T(1,128)S(1)} %bitcast.17), channel_id=1, replica_groups=mesh['leaf'=32,'tm'=4] {'leaf','tm'}, dimensions={0} | all-to-all | bytes 131072 | tf_op jit(solution)/shard_map/all_to_all | solution.py:498
  98.4 0.0 copy-done.5
  98.5 0.8 update.1
  (2 shorter events, 0.0 us)
Async XLA Ops:
  5.9 14.0 %collective-permute-start = (f32[104,512]{1,0:T(8,128)}, f32[104,512]{1,0:T(8,128)S(1)}, u32[]{:S(2)}, u32[]{:S(2)}) collective-permute-start(f32[104,512]{1,0:T(8,128)} %gather.1.halo_hbm.mid_ref), channel_id=1, source_target_pairs={{0,1},{1,2},{2,3},{4,5},{5,6},{6,7},{8,9},{9,10},{10,11},{12,13},{... | collective-permute-start | bytes 638984 | tf_op jit(solution)/shard_map/ppermute | solution.py:396
  9.8 10.1 %collective-permute-start.1 = (f32[104,512]{1,0:T(8,128)}, f32[104,512]{1,0:T(8,128)S(1)}, u32[]{:S(2)}, u32[]{:S(2)}) collective-permute-start(f32[104,512]{1,0:T(8,128)} %gather.1.halo_hbm.mid_ref), channel_id=1, source_target_pairs={{1,0},{2,1},{3,2},{5,4},{6,5},{7,6},{9,8},{10,9},{11,10},{13,12},{... | collective-permute-start | bytes 638984 | tf_op jit(solution)/shard_map/ppermute | solution.py:396
  11.1 8.8 %copy-start.2 = (f32[104,512]{1,0:T(8,128)S(1)}, f32[104,512]{1,0:T(8,128)}, u32[]{:S(2)}) copy-start(f32[104,512]{1,0:T(8,128)} %gather.1.halo_hbm.mid_ref) | copy-start | bytes 638980
  20.8 17.6 %collective-permute-start.2 = (f32[3,104,512]{2,1,0:T(8,128)}, f32[3,104,512]{2,1,0:T(8,128)S(1)}, u32[]{:S(2)}, u32[]{:S(2)}) collective-permute-start(f32[3,104,512]{2,1,0:T(8,128)} %pad_maximum_fusion), channel_id=1, source_target_pairs={{0,4},{4,8},{8,12},{12,16},{16,20},{20,24},{24,28},{28,32},{32,36}... | collective-permute-start | bytes 1916936 | tf_op jit(solution)/shard_map/ppermute | solution.py:396
  24.8 13.7 %collective-permute-start.3 = (f32[3,104,512]{2,1,0:T(8,128)}, f32[3,104,512]{2,1,0:T(8,128)S(1)}, u32[]{:S(2)}, u32[]{:S(2)}) collective-permute-start(f32[3,104,512]{2,1,0:T(8,128)} %pad_maximum_fusion), channel_id=1, source_target_pairs={{4,0},{8,4},{12,8},{16,12},{20,16},{24,20},{28,24},{32,28},{36,32}... | collective-permute-start | bytes 1916936 | tf_op jit(solution)/shard_map/ppermute | solution.py:396
  26.8 12.5 %copy-start.12 = (s32[8,8]{1,0:T(8,128)S(1)}, s32[8,8]{1,0:T(8,128)}, u32[]{:S(2)}) copy-start(s32[8,8]{1,0:T(8,128)} %far_ref.1) | copy-start | bytes 772
  26.8 42.5 %all-to-all-start = ((f32[128,8,128]{2,1,0:T(8,128)}), f32[128,8,128]{2,1,0:T(8,128)S(1)}, u32[]{:S(2)}, u32[]{:S(2)}) async-start(f32[128,8,128]{2,1,0:T(8,128)} %get-tuple-element.25), calls=%async_computation | async-start | bytes 1048576 | tf_op jit(solution)/shard_map/all_to_all | solution.py:463
  38.5 0.9 copy-start.10
  39.4 0.7 copy-start.8
  39.4 0.7 copy-start.14
  39.4 0.7 copy-start.15
  40.1 1.1 %copy-start.11 = (f32[3,104,512]{2,1,0:T(8,128)S(1)}, f32[3,104,512]{2,1,0:T(8,128)}, u32[]{:S(2)}) copy-start(f32[3,104,512]{2,1,0:T(8,128)} %copy-done.10) | copy-start | bytes 1916932
  41.1 0.9 copy-start.13
  42.0 27.3 %copy-start = (f32[8,64,512]{2,1,0:T(8,128)S(1)}, f32[8,64,512]{2,1,0:T(8,128)}, u32[]{:S(2)}) copy-start(f32[8,64,512]{2,1,0:T(8,128)} %bases_ref.1) | copy-start | bytes 3145732
  42.0 27.3 %copy-start.1 = (f32[8,4096]{1,0:T(8,128)S(1)}, f32[8,4096]{1,0:T(8,128)}, u32[]{:S(2)}) copy-start(f32[8,4096]{1,0:T(8,128)} %p_ref.3) | copy-start | bytes 393220
  42.0 27.3 %copy-start.3 = (f32[8,4096]{1,0:T(8,128)S(1)}, f32[8,4096]{1,0:T(8,128)}, u32[]{:S(2)}) copy-start(f32[8,4096]{1,0:T(8,128)} %res_ref.3) | copy-start | bytes 393220
  42.0 27.3 %copy-start.4 = (f32[1,64,512]{2,1,0:T(8,128)S(1)}, f32[1,64,512]{2,1,0:T(8,128)}, u32[]{:S(2)}) copy-start(f32[1,64,512]{2,1,0:T(8,128)} %param.19) | copy-start | bytes 393220
  42.1 27.4 %copy-start.6 = (s32[32,128]{1,0:T(8,128)S(1)}, s32[32,128]{1,0:T(8,128)}, u32[]{:S(2)}) copy-start(s32[32,128]{1,0:T(8,128)} %get-tuple-element.27.inv_ref) | copy-start | bytes 49156
  69.3 0.7 copy-start.7
  69.3 0.7 copy-start.9
  76.2 22.3 %copy-start.5 = (f32[8,4096]{1,0:T(8,128)S(1)}, f32[8,4096]{1,0:T(8,128)}, u32[]{:S(2)}) copy-start(f32[8,4096]{1,0:T(8,128)} %it_ref.1) | copy-start | bytes 393220

commit v8 on v7

--- a/solution.py
+++ b/solution.py
@@ -172,6 +172,13 @@
     inv_ref[...] = (64.0 * tally[0:chunks] + tally[chunks : 2 * chunks] + 0.5).astype(jnp.int32)
 
 
+def fetch(sources, targets, sems):
+    moves = [pltpu.make_async_copy(a, b, sems.at[i]) for i, (a, b) in enumerate(zip(sources, targets))]
+    for move in moves:
+        move.start()
+    return moves
+
+
 def scale_rows(scale_ref, shape):
     row = row_ids(shape) & 3
     picked = jnp.where(row == 0, scale_ref[0], jnp.where(row == 1, scale_ref[1], jnp.where(row == 2, scale_ref[2], scale_ref[3])))
@@ -314,7 +321,12 @@
     return jnp.dot(total[:8] + total[8:], transfer_ref[...], precision=EXACT, preferred_element_type=F32)
 
 
-def outside_body(pairs_ref, sizes_ref, far_ref, scale_ref, left_ref, mid_ref, right_ref, up_ref, down_ref, inside_ref, out_ref, far_out_ref, src, tgt, wgt, coef, far_src, far_wgt, z, high, low):
+def outside_body(pairs_ref, sizes_ref, far_ref, scale_ref, left_hbm, mid_hbm, right_hbm, up_hbm, down_hbm, inside_hbm, out_ref, far_out_ref, row, up, down, src, tgt, wgt, coef, far_src, far_wgt, z, high, low, sems):
+    moves = fetch(
+        [left_hbm, mid_hbm, right_hbm, up_hbm, down_hbm, inside_hbm],
+        [row.at[0], row.at[1], row.at[2], up, down, out_ref],
+        sems,
+    )
     leaf_dev, rhs, leaf_pts = out_ref.shape
     rank = coef.shape[2]
     scale = scale_rows(scale_ref, (8, leaf_pts))
@@ -322,12 +334,15 @@
     src[idle] = jnp.zeros(src.shape[1:], BF16)
     wgt[idle] = jnp.zeros(wgt.shape[1:], BF16)
     for k in range(3):
-        prepare(up_ref.at[k], scale, k * leaf_dev, src, wgt, None, coef)
-        prepare(down_ref.at[k], scale, (6 + k) * leaf_dev, src, wgt, None, coef)
-    prepare(left_ref, scale, 3 * leaf_dev, src, wgt, None, coef)
-    prepare(mid_ref, scale, 4 * leaf_dev, src, wgt, tgt, coef)
-    prepare(right_ref, scale, 5 * leaf_dev, src, wgt, None, coef)
-    out_ref[...] = inside_ref[...]
+        moves[k].wait()
+        prepare(row.at[k], scale, (3 + k) * leaf_dev, src, wgt, tgt if k == 1 else None, coef)
+    moves[3].wait()
+    for k in range(3):
+        prepare(up.at[k], scale, k * leaf_dev, src, wgt, None, coef)
+    moves[4].wait()
+    for k in range(3):
+        prepare(down.at[k], scale, (6 + k) * leaf_dev, src, wgt, None, coef)
+    moves[5].wait()
     near_pairs(pairs_ref, sizes_ref[1], 0, src, tgt, wgt, out_ref, z, high, low)
     for leaf in range(leaf_dev):
         for j in range(far_ref.shape[1]):
@@ -341,10 +356,19 @@
         far_out_ref[leaf] = far[:8] + far[8:]
 
 
-def tail_body(tm_size, place_ref, scale_ref, noise_ref, near_ref, far_ref, node_ref, own_ref, transfer_ref, bases_ref, inv_ref, p_ref, res_ref, image_ref, sums_ref, flat, node_src, node_wgt):
+def tail_body(tm_size, place_ref, scale_ref, noise_ref, node_hbm, own_hbm, transfer_hbm, near_hbm, far_hbm, bases_hbm, inv_hbm, p_hbm, res_hbm, image_ref, sums_ref, node_ref, own_ref, transfer_ref, near_ref, far_ref, bases_ref, inv_ref, p_ref, res_ref, flat, node_src, node_wgt, sems):
     leaf_dev, rank, leaf_pts = bases_ref.shape
+    moves = fetch(
+        [node_hbm, own_hbm, transfer_hbm, near_hbm, far_hbm, bases_hbm, inv_hbm, p_hbm, res_hbm],
+        [node_ref, own_ref, transfer_ref, near_ref, far_ref, bases_ref, inv_ref, p_ref, res_ref],
+        sems,
+    )
     scale = scale_rows(scale_ref, (8, 4 * 128))
+    for move in moves[:3]:
+        move.wait()
     pushed = node_field(tm_size, place_ref, scale, node_ref, own_ref, transfer_ref, node_src, node_wgt)
+    for move in moves[3:]:
+        move.wait()
     for leaf in range(leaf_dev):
         incoming = halves(far_ref[leaf] + pushed[:, leaf * rank : (leaf + 1) * rank])
         base_high, base_low = split(bases_ref[leaf])
@@ -468,40 +492,52 @@
 
     near, far = pl.pallas_call(
         outside_body,
-        in_specs=[SMEM] * 4 + [VMEM] * 6,
+        in_specs=[SMEM] * 4 + [ANY] * 6,
         out_specs=[VMEM] * 2,
         out_shape=[shape((leaf_dev, rhs, leaf_pts), F32), shape((leaf_dev, rhs, rank), F32)],
-        scratch_shapes=pipeline(9 * leaf_dev)
+        scratch_shapes=[pltpu.VMEM(row.shape, F32)] * 3
+        + pipeline(9 * leaf_dev)
         + [
             pltpu.VMEM((9 * leaf_dev, 16, rank), BF16),
             pltpu.VMEM((leaf_dev, 32, far_list.shape[1] * rank), BF16),
             pltpu.VMEM((leaf_dev, 16, far_list.shape[1] * rank), BF16),
         ]
-        + buffers,
-        compiler_params=params(14),
+        + buffers
+        + [pltpu.SemaphoreType.DMA((6,))],
+        compiler_params=params(58),
         cost_estimate=pl.CostEstimate(flops=3 * 10**10, bytes_accessed=2**21, transcendentals=3 * 10**7),
         name="outside",
     )(pairs, sizes, far_list, inv_scale, left, halo, right, up, down, inside)
     image, sums = pl.pallas_call(
         functools.partial(tail_body, lax.axis_size("tm")),
-        in_specs=[SMEM] * 3 + [VMEM] * 9,
+        in_specs=[SMEM] * 3 + [ANY] * 9,
         out_specs=[VMEM] * 2,
         out_shape=[shape((rhs, points), F32), shape((devices, 128), F32)],
         scratch_shapes=[
+            pltpu.VMEM((devices, 8, 128), F32),
+            pltpu.VMEM((8, 128), F32),
+            pltpu.VMEM(transfer.shape[1:], F32),
+            pltpu.VMEM((leaf_dev, rhs, leaf_pts), F32),
+            pltpu.VMEM((leaf_dev, rhs, rank), F32),
+            pltpu.VMEM(bases.shape, F32),
+            pltpu.VMEM((chunks, 128), jnp.int32),
+            pltpu.VMEM((rhs, points), F32),
+            pltpu.VMEM((rhs, points), F32),
             pltpu.VMEM((rhs, points), F32),
             pltpu.VMEM((32, devices * rank), BF16),
             pltpu.VMEM((16, devices * rank), BF16),
+            pltpu.SemaphoreType.DMA((9,)),
         ],
-        compiler_params=params(10),
+        compiler_params=params(58),
         name="tail",
-    )(place, inv_scale, noise, near, far, nodes, own, transfer[0], bases, inverse, direction, residual)
+    )(place, inv_scale, noise, nodes, own, transfer[0], near, far, bases, inverse, direction, residual)
     all_sums = lax.all_to_all(sums, axes, 0, 0, tiled=True)
     return pl.pallas_call(
         update_body,
         in_specs=[VMEM] * 5,
         out_specs=[VMEM] * 2,
         out_shape=[shape((rhs, points), F32)] * 2,
-        compiler_params=params(8),
+        compiler_params=params(58),
         name="update",
     )(all_sums, iterate, direction, residual, image)
 

time: 99.3 us -> 102 us (1.027)
  Pallas kernels: 48.2 us -> 52.1 us
  local copies, waits for them, and re-layouts: 4.17 us -> 2.51 us
    pallas_call x1, Pallas kernels: 6.17 us -> 8.09 us  [shards(): pl.pallas_call(functools.partial(tail_body, lax.axis_size('tm')), in_spec...]
    unnamed x32 -> x12, local copies, waits for them, and re-layouts: 4.17 us -> 2.51 us
    pallas_call x1, Pallas kernels: 0.82 us -> 1.94 us  [shards(): pl.pallas_call(update_body, in_specs=[VMEM] * 5, out_specs=[VMEM] * 2, ou...]
  transfers between devices with their start and end apart: 5 -> 5, of which waited for: 0 -> 0; matrix products, arithmetic and copies ran while one was open for 0% -> 1% of each run, Pallas kernels for 36% -> 36%
where the time goes in v8:
time: 102 us
  Pallas kernels  52.1 us (51%)
  starting transfers between devices  23 us (23%)
  blocking collectives  22.8 us (22%)
  local copies, waits for them, and re-layouts  2.51 us (2%)
    pallas_call x1, Pallas kernels, shards(): pl.pallas_call(outside_body, in_specs=[SMEM] * 4 + [ANY] * 6, out_specs=[...  28.1 us
    all_to_all x1, blocking collectives, shards(): all_sums = lax.all_to_all(sums, axes, 0, 0, tiled=True)  22.8 us
    all_to_all x1, starting transfers between devices, shards(): nodes = lax.all_to_all(node, axes, 0, 0)  11.8 us
    ppermute x4, starting transfers between devices, shifted(): lax.ppermute(x, axis, [(i, i + by) for i in range(n) if 0 <= i + by < n])  11.2 us
    pallas_call x1, Pallas kernels, shards(): pl.pallas_call(inside_body, in_specs=[SMEM] * 3 + [ANY] + [VMEM] * 3, out...  8.67 us
    pallas_call x1, Pallas kernels, shards(): pl.pallas_call(functools.partial(tail_body, lax.axis_size('tm')), in_spec...  8.09 us
    pallas_call x1, Pallas kernels, shards(): pl.pallas_call(gather_body, in_specs=[ANY] * 4, out_specs=VMEM, out_shape...  5.26 us
    unnamed x12, local copies, waits for them, and re-layouts  2.51 us
  transfers between devices with their start and end apart: 5, of which 0 were waited for; matrix products, arithmetic and copies ran while one was open for 1% of the time, Pallas kernels for 36%

profile of v8, /device:TPU:1, one launch (start us, length us, event | category | flops | bytes accessed | tf_op | source)
XLA Modules:
  0.0 101.9 jit_solution(5754027418776870071)
XLA Ops:
  0.6 5.3 %gather.1.halo_hbm.mid_hbm = f32[104,512]{1,0:T(8,128)} custom-call(s32[32,128]{1,0:T(8,128)} %bitcast.18, f32[4,4096]{1,0:T(4,128)} %x_hbm.1, f32[8,4096]{1,0:T(8,128)} %p_ref.1, f32[8,64,512]{2,1,0:T(8,128)} %bases_hbm.3), custom_call_target="tpu_custom_call" | custom-call | tf_op jit(solution)/shard_map/gather/pallas_call | solution.py:431
  5.9 4.0 %collective-permute-start = (f32[104,512]{1,0:T(8,128)}, f32[104,512]{1,0:T(8,128)S(1)}, u32[]{:S(2)}, u32[]{:S(2)}) collective-permute-start(f32[104,512]{1,0:T(8,128)} %gather.1.halo_hbm.mid_hbm), channel_id=1, source_target_pairs={{0,1},{1,2},{2,3},{4,5},{5,6},{6,7},{8,9},{9,10},{10,11},{12,13},{... | collective-permute-start | bytes 638984 | tf_op jit(solution)/shard_map/ppermute | solution.py:420
  9.9 1.3 %collective-permute-start.1 = (f32[104,512]{1,0:T(8,128)}, f32[104,512]{1,0:T(8,128)S(1)}, u32[]{:S(2)}, u32[]{:S(2)}) collective-permute-start(f32[104,512]{1,0:T(8,128)} %gather.1.halo_hbm.mid_hbm), channel_id=1, source_target_pairs={{1,0},{2,1},{3,2},{5,4},{6,5},{7,6},{9,8},{10,9},{11,10},{13,12},{... | collective-permute-start | bytes 638984 | tf_op jit(solution)/shard_map/ppermute | solution.py:420
  11.2 0.0 copy-start.1
  11.2 8.7 %inside.1 = (f32[8,8,512]{2,1,0:T(8,128)}, f32[128,8,128]{2,1,0:T(8,128)}, f32[8,128]{1,0:T(8,128)}, s32[32,128]{1,0:T(8,128)}, s32[68]{0:T(128)}, /*index=5*/s32[2]{0:T(128)}) custom-call(s32[8,8]{1,0:T(8,128)} %near_ref.1, s32[8]{0:T(128)} %count_ref.1, f32[4]{0:T(128)} %scale_ref.5, f32[104,512]{1,0:T(8,128)} %gather.1.halo_hbm.mid_hbm, ...), custom_call_target="tpu_custom_call" | custom-call | flops 10000000000 | bytes 2097152 | tf_op jit(solution)/shard_map/inside/pallas_call | solution.py:462
  19.9 0.0 collective-permute-done.left_hbm
  19.9 0.0 copy-start.2
  19.9 0.0 collective-permute-done.1.right_hbm
  19.9 0.0 copy-start.3
  19.9 0.0 copy-done.1
  20.0 0.6 copy-done.2
  20.5 0.1 copy-done.3
  20.6 4.0 %collective-permute-start.2 = (f32[3,104,512]{2,1,0:T(8,128)S(1)}, f32[3,104,512]{2,1,0:T(8,128)S(1)}, u32[]{:S(2)}, u32[]{:S(2)}) collective-permute-start(f32[3,104,512]{2,1,0:T(8,128)S(1)} %pad_maximum_fusion), channel_id=1, source_target_pairs={{0,4},{4,8},{8,12},{12,16},{16,20},{20,24},{24,28},{28,32},{32,36}... | collective-permute-start | bytes 1916936 | tf_op jit(solution)/shard_map/ppermute | solution.py:420
  24.6 1.9 %collective-permute-start.3 = (f32[3,104,512]{2,1,0:T(8,128)S(1)}, f32[3,104,512]{2,1,0:T(8,128)S(1)}, u32[]{:S(2)}, u32[]{:S(2)}) collective-permute-start(f32[3,104,512]{2,1,0:T(8,128)S(1)} %pad_maximum_fusion), channel_id=1, source_target_pairs={{4,0},{8,4},{12,8},{16,12},{20,16},{24,20},{28,24},{32,28},{36,32}... | collective-permute-start | bytes 1916936 | tf_op jit(solution)/shard_map/ppermute | solution.py:420
  26.6 0.7 pad_add_fusion.place_ref
  27.2 11.8 %all-to-all-start = ((f32[128,8,128]{2,1,0:T(8,128)}), f32[128,8,128]{2,1,0:T(8,128)S(1)}, u32[]{:S(2)}, u32[]{:S(2)}) async-start(f32[128,8,128]{2,1,0:T(8,128)} %get-tuple-element.18), calls=%async_computation | async-start | bytes 1048576 | tf_op jit(solution)/shard_map/all_to_all | solution.py:487
  39.1 0.0 collective-permute-done.2.up_hbm
  39.1 0.0 copy-start.4
  39.1 0.0 collective-permute-done.3.down_hbm
  39.1 0.0 copy-start.5
  39.1 0.8 copy-done.4
  39.9 0.2 copy-done.5
  40.1 28.1 %outside.1 = (f32[8,8,512]{2,1,0:T(8,128)}, f32[8,8,64]{2,1,0:T(8,128)}) custom-call(s32[68]{0:T(128)} %get-tuple-element.20.pairs_ref, s32[2]{0:T(128)} %get-tuple-element.21.sizes_ref, s32[8,8]{1,0:T(8,128)} %far_ref.1, f32[4]{0:T(128)} %scale_ref.5, f32[104,512]{1,0:T(8,128)} %copy-done.2, f32[104,512]{1,0:T(8,128)} %gather.1.halo_hbm.mid_hbm, ...), custom_call_target="tpu_custom_call" | custom-call | flops 30000001024 | bytes 2097152 | tf_op jit(solution)/shard_map/outside/pallas_call | solution.py:493
  68.3 0.0 all-to-all-done.node_hbm
  68.3 0.0 copy-start
  68.3 0.8 copy-done
  69.1 8.1 %tail.1 = (f32[8,4096]{1,0:T(8,128)}, f32[128,128]{1,0:T(8,128)}) custom-call(s32[2]{0:T(128)} %pad_add_fusion.place_ref, f32[4]{0:T(128)} %scale_ref.5, f32[8]{0:T(128)} %noise_ref.1, f32[128,8,128]{2,1,0:T(8,128)} %copy-done, f32[8,128]{1,0:T(8,128)} %get-tuple-element.19.own_hbm, f32[64,512]{1,0:T(8,128)} %bitcast.16, ...), custom_call_target="tpu_custom_call" | custom-call | tf_op jit(solution)/shard_map/tail/pallas_call | solution.py:511
  77.2 22.8 %all_to_all.16 = f32[128,1,128]{2,1,0:T(1,128)} all-to-all(f32[128,1,128]{2,1,0:T(1,128)} %bitcast.17), channel_id=1, replica_groups=mesh['leaf'=32,'tm'=4] {'leaf','tm'}, dimensions={0} | all-to-all | bytes 131072 | tf_op jit(solution)/shard_map/all_to_all | solution.py:534
  100.0 1.9 %update.1 = (f32[8,4096]{1,0:T(8,128)}, f32[8,4096]{1,0:T(8,128)}) custom-call(f32[128,128]{1,0:T(8,128)} %bitcast.12, f32[8,4096]{1,0:T(8,128)} %it_ref.1, f32[8,4096]{1,0:T(8,128)} %p_ref.1, f32[8,4096]{1,0:T(8,128)} %res_ref.1, f32[8,4096]{1,0:T(8,128)} %get-tuple-element.29.image_ref), custom_call_target="tpu_custom_call" | custom-call | tf_op jit(solution)/shard_map/update/pallas_call | solution.py:535
  (1 shorter events, 0.0 us)
Async XLA Ops:
  5.9 14.0 %collective-permute-start = (f32[104,512]{1,0:T(8,128)}, f32[104,512]{1,0:T(8,128)S(1)}, u32[]{:S(2)}, u32[]{:S(2)}) collective-permute-start(f32[104,512]{1,0:T(8,128)} %gather.1.halo_hbm.mid_hbm), channel_id=1, source_target_pairs={{0,1},{1,2},{2,3},{4,5},{5,6},{6,7},{8,9},{9,10},{10,11},{12,13},{... | collective-permute-start | bytes 638984 | tf_op jit(solution)/shard_map/ppermute | solution.py:420
  9.9 10.0 %collective-permute-start.1 = (f32[104,512]{1,0:T(8,128)}, f32[104,512]{1,0:T(8,128)S(1)}, u32[]{:S(2)}, u32[]{:S(2)}) collective-permute-start(f32[104,512]{1,0:T(8,128)} %gather.1.halo_hbm.mid_hbm), channel_id=1, source_target_pairs={{1,0},{2,1},{3,2},{5,4},{6,5},{7,6},{9,8},{10,9},{11,10},{13,12},{... | collective-permute-start | bytes 638984 | tf_op jit(solution)/shard_map/ppermute | solution.py:420
  11.2 8.7 %copy-start.1 = (f32[104,512]{1,0:T(8,128)S(1)}, f32[104,512]{1,0:T(8,128)}, u32[]{:S(2)}) copy-start(f32[104,512]{1,0:T(8,128)} %gather.1.halo_hbm.mid_hbm) | copy-start | bytes 638980
  19.9 0.7 copy-start.2
  19.9 0.7 copy-start.3
  20.6 18.4 %collective-permute-start.2 = (f32[3,104,512]{2,1,0:T(8,128)S(1)}, f32[3,104,512]{2,1,0:T(8,128)S(1)}, u32[]{:S(2)}, u32[]{:S(2)}) collective-permute-start(f32[3,104,512]{2,1,0:T(8,128)S(1)} %pad_maximum_fusion), channel_id=1, source_target_pairs={{0,4},{4,8},{8,12},{12,16},{16,20},{20,24},{24,28},{28,32},{32,36}... | collective-permute-start | bytes 1916936 | tf_op jit(solution)/shard_map/ppermute | solution.py:420
  24.6 14.4 %collective-permute-start.3 = (f32[3,104,512]{2,1,0:T(8,128)S(1)}, f32[3,104,512]{2,1,0:T(8,128)S(1)}, u32[]{:S(2)}, u32[]{:S(2)}) collective-permute-start(f32[3,104,512]{2,1,0:T(8,128)S(1)} %pad_maximum_fusion), channel_id=1, source_target_pairs={{4,0},{8,4},{12,8},{16,12},{20,16},{24,20},{28,24},{32,28},{36,32}... | collective-permute-start | bytes 1916936 | tf_op jit(solution)/shard_map/ppermute | solution.py:420
  27.2 41.1 %all-to-all-start = ((f32[128,8,128]{2,1,0:T(8,128)}), f32[128,8,128]{2,1,0:T(8,128)S(1)}, u32[]{:S(2)}, u32[]{:S(2)}) async-start(f32[128,8,128]{2,1,0:T(8,128)} %get-tuple-element.18), calls=%async_computation | async-start | bytes 1048576 | tf_op jit(solution)/shard_map/all_to_all | solution.py:487
  39.1 0.8 copy-start.4
  39.1 1.1 %copy-start.5 = (f32[3,104,512]{2,1,0:T(8,128)}, f32[3,104,512]{2,1,0:T(8,128)S(1)}, u32[]{:S(2)}) copy-start(f32[3,104,512]{2,1,0:T(8,128)S(1)} %collective-permute-done.3.down_hbm) | copy-start | bytes 1916932
  68.3 0.8 copy-start

commit v9 on v7

--- a/solution.py
+++ b/solution.py
@@ -96,7 +96,13 @@
     return picked
 
 
-def gather_body(order_hbm, x_hbm, p_hbm, bases_hbm, halo_ref, order_ref, xx, p_ref, bases_ref, sems):
+def scale_rows(scale_ref, shape):
+    row = row_ids(shape) & 3
+    picked = jnp.where(row == 0, scale_ref[0], jnp.where(row == 1, scale_ref[1], jnp.where(row == 2, scale_ref[2], scale_ref[3])))
+    return picked * UNIT
+
+
+def gather_body(scale_ref, order_hbm, x_hbm, p_hbm, bases_hbm, halo_ref, order_ref, xx, p_ref, bases_ref, sems):
     leaf_dev, rank, leaf_pts = bases_ref.shape
     points = p_ref.shape[1]
     chunks = points // 128
@@ -117,6 +123,7 @@
         move.start()
     for move in moves[:4]:
         move.wait()
+    scale = scale_rows(scale_ref, (8, 128))
 
     def loads(ref):
         return [lambda s=s: ref[:, s * 128 : (s + 1) * 128] for s in range(chunks)]
@@ -128,7 +135,7 @@
             for j in range(per_leaf):
                 ids = order_ref[pl.ds(leaf * per_leaf + j, 1), :]
                 got_x, got_p = gather_lanes([loads(xx), loads(p_ref)], jnp.broadcast_to(ids, (8, 128)))
-                kept.append(got_x)
+                kept.append(got_x * scale)
                 halo_ref[pl.ds(pl.multiple_of(32 + leaf * 8, 8), 8), j * 128 : (j + 1) * 128] = got_p
         for j in range(per_leaf):
             both = jnp.where(row_ids((8, 128)) < 4, kept[j], kept[per_leaf + j])
@@ -172,28 +179,20 @@
     inv_ref[...] = (64.0 * tally[0:chunks] + tally[chunks : 2 * chunks] + 0.5).astype(jnp.int32)
 
 
-def scale_rows(scale_ref, shape):
-    row = row_ids(shape) & 3
-    picked = jnp.where(row == 0, scale_ref[0], jnp.where(row == 1, scale_ref[1], jnp.where(row == 2, scale_ref[2], scale_ref[3])))
-    return picked * UNIT
-
-
-def prepare(ref, scale, base, src, wgt=None, tgt=None, coef=None):
+def prepare(ref, base, src, wgt, tgt=None, coef=None):
     leaf_dev = ref.shape[0] // 13
-    width = scale.shape[1]
-    row = row_ids(scale.shape)
+    row = row_ids((8, ref.shape[1]))
     for g in range(leaf_dev // 2):
-        both = ref[g * 8 : g * 8 + 8, 0:width] * scale
+        both = ref[g * 8 : g * 8 + 8, :]
         turned = pltpu.roll(both, 4, 0)
         for h in range(2):
             leaf = 2 * g + h
             xx = jnp.where(row < 4, both, turned) if h == 0 else jnp.where(row < 4, turned, both)
             made = features(xx, True, tgt is not None)
-            src[base + leaf, :, 0:width] = made[0]
+            src[base + leaf] = made[0]
             if tgt is not None:
-                tgt[leaf, :, 0:width] = made[1]
-            if wgt is not None:
-                wgt[base + leaf] = halves(ref[32 + leaf * 8 : 40 + leaf * 8, :] * FACTOR)
+                tgt[leaf] = made[1]
+            wgt[base + leaf] = halves(ref[32 + leaf * 8 : 40 + leaf * 8, :] * FACTOR)
             if coef is not None:
                 rank = coef.shape[2]
                 coef[base + leaf] = halves(ref[96:104, leaf * rank : (leaf + 1) * rank] * FACTOR)
@@ -262,7 +261,7 @@
     lax.fori_loop(0, (n + 1) // 2, two_pairs, 0)
 
 
-def inside_body(near_ref, count_ref, scale_ref, halo_hbm, order_ref, transfer_ref, skel_ref, out_ref, node_ref, own_ref, inv_ref, pairs_ref, sizes_ref, pairs, halo_ref, slot, src, tgt, wgt, z, high, low, sem):
+def inside_body(near_ref, count_ref, halo_hbm, order_ref, transfer_ref, skel_ref, out_ref, node_ref, own_ref, inv_ref, pairs_ref, sizes_ref, pairs, halo_ref, slot, src, tgt, wgt, z, high, low, sem):
     leaf_dev, rhs, leaf_pts = out_ref.shape
     move = pltpu.make_async_copy(halo_hbm, halo_ref, sem)
     move.start()
@@ -274,11 +273,11 @@
     out_ref[...] = jnp.zeros_like(out_ref)
     move.wait()
     node_work(order_ref, halo_ref, transfer_ref, skel_ref, node_ref, own_ref, inv_ref, slot)
-    prepare(halo_ref, scale_rows(scale_ref, (8, leaf_pts)), 0, src, wgt, tgt)
+    prepare(halo_ref, 0, src, wgt, tgt)
     near_pairs(pairs, n, 4 * leaf_dev, src, tgt, wgt, out_ref, z, high, low)
 
 
-def node_field(tm_size, place_ref, scale, node_ref, own_ref, transfer_ref, node_src, node_wgt):
+def node_field(tm_size, place_ref, node_ref, own_ref, transfer_ref, node_src, node_wgt):
     devices = node_ref.shape[0]
     rank = own_ref.shape[1] // 2
     lane = lane_ids((8, 128))
@@ -296,12 +295,12 @@
             xs.append(jnp.where(lane < rank, pltpu.roll(one, rank, 1), two))
             ws.append(jnp.where(lane < rank, one * distant(e), pltpu.roll(two, rank, 1) * distant(e + 1)))
         at = pl.ds(pl.multiple_of(g * 512, 512), 512)
-        node_src[:, at] = features(jnp.concatenate(xs, axis=1) * scale, True, False)[0]
+        node_src[:, at] = features(jnp.concatenate(xs, axis=1), True, False)[0]
         node_wgt[:, at] = halves(jnp.concatenate(ws, axis=1))
         return 0
 
     lax.fori_loop(0, devices // 8, unpack, 0, unroll=4)
-    own_xx = pltpu.roll(own_ref[...], rank, 1) * scale[:, 0 : 2 * rank]
+    own_xx = pltpu.roll(own_ref[...], rank, 1)
     target = features(own_xx, False, True)[0][:, :rank]
     total = jnp.zeros((16, rank), F32)
     step = 512
@@ -314,20 +313,17 @@
     return jnp.dot(total[:8] + total[8:], transfer_ref[...], precision=EXACT, preferred_element_type=F32)
 
 
-def outside_body(pairs_ref, sizes_ref, far_ref, scale_ref, left_ref, mid_ref, right_ref, up_ref, down_ref, inside_ref, out_ref, far_out_ref, src, tgt, wgt, coef, far_src, far_wgt, z, high, low):
+def outside_body(pairs_ref, sizes_ref, far_ref, row_ref, up_ref, down_ref, out_ref, far_out_ref, src, tgt, wgt, coef, far_src, far_wgt, z, high, low):
     leaf_dev, rhs, leaf_pts = out_ref.shape
     rank = coef.shape[2]
-    scale = scale_rows(scale_ref, (8, leaf_pts))
     idle = 9 * leaf_dev
     src[idle] = jnp.zeros(src.shape[1:], BF16)
     wgt[idle] = jnp.zeros(wgt.shape[1:], BF16)
     for k in range(3):
-        prepare(up_ref.at[k], scale, k * leaf_dev, src, wgt, None, coef)
-        prepare(down_ref.at[k], scale, (6 + k) * leaf_dev, src, wgt, None, coef)
-    prepare(left_ref, scale, 3 * leaf_dev, src, wgt, None, coef)
-    prepare(mid_ref, scale, 4 * leaf_dev, src, wgt, tgt, coef)
-    prepare(right_ref, scale, 5 * leaf_dev, src, wgt, None, coef)
-    out_ref[...] = inside_ref[...]
+        prepare(up_ref.at[k], k * leaf_dev, src, wgt, None, coef)
+        prepare(row_ref.at[k], (3 + k) * leaf_dev, src, wgt, tgt if k == 1 else None, coef)
+        prepare(down_ref.at[k], (6 + k) * leaf_dev, src, wgt, None, coef)
+    out_ref[...] = jnp.zeros_like(out_ref)
     near_pairs(pairs_ref, sizes_ref[1], 0, src, tgt, wgt, out_ref, z, high, low)
     for leaf in range(leaf_dev):
         for j in range(far_ref.shape[1]):
@@ -341,16 +337,15 @@
         far_out_ref[leaf] = far[:8] + far[8:]
 
 
-def tail_body(tm_size, place_ref, scale_ref, noise_ref, near_ref, far_ref, node_ref, own_ref, transfer_ref, bases_ref, inv_ref, p_ref, res_ref, image_ref, sums_ref, flat, node_src, node_wgt):
+def tail_body(tm_size, place_ref, noise_ref, inside_ref, near_ref, far_ref, node_ref, own_ref, transfer_ref, bases_ref, inv_ref, p_ref, res_ref, image_ref, sums_ref, flat, node_src, node_wgt):
     leaf_dev, rank, leaf_pts = bases_ref.shape
-    scale = scale_rows(scale_ref, (8, 4 * 128))
-    pushed = node_field(tm_size, place_ref, scale, node_ref, own_ref, transfer_ref, node_src, node_wgt)
+    pushed = node_field(tm_size, place_ref, node_ref, own_ref, transfer_ref, node_src, node_wgt)
     for leaf in range(leaf_dev):
         incoming = halves(far_ref[leaf] + pushed[:, leaf * rank : (leaf + 1) * rank])
         base_high, base_low = split(bases_ref[leaf])
         got = jnp.dot(incoming, base_high, preferred_element_type=F32)
         got = got + jnp.dot(incoming, base_low, preferred_element_type=F32)
-        flat[:, leaf * leaf_pts : (leaf + 1) * leaf_pts] = near_ref[leaf] + got[:8] + got[8:]
+        flat[:, leaf * leaf_pts : (leaf + 1) * leaf_pts] = inside_ref[leaf] + near_ref[leaf] + got[:8] + got[8:]
 
     chunks = flat.shape[1] // 128
     row = row_ids((8, 128))
@@ -406,7 +401,7 @@
     by_row = order.reshape(chunks, 128)
     halo = pl.pallas_call(
         gather_body,
-        in_specs=[ANY] * 4,
+        in_specs=[SMEM] + [ANY] * 4,
         out_specs=VMEM,
         out_shape=shape((13 * leaf_dev, leaf_pts), F32),
         scratch_shapes=[
@@ -418,7 +413,7 @@
         ],
         compiler_params=params(60),
         name="gather",
-    )(by_row, coords, direction, bases)
+    )(inv_scale, by_row, coords, direction, bases)
     left = shifted(halo, "tm", 1)
     right = shifted(halo, "tm", -1)
 
@@ -437,7 +432,7 @@
     entries = near_list.size + 4
     inside, node, own, inverse, pairs, sizes = pl.pallas_call(
         inside_body,
-        in_specs=[SMEM] * 3 + [ANY] + [VMEM] * 3,
+        in_specs=[SMEM] * 2 + [ANY] + [VMEM] * 3,
         out_specs=[VMEM] * 4 + [SMEM] * 2,
         out_shape=[
             shape((leaf_dev, rhs, leaf_pts), F32),
@@ -458,7 +453,7 @@
         compiler_params=params(58),
         cost_estimate=pl.CostEstimate(flops=10**10, bytes_accessed=2**21, transcendentals=10**7),
         name="inside",
-    )(near_list, near_count, inv_scale, halo, by_row, transfer[0], device_skel)
+    )(near_list, near_count, halo, by_row, transfer[0], device_skel)
     left, right, inside, node = lax.optimization_barrier((left, right, inside, node))
     nodes = lax.all_to_all(node, axes, 0, 0)
     row = jnp.stack([left, halo, right])
@@ -468,7 +463,7 @@
 
     near, far = pl.pallas_call(
         outside_body,
-        in_specs=[SMEM] * 4 + [VMEM] * 6,
+        in_specs=[SMEM] * 3 + [VMEM] * 3,
         out_specs=[VMEM] * 2,
         out_shape=[shape((leaf_dev, rhs, leaf_pts), F32), shape((leaf_dev, rhs, rank), F32)],
         scratch_shapes=pipeline(9 * leaf_dev)
@@ -481,10 +476,10 @@
         compiler_params=params(14),
         cost_estimate=pl.CostEstimate(flops=3 * 10**10, bytes_accessed=2**21, transcendentals=3 * 10**7),
         name="outside",
-    )(pairs, sizes, far_list, inv_scale, left, halo, right, up, down, inside)
+    )(pairs, sizes, far_list, row, up, down)
     image, sums = pl.pallas_call(
         functools.partial(tail_body, lax.axis_size("tm")),
-        in_specs=[SMEM] * 3 + [VMEM] * 9,
+        in_specs=[SMEM] * 2 + [VMEM] * 10,
         out_specs=[VMEM] * 2,
         out_shape=[shape((rhs, points), F32), shape((devices, 128), F32)],
         scratch_shapes=[
@@ -494,7 +489,7 @@
         ],
         compiler_params=params(10),
         name="tail",
-    )(place, inv_scale, noise, near, far, nodes, own, transfer[0], bases, inverse, direction, residual)
+    )(place, noise, inside, near, far, nodes, own, transfer[0], bases, inverse, direction, residual)
     all_sums = lax.all_to_all(sums, axes, 0, 0, tiled=True)
     return pl.pallas_call(
         update_body,

time: 99.3 us -> 97.6 us (0.983)
  blocking collectives: 22.2 us -> 20.7 us
  Pallas kernels: 48.2 us -> 49.4 us
    all_to_all x1, blocking collectives: 22.2 us -> 20.7 us  [shards(): all_sums = lax.all_to_all(sums, axes, 0, 0, tiled=True)]
    pallas_call x3, Pallas kernels: 41.2 us -> 42.4 us  [the longest x1 27.8 us: shards(): pl.pallas_call(outside_body, in_specs=[SMEM] * 3 + [VMEM] * 3, out_specs=...]
    unnamed x32 -> x30, local copies, waits for them, and re-layouts: 4.17 us -> 3.26 us
  transfers between devices with their start and end apart: 5 -> 5, of which waited for: 0 -> 0; matrix products, arithmetic and copies ran while one was open for 0% -> 0% of each run, Pallas kernels for 36% -> 38%
where the time goes in v9:
time: 97.6 us; the launch traced here: 97.2 us
  Pallas kernels  49.4 us (51%)
  starting transfers between devices  22.9 us (23%)
  blocking collectives  20.7 us (21%)
  local copies, waits for them, and re-layouts  3.26 us (3%)
    pallas_call x1, Pallas kernels, shards(): pl.pallas_call(outside_body, in_specs=[SMEM] * 3 + [VMEM] * 3, out_specs=...  27.8 us
    all_to_all x1, blocking collectives, shards(): all_sums = lax.all_to_all(sums, axes, 0, 0, tiled=True)  20.7 us
    all_to_all x1, starting transfers between devices, shards(): nodes = lax.all_to_all(node, axes, 0, 0)  11.8 us
    ppermute x4, starting transfers between devices, shifted(): lax.ppermute(x, axis, [(i, i + by) for i in range(n) if 0 <= i + by < n])  11.1 us
    pallas_call x1, Pallas kernels, shards(): pl.pallas_call(inside_body, in_specs=[SMEM] * 2 + [ANY] + [VMEM] * 3, out...  8.73 us
    pallas_call x1, Pallas kernels, shards(): pl.pallas_call(functools.partial(tail_body, lax.axis_size('tm')), in_spec...  6.16 us
    pallas_call x1, Pallas kernels, shards(): pl.pallas_call(gather_body, in_specs=[SMEM] + [ANY] * 4, out_specs=VMEM,...  5.92 us
    unnamed x30, local copies, waits for them, and re-layouts  3.26 us
  transfers between devices with their start and end apart: 5, of which 0 were waited for; matrix products, arithmetic and copies ran while one was open for 0% of the time, Pallas kernels for 38%

profile of v9, /device:TPU:1, one launch (start us, length us, event | category | flops | bytes accessed | tf_op | source)
XLA Modules:
  0.0 97.2 jit_solution(1942209027945430176)
XLA Ops:
  0.6 5.9 %gather.1.halo_hbm = f32[104,512]{1,0:T(8,128)} custom-call(f32[4]{0:T(128)} %scale_ref.1, s32[32,128]{1,0:T(8,128)} %bitcast.18, f32[4,4096]{1,0:T(4,128)} %x_hbm.1, f32[8,4096]{1,0:T(8,128)} %p_ref.3, f32[8,64,512]{2,1,0:T(8,128)} %bases_ref.1), custom_call_target="tpu_custom_call" | custom-call | tf_op jit(solution)/shard_map/gather/pallas_call | solution.py:402
  6.6 4.0 %collective-permute-start = (f32[104,512]{1,0:T(8,128)}, f32[104,512]{1,0:T(8,128)S(1)}, u32[]{:S(2)}, u32[]{:S(2)}) collective-permute-start(f32[104,512]{1,0:T(8,128)} %gather.1.halo_hbm), channel_id=1, source_target_pairs={{0,1},{1,2},{2,3},{4,5},{5,6},{6,7},{8,9},{9,10},{10,11},{12,13},{... | collective-permute-start | bytes 638984 | tf_op jit(solution)/shard_map/ppermute | solution.py:391
  10.5 1.3 %collective-permute-start.1 = (f32[104,512]{1,0:T(8,128)}, f32[104,512]{1,0:T(8,128)S(1)}, u32[]{:S(2)}, u32[]{:S(2)}) collective-permute-start(f32[104,512]{1,0:T(8,128)} %gather.1.halo_hbm), channel_id=1, source_target_pairs={{1,0},{2,1},{3,2},{5,4},{6,5},{7,6},{9,8},{10,9},{11,10},{13,12},{... | collective-permute-start | bytes 638984 | tf_op jit(solution)/shard_map/ppermute | solution.py:391
  11.8 0.0 copy-start.14
  11.8 8.7 %inside.1 = (f32[8,8,512]{2,1,0:T(8,128)}, f32[128,8,128]{2,1,0:T(8,128)}, f32[8,128]{1,0:T(8,128)}, s32[32,128]{1,0:T(8,128)}, s32[68]{0:T(128)}, /*index=5*/s32[2]{0:T(128)}) custom-call(s32[8,8]{1,0:T(8,128)} %near_ref.1, s32[8]{0:T(128)} %count_ref.1, f32[104,512]{1,0:T(8,128)} %gather.1.halo_hbm, s32[32,128]{1,0:T(8,128)} %bitcast.19, ...), custom_call_target="tpu_custom_call" | custom-call | flops 10000000000 | bytes 2097152 | tf_op jit(solution)/shard_map/inside/pallas_call | solution.py:433
  20.6 0.0 collective-permute-done
  20.6 0.0 collective-permute-done.1
  20.6 0.0 copy-done.14
  20.7 3.9 %collective-permute-start.2 = (f32[3,104,512]{2,1,0:T(8,128)S(1)}, f32[3,104,512]{2,1,0:T(8,128)S(1)}, u32[]{:S(2)}, u32[]{:S(2)}) collective-permute-start(f32[3,104,512]{2,1,0:T(8,128)S(1)} %pad_maximum_fusion.row_ref), channel_id=1, source_target_pairs={{0,4},{4,8},{8,12},{12,16},{16,20},{20,24},{24,28},{28,32},{32,36}... | collective-permute-start | bytes 1916936 | tf_op jit(solution)/shard_map/ppermute | solution.py:391
  24.6 1.9 %collective-permute-start.3 = (f32[3,104,512]{2,1,0:T(8,128)S(1)}, f32[3,104,512]{2,1,0:T(8,128)}, u32[]{:S(2)}, u32[]{:S(2)}) collective-permute-start(f32[3,104,512]{2,1,0:T(8,128)S(1)} %pad_maximum_fusion.row_ref), channel_id=1, source_target_pairs={{4,0},{8,4},{12,8},{16,12},{20,16},{24,20},{28,24},{32,28},{36,32}... | collective-permute-start | bytes 1916936 | tf_op jit(solution)/shard_map/ppermute | solution.py:391
  26.5 0.1 pad_add_fusion.place_ref
  26.6 0.0 copy-start.11
  26.6 11.8 %all-to-all-start = ((f32[128,8,128]{2,1,0:T(8,128)}), f32[128,8,128]{2,1,0:T(8,128)S(1)}, u32[]{:S(2)}, u32[]{:S(2)}) async-start(f32[128,8,128]{2,1,0:T(8,128)} %get-tuple-element.25), calls=%async_computation | async-start | bytes 1048576 | tf_op jit(solution)/shard_map/all_to_all | solution.py:458
  38.4 0.0 collective-permute-done.2.up_ref
  38.4 0.0 copy-start.9
  38.5 0.8 copy-done.9
  39.3 0.0 collective-permute-done.3.down_ref
  39.3 0.0 copy-start.12
  39.3 0.0 copy-start.13
  39.3 0.0 copy-done.11
  39.3 0.7 copy-done.12
  40.0 0.0 copy-done.13
  40.0 0.0 copy-start.10
  40.0 1.1 %copy-done.10 = f32[3,104,512]{2,1,0:T(8,128)S(1)} copy-done((f32[3,104,512]{2,1,0:T(8,128)S(1)}, f32[3,104,512]{2,1,0:T(8,128)}, u32[]{:S(2)}) %copy-start.10) | copy-done | bytes 639000
  41.1 0.0 copy-start
  41.1 0.0 copy-start.1
  41.1 0.0 copy-start.2
  41.1 0.0 copy-start.3
  41.1 0.0 copy-start.4
  41.1 0.0 copy-start.6
  41.1 27.8 %outside.1 = (f32[8,8,512]{2,1,0:T(8,128)S(1)}, f32[8,8,64]{2,1,0:T(8,128)S(1)}) custom-call(s32[68]{0:T(128)S(1)} %copy-done.12, s32[2]{0:T(128)S(1)} %copy-done.13, s32[8,8]{1,0:T(8,128)S(1)} %copy-done.11, f32[3,104,512]{2,1,0:T(8,128)S(1)} %pad_maximum_fusion.row_ref, f32[3,104,512]{2,1,0:T(8,128)S(1)} %copy-done.10, ...), custom_call_target="tpu_custom_call" | custom-call | flops 30000001024 | bytes 2097152 | tf_op jit(solution)/shard_map/outside/pallas_call | solution.py:464
  68.9 0.0 copy-start.7
  68.9 0.0 all-to-all-done.node_ref
  68.9 0.0 copy-start.8
  68.9 0.0 copy-done
  68.9 0.0 copy-done.1
  68.9 0.0 copy-done.2
  68.9 0.0 copy-done.3
  68.9 0.0 copy-done.4
  69.0 0.0 copy-done.6
  69.0 0.6 copy-done.7
  69.6 0.0 copy-done.8
  69.6 6.2 %tail.1 = (f32[8,4096]{1,0:T(8,128)S(1)}, f32[128,128]{1,0:T(8,128)S(1)}) custom-call(s32[2]{0:T(128)S(1)} %pad_add_fusion.place_ref, f32[8]{0:T(128)S(1)} %copy-done.8, f32[8,8,512]{2,1,0:T(8,128)S(1)} %copy-done.4, f32[8,8,512]{2,1,0:T(8,128)S(1)} %get-tuple-element.23.near_ref, f32[8,8,64]{2,1,0:T(8,128)S(1)} %get-tuple-element.24.far_ref, ...), custom_call_target="tpu_custom_call" | custom-call | tf_op jit(solution)/shard_map/tail/pallas_call | solution.py:480
  75.7 0.0 copy-start.5
  75.8 20.7 %all_to_all.16 = f32[128,1,128]{2,1,0:T(1,128)S(1)} all-to-all(f32[128,1,128]{2,1,0:T(1,128)S(1)} %bitcast.14), channel_id=1, replica_groups=mesh['leaf'=32,'tm'=4] {'leaf','tm'}, dimensions={0} | all-to-all | bytes 131072 | tf_op jit(solution)/shard_map/all_to_all | solution.py:493
  96.4 0.0 copy-done.5
  96.4 0.8 update.1
  (1 shorter events, 0.0 us)
Async XLA Ops:
  6.6 14.0 %collective-permute-start = (f32[104,512]{1,0:T(8,128)}, f32[104,512]{1,0:T(8,128)S(1)}, u32[]{:S(2)}, u32[]{:S(2)}) collective-permute-start(f32[104,512]{1,0:T(8,128)} %gather.1.halo_hbm), channel_id=1, source_target_pairs={{0,1},{1,2},{2,3},{4,5},{5,6},{6,7},{8,9},{9,10},{10,11},{12,13},{... | collective-permute-start | bytes 638984 | tf_op jit(solution)/shard_map/ppermute | solution.py:391
  10.5 10.1 %collective-permute-start.1 = (f32[104,512]{1,0:T(8,128)}, f32[104,512]{1,0:T(8,128)S(1)}, u32[]{:S(2)}, u32[]{:S(2)}) collective-permute-start(f32[104,512]{1,0:T(8,128)} %gather.1.halo_hbm), channel_id=1, source_target_pairs={{1,0},{2,1},{3,2},{5,4},{6,5},{7,6},{9,8},{10,9},{11,10},{13,12},{... | collective-permute-start | bytes 638984 | tf_op jit(solution)/shard_map/ppermute | solution.py:391
  11.8 8.8 %copy-start.14 = (f32[104,512]{1,0:T(8,128)S(1)}, f32[104,512]{1,0:T(8,128)}, u32[]{:S(2)}) copy-start(f32[104,512]{1,0:T(8,128)} %gather.1.halo_hbm) | copy-start | bytes 638980
  20.7 17.8 %collective-permute-start.2 = (f32[3,104,512]{2,1,0:T(8,128)S(1)}, f32[3,104,512]{2,1,0:T(8,128)S(1)}, u32[]{:S(2)}, u32[]{:S(2)}) collective-permute-start(f32[3,104,512]{2,1,0:T(8,128)S(1)} %pad_maximum_fusion.row_ref), channel_id=1, source_target_pairs={{0,4},{4,8},{8,12},{12,16},{16,20},{20,24},{24,28},{28,32},{32,36}... | collective-permute-start | bytes 1916936 | tf_op jit(solution)/shard_map/ppermute | solution.py:391
  24.6 14.7 %collective-permute-start.3 = (f32[3,104,512]{2,1,0:T(8,128)S(1)}, f32[3,104,512]{2,1,0:T(8,128)}, u32[]{:S(2)}, u32[]{:S(2)}) collective-permute-start(f32[3,104,512]{2,1,0:T(8,128)S(1)} %pad_maximum_fusion.row_ref), channel_id=1, source_target_pairs={{4,0},{8,4},{12,8},{16,12},{20,16},{24,20},{28,24},{32,28},{36,32}... | collective-permute-start | bytes 1916936 | tf_op jit(solution)/shard_map/ppermute | solution.py:391
  26.6 12.7 %copy-start.11 = (s32[8,8]{1,0:T(8,128)S(1)}, s32[8,8]{1,0:T(8,128)}, u32[]{:S(2)}) copy-start(s32[8,8]{1,0:T(8,128)} %far_ref.1) | copy-start | bytes 772
  26.6 42.3 %all-to-all-start = ((f32[128,8,128]{2,1,0:T(8,128)}), f32[128,8,128]{2,1,0:T(8,128)S(1)}, u32[]{:S(2)}, u32[]{:S(2)}) async-start(f32[128,8,128]{2,1,0:T(8,128)} %get-tuple-element.25), calls=%async_computation | async-start | bytes 1048576 | tf_op jit(solution)/shard_map/all_to_all | solution.py:458
  38.4 0.8 copy-start.9
  39.3 0.7 copy-start.12
  39.3 0.7 copy-start.13
  40.0 1.1 %copy-start.10 = (f32[3,104,512]{2,1,0:T(8,128)S(1)}, f32[3,104,512]{2,1,0:T(8,128)}, u32[]{:S(2)}) copy-start(f32[3,104,512]{2,1,0:T(8,128)} %copy-done.9) | copy-start | bytes 1916932
  41.1 27.8 %copy-start = (f32[8,64,512]{2,1,0:T(8,128)S(1)}, f32[8,64,512]{2,1,0:T(8,128)}, u32[]{:S(2)}) copy-start(f32[8,64,512]{2,1,0:T(8,128)} %bases_ref.1) | copy-start | bytes 3145732
  41.1 27.8 %copy-start.1 = (f32[8,4096]{1,0:T(8,128)S(1)}, f32[8,4096]{1,0:T(8,128)}, u32[]{:S(2)}) copy-start(f32[8,4096]{1,0:T(8,128)} %p_ref.3) | copy-start | bytes 393220
  41.1 27.8 %copy-start.2 = (f32[8,4096]{1,0:T(8,128)S(1)}, f32[8,4096]{1,0:T(8,128)}, u32[]{:S(2)}) copy-start(f32[8,4096]{1,0:T(8,128)} %res_ref.3) | copy-start | bytes 393220
  41.1 27.9 %copy-start.3 = (f32[1,64,512]{2,1,0:T(8,128)S(1)}, f32[1,64,512]{2,1,0:T(8,128)}, u32[]{:S(2)}) copy-start(f32[1,64,512]{2,1,0:T(8,128)} %param.19) | copy-start | bytes 393220
  41.1 27.9 %copy-start.4 = (f32[8,8,512]{2,1,0:T(8,128)S(1)}, f32[8,8,512]{2,1,0:T(8,128)}, u32[]{:S(2)}) copy-start(f32[8,8,512]{2,1,0:T(8,128)} %get-tuple-element.18.inside_ref) | copy-start | bytes 393220
  41.1 27.9 %copy-start.6 = (s32[32,128]{1,0:T(8,128)S(1)}, s32[32,128]{1,0:T(8,128)}, u32[]{:S(2)}) copy-start(s32[32,128]{1,0:T(8,128)} %get-tuple-element.27.inv_ref) | copy-start | bytes 49156
  68.9 0.7 copy-start.7
  68.9 0.7 copy-start.8
  75.7 20.7 %copy-start.5 = (f32[8,4096]{1,0:T(8,128)S(1)}, f32[8,4096]{1,0:T(8,128)}, u32[]{:S(2)}) copy-start(f32[8,4096]{1,0:T(8,128)} %it_ref.1) | copy-start | bytes 393220

commit v10 on v9

--- a/solution.py
+++ b/solution.py
@@ -96,32 +96,30 @@
     return picked
 
 
+def fetch(sources, targets, sems):
+    moves = [pltpu.make_async_copy(a, b, sems.at[i]) for i, (a, b) in enumerate(zip(sources, targets))]
+    for move in moves:
+        move.start()
+    return moves
+
+
 def scale_rows(scale_ref, shape):
     row = row_ids(shape) & 3
     picked = jnp.where(row == 0, scale_ref[0], jnp.where(row == 1, scale_ref[1], jnp.where(row == 2, scale_ref[2], scale_ref[3])))
     return picked * UNIT
 
 
-def gather_body(scale_ref, order_hbm, x_hbm, p_hbm, bases_hbm, halo_ref, order_ref, xx, p_ref, bases_ref, sems):
+def gather_body(scale_hbm, order_hbm, x_hbm, p_hbm, bases_hbm, transfer_hbm, skel_hbm, halo_ref, node_ref, own_ref, scale_ref, order_ref, xx, p_ref, bases_ref, transfer_ref, skel_ref, slot, sems):
     leaf_dev, rank, leaf_pts = bases_ref.shape
     points = p_ref.shape[1]
     chunks = points // 128
     per_leaf = leaf_pts // 128
-    moves = [
-        pltpu.make_async_copy(source, target, sems.at[i])
-        for i, (source, target) in enumerate(
-            [
-                (order_hbm, order_ref),
-                (x_hbm, xx.at[0:4, :]),
-                (x_hbm, xx.at[4:8, :]),
-                (p_hbm, p_ref),
-                (bases_hbm, bases_ref),
-            ]
-        )
-    ]
-    for move in moves:
-        move.start()
-    for move in moves[:4]:
+    moves = fetch(
+        [order_hbm, x_hbm, x_hbm, p_hbm, scale_hbm, bases_hbm, transfer_hbm, skel_hbm],
+        [order_ref, xx.at[0:4, :], xx.at[4:8, :], p_ref, scale_ref, bases_ref, transfer_ref, skel_ref],
+        sems,
+    )
+    for move in moves[:5]:
         move.wait()
     scale = scale_rows(scale_ref, (8, 128))
 
@@ -143,16 +141,11 @@
         return 0
 
     lax.fori_loop(0, leaf_dev // 2, two_leaves, 0)
-    moves[4].wait()
+    for move in moves[5:]:
+        move.wait()
     for leaf in range(leaf_dev):
         coef = contract(halo_ref[32 + leaf * 8 : 40 + leaf * 8, :], bases_ref[leaf], ((1,), (1,)), EXACT)
         halo_ref[96:104, leaf * rank : (leaf + 1) * rank] = coef
-
-
-def node_work(order_ref, halo_ref, transfer_ref, skel_ref, node_ref, own_ref, inv_ref, slot):
-    chunks = order_ref.shape[0]
-    rank = transfer_ref.shape[0]
-    leaf_dev = halo_ref.shape[0] // 13
     upper = row_ids((8, 128)) < 4
     for g in range(leaf_dev // 2):
         both = halo_ref[g * 8 : g * 8 + 8, 0:128]
@@ -166,6 +159,10 @@
     tile = jnp.concatenate([weights, node_x[:, :rank]], axis=1)
     own_ref[...] = tile
     node_ref[...] = jnp.broadcast_to(tile[None], node_ref.shape)
+
+
+def place_of(order_ref):
+    chunks = order_ref.shape[0]
     tally = jnp.zeros((2 * chunks, 128), F32)
     for c in range(chunks):
         ids = order_ref[c : c + 1, :]
@@ -176,7 +173,7 @@
         digit0 = jnp.where(row, (lane & 63).astype(F32), 0.0)
         digits = jnp.concatenate([digit1, digit0], axis=0).astype(BF16)
         tally = tally + contract(digits, low, ((1,), (1,)))
-    inv_ref[...] = (64.0 * tally[0:chunks] + tally[chunks : 2 * chunks] + 0.5).astype(jnp.int32)
+    return (64.0 * tally[0:chunks] + tally[chunks : 2 * chunks] + 0.5).astype(jnp.int32)
 
 
 def prepare(ref, base, src, wgt, tgt=None, coef=None):
@@ -261,7 +258,7 @@
     lax.fori_loop(0, (n + 1) // 2, two_pairs, 0)
 
 
-def inside_body(near_ref, count_ref, halo_hbm, order_ref, transfer_ref, skel_ref, out_ref, node_ref, own_ref, inv_ref, pairs_ref, sizes_ref, pairs, halo_ref, slot, src, tgt, wgt, z, high, low, sem):
+def inside_body(near_ref, count_ref, halo_hbm, order_ref, out_ref, inv_ref, pairs_ref, sizes_ref, pairs, halo_ref, src, tgt, wgt, z, high, low, sem):
     leaf_dev, rhs, leaf_pts = out_ref.shape
     move = pltpu.make_async_copy(halo_hbm, halo_ref, sem)
     move.start()
@@ -272,19 +269,19 @@
     wgt[leaf_dev] = jnp.zeros(wgt.shape[1:], BF16)
     out_ref[...] = jnp.zeros_like(out_ref)
     move.wait()
-    node_work(order_ref, halo_ref, transfer_ref, skel_ref, node_ref, own_ref, inv_ref, slot)
+    inv_ref[...] = place_of(order_ref)
     prepare(halo_ref, 0, src, wgt, tgt)
     near_pairs(pairs, n, 4 * leaf_dev, src, tgt, wgt, out_ref, z, high, low)
 
 
-def node_field(tm_size, place_ref, node_ref, own_ref, transfer_ref, node_src, node_wgt):
+def node_field(leaf_size, place_ref, node_ref, own_ref, transfer_ref, node_src, node_wgt):
     devices = node_ref.shape[0]
     rank = own_ref.shape[1] // 2
     lane = lane_ids((8, 128))
 
     def distant(e):
-        far_a = jnp.abs(e // tm_size - place_ref[0]) > 1
-        far_b = jnp.abs(e % tm_size - place_ref[1]) > 1
+        far_a = jnp.abs(e % leaf_size - place_ref[0]) > 1
+        far_b = jnp.abs(e // leaf_size - place_ref[1]) > 1
         return jnp.where(far_a | far_b, FACTOR, 0.0)
 
     def unpack(g, _):
@@ -337,9 +334,9 @@
         far_out_ref[leaf] = far[:8] + far[8:]
 
 
-def tail_body(tm_size, place_ref, noise_ref, inside_ref, near_ref, far_ref, node_ref, own_ref, transfer_ref, bases_ref, inv_ref, p_ref, res_ref, image_ref, sums_ref, flat, node_src, node_wgt):
+def tail_body(leaf_size, place_ref, noise_ref, inside_ref, near_ref, far_ref, node_ref, own_ref, transfer_ref, bases_ref, inv_ref, p_ref, res_ref, image_ref, sums_ref, flat, node_src, node_wgt):
     leaf_dev, rank, leaf_pts = bases_ref.shape
-    pushed = node_field(tm_size, place_ref, node_ref, own_ref, transfer_ref, node_src, node_wgt)
+    pushed = node_field(leaf_size, place_ref, node_ref, own_ref, transfer_ref, node_src, node_wgt)
     for leaf in range(leaf_dev):
         incoming = halves(far_ref[leaf] + pushed[:, leaf * rank : (leaf + 1) * rank])
         base_high, base_low = split(bases_ref[leaf])
@@ -399,21 +396,29 @@
     chunks = points // 128
     shape = jax.ShapeDtypeStruct
     by_row = order.reshape(chunks, 128)
-    halo = pl.pallas_call(
+    halo, node, own = pl.pallas_call(
         gather_body,
-        in_specs=[SMEM] + [ANY] * 4,
-        out_specs=VMEM,
-        out_shape=shape((13 * leaf_dev, leaf_pts), F32),
+        in_specs=[ANY] * 7,
+        out_specs=[VMEM] * 3,
+        out_shape=[
+            shape((13 * leaf_dev, leaf_pts), F32),
+            shape((lax.axis_size("leaf"), 8, 128), F32),
+            shape((8, 128), F32),
+        ],
         scratch_shapes=[
+            pltpu.SMEM(inv_scale.shape, F32),
             pltpu.VMEM((chunks, 128), jnp.int32),
             pltpu.VMEM((8, points), F32),
             pltpu.VMEM((rhs, points), F32),
             pltpu.VMEM(bases.shape, F32),
-            pltpu.SemaphoreType.DMA((5,)),
+            pltpu.VMEM(transfer.shape[1:], F32),
+            pltpu.VMEM(device_skel.shape, jnp.int32),
+            pltpu.VMEM((8, leaf_dev * rank), F32),
+            pltpu.SemaphoreType.DMA((8,)),
         ],
         compiler_params=params(60),
         name="gather",
-    )(inv_scale, by_row, coords, direction, bases)
+    )(inv_scale, by_row, coords, direction, bases, transfer[0], device_skel)
     left = shifted(halo, "tm", 1)
     right = shifted(halo, "tm", -1)
 
@@ -430,14 +435,13 @@
         pltpu.VMEM((2, PART, leaf_pts), BF16),
     ]
     entries = near_list.size + 4
-    inside, node, own, inverse, pairs, sizes = pl.pallas_call(
+    column = lax.all_to_all(node, "leaf", 0, 0)
+    inside, inverse, pairs, sizes = pl.pallas_call(
         inside_body,
-        in_specs=[SMEM] * 2 + [ANY] + [VMEM] * 3,
-        out_specs=[VMEM] * 4 + [SMEM] * 2,
+        in_specs=[SMEM] * 2 + [ANY] + [VMEM],
+        out_specs=[VMEM] * 2 + [SMEM] * 2,
         out_shape=[
             shape((leaf_dev, rhs, leaf_pts), F32),
-            shape((devices, 8, 128), F32),
-            shape((8, 128), F32),
             shape((chunks, 128), jnp.int32),
             shape((entries,), jnp.int32),
             shape((2,), jnp.int32),
@@ -445,7 +449,6 @@
         scratch_shapes=[
             pltpu.SMEM((entries,), jnp.int32),
             pltpu.VMEM(halo.shape, F32),
-            pltpu.VMEM((8, leaf_dev * rank), F32),
         ]
         + pipeline(leaf_dev)
         + buffers
@@ -453,9 +456,10 @@
         compiler_params=params(58),
         cost_estimate=pl.CostEstimate(flops=10**10, bytes_accessed=2**21, transcendentals=10**7),
         name="inside",
-    )(near_list, near_count, halo, by_row, transfer[0], device_skel)
-    left, right, inside, node = lax.optimization_barrier((left, right, inside, node))
-    nodes = lax.all_to_all(node, axes, 0, 0)
+    )(near_list, near_count, halo, by_row)
+    left, right, inside, column = lax.optimization_barrier((left, right, inside, column))
+    nodes = lax.all_to_all(jnp.broadcast_to(column[None], (lax.axis_size("tm"),) + column.shape), "tm", 0, 0)
+    nodes = nodes.reshape(devices, 8, 128)
     row = jnp.stack([left, halo, right])
     up = shifted(row, "leaf", 1)
     down = shifted(row, "leaf", -1)
@@ -478,7 +482,7 @@
         name="outside",
     )(pairs, sizes, far_list, row, up, down)
     image, sums = pl.pallas_call(
-        functools.partial(tail_body, lax.axis_size("tm")),
+        functools.partial(tail_body, lax.axis_size("leaf")),
         in_specs=[SMEM] * 2 + [VMEM] * 10,
         out_specs=[VMEM] * 2,
         out_shape=[shape((rhs, points), F32), shape((devices, 128), F32)],

time: 97.6 us -> 104 us (1.066)
  waiting for transfers between devices: 0.02 us -> 3.05 us
  starting transfers between devices: 22.9 us -> 24.9 us
  blocking collectives: 20.7 us -> 19 us
  Pallas kernels: 49.4 us -> 50.7 us
    ppermute x4, waiting for transfers between devices: 0.01 us -> 3.04 us  [shifted(): lax.ppermute(x, axis, [(i, i + by) for i in range(n) if 0 <= i + by < n])]
    all_to_all x1 -> x2, starting transfers between devices: 11.8 us -> 14.4 us  [the longest x1 9.06 us: shards(): column = lax.all_to_all(node, 'leaf', 0, 0)]
    pallas_call x1, Pallas kernels: 27.8 us -> 29.7 us  [shards(): pl.pallas_call(outside_body, in_specs=[SMEM] * 3 + [VMEM] * 3, out_specs=...]
    all_to_all x1, blocking collectives: 20.7 us -> 19 us  [shards(): all_sums = lax.all_to_all(sums, axes, 0, 0, tiled=True)]
  transfers between devices with their start and end apart: 5 -> 6, of which waited for: 0 -> 1; matrix products, arithmetic and copies ran while one was open for 0% -> 1% of each run, Pallas kernels for 38% -> 37%
where the time goes in v10:
time: 104 us; the launch traced here: 103 us
  Pallas kernels  50.7 us (49%)
  starting transfers between devices  24.9 us (24%)
  blocking collectives  19 us (18%)
  local copies, waits for them, and re-layouts  4.09 us (4%)
  waiting for transfers between devices  3.05 us (3%)
    pallas_call x1, Pallas kernels, shards(): pl.pallas_call(outside_body, in_specs=[SMEM] * 3 + [VMEM] * 3, out_specs=...  29.7 us
    all_to_all x1, blocking collectives, shards(): all_sums = lax.all_to_all(sums, axes, 0, 0, tiled=True)  19 us
    ppermute x4, starting transfers between devices, shifted(): lax.ppermute(x, axis, [(i, i + by) for i in range(n) if 0 <= i + by < n])  10.5 us
    all_to_all x1, starting transfers between devices, shards(): column = lax.all_to_all(node, 'leaf', 0, 0)  9.06 us
    pallas_call x1, Pallas kernels, shards(): pl.pallas_call(inside_body, in_specs=[SMEM] * 2 + [ANY] + [VMEM], out_spe...  8.44 us
    pallas_call x1, Pallas kernels, shards(): pl.pallas_call(functools.partial(tail_body, lax.axis_size('leaf')), in_sp...  6.17 us
    pallas_call x1, Pallas kernels, shards(): pl.pallas_call(gather_body, in_specs=[ANY] * 7, out_specs=[VMEM] * 3, out...  5.59 us
    all_to_all x1, starting transfers between devices, shards(): lax.all_to_all(jnp.broadcast_to(column[None], (lax.axis_size('tm'),) + co...  5.3 us
  transfers between devices with their start and end apart: 6, of which 1 were waited for; matrix products, arithmetic and copies ran while one was open for 1% of the time, Pallas kernels for 37%

profile of v10, /device:TPU:1, one launch (start us, length us, event | category | flops | bytes accessed | tf_op | source)
XLA Modules:
  0.0 102.7 jit_solution(2211982085102585054)
XLA Ops:
  0.6 5.6 %gather.1 = (f32[104,512]{1,0:T(8,128)}, f32[32,8,128]{2,1,0:T(8,128)}, f32[8,128]{1,0:T(8,128)}) custom-call(f32[4]{0:T(128)} %scale_hbm.1, s32[32,128]{1,0:T(8,128)} %bitcast.20, f32[4,4096]{1,0:T(4,128)} %x_hbm.1, f32[8,4096]{1,0:T(8,128)} %p_ref.3, f32[8,64,512]{2,1,0:T(8,128)} %bases_ref.1, f32[64,512]{1,0:T(8,128)} %bitcast.13, s32[1,64]{1,0:T(1,128)} %skel_hbm.1), custom_call_target="tpu_custom_call" | custom-call | tf_op jit(solution)/shard_map/gather/pallas_call | solution.py:399
  6.2 4.0 %collective-permute-start = (f32[104,512]{1,0:T(8,128)}, f32[104,512]{1,0:T(8,128)S(1)}, u32[]{:S(2)}, u32[]{:S(2)}) collective-permute-start(f32[104,512]{1,0:T(8,128)} %get-tuple-element.17.halo_hbm), channel_id=1, source_target_pairs={{0,1},{1,2},{2,3},{4,5},{5,6},{6,7},{8,9},{9,10},{10,11},{12,13},{... | collective-permute-start | bytes 638984 | tf_op jit(solution)/shard_map/ppermute | solution.py:388
  10.2 1.3 %collective-permute-start.1 = (f32[104,512]{1,0:T(8,128)}, f32[104,512]{1,0:T(8,128)S(1)}, u32[]{:S(2)}, u32[]{:S(2)}) collective-permute-start(f32[104,512]{1,0:T(8,128)} %get-tuple-element.17.halo_hbm), channel_id=1, source_target_pairs={{1,0},{2,1},{3,2},{5,4},{6,5},{7,6},{9,8},{10,9},{11,10},{13,12},{... | collective-permute-start | bytes 638984 | tf_op jit(solution)/shard_map/ppermute | solution.py:388
  11.5 9.1 %all-to-all-start = ((f32[32,8,128]{2,1,0:T(8,128)}), f32[32,8,128]{2,1,0:T(8,128)S(1)}, u32[]{:S(2)}, u32[]{:S(2)}) async-start(f32[32,8,128]{2,1,0:T(8,128)} %get-tuple-element.19), calls=%async_computation | async-start | bytes 262144 | tf_op jit(solution)/shard_map/all_to_all | solution.py:438
  20.6 0.0 copy-start.14
  20.6 8.4 %inside.1 = (f32[8,8,512]{2,1,0:T(8,128)}, s32[32,128]{1,0:T(8,128)}, s32[68]{0:T(128)}, s32[2]{0:T(128)}) custom-call(s32[8,8]{1,0:T(8,128)} %near_ref.1, s32[8]{0:T(128)} %count_ref.1, f32[104,512]{1,0:T(8,128)} %get-tuple-element.17.halo_hbm, s32[32,128]{1,0:T(8,128)} %bitcast.21), custom_call_target="tpu_custom_call" | custom-call | flops 10000000000 | bytes 2097152 | tf_op jit(solution)/shard_map/inside/pallas_call | solution.py:439
  29.0 0.0 all-to-all-done
  29.0 0.0 collective-permute-done
  29.0 0.0 collective-permute-done.1
  29.1 0.0 copy-done.14
  29.1 3.4 %collective-permute-start.2 = (f32[3,104,512]{2,1,0:T(8,128)S(1)}, f32[3,104,512]{2,1,0:T(8,128)S(1)}, u32[]{:S(2)}, u32[]{:S(2)}) collective-permute-start(f32[3,104,512]{2,1,0:T(8,128)S(1)} %pad_maximum_fusion.row_ref), channel_id=1, source_target_pairs={{0,4},{4,8},{8,12},{12,16},{16,20},{20,24},{24,28},{28,32},{32,36}... | collective-permute-start | bytes 1916936 | tf_op jit(solution)/shard_map/ppermute | solution.py:388
  32.5 1.9 %collective-permute-start.3 = (f32[3,104,512]{2,1,0:T(8,128)S(1)}, f32[3,104,512]{2,1,0:T(8,128)}, u32[]{:S(2)}, u32[]{:S(2)}) collective-permute-start(f32[3,104,512]{2,1,0:T(8,128)S(1)} %pad_maximum_fusion.row_ref), channel_id=1, source_target_pairs={{4,0},{8,4},{12,8},{16,12},{20,16},{24,20},{28,24},{32,28},{36,32}... | collective-permute-start | bytes 1916936 | tf_op jit(solution)/shard_map/ppermute | solution.py:388
  34.4 0.1 pad_add_fusion.place_ref
  34.5 0.8 broadcast_in_dim.2
  35.3 0.0 copy-start.11
  35.3 5.3 %all-to-all-start.1 = ((f32[4,32,8,128]{3,2,1,0:T(8,128)}), f32[4,32,8,128]{3,2,1,0:T(8,128)S(1)}, u32[]{:S(2)}, u32[]{:S(2)}) async-start(f32[4,32,8,128]{3,2,1,0:T(8,128)} %broadcast_in_dim.2), calls=%async_computation.1 | async-start | bytes 1048576 | tf_op jit(solution)/shard_map/all_to_all | solution.py:461
  40.6 0.0 collective-permute-done.2.up_ref
  40.6 0.0 copy-start.9
  40.6 0.8 copy-done.9
  41.5 3.0 %collective-permute-done.3.down_ref = f32[3,104,512]{2,1,0:T(8,128)} collective-permute-done((f32[3,104,512]{2,1,0:T(8,128)S(1)}, f32[3,104,512]{2,1,0:T(8,128)}, u32[]{:S(2)}, u32[]{:S(2)}) %collective-permute-start.3) | collective-permute-done | bytes 639008 | tf_op jit(solution)/shard_map/ppermute | solution.py:388
  44.5 0.0 copy-start.12
  44.5 0.0 copy-start.13
  44.5 0.0 copy-done.11
  44.5 0.7 copy-done.12
  45.2 0.0 copy-done.13
  45.2 0.0 copy-start.10
  45.2 1.1 %copy-done.10 = f32[3,104,512]{2,1,0:T(8,128)S(1)} copy-done((f32[3,104,512]{2,1,0:T(8,128)S(1)}, f32[3,104,512]{2,1,0:T(8,128)}, u32[]{:S(2)}) %copy-start.10) | copy-done | bytes 639000
  46.3 0.0 copy-start
  46.3 0.0 copy-start.1
  46.3 0.0 copy-start.4
  46.3 0.0 copy-start.6
  46.3 29.7 %outside.1 = (f32[8,8,512]{2,1,0:T(8,128)S(1)}, f32[8,8,64]{2,1,0:T(8,128)S(1)}) custom-call(s32[68]{0:T(128)S(1)} %copy-done.12, s32[2]{0:T(128)S(1)} %copy-done.13, s32[8,8]{1,0:T(8,128)S(1)} %copy-done.11, f32[3,104,512]{2,1,0:T(8,128)S(1)} %pad_maximum_fusion.row_ref, f32[3,104,512]{2,1,0:T(8,128)S(1)} %copy-done.10, ...), custom_call_target="tpu_custom_call" | custom-call | flops 30000001024 | bytes 2097152 | tf_op jit(solution)/shard_map/outside/pallas_call | solution.py:468
  76.0 0.0 all-to-all-done.1
  76.0 0.0 copy-start.7
  76.0 0.0 copy-start.8
  76.1 0.0 copy-done
  76.1 0.0 copy-done.1
  76.1 0.0 copy-done.2
  76.1 0.0 copy-done.3
  76.1 0.0 copy-done.4
  76.1 0.0 copy-done.6
  76.1 0.6 copy-done.7
  76.7 0.0 copy-done.8
  76.7 6.2 %tail.1 = (f32[8,4096]{1,0:T(8,128)S(1)}, f32[128,128]{1,0:T(8,128)S(1)}) custom-call(s32[2]{0:T(128)S(1)} %pad_add_fusion.place_ref, f32[8]{0:T(128)S(1)} %copy-done.8, f32[8,8,512]{2,1,0:T(8,128)S(1)} %copy-done.4, f32[8,8,512]{2,1,0:T(8,128)S(1)} %get-tuple-element.25.near_ref, f32[8,8,64]{2,1,0:T(8,128)S(1)} %get-tuple-element.26.far_ref, ...), custom_call_target="tpu_custom_call" | custom-call | tf_op jit(solution)/shard_map/tail/pallas_call | solution.py:484
  82.9 0.0 copy-start.5
  82.9 19.0 %all_to_all.21 = f32[128,1,128]{2,1,0:T(1,128)S(1)} all-to-all(f32[128,1,128]{2,1,0:T(1,128)S(1)} %bitcast.16), channel_id=1, replica_groups=mesh['leaf'=32,'tm'=4] {'leaf','tm'}, dimensions={0} | all-to-all | bytes 131072 | tf_op jit(solution)/shard_map/all_to_all | solution.py:497
  101.9 0.0 copy-done.5
  101.9 0.8 update.1
  (3 shorter events, 0.0 us)
Async XLA Ops:
  6.2 22.8 %collective-permute-start = (f32[104,512]{1,0:T(8,128)}, f32[104,512]{1,0:T(8,128)S(1)}, u32[]{:S(2)}, u32[]{:S(2)}) collective-permute-start(f32[104,512]{1,0:T(8,128)} %get-tuple-element.17.halo_hbm), channel_id=1, source_target_pairs={{0,1},{1,2},{2,3},{4,5},{5,6},{6,7},{8,9},{9,10},{10,11},{12,13},{... | collective-permute-start | bytes 638984 | tf_op jit(solution)/shard_map/ppermute | solution.py:388
  10.2 18.9 %collective-permute-start.1 = (f32[104,512]{1,0:T(8,128)}, f32[104,512]{1,0:T(8,128)S(1)}, u32[]{:S(2)}, u32[]{:S(2)}) collective-permute-start(f32[104,512]{1,0:T(8,128)} %get-tuple-element.17.halo_hbm), channel_id=1, source_target_pairs={{1,0},{2,1},{3,2},{5,4},{6,5},{7,6},{9,8},{10,9},{11,10},{13,12},{... | collective-permute-start | bytes 638984 | tf_op jit(solution)/shard_map/ppermute | solution.py:388
  11.5 17.5 %all-to-all-start = ((f32[32,8,128]{2,1,0:T(8,128)}), f32[32,8,128]{2,1,0:T(8,128)S(1)}, u32[]{:S(2)}, u32[]{:S(2)}) async-start(f32[32,8,128]{2,1,0:T(8,128)} %get-tuple-element.19), calls=%async_computation | async-start | bytes 262144 | tf_op jit(solution)/shard_map/all_to_all | solution.py:438
  20.6 8.5 %copy-start.14 = (f32[104,512]{1,0:T(8,128)S(1)}, f32[104,512]{1,0:T(8,128)}, u32[]{:S(2)}) copy-start(f32[104,512]{1,0:T(8,128)} %get-tuple-element.17.halo_hbm) | copy-start | bytes 638980
  29.1 11.5 %collective-permute-start.2 = (f32[3,104,512]{2,1,0:T(8,128)S(1)}, f32[3,104,512]{2,1,0:T(8,128)S(1)}, u32[]{:S(2)}, u32[]{:S(2)}) collective-permute-start(f32[3,104,512]{2,1,0:T(8,128)S(1)} %pad_maximum_fusion.row_ref), channel_id=1, source_target_pairs={{0,4},{4,8},{8,12},{12,16},{16,20},{20,24},{24,28},{28,32},{32,36}... | collective-permute-start | bytes 1916936 | tf_op jit(solution)/shard_map/ppermute | solution.py:388
  32.5 12.0 %collective-permute-start.3 = (f32[3,104,512]{2,1,0:T(8,128)S(1)}, f32[3,104,512]{2,1,0:T(8,128)}, u32[]{:S(2)}, u32[]{:S(2)}) collective-permute-start(f32[3,104,512]{2,1,0:T(8,128)S(1)} %pad_maximum_fusion.row_ref), channel_id=1, source_target_pairs={{4,0},{8,4},{12,8},{16,12},{20,16},{24,20},{28,24},{32,28},{36,32}... | collective-permute-start | bytes 1916936 | tf_op jit(solution)/shard_map/ppermute | solution.py:388
  35.3 9.2 %copy-start.11 = (s32[8,8]{1,0:T(8,128)S(1)}, s32[8,8]{1,0:T(8,128)}, u32[]{:S(2)}) copy-start(s32[8,8]{1,0:T(8,128)} %far_ref.1) | copy-start | bytes 772
  35.3 40.7 %all-to-all-start.1 = ((f32[4,32,8,128]{3,2,1,0:T(8,128)}), f32[4,32,8,128]{3,2,1,0:T(8,128)S(1)}, u32[]{:S(2)}, u32[]{:S(2)}) async-start(f32[4,32,8,128]{3,2,1,0:T(8,128)} %broadcast_in_dim.2), calls=%async_computation.1 | async-start | bytes 1048576 | tf_op jit(solution)/shard_map/all_to_all | solution.py:461
  40.6 0.8 copy-start.9
  44.5 0.7 copy-start.12
  44.5 0.7 copy-start.13
  45.2 1.1 %copy-start.10 = (f32[3,104,512]{2,1,0:T(8,128)S(1)}, f32[3,104,512]{2,1,0:T(8,128)}, u32[]{:S(2)}) copy-start(f32[3,104,512]{2,1,0:T(8,128)} %copy-done.9) | copy-start | bytes 1916932
  46.3 29.8 %copy-start = (f32[8,64,512]{2,1,0:T(8,128)S(1)}, f32[8,64,512]{2,1,0:T(8,128)}, u32[]{:S(2)}) copy-start(f32[8,64,512]{2,1,0:T(8,128)} %bases_ref.1) | copy-start | bytes 3145732
  46.3 29.8 %copy-start.1 = (f32[8,4096]{1,0:T(8,128)S(1)}, f32[8,4096]{1,0:T(8,128)}, u32[]{:S(2)}) copy-start(f32[8,4096]{1,0:T(8,128)} %p_ref.3) | copy-start | bytes 393220
  46.3 29.8 %copy-start.2 = (f32[1,64,512]{2,1,0:T(8,128)S(1)}, f32[1,64,512]{2,1,0:T(8,128)}, u32[]{:S(2)}) copy-start(f32[1,64,512]{2,1,0:T(8,128)} %param.19) | copy-start | bytes 393220
  46.3 29.8 %copy-start.3 = (f32[8,4096]{1,0:T(8,128)S(1)}, f32[8,4096]{1,0:T(8,128)}, u32[]{:S(2)}) copy-start(f32[8,4096]{1,0:T(8,128)} %res_ref.3) | copy-start | bytes 393220
  46.3 29.8 %copy-start.4 = (f32[8,8,512]{2,1,0:T(8,128)S(1)}, f32[8,8,512]{2,1,0:T(8,128)}, u32[]{:S(2)}) copy-start(f32[8,8,512]{2,1,0:T(8,128)} %get-tuple-element.20.inside_ref) | copy-start | bytes 393220
  46.3 29.8 %copy-start.6 = (s32[32,128]{1,0:T(8,128)S(1)}, s32[32,128]{1,0:T(8,128)}, u32[]{:S(2)}) copy-start(s32[32,128]{1,0:T(8,128)} %get-tuple-element.29.inv_ref) | copy-start | bytes 49156
  76.0 0.7 copy-start.7
  76.0 0.7 copy-start.8
  82.9 19.0 %copy-start.5 = (f32[8,4096]{1,0:T(8,128)S(1)}, f32[8,4096]{1,0:T(8,128)}, u32[]{:S(2)}) copy-start(f32[8,4096]{1,0:T(8,128)} %it_ref.1) | copy-start | bytes 393220

commit v11 on v10

--- a/solution.py
+++ b/solution.py
@@ -109,7 +109,7 @@
     return picked * UNIT
 
 
-def gather_body(scale_hbm, order_hbm, x_hbm, p_hbm, bases_hbm, transfer_hbm, skel_hbm, halo_ref, node_ref, own_ref, scale_ref, order_ref, xx, p_ref, bases_ref, transfer_ref, skel_ref, slot, sems):
+def gather_body(scale_hbm, order_hbm, x_hbm, p_hbm, bases_hbm, transfer_hbm, skel_hbm, halo_ref, own_ref, scale_ref, order_ref, xx, p_ref, bases_ref, transfer_ref, skel_ref, slot, sems):
     leaf_dev, rank, leaf_pts = bases_ref.shape
     points = p_ref.shape[1]
     chunks = points // 128
@@ -158,7 +158,6 @@
     (node_x,) = gather_lanes([slots], jnp.broadcast_to(ids, (8, 128)))
     tile = jnp.concatenate([weights, node_x[:, :rank]], axis=1)
     own_ref[...] = tile
-    node_ref[...] = jnp.broadcast_to(tile[None], node_ref.shape)
 
 
 def place_of(order_ref):
@@ -274,14 +273,15 @@
     near_pairs(pairs, n, 4 * leaf_dev, src, tgt, wgt, out_ref, z, high, low)
 
 
-def node_field(leaf_size, place_ref, node_ref, own_ref, transfer_ref, node_src, node_wgt):
+def node_field(cores, columns, place_ref, node_ref, own_ref, transfer_ref, node_src, node_wgt):
     devices = node_ref.shape[0]
     rank = own_ref.shape[1] // 2
     lane = lane_ids((8, 128))
 
     def distant(e):
-        far_a = jnp.abs(e % leaf_size - place_ref[0]) > 1
-        far_b = jnp.abs(e // leaf_size - place_ref[1]) > 1
+        leaf = e // (cores * columns) * cores + e % cores
+        far_a = jnp.abs(leaf - place_ref[0]) > 1
+        far_b = jnp.abs(e // cores % columns - place_ref[1]) > 1
         return jnp.where(far_a | far_b, FACTOR, 0.0)
 
     def unpack(g, _):
@@ -334,9 +334,9 @@
         far_out_ref[leaf] = far[:8] + far[8:]
 
 
-def tail_body(leaf_size, place_ref, noise_ref, inside_ref, near_ref, far_ref, node_ref, own_ref, transfer_ref, bases_ref, inv_ref, p_ref, res_ref, image_ref, sums_ref, flat, node_src, node_wgt):
+def tail_body(cores, columns, place_ref, noise_ref, inside_ref, near_ref, far_ref, node_ref, own_ref, transfer_ref, bases_ref, inv_ref, p_ref, res_ref, image_ref, sums_ref, flat, node_src, node_wgt):
     leaf_dev, rank, leaf_pts = bases_ref.shape
-    pushed = node_field(leaf_size, place_ref, node_ref, own_ref, transfer_ref, node_src, node_wgt)
+    pushed = node_field(cores, columns, place_ref, node_ref, own_ref, transfer_ref, node_src, node_wgt)
     for leaf in range(leaf_dev):
         incoming = halves(far_ref[leaf] + pushed[:, leaf * rank : (leaf + 1) * rank])
         base_high, base_low = split(bases_ref[leaf])
@@ -384,27 +384,25 @@
 
 
 def shifted(x, axis, by):
-    n = lax.axis_size(axis)
+    n = math.prod(lax.axis_size(part) for part in axis)
     return lax.ppermute(x, axis, [(i, i + by) for i in range(n) if 0 <= i + by < n])
 
 
 def shards(coords, direction, iterate, residual, order, bases, transfer, near_list, near_count, far_list, device_skel, inv_scale, noise):
     leaf_dev, rank, leaf_pts = bases.shape
     rhs, points = direction.shape
-    axes = ("leaf", "tm")
-    devices = lax.axis_size("leaf") * lax.axis_size("tm")
+    axes = ("chip", "core", "tm")
+    leaf_axes = ("chip", "core")
+    chips, cores, columns = (lax.axis_size(axis) for axis in axes)
+    devices = chips * cores * columns
     chunks = points // 128
     shape = jax.ShapeDtypeStruct
     by_row = order.reshape(chunks, 128)
-    halo, node, own = pl.pallas_call(
+    halo, own = pl.pallas_call(
         gather_body,
         in_specs=[ANY] * 7,
-        out_specs=[VMEM] * 3,
-        out_shape=[
-            shape((13 * leaf_dev, leaf_pts), F32),
-            shape((lax.axis_size("leaf"), 8, 128), F32),
-            shape((8, 128), F32),
-        ],
+        out_specs=[VMEM] * 2,
+        out_shape=[shape((13 * leaf_dev, leaf_pts), F32), shape((8, 128), F32)],
         scratch_shapes=[
             pltpu.SMEM(inv_scale.shape, F32),
             pltpu.VMEM((chunks, 128), jnp.int32),
@@ -419,8 +417,8 @@
         compiler_params=params(60),
         name="gather",
     )(inv_scale, by_row, coords, direction, bases, transfer[0], device_skel)
-    left = shifted(halo, "tm", 1)
-    right = shifted(halo, "tm", -1)
+    left = shifted(halo, ("tm",), 1)
+    right = shifted(halo, ("tm",), -1)
 
     def pipeline(sources):
         return [
@@ -435,7 +433,7 @@
         pltpu.VMEM((2, PART, leaf_pts), BF16),
     ]
     entries = near_list.size + 4
-    column = lax.all_to_all(node, "leaf", 0, 0)
+    other = lax.ppermute(own, "core", [(i, cores - 1 - i) for i in range(cores)])
     inside, inverse, pairs, sizes = pl.pallas_call(
         inside_body,
         in_specs=[SMEM] * 2 + [ANY] + [VMEM],
@@ -457,13 +455,15 @@
         cost_estimate=pl.CostEstimate(flops=10**10, bytes_accessed=2**21, transcendentals=10**7),
         name="inside",
     )(near_list, near_count, halo, by_row)
-    left, right, inside, column = lax.optimization_barrier((left, right, inside, column))
-    nodes = lax.all_to_all(jnp.broadcast_to(column[None], (lax.axis_size("tm"),) + column.shape), "tm", 0, 0)
+    left, right, inside, other = lax.optimization_barrier((left, right, inside, other))
+    core = lax.axis_index("core")
+    both = jnp.stack([jnp.where(core == 0, own, other), jnp.where(core == 0, other, own)])
+    nodes = lax.all_to_all(jnp.broadcast_to(both[None], (chips * columns,) + both.shape), ("chip", "tm"), 0, 0)
     nodes = nodes.reshape(devices, 8, 128)
     row = jnp.stack([left, halo, right])
-    up = shifted(row, "leaf", 1)
-    down = shifted(row, "leaf", -1)
-    place = jnp.stack([lax.axis_index("leaf"), lax.axis_index("tm")]).astype(jnp.int32)
+    up = shifted(row, leaf_axes, 1)
+    down = shifted(row, leaf_axes, -1)
+    place = jnp.stack([lax.axis_index(leaf_axes), lax.axis_index("tm")]).astype(jnp.int32)
 
     near, far = pl.pallas_call(
         outside_body,
@@ -482,7 +482,7 @@
         name="outside",
     )(pairs, sizes, far_list, row, up, down)
     image, sums = pl.pallas_call(
-        functools.partial(tail_body, lax.axis_size("leaf")),
+        functools.partial(tail_body, cores, columns),
         in_specs=[SMEM] * 2 + [VMEM] * 10,
         out_specs=[VMEM] * 2,
         out_shape=[shape((rhs, points), F32), shape((devices, 128), F32)],
@@ -506,11 +506,13 @@
 
 
 def solution(mesh):
-    whole = P(None, ("leaf", "tm"))
-    first = P(("leaf", "tm"))
+    leaf, columns = mesh.devices.shape
+    finer = jax.sharding.Mesh(mesh.devices.reshape(leaf // 2, 2, columns), ("chip", "core", "tm"))
+    whole = P(None, ("chip", "core", "tm"))
+    first = P(("chip", "core", "tm"))
     return jax.shard_map(
         shards,
-        mesh=mesh,
+        mesh=finer,
         in_specs=(whole,) * 4 + (first,) * 7 + (P(), P()),
         out_specs=(whole, whole),
         check_vma=False,

time: 104 us -> 100 us (0.962); the launches traced: 103 us -> 99.9 us
  blocking collectives: 19 us -> 29.7 us
  Pallas kernels: 50.7 us -> 40.6 us
  waiting for transfers between devices: 3.05 us -> 0.02 us
    all_to_all x1, blocking collectives: 19 us -> 29.7 us  [shards(): all_sums = lax.all_to_all(sums, axes, 0, 0, tiled=True)]
    pallas_call x1, Pallas kernels: 29.7 us -> 19.2 us  [shards(): pl.pallas_call(outside_body, in_specs=[SMEM] * 3 + [VMEM] * 3, out_specs=...]
    ppermute x4, waiting for transfers between devices: 3.04 us -> 0.01 us  [shifted(): lax.ppermute(x, axis, [(i, i + by) for i in range(n) if 0 <= i + by < n])]
    all_to_all x2 -> x1, starting transfers between devices: 14.4 us -> 12.6 us  [shards(): lax.all_to_all(jnp.broadcast_to(both[None], (chips * columns,) + both.sha...]
  transfers between devices with their start and end apart: 6 -> 6, of which waited for: 1 -> 0; matrix products, arithmetic and copies ran while one was open for 1% -> 1% of each run, Pallas kernels for 37% -> 27%
where the time goes in v11:
time: 100 us; the launch traced here: 99.9 us
  Pallas kernels  40.6 us (41%)
  blocking collectives  29.7 us (30%)
  starting transfers between devices  23.9 us (24%)
  local copies, waits for them, and re-layouts  4.65 us (5%)
    all_to_all x1, blocking collectives, shards(): all_sums = lax.all_to_all(sums, axes, 0, 0, tiled=True)  29.7 us
    pallas_call x1, Pallas kernels, shards(): pl.pallas_call(outside_body, in_specs=[SMEM] * 3 + [VMEM] * 3, out_specs=...  19.2 us
    all_to_all x1, starting transfers between devices, shards(): lax.all_to_all(jnp.broadcast_to(both[None], (chips * columns,) + both.sha...  12.6 us
    ppermute x4, starting transfers between devices, shifted(): lax.ppermute(x, axis, [(i, i + by) for i in range(n) if 0 <= i + by < n])  10.3 us
    pallas_call x1, Pallas kernels, shards(): pl.pallas_call(inside_body, in_specs=[SMEM] * 2 + [ANY] + [VMEM], out_spe...  8.12 us
    pallas_call x1, Pallas kernels, shards(): pl.pallas_call(functools.partial(tail_body, cores, columns), in_specs=[SM...  6.96 us
    pallas_call x1, Pallas kernels, shards(): pl.pallas_call(gather_body, in_specs=[ANY] * 7, out_specs=[VMEM] * 2, out...  5.52 us
    unnamed x30, local copies, waits for them, and re-layouts  3.82 us
  transfers between devices with their start and end apart: 6, of which 0 were waited for; matrix products, arithmetic and copies ran while one was open for 1% of the time, Pallas kernels for 27%

profile of v11, /device:TPU:1, one launch (start us, length us, event | category | flops | bytes accessed | tf_op | source)
XLA Modules:
  0.0 99.9 jit_solution(11652695576323003125)
XLA Ops:
  0.6 5.5 %gather.1 = (f32[104,512]{1,0:T(8,128)}, f32[8,128]{1,0:T(8,128)}) custom-call(f32[4]{0:T(128)} %scale_hbm.1, s32[32,128]{1,0:T(8,128)} %bitcast.24, f32[4,4096]{1,0:T(4,128)} %x_hbm.1, f32[8,4096]{1,0:T(8,128)} %p_ref.3, f32[8,64,512]{2,1,0:T(8,128)} %bases_ref.1, f32[64,512]{1,0:T(8,128)} %bitcast.17, s32[1,64]{1,0:T(1,128)} %skel_hbm.1), custom_call_target="tpu_custom_call" | custom-call | tf_op jit(solution)/shard_map/gather/pallas_call | solution.py:401
  6.2 4.0 %collective-permute-start = (f32[104,512]{1,0:T(8,128)}, f32[104,512]{1,0:T(8,128)S(1)}, u32[]{:S(2)}, u32[]{:S(2)}) collective-permute-start(f32[104,512]{1,0:T(8,128)} %get-tuple-element.16.halo_hbm), channel_id=1, source_target_pairs={{0,1},{1,2},{2,3},{4,5},{5,6},{6,7},{8,9},{9,10},{10,11},{12,13},{... | collective-permute-start | bytes 638984 | tf_op jit(solution)/shard_map/ppermute | solution.py:388
  10.1 1.3 %collective-permute-start.1 = (f32[104,512]{1,0:T(8,128)}, f32[104,512]{1,0:T(8,128)S(1)}, u32[]{:S(2)}, u32[]{:S(2)}) collective-permute-start(f32[104,512]{1,0:T(8,128)} %get-tuple-element.16.halo_hbm), channel_id=1, source_target_pairs={{1,0},{2,1},{3,2},{5,4},{6,5},{7,6},{9,8},{10,9},{11,10},{13,12},{... | collective-permute-start | bytes 638984 | tf_op jit(solution)/shard_map/ppermute | solution.py:388
  11.4 0.0 copy-start.14
  11.4 1.0 %collective-permute-start.2 = (f32[8,128]{1,0:T(8,128)}, f32[8,128]{1,0:T(8,128)S(1)}, u32[]{:S(2)}, u32[]{:S(2)}) collective-permute-start(f32[8,128]{1,0:T(8,128)} %get-tuple-element.18.own_ref), channel_id=1, source_target_pairs={{0,4},{4,0},{1,5},{5,1},{2,6},{6,2},{3,7},{7,3},{8,12},{12,8},{9,1... | collective-permute-start | bytes 12296 | tf_op jit(solution)/shard_map/ppermute | solution.py:436
  12.5 8.1 %inside.1 = (f32[8,8,512]{2,1,0:T(8,128)}, s32[32,128]{1,0:T(8,128)}, s32[68]{0:T(128)}, s32[2]{0:T(128)}) custom-call(s32[8,8]{1,0:T(8,128)} %near_ref.1, s32[8]{0:T(128)} %count_ref.1, f32[104,512]{1,0:T(8,128)} %get-tuple-element.16.halo_hbm, s32[32,128]{1,0:T(8,128)} %bitcast.25), custom_call_target="tpu_custom_call" | custom-call | flops 10000000000 | bytes 2097152 | tf_op jit(solution)/shard_map/inside/pallas_call | solution.py:437
  20.6 0.0 collective-permute-done.2
  20.6 0.0 collective-permute-done
  20.6 0.0 collective-permute-done.1
  20.6 0.0 copy-done.14
  20.7 3.1 %collective-permute-start.3 = (f32[3,104,512]{2,1,0:T(8,128)S(1)}, f32[3,104,512]{2,1,0:T(8,128)S(1)}, u32[]{:S(2)}, u32[]{:S(2)}) collective-permute-start(f32[3,104,512]{2,1,0:T(8,128)S(1)} %pad_maximum_fusion.row_ref), channel_id=1, source_target_pairs={{0,4},{4,8},{8,12},{12,16},{16,20},{20,24},{24,28},{28,32},{32,36}... | collective-permute-start | bytes 1916936 | tf_op jit(solution)/shard_map/ppermute | solution.py:388
  23.8 1.9 %collective-permute-start.4 = (f32[3,104,512]{2,1,0:T(8,128)S(1)}, f32[3,104,512]{2,1,0:T(8,128)}, u32[]{:S(2)}, u32[]{:S(2)}) collective-permute-start(f32[3,104,512]{2,1,0:T(8,128)S(1)} %pad_maximum_fusion.row_ref), channel_id=1, source_target_pairs={{4,0},{8,4},{12,8},{16,12},{20,16},{24,20},{28,24},{32,28},{36,32}... | collective-permute-start | bytes 1916936 | tf_op jit(solution)/shard_map/ppermute | solution.py:388
  25.7 0.0 copy-start.7
  25.7 0.1 pad_add_fusion.place_ref
  25.8 0.6 copy-done.7
  26.4 0.8 broadcast_in_dim.2
  27.3 0.0 copy-start.11
  27.3 12.6 %all-to-all-start = ((f32[64,2,8,128]{3,2,1,0:T(8,128)}), f32[64,2,8,128]{3,2,1,0:T(8,128)S(1)}, u32[]{:S(2)}, u32[]{:S(2)}) async-start(f32[64,2,8,128]{3,2,1,0:T(8,128)} %broadcast_in_dim.2), calls=%async_computation | async-start | bytes 1048576 | tf_op jit(solution)/shard_map/all_to_all | solution.py:461
  39.8 0.0 collective-permute-done.3.up_ref
  39.8 0.0 copy-start.9
  39.8 0.8 copy-done.9
  40.7 0.0 collective-permute-done.4.down_ref
  40.7 0.0 copy-start.12
  40.7 0.0 copy-start.13
  40.7 0.0 copy-done.11
  40.7 0.7 copy-done.12
  41.4 0.0 copy-done.13
  41.4 0.0 copy-start.10
  41.4 1.1 %copy-done.10 = f32[3,104,512]{2,1,0:T(8,128)S(1)} copy-done((f32[3,104,512]{2,1,0:T(8,128)S(1)}, f32[3,104,512]{2,1,0:T(8,128)}, u32[]{:S(2)}) %copy-start.10) | copy-done | bytes 639000
  42.4 0.0 copy-start
  42.4 0.0 copy-start.1
  42.4 0.0 copy-start.4
  42.5 0.0 copy-start.6
  42.5 19.2 %outside.1 = (f32[8,8,512]{2,1,0:T(8,128)S(1)}, f32[8,8,64]{2,1,0:T(8,128)S(1)}) custom-call(s32[68]{0:T(128)S(1)} %copy-done.12, s32[2]{0:T(128)S(1)} %copy-done.13, s32[8,8]{1,0:T(8,128)S(1)} %copy-done.11, f32[3,104,512]{2,1,0:T(8,128)S(1)} %pad_maximum_fusion.row_ref, f32[3,104,512]{2,1,0:T(8,128)S(1)} %copy-done.10, ...), custom_call_target="tpu_custom_call" | custom-call | flops 30000001024 | bytes 2097152 | tf_op jit(solution)/shard_map/outside/pallas_call | solution.py:468
  61.7 0.0 all-to-all-done
  61.7 0.0 copy-start.8
  61.7 0.0 copy-done
  61.7 0.0 copy-done.1
  61.7 0.0 copy-done.2
  61.7 0.0 copy-done.3
  61.7 0.0 copy-done.4
  61.7 0.0 copy-done.6
  61.8 0.6 copy-done.8
  62.3 7.0 %tail.1 = (f32[8,4096]{1,0:T(8,128)S(1)}, f32[128,128]{1,0:T(8,128)S(1)}) custom-call(s32[2]{0:T(128)S(1)} %pad_add_fusion.place_ref, f32[8]{0:T(128)S(1)} %copy-done.8, f32[8,8,512]{2,1,0:T(8,128)S(1)} %copy-done.4, f32[8,8,512]{2,1,0:T(8,128)S(1)} %get-tuple-element.24.near_ref, f32[8,8,64]{2,1,0:T(8,128)S(1)} %get-tuple-element.25.far_ref, ...), custom_call_target="tpu_custom_call" | custom-call | tf_op jit(solution)/shard_map/tail/pallas_call | solution.py:484
  69.3 0.0 copy-start.5
  69.3 29.7 %all_to_all.16 = f32[128,1,128]{2,1,0:T(1,128)S(1)} all-to-all(f32[128,1,128]{2,1,0:T(1,128)S(1)} %bitcast.20), channel_id=1, replica_groups=mesh['chip'=16,'core'=2,'tm'=4] {'chip','core','tm'}, dimensions={0} | all-to-all | bytes 131072 | tf_op jit(solution)/shard_map/all_to_all | solution.py:497
  99.1 0.0 copy-done.5
  99.1 0.8 update.1
  (5 shorter events, 0.1 us)
Async XLA Ops:
  6.2 14.4 %collective-permute-start = (f32[104,512]{1,0:T(8,128)}, f32[104,512]{1,0:T(8,128)S(1)}, u32[]{:S(2)}, u32[]{:S(2)}) collective-permute-start(f32[104,512]{1,0:T(8,128)} %get-tuple-element.16.halo_hbm), channel_id=1, source_target_pairs={{0,1},{1,2},{2,3},{4,5},{5,6},{6,7},{8,9},{9,10},{10,11},{12,13},{... | collective-permute-start | bytes 638984 | tf_op jit(solution)/shard_map/ppermute | solution.py:388
  10.1 10.5 %collective-permute-start.1 = (f32[104,512]{1,0:T(8,128)}, f32[104,512]{1,0:T(8,128)S(1)}, u32[]{:S(2)}, u32[]{:S(2)}) collective-permute-start(f32[104,512]{1,0:T(8,128)} %get-tuple-element.16.halo_hbm), channel_id=1, source_target_pairs={{1,0},{2,1},{3,2},{5,4},{6,5},{7,6},{9,8},{10,9},{11,10},{13,12},{... | collective-permute-start | bytes 638984 | tf_op jit(solution)/shard_map/ppermute | solution.py:388
  11.4 9.2 %copy-start.14 = (f32[104,512]{1,0:T(8,128)S(1)}, f32[104,512]{1,0:T(8,128)}, u32[]{:S(2)}) copy-start(f32[104,512]{1,0:T(8,128)} %get-tuple-element.16.halo_hbm) | copy-start | bytes 638980
  11.4 9.2 %collective-permute-start.2 = (f32[8,128]{1,0:T(8,128)}, f32[8,128]{1,0:T(8,128)S(1)}, u32[]{:S(2)}, u32[]{:S(2)}) collective-permute-start(f32[8,128]{1,0:T(8,128)} %get-tuple-element.18.own_ref), channel_id=1, source_target_pairs={{0,4},{4,0},{1,5},{5,1},{2,6},{6,2},{3,7},{7,3},{8,12},{12,8},{9,1... | collective-permute-start | bytes 12296 | tf_op jit(solution)/shard_map/ppermute | solution.py:436
  20.7 19.1 %collective-permute-start.3 = (f32[3,104,512]{2,1,0:T(8,128)S(1)}, f32[3,104,512]{2,1,0:T(8,128)S(1)}, u32[]{:S(2)}, u32[]{:S(2)}) collective-permute-start(f32[3,104,512]{2,1,0:T(8,128)S(1)} %pad_maximum_fusion.row_ref), channel_id=1, source_target_pairs={{0,4},{4,8},{8,12},{12,16},{16,20},{20,24},{24,28},{28,32},{32,36}... | collective-permute-start | bytes 1916936 | tf_op jit(solution)/shard_map/ppermute | solution.py:388
  23.8 16.9 %collective-permute-start.4 = (f32[3,104,512]{2,1,0:T(8,128)S(1)}, f32[3,104,512]{2,1,0:T(8,128)}, u32[]{:S(2)}, u32[]{:S(2)}) collective-permute-start(f32[3,104,512]{2,1,0:T(8,128)S(1)} %pad_maximum_fusion.row_ref), channel_id=1, source_target_pairs={{4,0},{8,4},{12,8},{16,12},{20,16},{24,20},{28,24},{32,28},{36,32}... | collective-permute-start | bytes 1916936 | tf_op jit(solution)/shard_map/ppermute | solution.py:388
  25.7 0.7 copy-start.7
  27.3 13.4 %copy-start.11 = (s32[8,8]{1,0:T(8,128)S(1)}, s32[8,8]{1,0:T(8,128)}, u32[]{:S(2)}) copy-start(s32[8,8]{1,0:T(8,128)} %far_ref.1) | copy-start | bytes 772
  27.3 34.4 %all-to-all-start = ((f32[64,2,8,128]{3,2,1,0:T(8,128)}), f32[64,2,8,128]{3,2,1,0:T(8,128)S(1)}, u32[]{:S(2)}, u32[]{:S(2)}) async-start(f32[64,2,8,128]{3,2,1,0:T(8,128)} %broadcast_in_dim.2), calls=%async_computation | async-start | bytes 1048576 | tf_op jit(solution)/shard_map/all_to_all | solution.py:461
  39.8 0.8 copy-start.9
  40.7 0.7 copy-start.12
  40.7 0.7 copy-start.13
  41.4 1.1 %copy-start.10 = (f32[3,104,512]{2,1,0:T(8,128)S(1)}, f32[3,104,512]{2,1,0:T(8,128)}, u32[]{:S(2)}) copy-start(f32[3,104,512]{2,1,0:T(8,128)} %copy-done.9) | copy-start | bytes 1916932
  42.4 19.3 %copy-start = (f32[8,64,512]{2,1,0:T(8,128)S(1)}, f32[8,64,512]{2,1,0:T(8,128)}, u32[]{:S(2)}) copy-start(f32[8,64,512]{2,1,0:T(8,128)} %bases_ref.1) | copy-start | bytes 3145732
  42.4 19.3 %copy-start.1 = (f32[8,4096]{1,0:T(8,128)S(1)}, f32[8,4096]{1,0:T(8,128)}, u32[]{:S(2)}) copy-start(f32[8,4096]{1,0:T(8,128)} %p_ref.3) | copy-start | bytes 393220
  42.4 19.3 %copy-start.2 = (f32[1,64,512]{2,1,0:T(8,128)S(1)}, f32[1,64,512]{2,1,0:T(8,128)}, u32[]{:S(2)}) copy-start(f32[1,64,512]{2,1,0:T(8,128)} %param.19) | copy-start | bytes 393220
  42.4 19.3 %copy-start.3 = (f32[8,4096]{1,0:T(8,128)S(1)}, f32[8,4096]{1,0:T(8,128)}, u32[]{:S(2)}) copy-start(f32[8,4096]{1,0:T(8,128)} %res_ref.3) | copy-start | bytes 393220
  42.4 19.3 %copy-start.4 = (f32[8,8,512]{2,1,0:T(8,128)S(1)}, f32[8,8,512]{2,1,0:T(8,128)}, u32[]{:S(2)}) copy-start(f32[8,8,512]{2,1,0:T(8,128)} %get-tuple-element.19.inside_ref) | copy-start | bytes 393220
  42.5 19.3 %copy-start.6 = (s32[32,128]{1,0:T(8,128)S(1)}, s32[32,128]{1,0:T(8,128)}, u32[]{:S(2)}) copy-start(s32[32,128]{1,0:T(8,128)} %get-tuple-element.27.inv_ref) | copy-start | bytes 49156
  61.7 0.7 copy-start.8
  69.3 29.7 %copy-start.5 = (f32[8,4096]{1,0:T(8,128)S(1)}, f32[8,4096]{1,0:T(8,128)}, u32[]{:S(2)}) copy-start(f32[8,4096]{1,0:T(8,128)} %it_ref.1) | copy-start | bytes 393220

commit v12 on v11

--- a/solution.py
+++ b/solution.py
@@ -194,27 +194,25 @@
                 coef[base + leaf] = halves(ref[96:104, leaf * rank : (leaf + 1) * rank] * FACTOR)
 
 
-def list_pairs(near_ref, count_ref, inside, outside, sizes):
+def lists_body(near_ref, count_ref, order_ref, inv_ref, inside_ref, outside_ref, sizes_ref):
     leaf_dev, slots = near_ref.shape
 
     def leaf_step(leaf, sums):
         def entry(j, sums):
             w = near_ref[leaf, j]
             here = jnp.where((w // leaf_dev == 4) & (sums[0] < FIRST_PAIRS), 1, 0)
-            code = leaf * 128 + w
-            inside[sums[0]] = code
-            outside[sums[1]] = code
+            inside_ref[sums[0]] = leaf * 128 + w
+            outside_ref[sums[1]] = leaf * 128 + w
             return sums[0] + here, sums[1] + 1 - here
 
         return lax.fori_loop(0, count_ref[leaf], entry, sums)
 
     sums = lax.fori_loop(0, leaf_dev, leaf_step, (0, 0))
-    idle = 9 * leaf_dev
     for extra in range(3):
-        inside[sums[0] + extra] = idle
-        outside[sums[1] + extra] = idle
-    sizes[0], sizes[1] = sums
-    return sums[0]
+        inside_ref[sums[0] + extra] = 5 * leaf_dev
+        outside_ref[sums[1] + extra] = 9 * leaf_dev
+    sizes_ref[0], sizes_ref[1] = sums
+    inv_ref[...] = place_of(order_ref)
 
 
 def near_pairs(pairs, n, first, src, tgt, wgt, out, z, high, low):
@@ -257,20 +255,13 @@
     lax.fori_loop(0, (n + 1) // 2, two_pairs, 0)
 
 
-def inside_body(near_ref, count_ref, halo_hbm, order_ref, out_ref, inv_ref, pairs_ref, sizes_ref, pairs, halo_ref, src, tgt, wgt, z, high, low, sem):
-    leaf_dev, rhs, leaf_pts = out_ref.shape
-    move = pltpu.make_async_copy(halo_hbm, halo_ref, sem)
-    move.start()
-    n = list_pairs(near_ref, count_ref, pairs, pairs_ref, sizes_ref)
-    for extra in range(3):
-        pairs[n + extra] = 5 * leaf_dev
+def inside_body(pairs_ref, sizes_ref, halo_ref, out_ref, src, tgt, wgt, z, high, low):
+    leaf_dev = out_ref.shape[0]
     src[leaf_dev] = jnp.zeros(src.shape[1:], BF16)
     wgt[leaf_dev] = jnp.zeros(wgt.shape[1:], BF16)
+    prepare(halo_ref, 0, src, wgt, tgt)
     out_ref[...] = jnp.zeros_like(out_ref)
-    move.wait()
-    inv_ref[...] = place_of(order_ref)
-    prepare(halo_ref, 0, src, wgt, tgt)
-    near_pairs(pairs, n, 4 * leaf_dev, src, tgt, wgt, out_ref, z, high, low)
+    near_pairs(pairs_ref, sizes_ref[0], 4 * leaf_dev, src, tgt, wgt, out_ref, z, high, low)
 
 
 def node_field(cores, columns, place_ref, node_ref, own_ref, transfer_ref, node_src, node_wgt):
@@ -278,25 +269,25 @@
     rank = own_ref.shape[1] // 2
     lane = lane_ids((8, 128))
 
-    def distant(e):
-        leaf = e // (cores * columns) * cores + e % cores
-        far_a = jnp.abs(leaf - place_ref[0]) > 1
-        far_b = jnp.abs(e // cores % columns - place_ref[1]) > 1
+    def distant(chip, core, column):
+        far_a = jnp.abs(chip * cores + core - place_ref[0]) > 1
+        far_b = jnp.abs(column - place_ref[1]) > 1
         return jnp.where(far_a | far_b, FACTOR, 0.0)
 
-    def unpack(g, _):
+    width = columns * cores * rank
+
+    def unpack(chip, _):
         xs, ws = [], []
-        for k in range(4):
-            e = 8 * g + 2 * k
-            one, two = node_ref[e], node_ref[e + 1]
+        for column in range(columns):
+            one, two = (node_ref[(chip * columns + column) * cores + core] for core in range(2))
             xs.append(jnp.where(lane < rank, pltpu.roll(one, rank, 1), two))
-            ws.append(jnp.where(lane < rank, one * distant(e), pltpu.roll(two, rank, 1) * distant(e + 1)))
-        at = pl.ds(pl.multiple_of(g * 512, 512), 512)
+            ws.append(jnp.where(lane < rank, one * distant(chip, 0, column), pltpu.roll(two, rank, 1) * distant(chip, 1, column)))
+        at = pl.ds(pl.multiple_of(chip * width, width), width)
         node_src[:, at] = features(jnp.concatenate(xs, axis=1), True, False)[0]
         node_wgt[:, at] = halves(jnp.concatenate(ws, axis=1))
         return 0
 
-    lax.fori_loop(0, devices // 8, unpack, 0, unroll=4)
+    lax.fori_loop(0, devices // (cores * columns), unpack, 0, unroll=4)
     own_xx = pltpu.roll(own_ref[...], rank, 1)
     target = features(own_xx, False, True)[0][:, :rank]
     total = jnp.zeros((16, rank), F32)
@@ -434,35 +425,39 @@
     ]
     entries = near_list.size + 4
     other = lax.ppermute(own, "core", [(i, cores - 1 - i) for i in range(cores)])
-    inside, inverse, pairs, sizes = pl.pallas_call(
-        inside_body,
-        in_specs=[SMEM] * 2 + [ANY] + [VMEM],
-        out_specs=[VMEM] * 2 + [SMEM] * 2,
-        out_shape=[
-            shape((leaf_dev, rhs, leaf_pts), F32),
-            shape((chunks, 128), jnp.int32),
-            shape((entries,), jnp.int32),
-            shape((2,), jnp.int32),
-        ],
-        scratch_shapes=[
-            pltpu.SMEM((entries,), jnp.int32),
-            pltpu.VMEM(halo.shape, F32),
-        ]
-        + pipeline(leaf_dev)
-        + buffers
-        + [pltpu.SemaphoreType.DMA(())],
-        compiler_params=params(58),
-        cost_estimate=pl.CostEstimate(flops=10**10, bytes_accessed=2**21, transcendentals=10**7),
-        name="inside",
-    )(near_list, near_count, halo, by_row)
-    left, right, inside, other = lax.optimization_barrier((left, right, inside, other))
     core = lax.axis_index("core")
     both = jnp.stack([jnp.where(core == 0, own, other), jnp.where(core == 0, other, own)])
     nodes = lax.all_to_all(jnp.broadcast_to(both[None], (chips * columns,) + both.shape), ("chip", "tm"), 0, 0)
     nodes = nodes.reshape(devices, 8, 128)
+    inverse, pairs, others, sizes = pl.pallas_call(
+        lists_body,
+        in_specs=[SMEM] * 2 + [VMEM],
+        out_specs=[VMEM] + [SMEM] * 3,
+        out_shape=[
+            shape((chunks, 128), jnp.int32),
+            shape((entries,), jnp.int32),
+            shape((entries,), jnp.int32),
+            shape((2,), jnp.int32),
+        ],
+        compiler_params=params(8),
+        cost_estimate=pl.CostEstimate(flops=10**10, bytes_accessed=2**21, transcendentals=10**7),
+        name="lists",
+    )(near_list, near_count, by_row)
+    left, right, nodes, pairs, halo = lax.optimization_barrier((left, right, nodes, pairs, halo))
     row = jnp.stack([left, halo, right])
     up = shifted(row, leaf_axes, 1)
     down = shifted(row, leaf_axes, -1)
+    inside = pl.pallas_call(
+        inside_body,
+        in_specs=[SMEM] * 2 + [VMEM],
+        out_specs=VMEM,
+        out_shape=shape((leaf_dev, rhs, leaf_pts), F32),
+        scratch_shapes=pipeline(leaf_dev) + buffers,
+        compiler_params=params(14),
+        cost_estimate=pl.CostEstimate(flops=10**10, bytes_accessed=2**21, transcendentals=10**7),
+        name="inside",
+    )(pairs, sizes, halo)
+    up, down, inside = lax.optimization_barrier((up, down, inside))
     place = jnp.stack([lax.axis_index(leaf_axes), lax.axis_index("tm")]).astype(jnp.int32)
 
     near, far = pl.pallas_call(
@@ -480,7 +475,7 @@
         compiler_params=params(14),
         cost_estimate=pl.CostEstimate(flops=3 * 10**10, bytes_accessed=2**21, transcendentals=3 * 10**7),
         name="outside",
-    )(pairs, sizes, far_list, row, up, down)
+    )(others, sizes, far_list, row, up, down)
     image, sums = pl.pallas_call(
         functools.partial(tail_body, cores, columns),
         in_specs=[SMEM] * 2 + [VMEM] * 10,

time: 100 us -> 105 us (1.050)
  waiting for transfers between devices: 0.02 us -> 11 us
  blocking collectives: 29.7 us -> 24.9 us
  local copies, waits for them, and re-layouts: 4.65 us -> 2.18 us
    all_to_all x1, waiting for transfers between devices: 0.01 us -> 9.56 us  [shards(): lax.all_to_all(jnp.broadcast_to(both[None], (chips * columns,) + both.sha...]
    all_to_all x1, blocking collectives: 29.7 us -> 24.9 us  [shards(): all_sums = lax.all_to_all(sums, axes, 0, 0, tiled=True)]
    unnamed x30 -> x24, local copies, waits for them, and re-layouts: 3.82 us -> 1.35 us
    ppermute x4, waiting for transfers between devices: 0.01 us -> 1.49 us  [shifted(): lax.ppermute(x, axis, [(i, i + by) for i in range(n) if 0 <= i + by < n])]
    pallas_call x1, Pallas kernels: 6.96 us -> 5.48 us  [shards(): pl.pallas_call(functools.partial(tail_body, cores, columns), in_specs=[SM...]
    pallas_call x1, Pallas kernels: 19.2 us -> 20.5 us  [shards(): pl.pallas_call(outside_body, in_specs=[SMEM] * 3 + [VMEM] * 3, out_specs=...]
    all_to_all x1, starting transfers between devices: 12.6 us -> 11.3 us  [shards(): lax.all_to_all(jnp.broadcast_to(both[None], (chips * columns,) + both.sha...]
    ppermute x4, starting transfers between devices: 10.3 us -> 11.4 us  [shifted(): lax.ppermute(x, axis, [(i, i + by) for i in range(n) if 0 <= i + by < n])]
  transfers between devices with their start and end apart: 6 -> 6, of which waited for: 0 -> 3; matrix products, arithmetic and copies ran while one was open for 1% -> 1% of each run, Pallas kernels for 27% -> 8%
where the time goes in v12:
time: 105 us; the launch traced here: 104 us
  Pallas kernels  40.7 us (39%)
  blocking collectives  24.9 us (24%)
  starting transfers between devices  24.2 us (23%)
  waiting for transfers between devices  11 us (10%)
  local copies, waits for them, and re-layouts  2.18 us (2%)
    all_to_all x1, blocking collectives, shards(): all_sums = lax.all_to_all(sums, axes, 0, 0, tiled=True)  24.9 us
    pallas_call x1, Pallas kernels, shards(): pl.pallas_call(outside_body, in_specs=[SMEM] * 3 + [VMEM] * 3, out_specs=...  20.5 us
    ppermute x4, starting transfers between devices, shifted(): lax.ppermute(x, axis, [(i, i + by) for i in range(n) if 0 <= i + by < n])  11.4 us
    all_to_all x1, starting transfers between devices, shards(): lax.all_to_all(jnp.broadcast_to(both[None], (chips * columns,) + both.sha...  11.3 us
    all_to_all x1, waiting for transfers between devices, shards(): lax.all_to_all(jnp.broadcast_to(both[None], (chips * columns,) + both.sha...  9.56 us
    pallas_call x1, Pallas kernels, shards(): pl.pallas_call(inside_body, in_specs=[SMEM] * 2 + [VMEM], out_specs=VMEM,...  5.83 us
    pallas_call x1, Pallas kernels, shards(): pl.pallas_call(gather_body, in_specs=[ANY] * 7, out_specs=[VMEM] * 2, out...  5.52 us
    pallas_call x1, Pallas kernels, shards(): pl.pallas_call(functools.partial(tail_body, cores, columns), in_specs=[SM...  5.48 us
  transfers between devices with their start and end apart: 6, of which 3 were waited for; matrix products, arithmetic and copies ran while one was open for 1% of the time, Pallas kernels for 8%

profile of v12, /device:TPU:1, one launch (start us, length us, event | category | flops | bytes accessed | tf_op | source)
XLA Modules:
  0.0 104.1 jit_solution(3477278271180716277)
XLA Ops:
  0.6 5.5 %gather.1 = (f32[104,512]{1,0:T(8,128)}, f32[8,128]{1,0:T(8,128)}) custom-call(f32[4]{0:T(128)} %scale_hbm.1, s32[32,128]{1,0:T(8,128)} %bitcast.22, f32[4,4096]{1,0:T(4,128)} %x_hbm.1, f32[8,4096]{1,0:T(8,128)} %p_ref.3, f32[8,64,512]{2,1,0:T(8,128)} %bases_ref.1, f32[64,512]{1,0:T(8,128)} %bitcast.17, s32[1,64]{1,0:T(1,128)} %skel_hbm.1), custom_call_target="tpu_custom_call" | custom-call | tf_op jit(solution)/shard_map/gather/pallas_call | solution.py:392
  6.2 1.5 %collective-permute-start.2 = (f32[8,128]{1,0:T(8,128)}, f32[8,128]{1,0:T(8,128)S(1)}, u32[]{:S(2)}, u32[]{:S(2)}) collective-permute-start(f32[8,128]{1,0:T(8,128)} %get-tuple-element.21.own_ref), channel_id=1, source_target_pairs={{0,4},{4,0},{1,5},{5,1},{2,6},{6,2},{3,7},{7,3},{8,12},{12,8},{9,1... | collective-permute-start | bytes 12296 | tf_op jit(solution)/shard_map/ppermute | solution.py:427
  7.7 1.3 %collective-permute-start.1 = (f32[104,512]{1,0:T(8,128)}, f32[104,512]{1,0:T(8,128)S(1)}, u32[]{:S(2)}, u32[]{:S(2)}) collective-permute-start(f32[104,512]{1,0:T(8,128)} %get-tuple-element.24.halo_ref), channel_id=1, source_target_pairs={{1,0},{2,1},{3,2},{5,4},{6,5},{7,6},{9,8},{10,9},{11,10},{13,12},{... | collective-permute-start | bytes 638984 | tf_op jit(solution)/shard_map/ppermute | solution.py:379
  8.9 4.0 %collective-permute-start = (f32[104,512]{1,0:T(8,128)}, f32[104,512]{1,0:T(8,128)S(1)}, u32[]{:S(2)}, u32[]{:S(2)}) collective-permute-start(f32[104,512]{1,0:T(8,128)} %get-tuple-element.24.halo_ref), channel_id=1, source_target_pairs={{0,1},{1,2},{2,3},{4,5},{5,6},{6,7},{8,9},{9,10},{10,11},{12,13},{... | collective-permute-start | bytes 638984 | tf_op jit(solution)/shard_map/ppermute | solution.py:379
  13.0 0.0 copy-start.7
  13.0 0.0 collective-permute-done.2
  13.0 0.7 copy-done.7
  13.7 0.8 broadcast_in_dim.2
  14.5 0.0 copy-start.6
  14.5 0.0 copy-start.9
  14.5 0.0 copy-start.11
  14.5 11.3 %all-to-all-start = ((f32[64,2,8,128]{3,2,1,0:T(8,128)}), f32[64,2,8,128]{3,2,1,0:T(8,128)S(1)}, u32[]{:S(2)}, u32[]{:S(2)}) async-start(f32[64,2,8,128]{3,2,1,0:T(8,128)} %broadcast_in_dim.2), calls=%async_computation | async-start | bytes 1048576 | tf_op jit(solution)/shard_map/all_to_all | solution.py:430
  25.9 0.0 copy-done.6
  25.9 0.0 copy-done.9
  25.9 0.0 copy-done.11
  25.9 0.0 copy-start.4
  25.9 2.5 %lists.1 = (s32[32,128]{1,0:T(8,128)S(1)}, s32[68]{0:T(128)S(1)}, s32[68]{0:T(128)S(1)}, s32[2]{0:T(128)S(1)}) custom-call(s32[8,8]{1,0:T(8,128)S(1)} %copy-done.9, s32[8]{0:T(128)S(1)} %copy-done.11, s32[32,128]{1,0:T(8,128)S(1)} %bitcast.23), custom_call_target="tpu_custom_call" | custom-call | flops 10000000000 | bytes 2097152 | tf_op jit(solution)/shard_map/lists/pallas_call | solution.py:432
  28.4 0.1 pad_add_fusion.place_ref
  28.5 0.0 collective-permute-done.1
  28.5 0.0 collective-permute-done
  28.5 9.6 %all-to-all-done = f32[64,2,8,128]{3,2,1,0:T(8,128)S(1)} async-done(((f32[64,2,8,128]{3,2,1,0:T(8,128)}), f32[64,2,8,128]{3,2,1,0:T(8,128)S(1)}, u32[]{:S(2)}, u32[]{:S(2)}) %all-to-all-start) | async-done | bytes 524320 | tf_op jit(solution)/shard_map/all_to_all | solution.py:430
  38.1 0.0 copy-done.4
  38.1 4.0 %collective-permute-start.4 = (f32[3,104,512]{2,1,0:T(8,128)S(1)}, f32[3,104,512]{2,1,0:T(8,128)S(1)}, u32[]{:S(2)}, u32[]{:S(2)}) collective-permute-start(f32[3,104,512]{2,1,0:T(8,128)S(1)} %pad_maximum_fusion.row_ref), channel_id=1, source_target_pairs={{4,0},{8,4},{12,8},{16,12},{20,16},{24,20},{28,24},{32,28},{36,32}... | collective-permute-start | bytes 1916936 | tf_op jit(solution)/shard_map/ppermute | solution.py:379
  42.2 2.1 %collective-permute-start.3 = (f32[3,104,512]{2,1,0:T(8,128)S(1)}, f32[3,104,512]{2,1,0:T(8,128)S(1)}, u32[]{:S(2)}, u32[]{:S(2)}) collective-permute-start(f32[3,104,512]{2,1,0:T(8,128)S(1)} %pad_maximum_fusion.row_ref), channel_id=1, source_target_pairs={{0,4},{4,8},{8,12},{12,16},{16,20},{20,24},{24,28},{28,32},{32,36}... | collective-permute-start | bytes 1916936 | tf_op jit(solution)/shard_map/ppermute | solution.py:379
  44.3 0.0 copy-start.10
  44.3 5.8 %inside.1.inside_ref = f32[8,8,512]{2,1,0:T(8,128)S(1)} custom-call(s32[68]{0:T(128)S(1)} %get-tuple-element.26.pairs_ref, s32[2]{0:T(128)S(1)} %get-tuple-element.27.sizes_ref, f32[104,512]{1,0:T(8,128)S(1)} %copy-done.4), custom_call_target="tpu_custom_call" | custom-call | flops 10000000000 | bytes 2097152 | tf_op jit(solution)/shard_map/inside/pallas_call | solution.py:450
  50.1 0.3 collective-permute-done.4.down_ref
  50.4 1.2 %collective-permute-done.3.up_ref = f32[3,104,512]{2,1,0:T(8,128)S(1)} collective-permute-done((f32[3,104,512]{2,1,0:T(8,128)S(1)}, f32[3,104,512]{2,1,0:T(8,128)S(1)}, u32[]{:S(2)}, u32[]{:S(2)}) %collective-permute-start.3) | collective-permute-done | bytes 639008 | tf_op jit(solution)/shard_map/ppermute | solution.py:379
  51.6 0.0 copy-done.10
  51.6 0.0 copy-start
  51.6 0.0 copy-start.1
  51.6 0.0 copy-start.2
  51.6 0.0 copy-start.3
  51.6 20.5 %outside.1 = (f32[8,8,512]{2,1,0:T(8,128)S(1)}, f32[8,8,64]{2,1,0:T(8,128)S(1)}) custom-call(s32[68]{0:T(128)S(1)} %get-tuple-element.29.pairs_ref, s32[2]{0:T(128)S(1)} %get-tuple-element.27.sizes_ref, s32[8,8]{1,0:T(8,128)S(1)} %copy-done.10, f32[3,104,512]{2,1,0:T(8,128)S(1)} %pad_maximum_fusion.row_ref, ...), custom_call_target="tpu_custom_call" | custom-call | flops 30000001024 | bytes 2097152 | tf_op jit(solution)/shard_map/outside/pallas_call | solution.py:463
  72.2 0.0 copy-start.8
  72.2 0.0 copy-done
  72.2 0.0 copy-done.1
  72.2 0.0 copy-done.2
  72.2 0.0 copy-done.3
  72.2 0.6 copy-done.8
  72.8 5.5 %tail.1 = (f32[8,4096]{1,0:T(8,128)S(1)}, f32[128,128]{1,0:T(8,128)S(1)}) custom-call(s32[2]{0:T(128)S(1)} %pad_add_fusion.place_ref, f32[8]{0:T(128)S(1)} %copy-done.8, f32[8,8,512]{2,1,0:T(8,128)S(1)} %inside.1.inside_ref, f32[8,8,512]{2,1,0:T(8,128)S(1)} %get-tuple-element.32.near_ref, f32[8,8,64]{2,1,0:T(8,128)S(1)} %get-tuple-element.33.far_ref, ...), custom_call_target="tpu_custom_call" | custom-call | tf_op jit(solution)/shard_map/tail/pallas_call | solution.py:479
  78.3 0.0 copy-start.5
  78.3 24.9 %all_to_all.16 = f32[128,1,128]{2,1,0:T(1,128)S(1)} all-to-all(f32[128,1,128]{2,1,0:T(1,128)S(1)} %bitcast.21), channel_id=1, replica_groups=mesh['chip'=16,'core'=2,'tm'=4] {'chip','core','tm'}, dimensions={0} | all-to-all | bytes 131072 | tf_op jit(solution)/shard_map/all_to_all | solution.py:492
  103.2 0.0 copy-done.5
  103.2 0.8 update.1
  (3 shorter events, 0.1 us)
Async XLA Ops:
  6.2 6.8 %collective-permute-start.2 = (f32[8,128]{1,0:T(8,128)}, f32[8,128]{1,0:T(8,128)S(1)}, u32[]{:S(2)}, u32[]{:S(2)}) collective-permute-start(f32[8,128]{1,0:T(8,128)} %get-tuple-element.21.own_ref), channel_id=1, source_target_pairs={{0,4},{4,0},{1,5},{5,1},{2,6},{6,2},{3,7},{7,3},{8,12},{12,8},{9,1... | collective-permute-start | bytes 12296 | tf_op jit(solution)/shard_map/ppermute | solution.py:427
  7.7 20.9 %collective-permute-start.1 = (f32[104,512]{1,0:T(8,128)}, f32[104,512]{1,0:T(8,128)S(1)}, u32[]{:S(2)}, u32[]{:S(2)}) collective-permute-start(f32[104,512]{1,0:T(8,128)} %get-tuple-element.24.halo_ref), channel_id=1, source_target_pairs={{1,0},{2,1},{3,2},{5,4},{6,5},{7,6},{9,8},{10,9},{11,10},{13,12},{... | collective-permute-start | bytes 638984 | tf_op jit(solution)/shard_map/ppermute | solution.py:379
  8.9 19.6 %collective-permute-start = (f32[104,512]{1,0:T(8,128)}, f32[104,512]{1,0:T(8,128)S(1)}, u32[]{:S(2)}, u32[]{:S(2)}) collective-permute-start(f32[104,512]{1,0:T(8,128)} %get-tuple-element.24.halo_ref), channel_id=1, source_target_pairs={{0,1},{1,2},{2,3},{4,5},{5,6},{6,7},{8,9},{9,10},{10,11},{12,13},{... | collective-permute-start | bytes 638984 | tf_op jit(solution)/shard_map/ppermute | solution.py:379
  13.0 0.7 copy-start.7
  14.5 11.4 %copy-start.6 = (s32[4096]{0:T(1024)S(1)}, s32[4096]{0:T(1024)}, u32[]{:S(2)}) copy-start(s32[4096]{0:T(1024)} %param.17) | copy-start | bytes 49156
  14.5 11.4 %copy-start.9 = (s32[8,8]{1,0:T(8,128)S(1)}, s32[8,8]{1,0:T(8,128)}, u32[]{:S(2)}) copy-start(s32[8,8]{1,0:T(8,128)} %near_ref.1) | copy-start | bytes 772
  14.5 11.4 %copy-start.11 = (s32[8]{0:T(128)S(1)}, s32[8]{0:T(128)}, u32[]{:S(2)}) copy-start(s32[8]{0:T(128)} %count_ref.1) | copy-start | bytes 100
  14.5 23.6 %all-to-all-start = ((f32[64,2,8,128]{3,2,1,0:T(8,128)}), f32[64,2,8,128]{3,2,1,0:T(8,128)S(1)}, u32[]{:S(2)}, u32[]{:S(2)}) async-start(f32[64,2,8,128]{3,2,1,0:T(8,128)} %broadcast_in_dim.2), calls=%async_computation | async-start | bytes 1048576 | tf_op jit(solution)/shard_map/all_to_all | solution.py:430
  25.9 12.2 %copy-start.4 = (f32[104,512]{1,0:T(8,128)S(1)}, f32[104,512]{1,0:T(8,128)}, u32[]{:S(2)}) copy-start(f32[104,512]{1,0:T(8,128)} %get-tuple-element.24.halo_ref) | copy-start | bytes 638980
  38.1 12.3 %collective-permute-start.4 = (f32[3,104,512]{2,1,0:T(8,128)S(1)}, f32[3,104,512]{2,1,0:T(8,128)S(1)}, u32[]{:S(2)}, u32[]{:S(2)}) collective-permute-start(f32[3,104,512]{2,1,0:T(8,128)S(1)} %pad_maximum_fusion.row_ref), channel_id=1, source_target_pairs={{4,0},{8,4},{12,8},{16,12},{20,16},{24,20},{28,24},{32,28},{36,32}... | collective-permute-start | bytes 1916936 | tf_op jit(solution)/shard_map/ppermute | solution.py:379
  42.2 9.5 %collective-permute-start.3 = (f32[3,104,512]{2,1,0:T(8,128)S(1)}, f32[3,104,512]{2,1,0:T(8,128)S(1)}, u32[]{:S(2)}, u32[]{:S(2)}) collective-permute-start(f32[3,104,512]{2,1,0:T(8,128)S(1)} %pad_maximum_fusion.row_ref), channel_id=1, source_target_pairs={{0,4},{4,8},{8,12},{12,16},{16,20},{20,24},{24,28},{28,32},{32,36}... | collective-permute-start | bytes 1916936 | tf_op jit(solution)/shard_map/ppermute | solution.py:379
  44.3 7.3 %copy-start.10 = (s32[8,8]{1,0:T(8,128)S(1)}, s32[8,8]{1,0:T(8,128)}, u32[]{:S(2)}) copy-start(s32[8,8]{1,0:T(8,128)} %far_ref.1) | copy-start | bytes 772
  51.6 20.6 %copy-start = (f32[8,64,512]{2,1,0:T(8,128)S(1)}, f32[8,64,512]{2,1,0:T(8,128)}, u32[]{:S(2)}) copy-start(f32[8,64,512]{2,1,0:T(8,128)} %bases_ref.1) | copy-start | bytes 3145732
  51.6 20.6 %copy-start.1 = (f32[8,4096]{1,0:T(8,128)S(1)}, f32[8,4096]{1,0:T(8,128)}, u32[]{:S(2)}) copy-start(f32[8,4096]{1,0:T(8,128)} %p_ref.3) | copy-start | bytes 393220
  51.6 20.6 %copy-start.2 = (f32[1,64,512]{2,1,0:T(8,128)S(1)}, f32[1,64,512]{2,1,0:T(8,128)}, u32[]{:S(2)}) copy-start(f32[1,64,512]{2,1,0:T(8,128)} %param.19) | copy-start | bytes 393220
  51.6 20.6 %copy-start.3 = (f32[8,4096]{1,0:T(8,128)S(1)}, f32[8,4096]{1,0:T(8,128)}, u32[]{:S(2)}) copy-start(f32[8,4096]{1,0:T(8,128)} %res_ref.3) | copy-start | bytes 393220
  72.2 0.7 copy-start.8
  78.3 24.9 %copy-start.5 = (f32[8,4096]{1,0:T(8,128)S(1)}, f32[8,4096]{1,0:T(8,128)}, u32[]{:S(2)}) copy-start(f32[8,4096]{1,0:T(8,128)} %it_ref.1) | copy-start | bytes 393220

commit v13 on v9

--- a/solution.py
+++ b/solution.py
@@ -102,7 +102,7 @@
     return picked * UNIT
 
 
-def gather_body(scale_ref, order_hbm, x_hbm, p_hbm, bases_hbm, halo_ref, order_ref, xx, p_ref, bases_ref, sems):
+def gather_body(scale_hbm, order_hbm, x_hbm, p_hbm, bases_hbm, halo_ref, scale_ref, order_ref, xx, p_ref, bases_ref, sems):
     leaf_dev, rank, leaf_pts = bases_ref.shape
     points = p_ref.shape[1]
     chunks = points // 128
@@ -115,13 +115,14 @@
                 (x_hbm, xx.at[0:4, :]),
                 (x_hbm, xx.at[4:8, :]),
                 (p_hbm, p_ref),
+                (scale_hbm, scale_ref),
                 (bases_hbm, bases_ref),
             ]
         )
     ]
     for move in moves:
         move.start()
-    for move in moves[:4]:
+    for move in moves[:5]:
         move.wait()
     scale = scale_rows(scale_ref, (8, 128))
 
@@ -143,7 +144,7 @@
         return 0
 
     lax.fori_loop(0, leaf_dev // 2, two_leaves, 0)
-    moves[4].wait()
+    moves[5].wait()
     for leaf in range(leaf_dev):
         coef = contract(halo_ref[32 + leaf * 8 : 40 + leaf * 8, :], bases_ref[leaf], ((1,), (1,)), EXACT)
         halo_ref[96:104, leaf * rank : (leaf + 1) * rank] = coef
@@ -282,24 +283,27 @@
     rank = own_ref.shape[1] // 2
     lane = lane_ids((8, 128))
 
-    def distant(e):
-        far_a = jnp.abs(e // tm_size - place_ref[0]) > 1
-        far_b = jnp.abs(e % tm_size - place_ref[1]) > 1
+    def distant(leaf, column):
+        far_a = jnp.abs(leaf - place_ref[0]) > 1
+        far_b = jnp.abs(column - place_ref[1]) > 1
         return jnp.where(far_a | far_b, FACTOR, 0.0)
+
+    group = 2 * tm_size
 
     def unpack(g, _):
         xs, ws = [], []
-        for k in range(4):
-            e = 8 * g + 2 * k
-            one, two = node_ref[e], node_ref[e + 1]
+        for j in range(0, group, 2):
+            one, two = node_ref[group * g + j], node_ref[group * g + j + 1]
+            keep_one = distant(2 * g + j // tm_size, j % tm_size)
+            keep_two = distant(2 * g + (j + 1) // tm_size, (j + 1) % tm_size)
             xs.append(jnp.where(lane < rank, pltpu.roll(one, rank, 1), two))
-            ws.append(jnp.where(lane < rank, one * distant(e), pltpu.roll(two, rank, 1) * distant(e + 1)))
-        at = pl.ds(pl.multiple_of(g * 512, 512), 512)
+            ws.append(jnp.where(lane < rank, one * keep_one, pltpu.roll(two, rank, 1) * keep_two))
+        at = pl.ds(pl.multiple_of(g * group * rank, group * rank), group * rank)
         node_src[:, at] = features(jnp.concatenate(xs, axis=1), True, False)[0]
         node_wgt[:, at] = halves(jnp.concatenate(ws, axis=1))
         return 0
 
-    lax.fori_loop(0, devices // 8, unpack, 0, unroll=4)
+    lax.fori_loop(0, devices // group, unpack, 0, unroll=4)
     own_xx = pltpu.roll(own_ref[...], rank, 1)
     target = features(own_xx, False, True)[0][:, :rank]
     total = jnp.zeros((16, rank), F32)
@@ -401,15 +405,16 @@
     by_row = order.reshape(chunks, 128)
     halo = pl.pallas_call(
         gather_body,
-        in_specs=[SMEM] + [ANY] * 4,
+        in_specs=[ANY] * 5,
         out_specs=VMEM,
         out_shape=shape((13 * leaf_dev, leaf_pts), F32),
         scratch_shapes=[
+            pltpu.SMEM(inv_scale.shape, F32),
             pltpu.VMEM((chunks, 128), jnp.int32),
             pltpu.VMEM((8, points), F32),
             pltpu.VMEM((rhs, points), F32),
             pltpu.VMEM(bases.shape, F32),
-            pltpu.SemaphoreType.DMA((5,)),
+            pltpu.SemaphoreType.DMA((6,)),
         ],
         compiler_params=params(60),
         name="gather",

time: 97.6 us -> 96 us (0.984)
  blocking collectives: 20.7 us -> 17.7 us
    all_to_all x1, blocking collectives: 20.7 us -> 17.7 us  [shards(): all_sums = lax.all_to_all(sums, axes, 0, 0, tiled=True)]
    pallas_call x1, Pallas kernels: 27.8 us -> 29.7 us  [shards(): pl.pallas_call(outside_body, in_specs=[SMEM] * 3 + [VMEM] * 3, out_specs=...]
  transfers between devices with their start and end apart: 5 -> 5, of which waited for: 0 -> 0; matrix products, arithmetic and copies ran while one was open for 0% -> 0% of each run, Pallas kernels for 38% -> 41%
where the time goes in v13:
time: 96 us; the launch traced here: 94.8 us
  Pallas kernels  50 us (52%)
  starting transfers between devices  22.8 us (24%)
  blocking collectives  17.7 us (18%)
  local copies, waits for them, and re-layouts  3.26 us (3%)
    pallas_call x1, Pallas kernels, shards(): pl.pallas_call(outside_body, in_specs=[SMEM] * 3 + [VMEM] * 3, out_specs=...  29.7 us
    all_to_all x1, blocking collectives, shards(): all_sums = lax.all_to_all(sums, axes, 0, 0, tiled=True)  17.7 us
    all_to_all x1, starting transfers between devices, shards(): nodes = lax.all_to_all(node, axes, 0, 0)  11.7 us
    ppermute x4, starting transfers between devices, shifted(): lax.ppermute(x, axis, [(i, i + by) for i in range(n) if 0 <= i + by < n])  11.2 us
    pallas_call x1, Pallas kernels, shards(): pl.pallas_call(inside_body, in_specs=[SMEM] * 2 + [ANY] + [VMEM] * 3, out...  8.8 us
    pallas_call x1, Pallas kernels, shards(): pl.pallas_call(functools.partial(tail_body, lax.axis_size('tm')), in_spec...  5.49 us
    pallas_call x1, Pallas kernels, shards(): pl.pallas_call(gather_body, in_specs=[ANY] * 5, out_specs=VMEM, out_shape...  5.28 us
    unnamed x30, local copies, waits for them, and re-layouts  3.26 us
  transfers between devices with their start and end apart: 5, of which 0 were waited for; matrix products, arithmetic and copies ran while one was open for 0% of the time, Pallas kernels for 41%

profile of v13, /device:TPU:1, one launch (start us, length us, event | category | flops | bytes accessed | tf_op | source)
XLA Modules:
  0.0 94.8 jit_solution(2936482565581766220)
XLA Ops:
  0.6 5.3 %gather.1.halo_hbm = f32[104,512]{1,0:T(8,128)} custom-call(f32[4]{0:T(128)} %scale_hbm.1, s32[32,128]{1,0:T(8,128)} %bitcast.18, f32[4,4096]{1,0:T(4,128)} %x_hbm.1, f32[8,4096]{1,0:T(8,128)} %p_ref.3, f32[8,64,512]{2,1,0:T(8,128)} %bases_ref.1), custom_call_target="tpu_custom_call" | custom-call | tf_op jit(solution)/shard_map/gather/pallas_call | solution.py:406
  5.9 4.0 %collective-permute-start = (f32[104,512]{1,0:T(8,128)}, f32[104,512]{1,0:T(8,128)S(1)}, u32[]{:S(2)}, u32[]{:S(2)}) collective-permute-start(f32[104,512]{1,0:T(8,128)} %gather.1.halo_hbm), channel_id=1, source_target_pairs={{0,1},{1,2},{2,3},{4,5},{5,6},{6,7},{8,9},{9,10},{10,11},{12,13},{... | collective-permute-start | bytes 638984 | tf_op jit(solution)/shard_map/ppermute | solution.py:395
  9.9 1.3 %collective-permute-start.1 = (f32[104,512]{1,0:T(8,128)}, f32[104,512]{1,0:T(8,128)S(1)}, u32[]{:S(2)}, u32[]{:S(2)}) collective-permute-start(f32[104,512]{1,0:T(8,128)} %gather.1.halo_hbm), channel_id=1, source_target_pairs={{1,0},{2,1},{3,2},{5,4},{6,5},{7,6},{9,8},{10,9},{11,10},{13,12},{... | collective-permute-start | bytes 638984 | tf_op jit(solution)/shard_map/ppermute | solution.py:395
  11.2 0.0 copy-start.14
  11.2 8.8 %inside.1 = (f32[8,8,512]{2,1,0:T(8,128)}, f32[128,8,128]{2,1,0:T(8,128)}, f32[8,128]{1,0:T(8,128)}, s32[32,128]{1,0:T(8,128)}, s32[68]{0:T(128)}, /*index=5*/s32[2]{0:T(128)}) custom-call(s32[8,8]{1,0:T(8,128)} %near_ref.1, s32[8]{0:T(128)} %count_ref.1, f32[104,512]{1,0:T(8,128)} %gather.1.halo_hbm, s32[32,128]{1,0:T(8,128)} %bitcast.19, ...), custom_call_target="tpu_custom_call" | custom-call | flops 10000000000 | bytes 2097152 | tf_op jit(solution)/shard_map/inside/pallas_call | solution.py:438
  20.0 0.0 collective-permute-done
  20.0 0.0 collective-permute-done.1
  20.0 0.0 copy-done.14
  20.1 4.0 %collective-permute-start.2 = (f32[3,104,512]{2,1,0:T(8,128)S(1)}, f32[3,104,512]{2,1,0:T(8,128)S(1)}, u32[]{:S(2)}, u32[]{:S(2)}) collective-permute-start(f32[3,104,512]{2,1,0:T(8,128)S(1)} %pad_maximum_fusion.row_ref), channel_id=1, source_target_pairs={{0,4},{4,8},{8,12},{12,16},{16,20},{20,24},{24,28},{28,32},{32,36}... | collective-permute-start | bytes 1916936 | tf_op jit(solution)/shard_map/ppermute | solution.py:395
  24.1 1.9 %collective-permute-start.3 = (f32[3,104,512]{2,1,0:T(8,128)S(1)}, f32[3,104,512]{2,1,0:T(8,128)}, u32[]{:S(2)}, u32[]{:S(2)}) collective-permute-start(f32[3,104,512]{2,1,0:T(8,128)S(1)} %pad_maximum_fusion.row_ref), channel_id=1, source_target_pairs={{4,0},{8,4},{12,8},{16,12},{20,16},{24,20},{28,24},{32,28},{36,32}... | collective-permute-start | bytes 1916936 | tf_op jit(solution)/shard_map/ppermute | solution.py:395
  26.0 0.1 pad_add_fusion.place_ref
  26.1 0.0 copy-start.11
  26.1 11.7 %all-to-all-start = ((f32[128,8,128]{2,1,0:T(8,128)}), f32[128,8,128]{2,1,0:T(8,128)S(1)}, u32[]{:S(2)}, u32[]{:S(2)}) async-start(f32[128,8,128]{2,1,0:T(8,128)} %get-tuple-element.25), calls=%async_computation | async-start | bytes 1048576 | tf_op jit(solution)/shard_map/all_to_all | solution.py:463
  37.8 0.0 collective-permute-done.2.up_ref
  37.8 0.0 copy-start.9
  37.8 0.8 copy-done.9
  38.6 0.0 collective-permute-done.3.down_ref
  38.6 0.0 copy-start.12
  38.6 0.0 copy-start.13
  38.6 0.0 copy-done.11
  38.6 0.7 copy-done.12
  39.3 0.0 copy-done.13
  39.3 0.0 copy-start.10
  39.3 1.1 %copy-done.10 = f32[3,104,512]{2,1,0:T(8,128)S(1)} copy-done((f32[3,104,512]{2,1,0:T(8,128)S(1)}, f32[3,104,512]{2,1,0:T(8,128)}, u32[]{:S(2)}) %copy-start.10) | copy-done | bytes 639000
  40.4 0.0 copy-start
  40.4 0.0 copy-start.1
  40.4 0.0 copy-start.2
  40.4 0.0 copy-start.3
  40.4 0.0 copy-start.4
  40.4 0.0 copy-start.6
  40.4 29.7 %outside.1 = (f32[8,8,512]{2,1,0:T(8,128)S(1)}, f32[8,8,64]{2,1,0:T(8,128)S(1)}) custom-call(s32[68]{0:T(128)S(1)} %copy-done.12, s32[2]{0:T(128)S(1)} %copy-done.13, s32[8,8]{1,0:T(8,128)S(1)} %copy-done.11, f32[3,104,512]{2,1,0:T(8,128)S(1)} %pad_maximum_fusion.row_ref, f32[3,104,512]{2,1,0:T(8,128)S(1)} %copy-done.10, ...), custom_call_target="tpu_custom_call" | custom-call | flops 30000001024 | bytes 2097152 | tf_op jit(solution)/shard_map/outside/pallas_call | solution.py:469
  70.1 0.0 copy-start.7
  70.1 0.0 all-to-all-done.node_ref
  70.1 0.0 copy-start.8
  70.1 0.0 copy-done
  70.1 0.0 copy-done.1
  70.2 0.0 copy-done.2
  70.2 0.0 copy-done.3
  70.2 0.0 copy-done.4
  70.2 0.0 copy-done.6
  70.2 0.6 copy-done.7
  70.8 0.0 copy-done.8
  70.8 5.5 %tail.1 = (f32[8,4096]{1,0:T(8,128)S(1)}, f32[128,128]{1,0:T(8,128)S(1)}) custom-call(s32[2]{0:T(128)S(1)} %pad_add_fusion.place_ref, f32[8]{0:T(128)S(1)} %copy-done.8, f32[8,8,512]{2,1,0:T(8,128)S(1)} %copy-done.4, f32[8,8,512]{2,1,0:T(8,128)S(1)} %get-tuple-element.23.near_ref, f32[8,8,64]{2,1,0:T(8,128)S(1)} %get-tuple-element.24.far_ref, ...), custom_call_target="tpu_custom_call" | custom-call | tf_op jit(solution)/shard_map/tail/pallas_call | solution.py:485
  76.3 0.0 copy-start.5
  76.3 17.7 %all_to_all.16 = f32[128,1,128]{2,1,0:T(1,128)S(1)} all-to-all(f32[128,1,128]{2,1,0:T(1,128)S(1)} %bitcast.14), channel_id=1, replica_groups=mesh['leaf'=32,'tm'=4] {'leaf','tm'}, dimensions={0} | all-to-all | bytes 131072 | tf_op jit(solution)/shard_map/all_to_all | solution.py:498
  94.0 0.0 copy-done.5
  94.0 0.8 update.1
  (1 shorter events, 0.0 us)
Async XLA Ops:
  5.9 14.1 %collective-permute-start = (f32[104,512]{1,0:T(8,128)}, f32[104,512]{1,0:T(8,128)S(1)}, u32[]{:S(2)}, u32[]{:S(2)}) collective-permute-start(f32[104,512]{1,0:T(8,128)} %gather.1.halo_hbm), channel_id=1, source_target_pairs={{0,1},{1,2},{2,3},{4,5},{5,6},{6,7},{8,9},{9,10},{10,11},{12,13},{... | collective-permute-start | bytes 638984 | tf_op jit(solution)/shard_map/ppermute | solution.py:395
  9.9 10.1 %collective-permute-start.1 = (f32[104,512]{1,0:T(8,128)}, f32[104,512]{1,0:T(8,128)S(1)}, u32[]{:S(2)}, u32[]{:S(2)}) collective-permute-start(f32[104,512]{1,0:T(8,128)} %gather.1.halo_hbm), channel_id=1, source_target_pairs={{1,0},{2,1},{3,2},{5,4},{6,5},{7,6},{9,8},{10,9},{11,10},{13,12},{... | collective-permute-start | bytes 638984 | tf_op jit(solution)/shard_map/ppermute | solution.py:395
  11.2 8.8 %copy-start.14 = (f32[104,512]{1,0:T(8,128)S(1)}, f32[104,512]{1,0:T(8,128)}, u32[]{:S(2)}) copy-start(f32[104,512]{1,0:T(8,128)} %gather.1.halo_hbm) | copy-start | bytes 638980
  20.1 17.7 %collective-permute-start.2 = (f32[3,104,512]{2,1,0:T(8,128)S(1)}, f32[3,104,512]{2,1,0:T(8,128)S(1)}, u32[]{:S(2)}, u32[]{:S(2)}) collective-permute-start(f32[3,104,512]{2,1,0:T(8,128)S(1)} %pad_maximum_fusion.row_ref), channel_id=1, source_target_pairs={{0,4},{4,8},{8,12},{12,16},{16,20},{20,24},{24,28},{28,32},{32,36}... | collective-permute-start | bytes 1916936 | tf_op jit(solution)/shard_map/ppermute | solution.py:395
  24.1 14.5 %collective-permute-start.3 = (f32[3,104,512]{2,1,0:T(8,128)S(1)}, f32[3,104,512]{2,1,0:T(8,128)}, u32[]{:S(2)}, u32[]{:S(2)}) collective-permute-start(f32[3,104,512]{2,1,0:T(8,128)S(1)} %pad_maximum_fusion.row_ref), channel_id=1, source_target_pairs={{4,0},{8,4},{12,8},{16,12},{20,16},{24,20},{28,24},{32,28},{36,32}... | collective-permute-start | bytes 1916936 | tf_op jit(solution)/shard_map/ppermute | solution.py:395
  26.1 12.5 %copy-start.11 = (s32[8,8]{1,0:T(8,128)S(1)}, s32[8,8]{1,0:T(8,128)}, u32[]{:S(2)}) copy-start(s32[8,8]{1,0:T(8,128)} %far_ref.1) | copy-start | bytes 772
  26.1 44.0 %all-to-all-start = ((f32[128,8,128]{2,1,0:T(8,128)}), f32[128,8,128]{2,1,0:T(8,128)S(1)}, u32[]{:S(2)}, u32[]{:S(2)}) async-start(f32[128,8,128]{2,1,0:T(8,128)} %get-tuple-element.25), calls=%async_computation | async-start | bytes 1048576 | tf_op jit(solution)/shard_map/all_to_all | solution.py:463
  37.8 0.8 copy-start.9
  38.6 0.7 copy-start.12
  38.6 0.7 copy-start.13
  39.3 1.1 %copy-start.10 = (f32[3,104,512]{2,1,0:T(8,128)S(1)}, f32[3,104,512]{2,1,0:T(8,128)}, u32[]{:S(2)}) copy-start(f32[3,104,512]{2,1,0:T(8,128)} %copy-done.9) | copy-start | bytes 1916932
  40.4 29.7 %copy-start = (f32[8,64,512]{2,1,0:T(8,128)S(1)}, f32[8,64,512]{2,1,0:T(8,128)}, u32[]{:S(2)}) copy-start(f32[8,64,512]{2,1,0:T(8,128)} %bases_ref.1) | copy-start | bytes 3145732
  40.4 29.7 %copy-start.1 = (f32[8,4096]{1,0:T(8,128)S(1)}, f32[8,4096]{1,0:T(8,128)}, u32[]{:S(2)}) copy-start(f32[8,4096]{1,0:T(8,128)} %p_ref.3) | copy-start | bytes 393220
  40.4 29.7 %copy-start.2 = (f32[8,4096]{1,0:T(8,128)S(1)}, f32[8,4096]{1,0:T(8,128)}, u32[]{:S(2)}) copy-start(f32[8,4096]{1,0:T(8,128)} %res_ref.3) | copy-start | bytes 393220
  40.4 29.8 %copy-start.3 = (f32[1,64,512]{2,1,0:T(8,128)S(1)}, f32[1,64,512]{2,1,0:T(8,128)}, u32[]{:S(2)}) copy-start(f32[1,64,512]{2,1,0:T(8,128)} %param.19) | copy-start | bytes 393220
  40.4 29.8 %copy-start.4 = (f32[8,8,512]{2,1,0:T(8,128)S(1)}, f32[8,8,512]{2,1,0:T(8,128)}, u32[]{:S(2)}) copy-start(f32[8,8,512]{2,1,0:T(8,128)} %get-tuple-element.18.inside_ref) | copy-start | bytes 393220
  40.4 29.8 %copy-start.6 = (s32[32,128]{1,0:T(8,128)S(1)}, s32[32,128]{1,0:T(8,128)}, u32[]{:S(2)}) copy-start(s32[32,128]{1,0:T(8,128)} %get-tuple-element.27.inv_ref) | copy-start | bytes 49156
  70.1 0.7 copy-start.7
  70.1 0.7 copy-start.8
  76.3 17.7 %copy-start.5 = (f32[8,4096]{1,0:T(8,128)S(1)}, f32[8,4096]{1,0:T(8,128)}, u32[]{:S(2)}) copy-start(f32[8,4096]{1,0:T(8,128)} %it_ref.1) | copy-start | bytes 393220

commit v14 on v13

--- a/solution.py
+++ b/solution.py
@@ -130,24 +130,25 @@
         return [lambda s=s: ref[:, s * 128 : (s + 1) * 128] for s in range(chunks)]
 
     def two_leaves(g, _):
-        kept = []
-        for h in range(2):
-            leaf = 2 * g + h
-            for j in range(per_leaf):
-                ids = order_ref[pl.ds(leaf * per_leaf + j, 1), :]
-                got_x, got_p = gather_lanes([loads(xx), loads(p_ref)], jnp.broadcast_to(ids, (8, 128)))
-                kept.append(got_x * scale)
+        upper = row_ids((8, 128)) < 4
+        for j in range(per_leaf):
+            ids = []
+            for h in range(2):
+                leaf = 2 * g + h
+                ids.append(jnp.broadcast_to(order_ref[pl.ds(leaf * per_leaf + j, 1), :], (8, 128)))
+                (got_p,) = gather_lanes([loads(p_ref)], ids[h])
                 halo_ref[pl.ds(pl.multiple_of(32 + leaf * 8, 8), 8), j * 128 : (j + 1) * 128] = got_p
-        for j in range(per_leaf):
-            both = jnp.where(row_ids((8, 128)) < 4, kept[j], kept[per_leaf + j])
-            halo_ref[pl.ds(pl.multiple_of(g * 8, 8), 8), j * 128 : (j + 1) * 128] = both
+            (got_x,) = gather_lanes([loads(xx)], jnp.where(upper, ids[0], ids[1]))
+            halo_ref[pl.ds(pl.multiple_of(g * 8, 8), 8), j * 128 : (j + 1) * 128] = got_x * scale
         return 0
 
     lax.fori_loop(0, leaf_dev // 2, two_leaves, 0)
     moves[5].wait()
     for leaf in range(leaf_dev):
-        coef = contract(halo_ref[32 + leaf * 8 : 40 + leaf * 8, :], bases_ref[leaf], ((1,), (1,)), EXACT)
-        halo_ref[96:104, leaf * rank : (leaf + 1) * rank] = coef
+        weight = halves(halo_ref[32 + leaf * 8 : 40 + leaf * 8, :])
+        base_high, base_low = split(bases_ref[leaf])
+        got = contract(weight, base_high, ((1,), (1,))) + contract(weight, base_low, ((1,), (1,)))
+        halo_ref[96:104, leaf * rank : (leaf + 1) * rank] = got[:8] + got[8:]
 
 
 def node_work(order_ref, halo_ref, transfer_ref, skel_ref, node_ref, own_ref, inv_ref, slot):

time: 96 us -> 95.7 us (level)
  blocking collectives: 17.7 us -> 37.3 us
  Pallas kernels: 50 us -> 30.8 us
    all_to_all x1, blocking collectives: 17.7 us -> 37.3 us  [shards(): all_sums = lax.all_to_all(sums, axes, 0, 0, tiled=True)]
    pallas_call x1, Pallas kernels: 29.7 us -> 11.6 us  [shards(): pl.pallas_call(outside_body, in_specs=[SMEM] * 3 + [VMEM] * 3, out_specs=...]
    pallas_call x1, Pallas kernels: 5.28 us -> 4.26 us  [shards(): pl.pallas_call(gather_body, in_specs=[ANY] * 5, out_specs=VMEM, out_shape...]
  transfers between devices with their start and end apart: 5 -> 5, of which waited for: 0 -> 0; matrix products, arithmetic and copies ran while one was open for 0% -> 0% of each run, Pallas kernels for 41% -> 21%
where the time goes in v14:
time: 95.7 us; the launch traced here: 95.4 us
  blocking collectives  37.3 us (39%)
  Pallas kernels  30.8 us (32%)
  starting transfers between devices  23.1 us (24%)
  local copies, waits for them, and re-layouts  3.26 us (3%)
    all_to_all x1, blocking collectives, shards(): all_sums = lax.all_to_all(sums, axes, 0, 0, tiled=True)  37.3 us
    all_to_all x1, starting transfers between devices, shards(): nodes = lax.all_to_all(node, axes, 0, 0)  11.9 us
    pallas_call x1, Pallas kernels, shards(): pl.pallas_call(outside_body, in_specs=[SMEM] * 3 + [VMEM] * 3, out_specs=...  11.6 us
    ppermute x4, starting transfers between devices, shifted(): lax.ppermute(x, axis, [(i, i + by) for i in range(n) if 0 <= i + by < n])  11.2 us
    pallas_call x1, Pallas kernels, shards(): pl.pallas_call(inside_body, in_specs=[SMEM] * 2 + [ANY] + [VMEM] * 3, out...  8.61 us
    pallas_call x1, Pallas kernels, shards(): pl.pallas_call(functools.partial(tail_body, lax.axis_size('tm')), in_spec...  5.49 us
    pallas_call x1, Pallas kernels, shards(): pl.pallas_call(gather_body, in_specs=[ANY] * 5, out_specs=VMEM, out_shape...  4.26 us
    unnamed x30, local copies, waits for them, and re-layouts  3.26 us
  transfers between devices with their start and end apart: 5, of which 0 were waited for; matrix products, arithmetic and copies ran while one was open for 0% of the time, Pallas kernels for 21%

profile of v14, /device:TPU:1, one launch (start us, length us, event | category | flops | bytes accessed | tf_op | source)
XLA Modules:
  0.0 95.4 jit_solution(791109825454489868)
XLA Ops:
  0.6 4.3 %gather.1.halo_hbm = f32[104,512]{1,0:T(8,128)} custom-call(f32[4]{0:T(128)} %scale_hbm.1, s32[32,128]{1,0:T(8,128)} %bitcast.18, f32[4,4096]{1,0:T(4,128)} %x_hbm.1, f32[8,4096]{1,0:T(8,128)} %p_ref.3, f32[8,64,512]{2,1,0:T(8,128)} %bases_ref.1), custom_call_target="tpu_custom_call" | custom-call | tf_op jit(solution)/shard_map/gather/pallas_call | solution.py:407
  4.9 4.0 %collective-permute-start = (f32[104,512]{1,0:T(8,128)}, f32[104,512]{1,0:T(8,128)S(1)}, u32[]{:S(2)}, u32[]{:S(2)}) collective-permute-start(f32[104,512]{1,0:T(8,128)} %gather.1.halo_hbm), channel_id=1, source_target_pairs={{0,1},{1,2},{2,3},{4,5},{5,6},{6,7},{8,9},{9,10},{10,11},{12,13},{... | collective-permute-start | bytes 638984 | tf_op jit(solution)/shard_map/ppermute | solution.py:396
  8.9 1.3 %collective-permute-start.1 = (f32[104,512]{1,0:T(8,128)}, f32[104,512]{1,0:T(8,128)S(1)}, u32[]{:S(2)}, u32[]{:S(2)}) collective-permute-start(f32[104,512]{1,0:T(8,128)} %gather.1.halo_hbm), channel_id=1, source_target_pairs={{1,0},{2,1},{3,2},{5,4},{6,5},{7,6},{9,8},{10,9},{11,10},{13,12},{... | collective-permute-start | bytes 638984 | tf_op jit(solution)/shard_map/ppermute | solution.py:396
  10.2 0.0 copy-start.14
  10.2 8.6 %inside.1 = (f32[8,8,512]{2,1,0:T(8,128)}, f32[128,8,128]{2,1,0:T(8,128)}, f32[8,128]{1,0:T(8,128)}, s32[32,128]{1,0:T(8,128)}, s32[68]{0:T(128)}, /*index=5*/s32[2]{0:T(128)}) custom-call(s32[8,8]{1,0:T(8,128)} %near_ref.1, s32[8]{0:T(128)} %count_ref.1, f32[104,512]{1,0:T(8,128)} %gather.1.halo_hbm, s32[32,128]{1,0:T(8,128)} %bitcast.19, ...), custom_call_target="tpu_custom_call" | custom-call | flops 10000000000 | bytes 2097152 | tf_op jit(solution)/shard_map/inside/pallas_call | solution.py:439
  18.8 0.0 collective-permute-done
  18.8 0.0 collective-permute-done.1
  18.8 0.0 copy-done.14
  18.9 4.0 %collective-permute-start.2 = (f32[3,104,512]{2,1,0:T(8,128)S(1)}, f32[3,104,512]{2,1,0:T(8,128)S(1)}, u32[]{:S(2)}, u32[]{:S(2)}) collective-permute-start(f32[3,104,512]{2,1,0:T(8,128)S(1)} %pad_maximum_fusion.row_ref), channel_id=1, source_target_pairs={{0,4},{4,8},{8,12},{12,16},{16,20},{20,24},{24,28},{28,32},{32,36}... | collective-permute-start | bytes 1916936 | tf_op jit(solution)/shard_map/ppermute | solution.py:396
  22.9 1.9 %collective-permute-start.3 = (f32[3,104,512]{2,1,0:T(8,128)S(1)}, f32[3,104,512]{2,1,0:T(8,128)}, u32[]{:S(2)}, u32[]{:S(2)}) collective-permute-start(f32[3,104,512]{2,1,0:T(8,128)S(1)} %pad_maximum_fusion.row_ref), channel_id=1, source_target_pairs={{4,0},{8,4},{12,8},{16,12},{20,16},{24,20},{28,24},{32,28},{36,32}... | collective-permute-start | bytes 1916936 | tf_op jit(solution)/shard_map/ppermute | solution.py:396
  24.9 0.1 pad_add_fusion.place_ref
  24.9 0.0 copy-start.11
  24.9 11.9 %all-to-all-start = ((f32[128,8,128]{2,1,0:T(8,128)}), f32[128,8,128]{2,1,0:T(8,128)S(1)}, u32[]{:S(2)}, u32[]{:S(2)}) async-start(f32[128,8,128]{2,1,0:T(8,128)} %get-tuple-element.25), calls=%async_computation | async-start | bytes 1048576 | tf_op jit(solution)/shard_map/all_to_all | solution.py:464
  36.8 0.0 collective-permute-done.2.up_ref
  36.8 0.0 copy-start.9
  36.8 0.8 copy-done.9
  37.7 0.0 collective-permute-done.3.down_ref
  37.7 0.0 copy-start.12
  37.7 0.0 copy-start.13
  37.7 0.0 copy-done.11
  37.7 0.7 copy-done.12
  38.3 0.0 copy-done.13
  38.4 0.0 copy-start.10
  38.4 1.1 %copy-done.10 = f32[3,104,512]{2,1,0:T(8,128)S(1)} copy-done((f32[3,104,512]{2,1,0:T(8,128)S(1)}, f32[3,104,512]{2,1,0:T(8,128)}, u32[]{:S(2)}) %copy-start.10) | copy-done | bytes 639000
  39.5 0.0 copy-start
  39.5 0.0 copy-start.1
  39.5 0.0 copy-start.2
  39.5 0.0 copy-start.3
  39.5 0.0 copy-start.4
  39.5 0.0 copy-start.6
  39.5 11.6 %outside.1 = (f32[8,8,512]{2,1,0:T(8,128)S(1)}, f32[8,8,64]{2,1,0:T(8,128)S(1)}) custom-call(s32[68]{0:T(128)S(1)} %copy-done.12, s32[2]{0:T(128)S(1)} %copy-done.13, s32[8,8]{1,0:T(8,128)S(1)} %copy-done.11, f32[3,104,512]{2,1,0:T(8,128)S(1)} %pad_maximum_fusion.row_ref, f32[3,104,512]{2,1,0:T(8,128)S(1)} %copy-done.10, ...), custom_call_target="tpu_custom_call" | custom-call | flops 30000001024 | bytes 2097152 | tf_op jit(solution)/shard_map/outside/pallas_call | solution.py:470
  51.1 0.0 copy-start.7
  51.1 0.0 all-to-all-done.node_ref
  51.1 0.0 copy-start.8
  51.2 0.0 copy-done
  51.2 0.0 copy-done.1
  51.2 0.0 copy-done.2
  51.2 0.0 copy-done.3
  51.2 0.0 copy-done.4
  51.2 0.0 copy-done.6
  51.2 0.6 copy-done.7
  51.8 0.0 copy-done.8
  51.8 5.5 %tail.1 = (f32[8,4096]{1,0:T(8,128)S(1)}, f32[128,128]{1,0:T(8,128)S(1)}) custom-call(s32[2]{0:T(128)S(1)} %pad_add_fusion.place_ref, f32[8]{0:T(128)S(1)} %copy-done.8, f32[8,8,512]{2,1,0:T(8,128)S(1)} %copy-done.4, f32[8,8,512]{2,1,0:T(8,128)S(1)} %get-tuple-element.23.near_ref, f32[8,8,64]{2,1,0:T(8,128)S(1)} %get-tuple-element.24.far_ref, ...), custom_call_target="tpu_custom_call" | custom-call | tf_op jit(solution)/shard_map/tail/pallas_call | solution.py:486
  57.3 0.0 copy-start.5
  57.3 37.3 %all_to_all.16 = f32[128,1,128]{2,1,0:T(1,128)S(1)} all-to-all(f32[128,1,128]{2,1,0:T(1,128)S(1)} %bitcast.14), channel_id=1, replica_groups=mesh['leaf'=32,'tm'=4] {'leaf','tm'}, dimensions={0} | all-to-all | bytes 131072 | tf_op jit(solution)/shard_map/all_to_all | solution.py:499
  94.6 0.0 copy-done.5
  94.6 0.8 update.1
  (1 shorter events, 0.0 us)
Async XLA Ops:
  4.9 13.9 %collective-permute-start = (f32[104,512]{1,0:T(8,128)}, f32[104,512]{1,0:T(8,128)S(1)}, u32[]{:S(2)}, u32[]{:S(2)}) collective-permute-start(f32[104,512]{1,0:T(8,128)} %gather.1.halo_hbm), channel_id=1, source_target_pairs={{0,1},{1,2},{2,3},{4,5},{5,6},{6,7},{8,9},{9,10},{10,11},{12,13},{... | collective-permute-start | bytes 638984 | tf_op jit(solution)/shard_map/ppermute | solution.py:396
  8.9 9.9 %collective-permute-start.1 = (f32[104,512]{1,0:T(8,128)}, f32[104,512]{1,0:T(8,128)S(1)}, u32[]{:S(2)}, u32[]{:S(2)}) collective-permute-start(f32[104,512]{1,0:T(8,128)} %gather.1.halo_hbm), channel_id=1, source_target_pairs={{1,0},{2,1},{3,2},{5,4},{6,5},{7,6},{9,8},{10,9},{11,10},{13,12},{... | collective-permute-start | bytes 638984 | tf_op jit(solution)/shard_map/ppermute | solution.py:396
  10.2 8.7 %copy-start.14 = (f32[104,512]{1,0:T(8,128)S(1)}, f32[104,512]{1,0:T(8,128)}, u32[]{:S(2)}) copy-start(f32[104,512]{1,0:T(8,128)} %gather.1.halo_hbm) | copy-start | bytes 638980
  18.9 18.0 %collective-permute-start.2 = (f32[3,104,512]{2,1,0:T(8,128)S(1)}, f32[3,104,512]{2,1,0:T(8,128)S(1)}, u32[]{:S(2)}, u32[]{:S(2)}) collective-permute-start(f32[3,104,512]{2,1,0:T(8,128)S(1)} %pad_maximum_fusion.row_ref), channel_id=1, source_target_pairs={{0,4},{4,8},{8,12},{12,16},{16,20},{20,24},{24,28},{28,32},{32,36}... | collective-permute-start | bytes 1916936 | tf_op jit(solution)/shard_map/ppermute | solution.py:396
  22.9 14.8 %collective-permute-start.3 = (f32[3,104,512]{2,1,0:T(8,128)S(1)}, f32[3,104,512]{2,1,0:T(8,128)}, u32[]{:S(2)}, u32[]{:S(2)}) collective-permute-start(f32[3,104,512]{2,1,0:T(8,128)S(1)} %pad_maximum_fusion.row_ref), channel_id=1, source_target_pairs={{4,0},{8,4},{12,8},{16,12},{20,16},{24,20},{28,24},{32,28},{36,32}... | collective-permute-start | bytes 1916936 | tf_op jit(solution)/shard_map/ppermute | solution.py:396
  24.9 12.7 %copy-start.11 = (s32[8,8]{1,0:T(8,128)S(1)}, s32[8,8]{1,0:T(8,128)}, u32[]{:S(2)}) copy-start(s32[8,8]{1,0:T(8,128)} %far_ref.1) | copy-start | bytes 772
  24.9 26.2 %all-to-all-start = ((f32[128,8,128]{2,1,0:T(8,128)}), f32[128,8,128]{2,1,0:T(8,128)S(1)}, u32[]{:S(2)}, u32[]{:S(2)}) async-start(f32[128,8,128]{2,1,0:T(8,128)} %get-tuple-element.25), calls=%async_computation | async-start | bytes 1048576 | tf_op jit(solution)/shard_map/all_to_all | solution.py:464
  36.8 0.8 copy-start.9
  37.7 0.7 copy-start.12
  37.7 0.7 copy-start.13
  38.4 1.1 %copy-start.10 = (f32[3,104,512]{2,1,0:T(8,128)S(1)}, f32[3,104,512]{2,1,0:T(8,128)}, u32[]{:S(2)}) copy-start(f32[3,104,512]{2,1,0:T(8,128)} %copy-done.9) | copy-start | bytes 1916932
  39.5 11.7 %copy-start = (f32[8,64,512]{2,1,0:T(8,128)S(1)}, f32[8,64,512]{2,1,0:T(8,128)}, u32[]{:S(2)}) copy-start(f32[8,64,512]{2,1,0:T(8,128)} %bases_ref.1) | copy-start | bytes 3145732
  39.5 11.7 %copy-start.1 = (f32[8,4096]{1,0:T(8,128)S(1)}, f32[8,4096]{1,0:T(8,128)}, u32[]{:S(2)}) copy-start(f32[8,4096]{1,0:T(8,128)} %p_ref.3) | copy-start | bytes 393220
  39.5 11.7 %copy-start.2 = (f32[8,4096]{1,0:T(8,128)S(1)}, f32[8,4096]{1,0:T(8,128)}, u32[]{:S(2)}) copy-start(f32[8,4096]{1,0:T(8,128)} %res_ref.3) | copy-start | bytes 393220
  39.5 11.7 %copy-start.3 = (f32[1,64,512]{2,1,0:T(8,128)S(1)}, f32[1,64,512]{2,1,0:T(8,128)}, u32[]{:S(2)}) copy-start(f32[1,64,512]{2,1,0:T(8,128)} %param.19) | copy-start | bytes 393220
  39.5 11.7 %copy-start.4 = (f32[8,8,512]{2,1,0:T(8,128)S(1)}, f32[8,8,512]{2,1,0:T(8,128)}, u32[]{:S(2)}) copy-start(f32[8,8,512]{2,1,0:T(8,128)} %get-tuple-element.18.inside_ref) | copy-start | bytes 393220
  39.5 11.7 %copy-start.6 = (s32[32,128]{1,0:T(8,128)S(1)}, s32[32,128]{1,0:T(8,128)}, u32[]{:S(2)}) copy-start(s32[32,128]{1,0:T(8,128)} %get-tuple-element.27.inv_ref) | copy-start | bytes 49156
  51.1 0.7 copy-start.7
  51.1 0.7 copy-start.8
  57.3 37.3 %copy-start.5 = (f32[8,4096]{1,0:T(8,128)S(1)}, f32[8,4096]{1,0:T(8,128)}, u32[]{:S(2)}) copy-start(f32[8,4096]{1,0:T(8,128)} %it_ref.1) | copy-start | bytes 393220
